TPU v7x, 32 devices: a whole 2x2x4 slice. The times are simulated.
32 devices in a mesh: branch: 2 (over core), gi: 8 (over z, y), gj: 2 (over x).
Axes of the slice: x: 2, y: 2, z: 4, core: 2. Of those that a mesh axis runs over, the one named last changes fastest.
Arguments:
- homolog_embedding: float32 [32, 128, 256], P(('branch', 'gj'), 'gi'), may hold values from -6 to 6
- pair_input_tensor: float32 [128, 128, 128], P('gi', ('branch', 'gj')), may hold values from -6 to 6
- layernorm_scales: float32 [4, 256], replicated, may hold values from 0.5 to 1.5
- pair_norm_gains: float32 [3, 128], replicated, may hold values from 0.5 to 1.5
- pair_bias_matrix: float32 [128, 8], replicated
- horizontal_qkvg_kernel: float32 [256, 1024], replicated, may hold values from -0.375 to 0.375
- horizontal_final_kernel: float32 [256, 256], replicated, may hold values from -0.375 to 0.375
- vertical_qkvg_kernel: float32 [256, 1024], replicated, may hold values from -0.375 to 0.375
- vertical_final_kernel: float32 [256, 256], replicated, may hold values from -0.375 to 0.375
- feedforward_expand_kernel: float32 [256, 1024], replicated, may hold values from -0.375 to 0.375
- feedforward_shrink_kernel: float32 [1024, 256], replicated, may hold values from -0.1875 to 0.1875
- dyadic_sides_kernel: float32 [256, 64], replicated, may hold values from -0.375 to 0.375
- outer_output_matrix: float32 [1024, 128], replicated, may hold values from -1 to 1
- triangle_input_matrix: float32 [128, 640], replicated, may hold values from -0.5 to 0.5
- triangle_output_matrix: float32 [128, 128], replicated, may hold values from -0.5 to 0.5
Outputs:
- alignment_output: float32 [32, 128, 256], P(('branch', 'gj'), 'gi')
- pair_output_tensor: float32 [128, 128, 128], P('gi', ('branch', 'gj'))
All inputs are finite; a program needn't handle non-finite values.
Results may differ from a plain program's by a relative error of at most 0.0003.
Values sent between devices are 32-bit elements; how exact they have to be, the bound alone decides.
No kernel may reach another device: no remote copies, remote signals or barrier semaphores. Data moves between devices by JAX's collectives and lax.ppermute only.
A program may use at most 64 MiB of HBM per device.

v0:
```python
import functools
import math

import jax
import jax.numpy as jnp
from jax import lax
from jax.experimental import pallas as pl
from jax.experimental.pallas import tpu as pltpu
from jax.sharding import PartitionSpec as P

epsilon = 1e-05
precise = lax.Precision.HIGH
everyone = ("branch", "gi", "gj")
columns = ("branch", "gj")
lanes = 128
vmem = pl.BlockSpec(memory_space=pltpu.VMEM)
smem = pl.BlockSpec(memory_space=pltpu.SMEM)
params = pltpu.CompilerParams(vmem_limit_bytes=48 * 1024 * 1024)


def layer_normalise(values, norm_gain, axis=-1):
    average = jnp.mean(values, axis=axis, keepdims=True)
    centred = values - average
    variance = jnp.mean(centred * centred, axis=axis, keepdims=True)
    return centred * lax.rsqrt(variance + epsilon) * norm_gain


def apply_projection(values, weight):
    return jnp.einsum("...c,cd->...d", values, weight, precision=precise)


def sigmoid(values):
    return 1.0 / (1.0 + jnp.exp(-values))


def split(values):
    high = values.astype(jnp.bfloat16)
    return high, (values - high.astype(jnp.float32)).astype(jnp.bfloat16)


def multiply(left, right, across=False):
    numbers = (((1,), (1 if across else 0,)), ((), ()))

    def one(a, b):
        return lax.dot_general(a, b, numbers, preferred_element_type=jnp.float32)

    (lh, ll), (rh, rl) = split(left), split(right)
    return one(lh, rh) + (one(lh, rl) + one(ll, rh))


def swap_lane_groups(arrays):
    n, arrays = len(arrays), list(arrays)
    width = lanes // n
    wide = arrays[0].shape[-1]
    lane = lax.broadcasted_iota(jnp.int32, arrays[0].shape, arrays[0].ndim - 1)
    group = lax.rem(lane, lanes) // width
    axis = arrays[0].ndim - 1
    step = 1
    while step < n:
        upper = (group // step) % 2 == 1
        for low in range(n):
            if low & step:
                continue
            a, b = arrays[low], arrays[low + step]
            arrays[low] = jnp.where(upper, pltpu.roll(b, step * width, axis), a)
            arrays[low + step] = jnp.where(
                upper, b, pltpu.roll(a, wide - step * width, axis)
            )
        step *= 2
    return arrays


def head_masks(shape, heads):
    column = lax.broadcasted_iota(jnp.int32, shape, 1)
    return [column // (shape[1] // heads) == h for h in range(heads)]


def attend(query, key, value, bias, heads, allowed=None):
    count, inner = query.shape
    masks = head_masks((count, inner), heads)
    spread = jnp.concatenate([jnp.where(m, query, 0.0) for m in masks], axis=0)
    scores = multiply(spread, key, across=True) * (1.0 / math.sqrt(inner // heads))
    if bias is not None:
        scores = scores + bias
    if allowed is not None:
        scores = jnp.where(allowed, scores, -1e30)
    weights = jnp.exp(scores - jnp.max(scores, axis=-1, keepdims=True))
    weights = weights / jnp.sum(weights, axis=-1, keepdims=True)
    mixed = multiply(weights, value)
    result = jnp.where(masks[0], mixed[:count], 0.0)
    for h in range(1, heads):
        result = result + jnp.where(masks[h], mixed[h * count : (h + 1) * count], 0.0)
    return result


def spread(me, refs, slots):
    for k, ref in enumerate(refs):
        slots[me ^ k] = ref[...]


def spread_rows(me, refs, slots):
    for k, ref in enumerate(refs):
        count = ref.shape[0]
        slots[pl.ds(pl.multiple_of((me ^ k) * count, 8), count), :] = ref[...]


def bias_kernel(few, me_ref, pair_ref, gains_ref, matrix_ref, out_ref, *rest):
    chunks, slots = rest[:-1], rest[-1]
    residues, pair_cols, _ = pair_ref.shape
    heads = matrix_ref.shape[0]
    n_cols = len(chunks)
    groups = pair_cols // (n_cols * few)
    per = lanes // pair_cols
    normal = layer_normalise(pair_ref[...], gains_ref[0:1, :][None])
    for i in range(residues):
        here = multiply(matrix_ref[...], normal[i], across=True)
        for h in range(heads):
            out_ref[h // per, i : i + 1, pl.ds(h % per * pair_cols, pair_cols)] = here[h : h + 1]
    for c in range(n_cols):
        for o in range(groups):
            for f in range(few):
                start = (o * n_cols + c) * few + f
                slots[c, :, f * groups + o, :] = pair_ref[:, start, :]
    for k in range(n_cols):
        chunks[k][...] = slots[me_ref[0] ^ k]


def bias_rows_kernel(n_cols, me_ref, *rest):
    blocks, (out_ref, slots) = rest[:n_cols], rest[n_cols:]
    spread(me_ref[0], blocks, slots)
    count = slots.shape[1]
    per = out_ref.shape[0] // count
    for block in range(count):
        tiles = [[] for _ in range(per)]
        for tile in range(n_cols // per):
            group = [slots[c, block] for c in range(tile * per, (tile + 1) * per)]
            for k, piece in enumerate(swap_lane_groups(group)):
                tiles[k].append(piece)
        for k in range(per):
            out_ref[block * per + k] = jnp.concatenate(tiles[k], axis=1)


def row_kernel(n_branch, n_gj, per_part, few, me_ref, msa_ref, *rest):
    bias_refs, (gains_ref, qkvg_ref, final_ref, out_ref, slots) = (
        rest[:per_part],
        rest[per_part:],
    )
    _, residues, width = msa_ref.shape
    heads, _, length = bias_refs[0].shape
    n_gi = length // residues
    rows = msa_ref.shape[0] // n_gi
    inner = final_ref.shape[0]
    queries = per_part * residues
    gain = gains_ref[0:1, :]
    spread(me_ref[1], bias_refs, slots)
    bias = jnp.concatenate(
        [slots[g, h] for h in range(heads) for g in range(per_part)], axis=0
    )
    tokens = jnp.concatenate(
        [msa_ref[g * rows + r] for r in range(rows) for g in range(n_gi)], axis=0
    )
    first = me_ref[2] * (per_part * rows)
    asking = msa_ref[pl.ds(first, per_part * rows)]
    asking = jnp.concatenate(
        [asking[g * rows + r] for r in range(rows) for g in range(per_part)], axis=0
    )
    key_value = multiply(layer_normalise(tokens, gain), qkvg_ref[:, inner : 3 * inner])
    normal = layer_normalise(asking, gain)
    query = multiply(normal, qkvg_ref[:, :inner])
    gate = multiply(normal, qkvg_ref[:, 3 * inner :])
    attended = []
    for r in range(rows):
        keys = key_value[r * length : (r + 1) * length, :inner]
        values = key_value[r * length : (r + 1) * length, inner:]
        attended.append(
            attend(query[r * queries : (r + 1) * queries], keys, values, bias, heads)
        )
    attended = jnp.concatenate(attended, axis=0)
    result = asking + multiply(sigmoid(gate) * attended, final_ref[...])
    for b in range(n_branch):
        for g in range(per_part):
            for j in range(n_gj):
                start = g * residues + (b * n_gj + j) * few
                out_ref[(b * per_part + g) * n_gj + j] = jnp.concatenate(
                    [result[r * queries + start : r * queries + start + few] for r in range(rows)],
                    axis=0,
                )


def column_kernel(
    n_branch, n_gj, few, heads, me_ref, msa_ref, gains_ref, qkvg_ref, final_ref, expand_ref,
    shrink_ref, sides_ref, left_ref, right_ref, *rest
):
    count, width = msa_ref.shape
    inner = final_ref.shape[0]
    half = sides_ref.shape[0] // 2
    first = msa_ref[...]
    projected = multiply(layer_normalise(first, gains_ref[1:2, :]), qkvg_ref[...])
    query, key, value, gate = (projected[:, k * inner : (k + 1) * inner] for k in range(4))
    allowed = None
    if few > 1:
        shape = (heads * count, count)
        asks = lax.broadcasted_iota(jnp.int32, shape, 0)
        holds = lax.broadcasted_iota(jnp.int32, shape, 1)
        allowed = lax.rem(asks, few) == lax.rem(holds, few)
    attended = attend(query, key, value, None, heads, allowed)
    second = first + multiply(sigmoid(gate) * attended, final_ref[...])
    expanded = multiply(layer_normalise(second, gains_ref[2:3, :]), expand_ref[...])
    third = second + multiply(jnp.maximum(expanded, 0.0), shrink_ref[...])
    factors = multiply(sides_ref[...], layer_normalise(third, gains_ref[3:4, :]), across=True)
    left_ref[...] = factors[:half]
    for g in range(right_ref.shape[0]):
        right_ref[g] = factors[half:]
    chunks, slots = rest[:-1], rest[-1]
    per_part, each = slots.shape[1:3]
    for b in range(n_branch):
        for g in range(per_part):
            for j in range(n_gj):
                start = ((b * per_part + g) * n_gj + j) * each
                slots[b * n_gj + j, g] = third[start : start + each]
    for k, chunk in enumerate(chunks):
        chunk[...] = slots[me_ref[0] ^ k]


def alignment_kernel(n_cols, few, me_ref, *rest):
    blocks, (out_ref, slots) = rest[:n_cols], rest[n_cols:]
    spread(me_ref[0], blocks, slots)
    rows, residues, _ = out_ref.shape
    for r in range(rows):
        out_ref[r] = jnp.concatenate(
            [slots[c, r * few : (r + 1) * few] for c in range(n_cols)], axis=0
        )


def pair_kernel(
    few, n_gi, n_cols, me_ref, *rest
):
    left_refs, pair_refs = rest[:n_cols], rest[n_cols : 2 * n_cols]
    right_ref, gain_ref, matrix_ref, triangle_ref, tri_ref = rest[2 * n_cols : 2 * n_cols + 5]
    chunks = rest[2 * n_cols + 5 : 3 * n_cols + 5]
    left_ref, slots, pair_ref, first_ref, gate_ref = rest[3 * n_cols + 5 :]
    me = me_ref[0]
    groups_j = n_gi // n_cols
    spread(me, left_refs, left_ref)
    spread_rows(me, pair_refs, slots)
    _, wide, count = left_ref.shape
    block = pair_refs[0].shape[0]
    half = block // groups_j
    for c in range(n_cols):
        for o in range(groups_j):
            pair_ref[pl.ds(c * groups_j + o, half, stride=n_gi), :] = slots[
                pl.ds(c * block + o, half, stride=groups_j), :
            ]
    all_rows = count // few
    residues = n_cols * few
    pair_cols = n_gi * few
    per = lanes // pair_cols
    groups = residues // per
    width = pair_ref.shape[1]
    owner = lax.rem(lax.broadcasted_iota(jnp.int32, (1, count), 1), few)
    left = []
    for c in range(n_cols):
        here = left_ref[c]
        for f in range(few):
            own = jnp.where(owner == f, here, 0.0)
            total = own
            for other in range(few):
                if other != f:
                    total = total + pltpu.roll(own, (other - f) % count, 1)
            left.append(total)
    left = jnp.concatenate(left, axis=0) * (1.0 / all_rows)
    right = []
    for d in range(wide):
        here = right_ref[pl.ds(d, n_gi, stride=wide), :]
        right += [jnp.where(owner == f, here, 0.0) for f in range(few)]
    right = jnp.concatenate(right, axis=0)
    outer = multiply(left, right, across=True)
    outputs = []
    for g in range(groups):
        swapped = swap_lane_groups(
            [outer[(g * per + i) * wide : (g * per + i + 1) * wide] for i in range(per)]
        )
        stacked = [
            s[:, t * lanes : (t + 1) * lanes] for s in swapped for t in range(wide // per)
        ]
        outputs.append(jnp.concatenate(stacked, axis=0))
    update = multiply(matrix_ref[...], jnp.concatenate(outputs, axis=1))
    first = pair_ref[...].T + update
    projected = multiply(triangle_ref[...], layer_normalise(first, gain_ref[...], axis=0))
    tri = sigmoid(projected[2 * width : 4 * width]) * projected[: 2 * width]
    tri_ref[...] = tri.reshape(tri_ref.shape)
    first_ref[...] = first.T
    gate_ref[...] = sigmoid(projected[4 * width :]).T
    for k in range(n_cols):
        for o in range(groups_j):
            rows = pl.ds((me ^ k) * groups_j + o, half, stride=n_gi)
            chunks[k][pl.ds(o * half, half), :] = first_ref[rows, :]
            chunks[k][pl.ds(block + o * half, half), :] = gate_ref[rows, :]


def final_kernel(n_cols, few, residues, me_ref, product_ref, *rest):
    blocks, (gain_ref, matrix_ref, out_ref, slots, first_ref, gate_ref) = (
        rest[:n_cols],
        rest[n_cols:],
    )
    spread_rows(me_ref[0], blocks, slots)
    block = blocks[0].shape[0]
    pair_cols = product_ref.shape[1] // residues
    groups = pair_cols // (n_cols * few)
    for c in range(n_cols):
        for o in range(groups):
            for f in range(few):
                rows = pl.ds((o * n_cols + c) * few + f, residues, stride=pair_cols)
                start = c * block + o * residues * few + f
                first_ref[rows, :] = slots[pl.ds(start, residues, stride=few), :]
                start += block // 2
                gate_ref[rows, :] = slots[pl.ds(start, residues, stride=few), :]
    normal = layer_normalise(product_ref[...], gain_ref[...], axis=0)
    update = multiply(matrix_ref[...], normal)
    out_ref[...] = first_ref[...] + gate_ref[...] * update.T


def per_device(
    homolog_embedding,
    pair_input_tensor,
    layernorm_scales,
    pair_norm_gains,
    pair_bias_matrix,
    horizontal_qkvg_kernel,
    horizontal_final_kernel,
    vertical_qkvg_kernel,
    vertical_final_kernel,
    feedforward_expand_kernel,
    feedforward_shrink_kernel,
    dyadic_sides_kernel,
    outer_output_matrix,
    triangle_input_matrix,
    triangle_output_matrix,
):
    rows, residues, width = homolog_embedding.shape
    pair_cols, pair_width = pair_input_tensor.shape[1:]
    heads = pair_bias_matrix.shape[1]
    outer_width = dyadic_sides_kernel.shape[1] // 2
    n_branch, n_gi, n_gj = (lax.axis_size(name) for name in everyone)
    n_cols = n_branch * n_gj
    n_all = n_cols * n_gi
    length = residues * n_gi
    few = residues // n_cols
    groups = n_gi // n_cols
    parts = 2
    per_part = n_gi // parts
    own_rows = rows // per_part
    f32 = jnp.float32

    def call(kernel, outs, *operands, scratch=()):
        return pl.pallas_call(
            kernel,
            out_shape=[jax.ShapeDtypeStruct(shape, f32) for shape in outs],
            in_specs=[smem] + [vmem] * (len(operands) - 1),
            out_specs=[vmem] * len(outs),
            scratch_shapes=[pltpu.VMEM(shape, f32) for shape in scratch],
            compiler_params=params,
        )(*operands)

    def trade(blocks, axes):
        n = lax.axis_size(axes)
        return [blocks[0]] + [
            lax.ppermute(blocks[k], axes, [(t ^ k, t) for t in range(n) if t ^ k < n])
            for k in range(1, len(blocks))
        ]

    halves = [
        [
            (b * n_gi + part * per_part + g) * n_gj + j
            for b in range(n_branch)
            for g in range(per_part)
            for j in range(n_gj)
        ]
        for part in range(parts)
    ]
    n_half = n_cols * per_part
    mine = lax.axis_index("gi")
    me = jnp.stack([lax.axis_index(columns), mine % per_part, mine // per_part])
    me = me.astype(jnp.int32)
    positions = residues * pair_cols
    each = own_rows * few

    msa = lax.all_to_all(
        jnp.concatenate([homolog_embedding] * parts, axis=0), "gi", 0, 0, tiled=True
    )
    per = lanes // pair_cols
    bias_block = (heads // per, residues, lanes)
    bias, *pair = call(
        functools.partial(bias_kernel, few),
        [bias_block] + [(residues, groups * few, pair_width)] * n_cols,
        me,
        pair_input_tensor,
        pair_norm_gains,
        pair_bias_matrix.T,
        scratch=[(n_cols, residues, groups * few, pair_width)],
    )
    (bias,) = call(
        functools.partial(bias_rows_kernel, n_cols),
        [(heads, residues, length)],
        me,
        *trade([bias] * n_cols, columns),
        scratch=[(n_cols,) + bias_block],
    )
    bias = trade([bias] * per_part, "gi")
    pair = [block.reshape(-1, pair_width) for block in trade(pair, columns)]
    (msa_first,) = call(
        functools.partial(row_kernel, n_branch, n_gj, per_part, few),
        [(n_half, each, width)],
        me,
        msa,
        *bias,
        layernorm_scales,
        horizontal_qkvg_kernel,
        horizontal_final_kernel,
        scratch=[(per_part, heads, residues, length)],
    )

    msa_first = lax.all_to_all(msa_first, everyone, 0, 0, tiled=True, axis_index_groups=halves)
    count = n_half * each
    left, right, *alignment = call(
        functools.partial(column_kernel, n_branch, n_gj, few, heads),
        [(outer_width, count), (n_gi, outer_width, count)] + [(per_part, each, width)] * n_cols,
        me,
        msa_first.reshape(count, width),
        layernorm_scales,
        vertical_qkvg_kernel,
        vertical_final_kernel,
        feedforward_expand_kernel,
        feedforward_shrink_kernel,
        dyadic_sides_kernel.T,
        scratch=[(n_cols, per_part, each, width)],
    )
    right = lax.all_to_all(right, "gi", 0, 0, tiled=True)
    left = trade([left] * n_cols, columns)
    alignment = [block.reshape(-1, width) for block in trade(alignment, columns)]
    (alignment_output,) = call(
        functools.partial(alignment_kernel, n_cols, few),
        [(rows, residues, width)],
        me,
        *alignment,
        scratch=[(n_cols, rows * few, width)],
    )

    share = max(pair_width // n_all, 1)
    slots = pair_width // share
    triangle = triangle_input_matrix.T.reshape(5, slots, share, pair_width)
    sides = jnp.stack([triangle[0], triangle[2]], axis=1)
    gates = jnp.stack([triangle[1], triangle[3]], axis=1)
    triangle = jnp.concatenate(
        [side.reshape(2 * pair_width, pair_width) for side in (sides, gates)]
        + [triangle[4].reshape(pair_width, pair_width)],
        axis=0,
    )
    matrix = outer_output_matrix.reshape(outer_width, outer_width // per, per, pair_width)
    matrix = jnp.transpose(matrix, (3, 2, 1, 0)).reshape(pair_width, -1)
    tri, *first_gate = call(
        functools.partial(pair_kernel, few, n_gi, n_cols),
        [(slots, 2 * share, positions)]
        + [(2 * positions // n_cols, pair_width)] * n_cols,
        me,
        *left,
        *pair,
        right.reshape(n_gi * outer_width, count),
        pair_norm_gains[1][:, None],
        matrix,
        triangle,
        scratch=[
            (n_cols, outer_width, count),
            (positions, pair_width),
            (positions, pair_width),
            (positions, pair_width),
            (positions, pair_width),
        ],
    )

    if pair_width % n_all == 0:
        tri = lax.all_to_all(tri, everyone, 0, 0, tiled=True)
        tri = tri.reshape(n_branch, n_gi, n_gj, 2, share, residues, pair_cols)
        tri = jnp.transpose(tri, (3, 4, 1, 5, 0, 2, 6)).reshape(2, share, length, length)
        product = jnp.einsum("cik,cjk->cij", tri[0], tri[1], precision=precise)
        product = product.reshape(share, n_gi, residues, n_branch, n_gj, pair_cols)
        product = jnp.transpose(product, (3, 1, 4, 0, 2, 5)).reshape(
            n_all, share, positions
        )
        product = lax.all_to_all(product, everyone, 0, 0, tiled=True)
        product = product.reshape(pair_width, positions)
    else:
        tri = jnp.transpose(tri.reshape(slots, 2, share, positions), (1, 3, 0, 2))
        tri = tri.reshape(2, residues, pair_cols, pair_width)
        right_columns = lax.all_gather(tri[1], "gi", axis=0, tiled=True)
        product = lax.psum_scatter(
            jnp.einsum("jkc,ikc->jic", right_columns, tri[0], precision=precise),
            columns,
            scatter_dimension=0,
            tiled=True,
        )
        product = jnp.transpose(product, (2, 1, 0)).reshape(pair_width, positions)
    (pair_output_tensor,) = call(
        functools.partial(final_kernel, n_cols, few, residues),
        [(positions, pair_width)],
        me,
        product,
        *trade(first_gate, columns),
        pair_norm_gains[2][:, None],
        triangle_output_matrix.T,
        scratch=[
            (2 * positions, pair_width),
            (positions, pair_width),
            (positions, pair_width),
        ],
    )
    return (
        alignment_output,
        pair_output_tensor.reshape(residues, pair_cols, pair_width),
    )


def solution(mesh):
    tile, grid = P(("branch", "gj"), "gi", None), P("gi", ("branch", "gj"), None)
    return jax.shard_map(
        per_device,
        mesh=mesh,
        in_specs=(tile, grid) + (P(),) * 13,
        out_specs=(tile, grid),
        check_vma=False,
    )
```

profile of v0, /device:TPU:0, one launch (start us, length us, event | category | flops | bytes accessed | tf_op | source)
XLA Modules:
  0.0 126.3 jit_solution(9436915296190979576)
XLA Ops:
  0.6 1.7 %pad_maximum_fusion.1 = f32[16,16,256]{2,1,0:T(8,128)} fusion(f32[8,16,256]{2,1,0:T(8,128)} %param.15), kind=kLoop, calls=%fused_computation.1 | loop fusion | flops 65536 | bytes 393216 | tf_op jit(solution)/shard_map/concatenate | solution.py:389
  2.3 7.3 %all-to-all-start = ((f32[16,16,256]{2,1,0:T(8,128)}), f32[16,16,256]{2,1,0:T(8,128)S(1)}, u32[]{:S(2)}, u32[]{:S(2)}) async-start(f32[16,16,256]{2,1,0:T(8,128)} %pad_maximum_fusion.1), calls=%async_computation | async-start | bytes 524288 | tf_op jit(solution)/shard_map/all_to_all | solution.py:388
  12.0 1.9 %shard_map.158 = (f32[2,16,128]{2,1,0:T(8,128)S(1)}, f32[16,8,128]{2,1,0:T(8,128)S(1)}, f32[16,8,128]{2,1,0:T(8,128)}, f32[16,8,128]{2,1,0:T(8,128)}, f32[16,8,128]{2,1,0:T(8,128)S(1)}) custom-call(s32[3]{0:T(128)S(1)} %pad_add_fusion.me_ref, f32[16,32,128]{2,1,0:T(8,128)S(1)} %copy-done.6, f32[3,128]{1,0:T(4,128)S(1)} %copy-done.25, f32[8,128]{1,0:T(8,128)S(1)} %bitcast.47), custom_call_target="tpu_custom_call" | custom-call | tf_op jit(solution)/shard_map/pallas_call | solution.py:356
  14.5 1.5 %collective-permute-start = (f32[2,16,128]{2,1,0:T(8,128)S(1)}, f32[2,16,128]{2,1,0:T(8,128)S(1)}, u32[]{:S(2)}, u32[]{:S(2)}) collective-permute-start(f32[2,16,128]{2,1,0:T(8,128)S(1)} %get-tuple-element.18.rest_0_), channel_id=1, source_target_pairs={{1,0},{0,1},{17,16},{16,17},{3,2},{2,3},{19,18},{18,19},{5,4},{4,5... | collective-permute-start | bytes 49160 | tf_op jit(solution)/shard_map/ppermute | solution.py:368
  18.3 2.0 %copy.38 = f32[128,640]{0,1:T(8,128)} copy(f32[128,640]{1,0:T(8,128)} %param.28) | data formatting | bytes 655360 | tf_op args[13]
  25.7 2.1 %collective-permute-start.3 = (f32[8,16,128]{2,1,0:T(8,128)S(1)}, f32[8,16,128]{2,1,0:T(8,128)S(1)}, u32[]{:S(2)}, u32[]{:S(2)}) collective-permute-start(f32[8,16,128]{2,1,0:T(8,128)S(1)} %shard_map.159.rest_0_), channel_id=1, source_target_pairs={{2,0},{0,2},{6,4},{4,6},{10,8},{8,10},{14,12},{12,14},{3,1},{1,3},... | collective-permute-start | bytes 196616 | tf_op jit(solution)/shard_map/ppermute | solution.py:368
  29.3 1.7 %fusion.1 = (f32[128,128]{1,0:T(8,128)}, f32[128,128]{1,0:T(8,128)}, f32[128,128]{1,0:T(8,128)}, f32[128,128]{1,0:T(8,128)}, f32[128,128]{1,0:T(8,128)}) fusion(f32[640,128]{1,0:T(8,128)} %bitcast.51), kind=kLoop, calls=%fused_computation.8 | loop fusion | bytes 655360 | tf_op jit(solution)/shard_map/slice | solution.py:452
  39.7 3.6 %shard_map.160 = f32[16,8,256]{2,1,0:T(8,128)} custom-call(s32[3]{0:T(128)S(1)} %pad_add_fusion.me_ref, f32[16,16,256]{2,1,0:T(8,128)S(1)} %all-to-all-done.msa_ref, f32[8,16,128]{2,1,0:T(8,128)S(1)} %shard_map.159.rest_0_, f32[8,16,128]{2,1,0:T(8,128)S(1)} %copy-done.11, f32[8,16,128]{2,1,0:T(8,128)S(1)} %copy-done.13, f32[8,16,128]{2,1,0:T(8,128)S(1)} %copy-done.15, ...), custom_call_target="tpu_custom_call" | custom-call | tf_op jit(solution)/shard_map/pallas_call | solution.py:356
  43.3 3.5 %all-to-all-start.1 = ((f32[16,8,256]{2,1,0:T(8,128)}), f32[16,8,256]{2,1,0:T(8,128)S(1)}, u32[]{:S(2)}, u32[]{:S(2)}) async-start(f32[16,8,256]{2,1,0:T(8,128)} %shard_map.160), calls=%async_computation.1 | async-start | bytes 262144 | tf_op jit(solution)/shard_map/all_to_all | solution.py:423
  49.0 3.9 %all-to-all-done.1 = f32[16,8,256]{2,1,0:T(8,128)S(1)} async-done(((f32[16,8,256]{2,1,0:T(8,128)}), f32[16,8,256]{2,1,0:T(8,128)S(1)}, u32[]{:S(2)}, u32[]{:S(2)}) %all-to-all-start.1) | async-done | bytes 131104 | tf_op jit(solution)/shard_map/all_to_all | solution.py:423
  53.9 5.2 %shard_map.161 = (f32[32,128]{1,0:T(8,128)S(1)}, f32[8,32,128]{2,1,0:T(8,128)}, f32[4,8,256]{2,1,0:T(8,128)S(1)}, f32[4,8,256]{2,1,0:T(8,128)S(1)}, f32[4,8,256]{2,1,0:T(8,128)}, /*index=5*/f32[4,8,256]{2,1,0:T(8,128)S(1)}) custom-call(s32[3]{0:T(128)S(1)} %pad_add_fusion.me_ref, f32[128,256]{1,0:T(8,128)S(1)} %bitcast.39, f32[4,256]{1,0:T(4,128)S(1)} %copy-done.16, ...), custom_call_target="tpu_custom_call" | custom-call | tf_op jit(solution)/shard_map/pallas_call | solution.py:356
  59.7 3.9 %all-to-all-start.2 = ((f32[8,32,128]{2,1,0:T(8,128)}), f32[8,32,128]{2,1,0:T(8,128)S(1)}, u32[]{:S(2)}, u32[]{:S(2)}) async-start(f32[8,32,128]{2,1,0:T(8,128)} %get-tuple-element.28), calls=%async_computation.2 | async-start | bytes 262144 | tf_op jit(solution)/shard_map/all_to_all | solution.py:438
  65.2 1.5 %collective-permute-start.11 = (f32[32,128]{1,0:T(8,128)S(1)}, f32[32,128]{1,0:T(8,128)S(1)}, u32[]{:S(2)}, u32[]{:S(2)}) collective-permute-start(f32[32,128]{1,0:T(8,128)S(1)} %get-tuple-element.23.rest_0_), channel_id=1, source_target_pairs={{17,0},{16,1},{1,16},{0,17},{19,2},{18,3},{3,18},{2,19},{21,4},{20... | collective-permute-start | bytes 49160 | tf_op jit(solution)/shard_map/ppermute | solution.py:368
  69.5 1.5 %all-to-all-done.2 = f32[8,32,128]{2,1,0:T(8,128)S(1)} async-done(((f32[8,32,128]{2,1,0:T(8,128)}), f32[8,32,128]{2,1,0:T(8,128)S(1)}, u32[]{:S(2)}, u32[]{:S(2)}) %all-to-all-start.2) | async-done | bytes 131104 | tf_op jit(solution)/shard_map/all_to_all | solution.py:438
  71.0 4.4 %shard_map.163 = (f32[32,8,512]{2,1,0:T(8,128)S(1)}, f32[256,128]{1,0:T(8,128)S(1)}, f32[256,128]{1,0:T(8,128)S(1)}, f32[256,128]{1,0:T(8,128)S(1)}, f32[256,128]{1,0:T(8,128)S(1)}) custom-call(s32[3]{0:T(128)S(1)} %pad_add_fusion.me_ref, f32[32,128]{1,0:T(8,128)S(1)} %get-tuple-element.23.rest_0_, f32[32,128]{1,0:T(8,128)S(1)} %collective-permute-done.9.rest_1_, ...), custom_call_target="tpu_custom_call" | custom-call | tf_op jit(solution)/shard_map/pallas_call | solution.py:356
  75.4 20.3 %all_to_all.25 = f32[32,8,512]{2,1,0:T(8,128)S(1)} all-to-all(f32[32,8,512]{2,1,0:T(8,128)S(1)} %get-tuple-element.29), channel_id=1, replica_groups=mesh['branch'=2,'gi'=8,'gj'=2] {'branch','gi','gj'}, dimensions={0} | all-to-all | bytes 1048576 | tf_op jit(solution)/shard_map/all_to_all | solution.py:482
  95.7 1.9 %reshape.91 = f32[2,8,2,2,4,16,32]{6,5,4,3,2,1,0:T(8,128)} reshape(f32[32,8,512]{2,1,0:T(8,128)S(1)} %all_to_all.25) | data formatting | bytes 1048576 | tf_op jit(solution)/shard_map/reshape | solution.py:483
  97.6 1.7 %fusion = (f32[1,4,8,16,2,2,32]{6,3,1,0,5,2,4:T(8,128)S(1)}, f32[1,4,8,16,2,2,32]{6,3,1,0,5,2,4:T(8,128)S(1)}) fusion(f32[2,4,8,16,2,2,32]{6,3,1,0,5,2,4:T(8,128)} %bitcast.48), kind=kLoop, calls=%fused_computation.7 | loop fusion | bytes 1048576 | tf_op jit(solution)/shard_map/slice | solution.py:485
  105.1 2.6 %all-to-all-start.4 = ((f32[32,4,512]{2,1,0:T(4,128)}), f32[32,4,512]{2,1,0:T(4,128)S(1)}, u32[]{:S(2)}, u32[]{:S(2)}) async-start(f32[32,4,512]{2,1,0:T(4,128)} %reshape.93), calls=%async_computation.4 | async-start | bytes 524288 | tf_op jit(solution)/shard_map/all_to_all | solution.py:490
  107.7 1.7 %collective-permute-start.15 = (f32[256,128]{1,0:T(8,128)S(1)}, f32[256,128]{1,0:T(8,128)S(1)}, u32[]{:S(2)}, u32[]{:S(2)}) collective-permute-start(f32[256,128]{1,0:T(8,128)S(1)} %get-tuple-element.31), channel_id=1, source_target_pairs={{1,0},{0,1},{17,16},{16,17},{3,2},{2,3},{19,18},{18,19},{5,4},{4,5... | collective-permute-start | bytes 393224 | tf_op jit(solution)/shard_map/ppermute | solution.py:368
  109.9 1.6 %collective-permute-start.6 = (f32[4,8,256]{2,1,0:T(8,128)S(1)}, f32[4,8,256]{2,1,0:T(8,128)S(1)}, u32[]{:S(2)}, u32[]{:S(2)}) collective-permute-start(f32[4,8,256]{2,1,0:T(8,128)S(1)} %get-tuple-element.20), channel_id=1, source_target_pairs={{1,0},{0,1},{17,16},{16,17},{3,2},{2,3},{19,18},{18,19},{5,4},{4,5... | collective-permute-start | bytes 98312 | tf_op jit(solution)/shard_map/ppermute | solution.py:368
  111.5 8.0 %collective-permute-done.6 = f32[4,8,256]{2,1,0:T(8,128)S(1)} collective-permute-done((f32[4,8,256]{2,1,0:T(8,128)S(1)}, f32[4,8,256]{2,1,0:T(8,128)S(1)}, u32[]{:S(2)}, u32[]{:S(2)}) %collective-permute-start.6) | collective-permute-done | bytes 32800 | tf_op jit(solution)/shard_map/ppermute | solution.py:368
  119.8 3.1 %collective-permute-done.8 = f32[4,8,256]{2,1,0:T(8,128)S(1)} collective-permute-done((f32[4,8,256]{2,1,0:T(8,128)S(1)}, f32[4,8,256]{2,1,0:T(8,128)S(1)}, u32[]{:S(2)}, u32[]{:S(2)}) %collective-permute-start.8) | collective-permute-done | bytes 32800 | tf_op jit(solution)/shard_map/ppermute | solution.py:368
  124.2 2.1 %shard_map.164 = f32[512,128]{1,0:T(8,128)} custom-call(s32[3]{0:T(128)S(1)} %pad_add_fusion.me_ref, f32[128,512]{1,0:T(8,128)S(1)} %reshape.94.product_ref, f32[256,128]{1,0:T(8,128)S(1)} %get-tuple-element.30.rest_0_, f32[256,128]{1,0:T(8,128)S(1)} %collective-permute-done.15.rest_1_, f32[256,128]{1,0:T(8,128)S(1)} %collective-permute-done.16.rest_2_, ...), custom_call_target="tpu_custom_call" | custom-call | tf_op jit(solution)/shard_map/pallas_call | solution.py:356
  (122 shorter events, 36.6 us)
Async XLA Ops:
  2.3 32.7 %all-to-all-start = ((f32[16,16,256]{2,1,0:T(8,128)}), f32[16,16,256]{2,1,0:T(8,128)S(1)}, u32[]{:S(2)}, u32[]{:S(2)}) async-start(f32[16,16,256]{2,1,0:T(8,128)} %pad_maximum_fusion.1), calls=%async_computation | async-start | bytes 524288 | tf_op jit(solution)/shard_map/all_to_all | solution.py:388
  12.0 40.9 %copy-start.7 = (f32[256,64]{0,1:T(8,128)S(1)}, f32[256,64]{0,1:T(8,128)}, u32[]{:S(2)}) copy-start(f32[256,64]{0,1:T(8,128)} %param.26) | copy-start | bytes 196612
  14.5 5.7 %collective-permute-start = (f32[2,16,128]{2,1,0:T(8,128)S(1)}, f32[2,16,128]{2,1,0:T(8,128)S(1)}, u32[]{:S(2)}, u32[]{:S(2)}) collective-permute-start(f32[2,16,128]{2,1,0:T(8,128)S(1)} %get-tuple-element.18.rest_0_), channel_id=1, source_target_pairs={{1,0},{0,1},{17,16},{16,17},{3,2},{2,3},{19,18},{18,19},{5,4},{4,5... | collective-permute-start | bytes 49160 | tf_op jit(solution)/shard_map/ppermute | solution.py:368
  16.0 4.9 %collective-permute-start.1 = (f32[2,16,128]{2,1,0:T(8,128)S(1)}, f32[2,16,128]{2,1,0:T(8,128)S(1)}, u32[]{:S(2)}, u32[]{:S(2)}) collective-permute-start(f32[2,16,128]{2,1,0:T(8,128)S(1)} %get-tuple-element.18.rest_0_), channel_id=1, source_target_pairs={{16,0},{17,1},{0,16},{1,17},{18,2},{19,3},{2,18},{3,19},{20,4},{21... | collective-permute-start | bytes 49160 | tf_op jit(solution)/shard_map/ppermute | solution.py:368
  16.0 5.5 %collective-permute-start.2 = (f32[2,16,128]{2,1,0:T(8,128)S(1)}, f32[2,16,128]{2,1,0:T(8,128)S(1)}, u32[]{:S(2)}, u32[]{:S(2)}) collective-permute-start(f32[2,16,128]{2,1,0:T(8,128)S(1)} %get-tuple-element.18.rest_0_), channel_id=1, source_target_pairs={{17,0},{16,1},{1,16},{0,17},{19,2},{18,3},{3,18},{2,19},{21,4},{20... | collective-permute-start | bytes 49160 | tf_op jit(solution)/shard_map/ppermute | solution.py:368
  16.7 48.6 %collective-permute-start.12 = (f32[16,8,128]{2,1,0:T(8,128)}, f32[16,8,128]{2,1,0:T(8,128)}, u32[]{:S(2)}, u32[]{:S(2)}) collective-permute-start(f32[16,8,128]{2,1,0:T(8,128)} %get-tuple-element.25), channel_id=1, source_target_pairs={{1,0},{0,1},{17,16},{16,17},{3,2},{2,3},{19,18},{18,19},{5,4},{4,5... | collective-permute-start | bytes 196616 | tf_op jit(solution)/shard_map/ppermute | solution.py:368
  18.2 34.8 %copy-start.2 = (f32[1024,256]{1,0:T(8,128)S(1)}, f32[1024,256]{1,0:T(8,128)}, u32[]{:S(2)}) copy-start(f32[1024,256]{1,0:T(8,128)} %shrink_ref.1) | copy-start | bytes 3145732
  18.2 51.2 %collective-permute-start.13 = (f32[16,8,128]{2,1,0:T(8,128)}, f32[16,8,128]{2,1,0:T(8,128)}, u32[]{:S(2)}, u32[]{:S(2)}) collective-permute-start(f32[16,8,128]{2,1,0:T(8,128)} %get-tuple-element.26), channel_id=1, source_target_pairs={{16,0},{17,1},{0,16},{1,17},{18,2},{19,3},{2,18},{3,19},{20,4},{21... | collective-permute-start | bytes 196616 | tf_op jit(solution)/shard_map/ppermute | solution.py:368
  25.7 5.3 %collective-permute-start.3 = (f32[8,16,128]{2,1,0:T(8,128)S(1)}, f32[8,16,128]{2,1,0:T(8,128)S(1)}, u32[]{:S(2)}, u32[]{:S(2)}) collective-permute-start(f32[8,16,128]{2,1,0:T(8,128)S(1)} %shard_map.159.rest_0_), channel_id=1, source_target_pairs={{2,0},{0,2},{6,4},{4,6},{10,8},{8,10},{14,12},{12,14},{3,1},{1,3},... | collective-permute-start | bytes 196616 | tf_op jit(solution)/shard_map/ppermute | solution.py:368
  27.8 4.7 %collective-permute-start.4 = (f32[8,16,128]{2,1,0:T(8,128)S(1)}, f32[8,16,128]{2,1,0:T(8,128)S(1)}, u32[]{:S(2)}, u32[]{:S(2)}) collective-permute-start(f32[8,16,128]{2,1,0:T(8,128)S(1)} %shard_map.159.rest_0_), channel_id=1, source_target_pairs={{4,0},{6,2},{0,4},{2,6},{12,8},{14,10},{8,12},{10,14},{5,1},{7,3},... | collective-permute-start | bytes 196616 | tf_op jit(solution)/shard_map/ppermute | solution.py:368
  29.2 5.2 %collective-permute-start.5 = (f32[8,16,128]{2,1,0:T(8,128)S(1)}, f32[8,16,128]{2,1,0:T(8,128)S(1)}, u32[]{:S(2)}, u32[]{:S(2)}) collective-permute-start(f32[8,16,128]{2,1,0:T(8,128)S(1)} %shard_map.159.rest_0_), channel_id=1, source_target_pairs={{6,0},{4,2},{2,4},{0,6},{14,8},{12,10},{10,12},{8,14},{7,1},{5,3},... | collective-permute-start | bytes 196616 | tf_op jit(solution)/shard_map/ppermute | solution.py:368
  31.6 37.8 %collective-permute-start.14 = (f32[16,8,128]{2,1,0:T(8,128)}, f32[16,8,128]{2,1,0:T(8,128)}, u32[]{:S(2)}, u32[]{:S(2)}) collective-permute-start(f32[16,8,128]{2,1,0:T(8,128)} %copy-done.28), channel_id=1, source_target_pairs={{17,0},{16,1},{1,16},{0,17},{19,2},{18,3},{3,18},{2,19},{21,4},{20... | collective-permute-start | bytes 196616 | tf_op jit(solution)/shard_map/ppermute | solution.py:368
  43.3 9.6 %all-to-all-start.1 = ((f32[16,8,256]{2,1,0:T(8,128)}), f32[16,8,256]{2,1,0:T(8,128)S(1)}, u32[]{:S(2)}, u32[]{:S(2)}) async-start(f32[16,8,256]{2,1,0:T(8,128)} %shard_map.160), calls=%async_computation.1 | async-start | bytes 262144 | tf_op jit(solution)/shard_map/all_to_all | solution.py:423
  59.7 11.3 %all-to-all-start.2 = ((f32[8,32,128]{2,1,0:T(8,128)}), f32[8,32,128]{2,1,0:T(8,128)S(1)}, u32[]{:S(2)}, u32[]{:S(2)}) async-start(f32[8,32,128]{2,1,0:T(8,128)} %get-tuple-element.28), calls=%async_computation.2 | async-start | bytes 262144 | tf_op jit(solution)/shard_map/all_to_all | solution.py:438
  64.6 4.9 %collective-permute-start.9 = (f32[32,128]{1,0:T(8,128)S(1)}, f32[32,128]{1,0:T(8,128)S(1)}, u32[]{:S(2)}, u32[]{:S(2)}) collective-permute-start(f32[32,128]{1,0:T(8,128)S(1)} %get-tuple-element.23.rest_0_), channel_id=1, source_target_pairs={{1,0},{0,1},{17,16},{16,17},{3,2},{2,3},{19,18},{18,19},{5,4},{4,5... | collective-permute-start | bytes 49160 | tf_op jit(solution)/shard_map/ppermute | solution.py:368
  65.2 4.2 %collective-permute-start.10 = (f32[32,128]{1,0:T(8,128)S(1)}, f32[32,128]{1,0:T(8,128)S(1)}, u32[]{:S(2)}, u32[]{:S(2)}) collective-permute-start(f32[32,128]{1,0:T(8,128)S(1)} %get-tuple-element.23.rest_0_), channel_id=1, source_target_pairs={{16,0},{17,1},{0,16},{1,17},{18,2},{19,3},{2,18},{3,19},{20,4},{21... | collective-permute-start | bytes 49160 | tf_op jit(solution)/shard_map/ppermute | solution.py:368
  65.2 4.2 %collective-permute-start.11 = (f32[32,128]{1,0:T(8,128)S(1)}, f32[32,128]{1,0:T(8,128)S(1)}, u32[]{:S(2)}, u32[]{:S(2)}) collective-permute-start(f32[32,128]{1,0:T(8,128)S(1)} %get-tuple-element.23.rest_0_), channel_id=1, source_target_pairs={{17,0},{16,1},{1,16},{0,17},{19,2},{18,3},{3,18},{2,19},{21,4},{20... | collective-permute-start | bytes 49160 | tf_op jit(solution)/shard_map/ppermute | solution.py:368
  105.1 19.0 %all-to-all-start.4 = ((f32[32,4,512]{2,1,0:T(4,128)}), f32[32,4,512]{2,1,0:T(4,128)S(1)}, u32[]{:S(2)}, u32[]{:S(2)}) async-start(f32[32,4,512]{2,1,0:T(4,128)} %reshape.93), calls=%async_computation.4 | async-start | bytes 524288 | tf_op jit(solution)/shard_map/all_to_all | solution.py:490
  107.7 16.5 %collective-permute-start.15 = (f32[256,128]{1,0:T(8,128)S(1)}, f32[256,128]{1,0:T(8,128)S(1)}, u32[]{:S(2)}, u32[]{:S(2)}) collective-permute-start(f32[256,128]{1,0:T(8,128)S(1)} %get-tuple-element.31), channel_id=1, source_target_pairs={{1,0},{0,1},{17,16},{16,17},{3,2},{2,3},{19,18},{18,19},{5,4},{4,5... | collective-permute-start | bytes 393224 | tf_op jit(solution)/shard_map/ppermute | solution.py:368
  109.4 14.8 %collective-permute-start.16 = (f32[256,128]{1,0:T(8,128)S(1)}, f32[256,128]{1,0:T(8,128)S(1)}, u32[]{:S(2)}, u32[]{:S(2)}) collective-permute-start(f32[256,128]{1,0:T(8,128)S(1)} %get-tuple-element.32), channel_id=1, source_target_pairs={{16,0},{17,1},{0,16},{1,17},{18,2},{19,3},{2,18},{3,19},{20,4},{21... | collective-permute-start | bytes 393224 | tf_op jit(solution)/shard_map/ppermute | solution.py:368
  109.4 14.8 %collective-permute-start.17 = (f32[256,128]{1,0:T(8,128)S(1)}, f32[256,128]{1,0:T(8,128)S(1)}, u32[]{:S(2)}, u32[]{:S(2)}) collective-permute-start(f32[256,128]{1,0:T(8,128)S(1)} %get-tuple-element.33), channel_id=1, source_target_pairs={{17,0},{16,1},{1,16},{0,17},{19,2},{18,3},{3,18},{2,19},{21,4},{20... | collective-permute-start | bytes 393224 | tf_op jit(solution)/shard_map/ppermute | solution.py:368
  109.9 9.7 %collective-permute-start.6 = (f32[4,8,256]{2,1,0:T(8,128)S(1)}, f32[4,8,256]{2,1,0:T(8,128)S(1)}, u32[]{:S(2)}, u32[]{:S(2)}) collective-permute-start(f32[4,8,256]{2,1,0:T(8,128)S(1)} %get-tuple-element.20), channel_id=1, source_target_pairs={{1,0},{0,1},{17,16},{16,17},{3,2},{2,3},{19,18},{18,19},{5,4},{4,5... | collective-permute-start | bytes 98312 | tf_op jit(solution)/shard_map/ppermute | solution.py:368
  111.5 8.2 %collective-permute-start.7 = (f32[4,8,256]{2,1,0:T(8,128)}, f32[4,8,256]{2,1,0:T(8,128)S(1)}, u32[]{:S(2)}, u32[]{:S(2)}) collective-permute-start(f32[4,8,256]{2,1,0:T(8,128)} %get-tuple-element.21), channel_id=1, source_target_pairs={{16,0},{17,1},{0,16},{1,17},{18,2},{19,3},{2,18},{3,19},{20,4},{21... | collective-permute-start | bytes 98312 | tf_op jit(solution)/shard_map/ppermute | solution.py:368
  119.6 3.3 %collective-permute-start.8 = (f32[4,8,256]{2,1,0:T(8,128)S(1)}, f32[4,8,256]{2,1,0:T(8,128)S(1)}, u32[]{:S(2)}, u32[]{:S(2)}) collective-permute-start(f32[4,8,256]{2,1,0:T(8,128)S(1)} %copy-done.30), channel_id=1, source_target_pairs={{17,0},{16,1},{1,16},{0,17},{19,2},{18,3},{3,18},{2,19},{21,4},{20... | collective-permute-start | bytes 98312 | tf_op jit(solution)/shard_map/ppermute | solution.py:368
  (32 other events, 234.0 us)
where the time goes:
time: 128 us; the launch traced here: 126 us
  local copies, waits for them, and re-layouts  31.6 us (25%)
  starting transfers between devices  30.7 us (24%)
  blocking collectives  20.3 us (16%)
  Pallas kernels  19.1 us (15%)
  waiting for transfers between devices  18.7 us (15%)
  other arithmetic  4.52 us (4%)
    all_to_all x1, blocking collectives, per_device(): tri = lax.all_to_all(tri, everyone, 0, 0, tiled=True)  20.3 us
    pallas_call x7, Pallas kernels, call(): pl.pallas_call(kernel, out_shape=[jax.ShapeDtypeStruct(shape, f32) for sh...  19.1 us
    unnamed x70, local copies, waits for them, and re-layouts  17.9 us
    ppermute x18, starting transfers between devices, trade(): lax.ppermute(blocks[k], axes, [(t ^ k, t) for t in range(n) if t ^ k < n])  13.4 us
    ppermute x18, waiting for transfers between devices, trade(): lax.ppermute(blocks[k], axes, [(t ^ k, t) for t in range(n) if t ^ k < n])  13.3 us
    all_to_all x1, starting transfers between devices, per_device(): lax.all_to_all(jnp.concatenate([homolog_embedding] * parts, axis=0), 'gi'...  7.28 us
    all_to_all x1, starting transfers between devices, per_device(): right = lax.all_to_all(right, 'gi', 0, 0, tiled=True)  3.94 us
    all_to_all x1, waiting for transfers between devices, per_device(): lax.all_to_all(msa_first, everyone, 0, 0, tiled=True, axis_index_groups=h...  3.92 us
  transfers between devices with their start and end apart: 22, of which 6 were waited for; matrix products, arithmetic and copies ran while one was open for 8% of the time, Pallas kernels for 10%

commit v1 on v0

--- a/solution.py
+++ b/solution.py
@@ -15,7 +15,7 @@
 lanes = 128
 vmem = pl.BlockSpec(memory_space=pltpu.VMEM)
 smem = pl.BlockSpec(memory_space=pltpu.SMEM)
-params = pltpu.CompilerParams(vmem_limit_bytes=48 * 1024 * 1024)
+params = pltpu.CompilerParams(vmem_limit_bytes=16 * 1024 * 1024)
 
 
 def layer_normalise(values, norm_gain, axis=-1):
@@ -104,8 +104,11 @@
         slots[pl.ds(pl.multiple_of((me ^ k) * count, 8), count), :] = ref[...]
 
 
-def bias_kernel(few, me_ref, pair_ref, gains_ref, matrix_ref, out_ref, *rest):
+def bias_kernel(few, me_ref, msa_ref, pair_ref, gains_ref, matrix_ref, copies_ref, out_ref, *rest):
     chunks, slots = rest[:-1], rest[-1]
+    rows = msa_ref.shape[0]
+    for copy in range(copies_ref.shape[0] // rows):
+        copies_ref[pl.ds(copy * rows, rows)] = msa_ref[...]
     residues, pair_cols, _ = pair_ref.shape
     heads = matrix_ref.shape[0]
     n_cols = len(chunks)
@@ -222,14 +225,88 @@
         chunk[...] = slots[me_ref[0] ^ k]
 
 
-def alignment_kernel(n_cols, few, me_ref, *rest):
-    blocks, (out_ref, slots) = rest[:n_cols], rest[n_cols:]
-    spread(me_ref[0], blocks, slots)
-    rows, residues, _ = out_ref.shape
-    for r in range(rows):
-        out_ref[r] = jnp.concatenate(
-            [slots[c, r * few : (r + 1) * few] for c in range(n_cols)], axis=0
+def gather_tiles(few, me, alignment_refs, pair_refs, msa_out, pair_out, msa_slots, slots):
+    n_cols = len(alignment_refs)
+    spread(me, alignment_refs, msa_slots)
+    for r in range(msa_out.shape[0]):
+        msa_out[r] = jnp.concatenate(
+            [msa_slots[c, r * few : (r + 1) * few] for c in range(n_cols)], axis=0
         )
+    spread_rows(me, pair_refs, slots)
+    block = pair_refs[0].shape[0]
+    positions = n_cols * block // 2
+    residues = msa_out.shape[1]
+    groups = positions // (residues * few * n_cols)
+    count = residues * few
+    for c in range(n_cols):
+        for part in range(2):
+            for o in range(groups):
+                start = part * positions + o * n_cols + c
+                pair_out[pl.ds(start, count, stride=groups * n_cols), :] = slots[
+                    pl.ds(c * block + (part * groups + o) * count, count), :
+                ]
+
+
+def gather_kernel(few, n_cols, me_ref, *rest):
+    gather_tiles(few, me_ref[0], rest[:n_cols], rest[n_cols : 2 * n_cols], *rest[2 * n_cols :])
+
+
+def triangle_kernel(few, n_cols, me_ref, tri_ref, *rest):
+    blocks, (out_ref, msa_out, pair_out, product_ref, msa_slots, slots) = (
+        rest[: 2 * n_cols],
+        rest[2 * n_cols :],
+    )
+    gather_tiles(
+        few, me_ref[0], blocks[:n_cols], blocks[n_cols:], msa_out, pair_out, msa_slots, slots
+    )
+    n_all, rows, _ = out_ref.shape
+    n_gi = n_all // n_cols
+    share = few
+    tiles = rows // few
+    each = 2 * share
+    wide = lanes // few
+    group = lax.broadcasted_iota(jnp.int32, (n_gi * tiles, lanes), 1) // wide
+    products = []
+    for q in range(share):
+        left, right = [], []
+        for c in range(n_cols):
+            base = c * n_gi * tiles * each
+            here = jnp.concatenate(
+                [
+                    tri_ref[pl.ds(base + t * each + q, n_gi, stride=tiles * each), :]
+                    for t in range(tiles)
+                ],
+                axis=0,
+            )
+            left.append(
+                jnp.concatenate(
+                    [jnp.where(group == i, here, 0.0) for i in range(few)], axis=0
+                )
+            )
+            here = tri_ref[pl.ds(base + share + q, n_gi * tiles, stride=each), :]
+            rolled = [here] + [pltpu.roll(here, k * wide, 1) for k in range(1, few)]
+            copies = []
+            for j in range(few):
+                copy = rolled[0]
+                for k in range(1, few):
+                    copy = jnp.where(group == (j + k) % few, rolled[k], copy)
+                copies.append(copy)
+            step = n_gi * tiles // n_cols
+            right.append(
+                jnp.concatenate(
+                    [copy[k * step : (k + 1) * step] for k in range(n_cols) for copy in copies],
+                    axis=0,
+                )
+            )
+        products.append(
+            multiply(
+                jnp.concatenate(left, axis=1), jnp.concatenate(right, axis=1), across=True
+            )
+        )
+    for c, product in enumerate(swap_lane_groups(products)):
+        product_ref[...] = product
+        for g in range(n_gi):
+            out_ref[c * n_gi + g] = product_ref[pl.ds(g, rows, stride=n_gi), :]
 
 
 def pair_kernel(
@@ -288,7 +365,9 @@
     first = pair_ref[...].T + update
     projected = multiply(triangle_ref[...], layer_normalise(first, gain_ref[...], axis=0))
     tri = sigmoid(projected[2 * width : 4 * width]) * projected[: 2 * width]
-    tri_ref[...] = tri.reshape(tri_ref.shape)
+    slot_count, _, each, _ = tri_ref.shape
+    for g in range(groups):
+        tri_ref[:, g] = tri[:, g * lanes : (g + 1) * lanes].reshape(slot_count, each, lanes)
     first_ref[...] = first.T
     gate_ref[...] = sigmoid(projected[4 * width :]).T
     for k in range(n_cols):
@@ -298,26 +377,29 @@
             chunks[k][pl.ds(block + o * half, half), :] = gate_ref[rows, :]
 
 
-def final_kernel(n_cols, few, residues, me_ref, product_ref, *rest):
-    blocks, (gain_ref, matrix_ref, out_ref, slots, first_ref, gate_ref) = (
-        rest[:n_cols],
-        rest[n_cols:],
-    )
-    spread_rows(me_ref[0], blocks, slots)
-    block = blocks[0].shape[0]
-    pair_cols = product_ref.shape[1] // residues
-    groups = pair_cols // (n_cols * few)
-    for c in range(n_cols):
-        for o in range(groups):
-            for f in range(few):
-                rows = pl.ds((o * n_cols + c) * few + f, residues, stride=pair_cols)
-                start = c * block + o * residues * few + f
-                first_ref[rows, :] = slots[pl.ds(start, residues, stride=few), :]
-                start += block // 2
-                gate_ref[rows, :] = slots[pl.ds(start, residues, stride=few), :]
-    normal = layer_normalise(product_ref[...], gain_ref[...], axis=0)
-    update = multiply(matrix_ref[...], normal)
-    out_ref[...] = first_ref[...] + gate_ref[...] * update.T
+def final_kernel(few, n_cols, residues, packed, product_ref, pair_ref, gain_ref, matrix_ref, out_ref):
+    positions = out_ref.shape[0]
+    if packed:
+        tiles = residues // few
+        tall = product_ref.shape[0] // residues
+        product = []
+        for t in range(tiles):
+            here = [
+                product_ref[pl.ds(i * tiles + t, tall, stride=residues), :] for i in range(few)
+            ]
+            product.append(jnp.concatenate(swap_lane_groups(here), axis=0))
+        product = jnp.concatenate(product, axis=1)
+    else:
+        product = product_ref[...]
+    update = multiply(matrix_ref[...], layer_normalise(product, gain_ref[...], axis=0))
+    result = pair_ref[pl.ds(0, positions), :] + pair_ref[pl.ds(positions, positions), :] * update.T
+    count = positions // (residues * few)
+    for i in range(residues):
+        for f in range(few):
+            start = (i * few + f) * count
+            out_ref[pl.ds(i * few * count + f, count, stride=few), :] = result[
+                start : start + count
+            ]
 
 
 def per_device(
@@ -385,20 +467,20 @@
     positions = residues * pair_cols
     each = own_rows * few
 
-    msa = lax.all_to_all(
-        jnp.concatenate([homolog_embedding] * parts, axis=0), "gi", 0, 0, tiled=True
-    )
     per = lanes // pair_cols
     bias_block = (heads // per, residues, lanes)
-    bias, *pair = call(
+    msa, bias, *pair = call(
         functools.partial(bias_kernel, few),
-        [bias_block] + [(residues, groups * few, pair_width)] * n_cols,
+        [(parts * rows, residues, width), bias_block]
+        + [(residues, groups * few, pair_width)] * n_cols,
         me,
+        homolog_embedding,
         pair_input_tensor,
         pair_norm_gains,
         pair_bias_matrix.T,
         scratch=[(n_cols, residues, groups * few, pair_width)],
     )
+    msa = lax.all_to_all(msa, "gi", 0, 0, tiled=True)
     (bias,) = call(
         functools.partial(bias_rows_kernel, n_cols),
         [(heads, residues, length)],
@@ -438,14 +520,6 @@
     right = lax.all_to_all(right, "gi", 0, 0, tiled=True)
     left = trade([left] * n_cols, columns)
     alignment = [block.reshape(-1, width) for block in trade(alignment, columns)]
-    (alignment_output,) = call(
-        functools.partial(alignment_kernel, n_cols, few),
-        [(rows, residues, width)],
-        me,
-        *alignment,
-        scratch=[(n_cols, rows * few, width)],
-    )
-
     share = max(pair_width // n_all, 1)
     slots = pair_width // share
     triangle = triangle_input_matrix.T.reshape(5, slots, share, pair_width)
@@ -460,7 +534,7 @@
     matrix = jnp.transpose(matrix, (3, 2, 1, 0)).reshape(pair_width, -1)
     tri, *first_gate = call(
         functools.partial(pair_kernel, few, n_gi, n_cols),
-        [(slots, 2 * share, positions)]
+        [(slots, positions // lanes, 2 * share, lanes)]
         + [(2 * positions // n_cols, pair_width)] * n_cols,
         me,
         *left,
@@ -478,19 +552,37 @@
         ],
     )
 
-    if pair_width % n_all == 0:
-        tri = lax.all_to_all(tri, everyone, 0, 0, tiled=True)
-        tri = tri.reshape(n_branch, n_gi, n_gj, 2, share, residues, pair_cols)
-        tri = jnp.transpose(tri, (3, 4, 1, 5, 0, 2, 6)).reshape(2, share, length, length)
-        product = jnp.einsum("cik,cjk->cij", tri[0], tri[1], precision=precise)
-        product = product.reshape(share, n_gi, residues, n_branch, n_gj, pair_cols)
-        product = jnp.transpose(product, (3, 1, 4, 0, 2, 5)).reshape(
-            n_all, share, positions
+    first_gate = trade(first_gate, columns)
+    tiles = [(rows, residues, width), (2 * positions, pair_width)]
+    scratch = [(n_cols, rows * few, width), (2 * positions, pair_width)]
+    packed = share * n_all == pair_width and share == few and few == per
+    gain, last = pair_norm_gains[2], triangle_output_matrix
+    if packed:
+        order = [[(c // n_gj * n_gi + g) * n_gj + c % n_gj for c in range(n_cols) for g in range(n_gi)]]
+        tri = lax.all_to_all(tri, everyone, 0, 0, tiled=True, axis_index_groups=order)
+        product, alignment_output, first_gate = call(
+            functools.partial(triangle_kernel, few, n_cols),
+            [(n_all, residues, lanes)] + tiles,
+            me,
+            tri.reshape(-1, lanes),
+            *alignment,
+            *first_gate,
+            scratch=[(lanes, lanes)] + scratch,
         )
-        product = lax.all_to_all(product, everyone, 0, 0, tiled=True)
-        product = product.reshape(pair_width, positions)
+        product = lax.all_to_all(product, everyone, 0, 0, tiled=True, axis_index_groups=order)
+        product = product.reshape(n_all * residues, lanes)
+        gain = gain.reshape(n_all, share).T.reshape(-1)
+        last = jnp.swapaxes(last.reshape(n_all, share, pair_width), 0, 1).reshape(last.shape)
     else:
-        tri = jnp.transpose(tri.reshape(slots, 2, share, positions), (1, 3, 0, 2))
+        alignment_output, first_gate = call(
+            functools.partial(gather_kernel, few, n_cols),
+            tiles,
+            me,
+            *alignment,
+            *first_gate,
+            scratch=scratch,
+        )
+        tri = jnp.transpose(tri.reshape(slots, -1, 2, share, lanes), (2, 1, 4, 0, 3))
         tri = tri.reshape(2, residues, pair_cols, pair_width)
         right_columns = lax.all_gather(tri[1], "gi", axis=0, tiled=True)
         product = lax.psum_scatter(
@@ -498,22 +590,15 @@
             columns,
             scatter_dimension=0,
             tiled=True,
-        )
-        product = jnp.transpose(product, (2, 1, 0)).reshape(pair_width, positions)
-    (pair_output_tensor,) = call(
-        functools.partial(final_kernel, n_cols, few, residues),
-        [(positions, pair_width)],
-        me,
-        product,
-        *trade(first_gate, columns),
-        pair_norm_gains[2][:, None],
-        triangle_output_matrix.T,
-        scratch=[
-            (2 * positions, pair_width),
-            (positions, pair_width),
-            (positions, pair_width),
-        ],
-    )
+        ).reshape(groups, n_cols, few, residues, pair_width)
+        product = jnp.transpose(product, (4, 3, 2, 0, 1)).reshape(pair_width, positions)
+    (pair_output_tensor,) = pl.pallas_call(
+        functools.partial(final_kernel, few, n_cols, residues, packed),
+        out_shape=[jax.ShapeDtypeStruct((positions, pair_width), f32)],
+        in_specs=[vmem] * 4,
+        out_specs=[vmem],
+        compiler_params=params,
+    )(product, first_gate, gain[:, None], last.T)
     return (
         alignment_output,
         pair_output_tensor.reshape(residues, pair_cols, pair_width),

time: 128 us -> 112 us (0.88)
  blocking collectives: 20.3 us -> 0 us
  waiting for transfers between devices: 18.7 us -> 34.6 us
  local copies, waits for them, and re-layouts: 31.6 us -> 17.2 us
  starting transfers between devices: 30.7 us -> 38 us
  other arithmetic: 4.52 us -> 1.07 us
    all_to_all x1 -> x0, blocking collectives: 20.3 us -> none  [per_device(): tri = lax.all_to_all(tri, everyone, 0, 0, tiled=True)]
    all_to_all x2 -> x3, waiting for transfers between devices: 0.01 us -> 9.71 us  [the longest x1 9.7 us: per_device(): lax.all_to_all(product, everyone, 0, 0, tiled=True, axis_index_groups=order)]
    all_to_all x2 -> x3, starting transfers between devices: 9.87 us -> 16.2 us  [the longest x1 7.41 us: per_device(): msa = lax.all_to_all(msa, 'gi', 0, 0, tiled=True)]
    ppermute x18, waiting for transfers between devices: 13.3 us -> 18.4 us  [trade(): lax.ppermute(blocks[k], axes, [(t ^ k, t) for t in range(n) if t ^ k < n])]
    reshape x4 -> x1, local copies, waits for them, and re-layouts: 3.94 us -> 0.09 us  [per_device(): jnp.swapaxes(last.reshape(n_all, share, pair_width), 0, 1)]
    unnamed x70 -> x75, local copies, waits for them, and re-layouts: 17.9 us -> 14.1 us
    slice x3 -> x1, local copies, waits for them, and re-layouts: 3.31 us -> 0.59 us  [per_device(): gain, last = (pair_norm_gains[2], triangle_output_matrix)]
    concatenate x1 -> x0, other arithmetic: 1.7 us -> none  [per_device(): jnp.concatenate([homolog_embedding] * parts, axis=0)]
  transfers between devices with their start and end apart: 22 -> 23, of which waited for: 6 -> 11; matrix products, arithmetic and copies ran while one was open for 8% -> 4% of each run, Pallas kernels for 10% -> 8%
where the time goes in v1:
time: 112 us; the launch traced here: 111 us
  starting transfers between devices  38 us (34%)
  waiting for transfers between devices  34.6 us (31%)
  Pallas kernels  19.5 us (17%)
  local copies, waits for them, and re-layouts  17.2 us (15%)
    ppermute x18, waiting for transfers between devices, trade(): lax.ppermute(blocks[k], axes, [(t ^ k, t) for t in range(n) if t ^ k < n])  18.4 us
    pallas_call x6, Pallas kernels, call(): pl.pallas_call(kernel, out_shape=[jax.ShapeDtypeStruct(shape, f32) for sh...  18.2 us
    ppermute x18, starting transfers between devices, trade(): lax.ppermute(blocks[k], axes, [(t ^ k, t) for t in range(n) if t ^ k < n])  14.3 us
    unnamed x75, local copies, waits for them, and re-layouts  14.1 us
    all_to_all x1, waiting for transfers between devices, per_device(): lax.all_to_all(product, everyone, 0, 0, tiled=True, axis_index_groups=order)  9.7 us
    all_to_all x1, starting transfers between devices, per_device(): msa = lax.all_to_all(msa, 'gi', 0, 0, tiled=True)  7.41 us
    all_to_all x1, starting transfers between devices, per_device(): lax.all_to_all(product, everyone, 0, 0, tiled=True, axis_index_groups=order)  5.51 us
    all_to_all x1, starting transfers between devices, per_device(): right = lax.all_to_all(right, 'gi', 0, 0, tiled=True)  3.96 us
  transfers between devices with their start and end apart: 23, of which 11 were waited for; matrix products, arithmetic and copies ran while one was open for 4% of the time, Pallas kernels for 8%

profile of v1, /device:TPU:0, one launch (start us, length us, event | category | flops | bytes accessed | tf_op | source)
XLA Modules:
  0.0 111.3 jit_solution(1610642977082938881)
XLA Ops:
  3.2 2.0 %shard_map.158 = (f32[16,16,256]{2,1,0:T(8,128)}, f32[2,16,128]{2,1,0:T(8,128)S(1)}, f32[16,8,128]{2,1,0:T(8,128)S(1)}, f32[16,8,128]{2,1,0:T(8,128)}, f32[16,8,128]{2,1,0:T(8,128)}, /*index=5*/f32[16,8,128]{2,1,0:T(8,128)}) custom-call(s32[3]{0:T(128)S(1)} %pad_add_fusion.me_ref, f32[8,16,256]{2,1,0:T(8,128)S(1)} %copy-done.7, ...), custom_call_target="tpu_custom_call" | custom-call | tf_op jit(solution)/shard_map/pallas_call | solution.py:438
  5.8 7.4 %all-to-all-start = ((f32[16,16,256]{2,1,0:T(8,128)}), f32[16,16,256]{2,1,0:T(8,128)S(1)}, u32[]{:S(2)}, u32[]{:S(2)}) async-start(f32[16,16,256]{2,1,0:T(8,128)} %get-tuple-element.22), calls=%async_computation | async-start | bytes 524288 | tf_op jit(solution)/shard_map/all_to_all | solution.py:483
  13.2 1.5 %collective-permute-start = (f32[2,16,128]{2,1,0:T(8,128)S(1)}, f32[2,16,128]{2,1,0:T(8,128)S(1)}, u32[]{:S(2)}, u32[]{:S(2)}) collective-permute-start(f32[2,16,128]{2,1,0:T(8,128)S(1)} %get-tuple-element.23.rest_0_), channel_id=1, source_target_pairs={{1,0},{0,1},{17,16},{16,17},{3,2},{2,3},{19,18},{18,19},{5,4},{4,5... | collective-permute-start | bytes 49160 | tf_op jit(solution)/shard_map/ppermute | solution.py:450
  15.4 1.5 %collective-permute-start.9 = (f32[16,8,128]{2,1,0:T(8,128)}, f32[16,8,128]{2,1,0:T(8,128)}, u32[]{:S(2)}, u32[]{:S(2)}) collective-permute-start(f32[16,8,128]{2,1,0:T(8,128)} %get-tuple-element.26), channel_id=1, source_target_pairs={{1,0},{0,1},{17,16},{16,17},{3,2},{2,3},{19,18},{18,19},{5,4},{4,5... | collective-permute-start | bytes 196616 | tf_op jit(solution)/shard_map/ppermute | solution.py:450
  18.6 2.1 %collective-permute-start.3 = (f32[8,16,128]{2,1,0:T(8,128)S(1)}, f32[8,16,128]{2,1,0:T(8,128)S(1)}, u32[]{:S(2)}, u32[]{:S(2)}) collective-permute-start(f32[8,16,128]{2,1,0:T(8,128)S(1)} %shard_map.159.rest_0_), channel_id=1, source_target_pairs={{2,0},{0,2},{6,4},{4,6},{10,8},{8,10},{14,12},{12,14},{3,1},{1,3},... | collective-permute-start | bytes 196616 | tf_op jit(solution)/shard_map/ppermute | solution.py:450
  20.7 1.5 %collective-permute-start.4 = (f32[8,16,128]{2,1,0:T(8,128)S(1)}, f32[8,16,128]{2,1,0:T(8,128)S(1)}, u32[]{:S(2)}, u32[]{:S(2)}) collective-permute-start(f32[8,16,128]{2,1,0:T(8,128)S(1)} %shard_map.159.rest_0_), channel_id=1, source_target_pairs={{4,0},{6,2},{0,4},{2,6},{12,8},{14,10},{8,12},{10,14},{5,1},{7,3},... | collective-permute-start | bytes 196616 | tf_op jit(solution)/shard_map/ppermute | solution.py:450
  24.3 1.3 %collective-permute-done.4.rest_2_ = f32[8,16,128]{2,1,0:T(8,128)S(1)} collective-permute-done((f32[8,16,128]{2,1,0:T(8,128)S(1)}, f32[8,16,128]{2,1,0:T(8,128)S(1)}, u32[]{:S(2)}, u32[]{:S(2)}) %collective-permute-start.4) | collective-permute-done | bytes 65568 | tf_op jit(solution)/shard_map/ppermute | solution.py:450
  32.0 3.6 %shard_map.160 = f32[16,8,256]{2,1,0:T(8,128)} custom-call(s32[3]{0:T(128)S(1)} %pad_add_fusion.me_ref, f32[16,16,256]{2,1,0:T(8,128)S(1)} %all-to-all-done.msa_ref, f32[8,16,128]{2,1,0:T(8,128)S(1)} %shard_map.159.rest_0_, f32[8,16,128]{2,1,0:T(8,128)S(1)} %collective-permute-done.3.rest_1_, f32[8,16,128]{2,1,0:T(8,128)S(1)} %copy-done.13, ...), custom_call_target="tpu_custom_call" | custom-call | tf_op jit(solution)/shard_map/pallas_call | solution.py:438
  35.6 3.5 %all-to-all-start.1 = ((f32[16,8,256]{2,1,0:T(8,128)}), f32[16,8,256]{2,1,0:T(8,128)S(1)}, u32[]{:S(2)}, u32[]{:S(2)}) async-start(f32[16,8,256]{2,1,0:T(8,128)} %shard_map.160), calls=%async_computation.1 | async-start | bytes 262144 | tf_op jit(solution)/shard_map/all_to_all | solution.py:505
  41.4 3.9 %all-to-all-done.1 = f32[16,8,256]{2,1,0:T(8,128)S(1)} async-done(((f32[16,8,256]{2,1,0:T(8,128)}), f32[16,8,256]{2,1,0:T(8,128)S(1)}, u32[]{:S(2)}, u32[]{:S(2)}) %all-to-all-start.1) | async-done | bytes 131104 | tf_op jit(solution)/shard_map/all_to_all | solution.py:505
  46.1 4.5 %shard_map.161 = (f32[32,128]{1,0:T(8,128)S(1)}, f32[8,32,128]{2,1,0:T(8,128)S(1)}, f32[4,8,256]{2,1,0:T(8,128)S(1)}, f32[4,8,256]{2,1,0:T(8,128)S(1)}, f32[4,8,...) custom-call(s32[3]{0:T(128)S(1)} %pad_add_fusion.me_ref, f32[128,256]{1,0:T(8,128)S(1)} %bitcast.40, f32[4,256]{1,0:T(4,128)S(1)} %copy-done.20, ...), custom_call_target="tpu_custom_call" | custom-call | tf_op jit(solution)/shard_map/pallas_call | solution.py:438
  54.3 4.0 %all-to-all-start.2 = ((f32[8,32,128]{2,1,0:T(8,128)}), f32[8,32,128]{2,1,0:T(8,128)S(1)}, u32[]{:S(2)}, u32[]{:S(2)}) async-start(f32[8,32,128]{2,1,0:T(8,128)} %copy-done.8), calls=%async_computation.2 | async-start | bytes 262144 | tf_op jit(solution)/shard_map/all_to_all | solution.py:520
  59.7 1.5 %collective-permute-start.8 = (f32[32,128]{1,0:T(8,128)S(1)}, f32[32,128]{1,0:T(8,128)S(1)}, u32[]{:S(2)}, u32[]{:S(2)}) collective-permute-start(f32[32,128]{1,0:T(8,128)S(1)} %copy-done.19), channel_id=1, source_target_pairs={{17,0},{16,1},{1,16},{0,17},{19,2},{18,3},{3,18},{2,19},{21,4},{20... | collective-permute-start | bytes 49160 | tf_op jit(solution)/shard_map/ppermute | solution.py:450
  62.9 2.6 %all-to-all-done.2 = f32[8,32,128]{2,1,0:T(8,128)S(1)} async-done(((f32[8,32,128]{2,1,0:T(8,128)}), f32[8,32,128]{2,1,0:T(8,128)S(1)}, u32[]{:S(2)}, u32[]{:S(2)}) %all-to-all-start.2) | async-done | bytes 131104 | tf_op jit(solution)/shard_map/all_to_all | solution.py:520
  65.6 5.1 %shard_map.162 = (f32[32,4,8,128]{3,2,1,0:T(8,128)}, f32[256,128]{1,0:T(8,128)S(1)}, f32[256,128]{1,0:T(8,128)S(1)}, f32[256,128]{1,0:T(8,128)S(1)}, f32[256,128]{1,0:T(8,128)S(1)}) custom-call(s32[3]{0:T(128)S(1)} %pad_add_fusion.me_ref, f32[32,128]{1,0:T(8,128)S(1)} %copy-done.19, f32[32,128]{1,0:T(8,128)S(1)} %collective-permute-done.6.rest_1_, ...), custom_call_target="tpu_custom_call" | custom-call | tf_op jit(solution)/shard_map/pallas_call | solution.py:438
  70.7 3.3 %all-to-all-start.3 = ((f32[32,4,8,128]{3,2,1,0:T(8,128)}), f32[32,4,8,128]{3,2,1,0:T(8,128)S(1)}, u32[]{:S(2)}, u32[]{:S(2)}) async-start(f32[32,4,8,128]{3,2,1,0:T(8,128)} %get-tuple-element.30), calls=%async_computation.3 | async-start | bytes 1048576 | tf_op jit(solution)/shard_map/all_to_all | solution.py:562
  74.0 1.8 %collective-permute-start.15 = (f32[256,128]{1,0:T(8,128)S(1)}, f32[256,128]{1,0:T(8,128)S(1)}, u32[]{:S(2)}, u32[]{:S(2)}) collective-permute-start(f32[256,128]{1,0:T(8,128)S(1)} %get-tuple-element.36), channel_id=1, source_target_pairs={{1,0},{0,1},{17,16},{16,17},{3,2},{2,3},{19,18},{18,19},{5,4},{4,5... | collective-permute-start | bytes 393224 | tf_op jit(solution)/shard_map/ppermute | solution.py:450
  76.2 1.8 %collective-permute-start.12 = (f32[4,8,256]{2,1,0:T(8,128)S(1)}, f32[4,8,256]{2,1,0:T(8,128)S(1)}, u32[]{:S(2)}, u32[]{:S(2)}) collective-permute-start(f32[4,8,256]{2,1,0:T(8,128)S(1)} %copy-done.28), channel_id=1, source_target_pairs={{1,0},{0,1},{17,16},{16,17},{3,2},{2,3},{19,18},{18,19},{5,4},{4,5... | collective-permute-start | bytes 98312 | tf_op jit(solution)/shard_map/ppermute | solution.py:450
  78.0 10.2 %collective-permute-done.12 = f32[4,8,256]{2,1,0:T(8,128)S(1)} collective-permute-done((f32[4,8,256]{2,1,0:T(8,128)S(1)}, f32[4,8,256]{2,1,0:T(8,128)S(1)}, u32[]{:S(2)}, u32[]{:S(2)}) %collective-permute-start.12) | collective-permute-done | bytes 32800 | tf_op jit(solution)/shard_map/ppermute | solution.py:450
  88.1 3.3 %collective-permute-done.14 = f32[4,8,256]{2,1,0:T(8,128)S(1)} collective-permute-done((f32[4,8,256]{2,1,0:T(8,128)S(1)}, f32[4,8,256]{2,1,0:T(8,128)S(1)}, u32[]{:S(2)}, u32[]{:S(2)}) %collective-permute-start.14) | collective-permute-done | bytes 32800 | tf_op jit(solution)/shard_map/ppermute | solution.py:450
  91.5 2.3 %shard_map.163 = (f32[32,16,128]{2,1,0:T(8,128)}, f32[8,16,256]{2,1,0:T(8,128)}, f32[1024,128]{1,0:T(8,128)S(1)}) custom-call(s32[3]{0:T(128)S(1)} %pad_add_fusion.me_ref, f32[1024,128]{1,0:T(8,128)S(1)} %bitcast.37, f32[32,256]{1,0:T(8,128)S(1)} %bitcast.44, f32[32,256]{1,0:T(8,128)S(1)} %bitcast.45, f32[32,256]{1,0:T(8,128)S(1)} %bitcast.46, ...), custom_call_target="tpu_custom_call" | custom-call | tf_op jit(solution)/shard_map/pallas_call | solution.py:438
  93.8 5.5 %all-to-all-start.4 = ((f32[32,16,128]{2,1,0:T(8,128)}), f32[32,16,128]{2,1,0:T(8,128)S(1)}, u32[]{:S(2)}, u32[]{:S(2)}) async-start(f32[32,16,128]{2,1,0:T(8,128)} %get-tuple-element.40), calls=%async_computation.4 | async-start | bytes 524288 | tf_op jit(solution)/shard_map/all_to_all | solution.py:572
  100.3 9.7 %all-to-all-done.4 = f32[32,16,128]{2,1,0:T(8,128)S(1)} async-done(((f32[32,16,128]{2,1,0:T(8,128)}), f32[32,16,128]{2,1,0:T(8,128)S(1)}, u32[]{:S(2)}, u32[]{:S(2)}) %all-to-all-start.4) | async-done | bytes 262176 | tf_op jit(solution)/shard_map/all_to_all | solution.py:572
  110.0 1.3 %shard_map.164 = f32[512,128]{1,0:T(8,128)} custom-call(f32[512,128]{1,0:T(8,128)S(1)} %bitcast.38, f32[1024,128]{1,0:T(8,128)S(1)} %get-tuple-element.41.pair_ref, f32[128,1]{1,0:T(8,128)S(1)} %broadcast_in_dim_reshape.4.gain_ref, f32[128,128]{1,0:T(8,128)S(1)} %bitcast.41), custom_call_target="tpu_custom_call" | custom-call | tf_op jit(solution)/shard_map/pallas_call | solution.py:595
  (120 shorter events, 25.2 us)
Async XLA Ops:
  5.8 22.3 %all-to-all-start = ((f32[16,16,256]{2,1,0:T(8,128)}), f32[16,16,256]{2,1,0:T(8,128)S(1)}, u32[]{:S(2)}, u32[]{:S(2)}) async-start(f32[16,16,256]{2,1,0:T(8,128)} %get-tuple-element.22), calls=%async_computation | async-start | bytes 524288 | tf_op jit(solution)/shard_map/all_to_all | solution.py:483
  13.2 3.8 %collective-permute-start = (f32[2,16,128]{2,1,0:T(8,128)S(1)}, f32[2,16,128]{2,1,0:T(8,128)S(1)}, u32[]{:S(2)}, u32[]{:S(2)}) collective-permute-start(f32[2,16,128]{2,1,0:T(8,128)S(1)} %get-tuple-element.23.rest_0_), channel_id=1, source_target_pairs={{1,0},{0,1},{17,16},{16,17},{3,2},{2,3},{19,18},{18,19},{5,4},{4,5... | collective-permute-start | bytes 49160 | tf_op jit(solution)/shard_map/ppermute | solution.py:450
  14.7 2.3 %collective-permute-start.1 = (f32[2,16,128]{2,1,0:T(8,128)S(1)}, f32[2,16,128]{2,1,0:T(8,128)S(1)}, u32[]{:S(2)}, u32[]{:S(2)}) collective-permute-start(f32[2,16,128]{2,1,0:T(8,128)S(1)} %get-tuple-element.23.rest_0_), channel_id=1, source_target_pairs={{16,0},{17,1},{0,16},{1,17},{18,2},{19,3},{2,18},{3,19},{20,4},{21... | collective-permute-start | bytes 49160 | tf_op jit(solution)/shard_map/ppermute | solution.py:450
  14.7 3.2 %collective-permute-start.2 = (f32[2,16,128]{2,1,0:T(8,128)S(1)}, f32[2,16,128]{2,1,0:T(8,128)S(1)}, u32[]{:S(2)}, u32[]{:S(2)}) collective-permute-start(f32[2,16,128]{2,1,0:T(8,128)S(1)} %get-tuple-element.23.rest_0_), channel_id=1, source_target_pairs={{17,0},{16,1},{1,16},{0,17},{19,2},{18,3},{3,18},{2,19},{21,4},{20... | collective-permute-start | bytes 49160 | tf_op jit(solution)/shard_map/ppermute | solution.py:450
  15.4 44.3 %collective-permute-start.9 = (f32[16,8,128]{2,1,0:T(8,128)}, f32[16,8,128]{2,1,0:T(8,128)}, u32[]{:S(2)}, u32[]{:S(2)}) collective-permute-start(f32[16,8,128]{2,1,0:T(8,128)} %get-tuple-element.26), channel_id=1, source_target_pairs={{1,0},{0,1},{17,16},{16,17},{3,2},{2,3},{19,18},{18,19},{5,4},{4,5... | collective-permute-start | bytes 196616 | tf_op jit(solution)/shard_map/ppermute | solution.py:450
  16.9 45.0 %collective-permute-start.10 = (f32[16,8,128]{2,1,0:T(8,128)}, f32[16,8,128]{2,1,0:T(8,128)}, u32[]{:S(2)}, u32[]{:S(2)}) collective-permute-start(f32[16,8,128]{2,1,0:T(8,128)} %get-tuple-element.27), channel_id=1, source_target_pairs={{16,0},{17,1},{0,16},{1,17},{18,2},{19,3},{2,18},{3,19},{20,4},{21... | collective-permute-start | bytes 196616 | tf_op jit(solution)/shard_map/ppermute | solution.py:450
  18.6 4.7 %collective-permute-start.3 = (f32[8,16,128]{2,1,0:T(8,128)S(1)}, f32[8,16,128]{2,1,0:T(8,128)S(1)}, u32[]{:S(2)}, u32[]{:S(2)}) collective-permute-start(f32[8,16,128]{2,1,0:T(8,128)S(1)} %shard_map.159.rest_0_), channel_id=1, source_target_pairs={{2,0},{0,2},{6,4},{4,6},{10,8},{8,10},{14,12},{12,14},{3,1},{1,3},... | collective-permute-start | bytes 196616 | tf_op jit(solution)/shard_map/ppermute | solution.py:450
  20.7 4.9 %collective-permute-start.4 = (f32[8,16,128]{2,1,0:T(8,128)S(1)}, f32[8,16,128]{2,1,0:T(8,128)S(1)}, u32[]{:S(2)}, u32[]{:S(2)}) collective-permute-start(f32[8,16,128]{2,1,0:T(8,128)S(1)} %shard_map.159.rest_0_), channel_id=1, source_target_pairs={{4,0},{6,2},{0,4},{2,6},{12,8},{14,10},{8,12},{10,14},{5,1},{7,3},... | collective-permute-start | bytes 196616 | tf_op jit(solution)/shard_map/ppermute | solution.py:450
  22.2 5.3 %collective-permute-start.5 = (f32[8,16,128]{2,1,0:T(8,128)S(1)}, f32[8,16,128]{2,1,0:T(8,128)S(1)}, u32[]{:S(2)}, u32[]{:S(2)}) collective-permute-start(f32[8,16,128]{2,1,0:T(8,128)S(1)} %shard_map.159.rest_0_), channel_id=1, source_target_pairs={{6,0},{4,2},{2,4},{0,6},{14,8},{12,10},{10,12},{8,14},{7,1},{5,3},... | collective-permute-start | bytes 196616 | tf_op jit(solution)/shard_map/ppermute | solution.py:450
  22.2 23.0 %copy-start.2 = (f32[1024,256]{1,0:T(8,128)S(1)}, f32[1024,256]{1,0:T(8,128)}, u32[]{:S(2)}) copy-start(f32[1024,256]{1,0:T(8,128)} %shrink_ref.1) | copy-start | bytes 3145732
  23.4 38.5 %collective-permute-start.11 = (f32[16,8,128]{2,1,0:T(8,128)}, f32[16,8,128]{2,1,0:T(8,128)}, u32[]{:S(2)}, u32[]{:S(2)}) collective-permute-start(f32[16,8,128]{2,1,0:T(8,128)} %get-tuple-element.28), channel_id=1, source_target_pairs={{17,0},{16,1},{1,16},{0,17},{19,2},{18,3},{3,18},{2,19},{21,4},{20... | collective-permute-start | bytes 196616 | tf_op jit(solution)/shard_map/ppermute | solution.py:450
  35.6 9.6 %all-to-all-start.1 = ((f32[16,8,256]{2,1,0:T(8,128)}), f32[16,8,256]{2,1,0:T(8,128)S(1)}, u32[]{:S(2)}, u32[]{:S(2)}) async-start(f32[16,8,256]{2,1,0:T(8,128)} %shard_map.160), calls=%async_computation.1 | async-start | bytes 262144 | tf_op jit(solution)/shard_map/all_to_all | solution.py:505
  54.3 11.3 %all-to-all-start.2 = ((f32[8,32,128]{2,1,0:T(8,128)}), f32[8,32,128]{2,1,0:T(8,128)S(1)}, u32[]{:S(2)}, u32[]{:S(2)}) async-start(f32[8,32,128]{2,1,0:T(8,128)} %copy-done.8), calls=%async_computation.2 | async-start | bytes 262144 | tf_op jit(solution)/shard_map/all_to_all | solution.py:520
  59.0 3.9 %collective-permute-start.6 = (f32[32,128]{1,0:T(8,128)S(1)}, f32[32,128]{1,0:T(8,128)S(1)}, u32[]{:S(2)}, u32[]{:S(2)}) collective-permute-start(f32[32,128]{1,0:T(8,128)S(1)} %copy-done.19), channel_id=1, source_target_pairs={{1,0},{0,1},{17,16},{16,17},{3,2},{2,3},{19,18},{18,19},{5,4},{4,5... | collective-permute-start | bytes 49160 | tf_op jit(solution)/shard_map/ppermute | solution.py:450
  59.7 3.2 %collective-permute-start.7 = (f32[32,128]{1,0:T(8,128)S(1)}, f32[32,128]{1,0:T(8,128)S(1)}, u32[]{:S(2)}, u32[]{:S(2)}) collective-permute-start(f32[32,128]{1,0:T(8,128)S(1)} %copy-done.19), channel_id=1, source_target_pairs={{16,0},{17,1},{0,16},{1,17},{18,2},{19,3},{2,18},{3,19},{20,4},{21... | collective-permute-start | bytes 49160 | tf_op jit(solution)/shard_map/ppermute | solution.py:450
  59.7 3.3 %collective-permute-start.8 = (f32[32,128]{1,0:T(8,128)S(1)}, f32[32,128]{1,0:T(8,128)S(1)}, u32[]{:S(2)}, u32[]{:S(2)}) collective-permute-start(f32[32,128]{1,0:T(8,128)S(1)} %copy-done.19), channel_id=1, source_target_pairs={{17,0},{16,1},{1,16},{0,17},{19,2},{18,3},{3,18},{2,19},{21,4},{20... | collective-permute-start | bytes 49160 | tf_op jit(solution)/shard_map/ppermute | solution.py:450
  70.7 20.8 %all-to-all-start.3 = ((f32[32,4,8,128]{3,2,1,0:T(8,128)}), f32[32,4,8,128]{3,2,1,0:T(8,128)S(1)}, u32[]{:S(2)}, u32[]{:S(2)}) async-start(f32[32,4,8,128]{3,2,1,0:T(8,128)} %get-tuple-element.30), calls=%async_computation.3 | async-start | bytes 1048576 | tf_op jit(solution)/shard_map/all_to_all | solution.py:562
  74.0 17.5 %collective-permute-start.15 = (f32[256,128]{1,0:T(8,128)S(1)}, f32[256,128]{1,0:T(8,128)S(1)}, u32[]{:S(2)}, u32[]{:S(2)}) collective-permute-start(f32[256,128]{1,0:T(8,128)S(1)} %get-tuple-element.36), channel_id=1, source_target_pairs={{1,0},{0,1},{17,16},{16,17},{3,2},{2,3},{19,18},{18,19},{5,4},{4,5... | collective-permute-start | bytes 393224 | tf_op jit(solution)/shard_map/ppermute | solution.py:450
  75.8 15.7 %collective-permute-start.16 = (f32[256,128]{1,0:T(8,128)S(1)}, f32[256,128]{1,0:T(8,128)S(1)}, u32[]{:S(2)}, u32[]{:S(2)}) collective-permute-start(f32[256,128]{1,0:T(8,128)S(1)} %get-tuple-element.37), channel_id=1, source_target_pairs={{16,0},{17,1},{0,16},{1,17},{18,2},{19,3},{2,18},{3,19},{20,4},{21... | collective-permute-start | bytes 393224 | tf_op jit(solution)/shard_map/ppermute | solution.py:450
  75.8 15.7 %collective-permute-start.17 = (f32[256,128]{1,0:T(8,128)S(1)}, f32[256,128]{1,0:T(8,128)S(1)}, u32[]{:S(2)}, u32[]{:S(2)}) collective-permute-start(f32[256,128]{1,0:T(8,128)S(1)} %get-tuple-element.38), channel_id=1, source_target_pairs={{17,0},{16,1},{1,16},{0,17},{19,2},{18,3},{3,18},{2,19},{21,4},{20... | collective-permute-start | bytes 393224 | tf_op jit(solution)/shard_map/ppermute | solution.py:450
  76.2 12.0 %collective-permute-start.12 = (f32[4,8,256]{2,1,0:T(8,128)S(1)}, f32[4,8,256]{2,1,0:T(8,128)S(1)}, u32[]{:S(2)}, u32[]{:S(2)}) collective-permute-start(f32[4,8,256]{2,1,0:T(8,128)S(1)} %copy-done.28), channel_id=1, source_target_pairs={{1,0},{0,1},{17,16},{16,17},{3,2},{2,3},{19,18},{18,19},{5,4},{4,5... | collective-permute-start | bytes 98312 | tf_op jit(solution)/shard_map/ppermute | solution.py:450
  78.0 10.2 %collective-permute-start.13 = (f32[4,8,256]{2,1,0:T(8,128)S(1)}, f32[4,8,256]{2,1,0:T(8,128)S(1)}, u32[]{:S(2)}, u32[]{:S(2)}) collective-permute-start(f32[4,8,256]{2,1,0:T(8,128)S(1)} %copy-done.26), channel_id=1, source_target_pairs={{16,0},{17,1},{0,16},{1,17},{18,2},{19,3},{2,18},{3,19},{20,4},{21... | collective-permute-start | bytes 98312 | tf_op jit(solution)/shard_map/ppermute | solution.py:450
  88.1 3.3 %collective-permute-start.14 = (f32[4,8,256]{2,1,0:T(8,128)S(1)}, f32[4,8,256]{2,1,0:T(8,128)S(1)}, u32[]{:S(2)}, u32[]{:S(2)}) collective-permute-start(f32[4,8,256]{2,1,0:T(8,128)S(1)} %copy-done.24), channel_id=1, source_target_pairs={{17,0},{16,1},{1,16},{0,17},{19,2},{18,3},{3,18},{2,19},{21,4},{20... | collective-permute-start | bytes 98312 | tf_op jit(solution)/shard_map/ppermute | solution.py:450
  93.8 16.2 %all-to-all-start.4 = ((f32[32,16,128]{2,1,0:T(8,128)}), f32[32,16,128]{2,1,0:T(8,128)S(1)}, u32[]{:S(2)}, u32[]{:S(2)}) async-start(f32[32,16,128]{2,1,0:T(8,128)} %get-tuple-element.40), calls=%async_computation.4 | async-start | bytes 524288 | tf_op jit(solution)/shard_map/all_to_all | solution.py:572
  (36 other events, 163.5 us)

commit v2 on v1

--- a/solution.py
+++ b/solution.py
@@ -15,6 +15,7 @@
 lanes = 128
 vmem = pl.BlockSpec(memory_space=pltpu.VMEM)
 smem = pl.BlockSpec(memory_space=pltpu.SMEM)
+hbm = pl.BlockSpec(memory_space=pltpu.HBM)
 params = pltpu.CompilerParams(vmem_limit_bytes=16 * 1024 * 1024)
 
 
@@ -93,6 +94,18 @@
     return result
 
 
+def start_copies(pairs, sems):
+    copies = [pltpu.make_async_copy(a, b, sems.at[n]) for n, (a, b) in enumerate(pairs)]
+    for copy in copies:
+        copy.start()
+    return copies
+
+
+def wait_all(copies):
+    for copy in copies:
+        copy.wait()
+
+
 def spread(me, refs, slots):
     for k, ref in enumerate(refs):
         slots[me ^ k] = ref[...]
@@ -104,28 +117,42 @@
         slots[pl.ds(pl.multiple_of((me ^ k) * count, 8), count), :] = ref[...]
 
 
-def bias_kernel(few, me_ref, msa_ref, pair_ref, gains_ref, matrix_ref, copies_ref, out_ref, *rest):
-    chunks, slots = rest[:-1], rest[-1]
-    rows = msa_ref.shape[0]
-    for copy in range(copies_ref.shape[0] // rows):
-        copies_ref[pl.ds(copy * rows, rows)] = msa_ref[...]
+def bias_kernel(
+    msa_far, pair_far, gains_far, matrix_far, copies_far, out_ref, pair_ref, gains_ref, matrix_ref, sems
+):
+    rows = msa_far.shape[0]
+    repeats = copies_far.shape[0] // rows
+    copies = start_copies(
+        [(gains_far, gains_ref), (matrix_far, matrix_ref), (pair_far, pair_ref)]
+        + [(msa_far, copies_far.at[pl.ds(n * rows, rows)]) for n in range(repeats)],
+        sems,
+    )
     residues, pair_cols, _ = pair_ref.shape
     heads = matrix_ref.shape[0]
-    n_cols = len(chunks)
-    groups = pair_cols // (n_cols * few)
     per = lanes // pair_cols
+    wait_all(copies[:3])
     normal = layer_normalise(pair_ref[...], gains_ref[0:1, :][None])
     for i in range(residues):
         here = multiply(matrix_ref[...], normal[i], across=True)
         for h in range(heads):
             out_ref[h // per, i : i + 1, pl.ds(h % per * pair_cols, pair_cols)] = here[h : h + 1]
+    wait_all(copies[3:])
+
+
+def pair_blocks_kernel(few, residues, me_ref, pair_ref, *rest):
+    chunks, slots = rest[:-1], rest[-1]
+    n_cols = len(chunks)
+    block = chunks[0].shape[0]
+    groups = block // (residues * few)
     for c in range(n_cols):
         for o in range(groups):
             for f in range(few):
-                start = (o * n_cols + c) * few + f
-                slots[c, :, f * groups + o, :] = pair_ref[:, start, :]
+                source = pl.ds((o * n_cols + c) * few + f, residues, stride=groups * n_cols * few)
+                target = pl.ds(c * block + f * groups + o, residues, stride=few * groups)
+                slots[target, :] = pair_ref[source, :]
     for k in range(n_cols):
-        chunks[k][...] = slots[me_ref[0] ^ k]
+        start = pl.multiple_of((me_ref[0] ^ k) * block, 8)
+        chunks[k][...] = slots[pl.ds(start, block), :]
 
 
 def bias_rows_kernel(n_cols, me_ref, *rest):
@@ -144,21 +171,19 @@
 
 
 def row_kernel(n_branch, n_gj, per_part, few, me_ref, msa_ref, *rest):
-    bias_refs, (gains_ref, qkvg_ref, final_ref, out_ref, slots) = (
-        rest[:per_part],
-        rest[per_part:],
+    bias_refs, rest = rest[:per_part], rest[per_part:]
+    gains_far, qkvg_far, final_far, out_ref, slots, gains_ref, qkvg_ref, final_ref, sems = rest
+    copies = start_copies(
+        [(gains_far, gains_ref), (qkvg_far, qkvg_ref), (final_far, final_ref)]
+        + [(ref, slots.at[me_ref[1] ^ k]) for k, ref in enumerate(bias_refs)],
+        sems,
     )
     _, residues, width = msa_ref.shape
-    heads, _, length = bias_refs[0].shape
+    _, heads, _, length = slots.shape
     n_gi = length // residues
     rows = msa_ref.shape[0] // n_gi
     inner = final_ref.shape[0]
     queries = per_part * residues
-    gain = gains_ref[0:1, :]
-    spread(me_ref[1], bias_refs, slots)
-    bias = jnp.concatenate(
-        [slots[g, h] for h in range(heads) for g in range(per_part)], axis=0
-    )
     tokens = jnp.concatenate(
         [msa_ref[g * rows + r] for r in range(rows) for g in range(n_gi)], axis=0
     )
@@ -167,10 +192,18 @@
     asking = jnp.concatenate(
         [asking[g * rows + r] for r in range(rows) for g in range(per_part)], axis=0
     )
-    key_value = multiply(layer_normalise(tokens, gain), qkvg_ref[:, inner : 3 * inner])
-    normal = layer_normalise(asking, gain)
+    tokens = layer_normalise(tokens, 1.0)
+    normal = layer_normalise(asking, 1.0)
+    wait_all(copies[:2])
+    gain = gains_ref[0:1, :]
+    key_value = multiply(tokens * gain, qkvg_ref[:, inner : 3 * inner])
+    normal = normal * gain
     query = multiply(normal, qkvg_ref[:, :inner])
     gate = multiply(normal, qkvg_ref[:, 3 * inner :])
+    wait_all(copies[2:])
+    bias = jnp.concatenate(
+        [slots[g, h] for h in range(heads) for g in range(per_part)], axis=0
+    )
     attended = []
     for r in range(rows):
         keys = key_value[r * length : (r + 1) * length, :inner]
@@ -190,15 +223,20 @@
                 )
 
 
-def column_kernel(
-    n_branch, n_gj, few, heads, me_ref, msa_ref, gains_ref, qkvg_ref, final_ref, expand_ref,
-    shrink_ref, sides_ref, left_ref, right_ref, *rest
-):
+def column_kernel(n_branch, n_gj, few, heads, me_ref, msa_ref, *rest):
+    n_cols = n_branch * n_gj
+    far, rest = rest[:6], rest[6:]
+    left_far, right_far, chunks, rest = rest[0], rest[1], rest[2 : 2 + n_cols], rest[2 + n_cols :]
+    gains_ref, qkvg_ref, final_ref, expand_ref, shrink_ref, sides_ref = rest[:6]
+    slots, factors_ref, sems, out_sems = rest[6:]
+    copies = start_copies(list(zip(far, rest[:6])), sems)
     count, width = msa_ref.shape
     inner = final_ref.shape[0]
     half = sides_ref.shape[0] // 2
     first = msa_ref[...]
-    projected = multiply(layer_normalise(first, gains_ref[1:2, :]), qkvg_ref[...])
+    normal = layer_normalise(first, 1.0)
+    wait_all(copies[:2])
+    projected = multiply(normal * gains_ref[1:2, :], qkvg_ref[...])
     query, key, value, gate = (projected[:, k * inner : (k + 1) * inner] for k in range(4))
     allowed = None
     if few > 1:
@@ -207,14 +245,17 @@
         holds = lax.broadcasted_iota(jnp.int32, shape, 1)
         allowed = lax.rem(asks, few) == lax.rem(holds, few)
     attended = attend(query, key, value, None, heads, allowed)
+    wait_all(copies[2:])
     second = first + multiply(sigmoid(gate) * attended, final_ref[...])
     expanded = multiply(layer_normalise(second, gains_ref[2:3, :]), expand_ref[...])
     third = second + multiply(jnp.maximum(expanded, 0.0), shrink_ref[...])
-    factors = multiply(sides_ref[...], layer_normalise(third, gains_ref[3:4, :]), across=True)
-    left_ref[...] = factors[:half]
-    for g in range(right_ref.shape[0]):
-        right_ref[g] = factors[half:]
-    chunks, slots = rest[:-1], rest[-1]
+    factors_ref[...] = multiply(
+        sides_ref[...], layer_normalise(third, gains_ref[3:4, :]), across=True
+    )
+    pairs = [(factors_ref.at[pl.ds(0, half)], left_far)]
+    for g in range(right_far.shape[0]):
+        pairs.append((factors_ref.at[pl.ds(half, half)], right_far.at[g]))
+    copies = start_copies(pairs, out_sems)
     per_part, each = slots.shape[1:3]
     for b in range(n_branch):
         for g in range(per_part):
@@ -223,6 +264,7 @@
                 slots[b * n_gj + j, g] = third[start : start + each]
     for k, chunk in enumerate(chunks):
         chunk[...] = slots[me_ref[0] ^ k]
+    wait_all(copies)
 
 
 def gather_tiles(few, me, alignment_refs, pair_refs, msa_out, pair_out, msa_slots, slots):
@@ -314,20 +356,22 @@
 ):
     left_refs, pair_refs = rest[:n_cols], rest[n_cols : 2 * n_cols]
     right_ref, gain_ref, matrix_ref, triangle_ref, tri_ref = rest[2 * n_cols : 2 * n_cols + 5]
+    matrix_far, triangle_far = matrix_ref, triangle_ref
     chunks = rest[2 * n_cols + 5 : 3 * n_cols + 5]
-    left_ref, slots, pair_ref, first_ref, gate_ref = rest[3 * n_cols + 5 :]
+    rest = rest[3 * n_cols + 5 :]
+    left_ref, slots, pair_ref, first_ref, gate_ref, matrix_ref, triangle_ref, sems = rest
     me = me_ref[0]
     groups_j = n_gi // n_cols
-    spread(me, left_refs, left_ref)
-    spread_rows(me, pair_refs, slots)
+    block = pair_refs[0].shape[0]
+    pairs = [(ref, left_ref.at[me ^ k]) for k, ref in enumerate(left_refs)]
+    for k, ref in enumerate(pair_refs):
+        start = pl.multiple_of((me ^ k) * block, 8)
+        pairs.append((ref, slots.at[pl.ds(start, block)]))
+    pairs += [(matrix_far, matrix_ref), (triangle_far, triangle_ref)]
+    copies = start_copies(pairs, sems)
     _, wide, count = left_ref.shape
-    block = pair_refs[0].shape[0]
     half = block // groups_j
-    for c in range(n_cols):
-        for o in range(groups_j):
-            pair_ref[pl.ds(c * groups_j + o, half, stride=n_gi), :] = slots[
-                pl.ds(c * block + o, half, stride=groups_j), :
-            ]
+    wait_all(copies[:n_cols])
     all_rows = count // few
     residues = n_cols * few
     pair_cols = n_gi * few
@@ -361,6 +405,12 @@
             s[:, t * lanes : (t + 1) * lanes] for s in swapped for t in range(wide // per)
         ]
         outputs.append(jnp.concatenate(stacked, axis=0))
+    wait_all(copies[n_cols:])
+    for c in range(n_cols):
+        for o in range(groups_j):
+            pair_ref[pl.ds(c * groups_j + o, half, stride=n_gi), :] = slots[
+                pl.ds(c * block + o, half, stride=groups_j), :
+            ]
     update = multiply(matrix_ref[...], jnp.concatenate(outputs, axis=1))
     first = pair_ref[...].T + update
     projected = multiply(triangle_ref[...], layer_normalise(first, gain_ref[...], axis=0))
@@ -434,15 +484,25 @@
     own_rows = rows // per_part
     f32 = jnp.float32
 
-    def call(kernel, outs, *operands, scratch=()):
+    def call(kernel, outs, *operands, scratch=(), sems=()):
+        def bare(item):
+            return item[0] if isinstance(item, list) else item
+
+        def spec(item):
+            return hbm if isinstance(item, list) else vmem
+
         return pl.pallas_call(
             kernel,
-            out_shape=[jax.ShapeDtypeStruct(shape, f32) for shape in outs],
-            in_specs=[smem] + [vmem] * (len(operands) - 1),
-            out_specs=[vmem] * len(outs),
-            scratch_shapes=[pltpu.VMEM(shape, f32) for shape in scratch],
+            out_shape=[jax.ShapeDtypeStruct(bare(out), f32) for out in outs],
+            in_specs=[
+                smem if getattr(operand, "dtype", f32) == jnp.int32 else spec(operand)
+                for operand in operands
+            ],
+            out_specs=[spec(out) for out in outs],
+            scratch_shapes=[pltpu.VMEM(shape, f32) for shape in scratch]
+            + [pltpu.SemaphoreType.DMA((n,)) for n in sems],
             compiler_params=params,
-        )(*operands)
+        )(*[bare(operand) for operand in operands])
 
     def trade(blocks, axes):
         n = lax.axis_size(axes)
@@ -469,16 +529,15 @@
 
     per = lanes // pair_cols
     bias_block = (heads // per, residues, lanes)
-    msa, bias, *pair = call(
-        functools.partial(bias_kernel, few),
-        [(parts * rows, residues, width), bias_block]
-        + [(residues, groups * few, pair_width)] * n_cols,
-        me,
-        homolog_embedding,
-        pair_input_tensor,
-        pair_norm_gains,
-        pair_bias_matrix.T,
-        scratch=[(n_cols, residues, groups * few, pair_width)],
+    msa, bias = call(
+        bias_kernel,
+        [[(parts * rows, residues, width)], bias_block],
+        [homolog_embedding],
+        [pair_input_tensor],
+        [pair_norm_gains],
+        [pair_bias_matrix.T],
+        scratch=[pair_input_tensor.shape, pair_norm_gains.shape, (heads, pair_width)],
+        sems=[3 + parts],
     )
     msa = lax.all_to_all(msa, "gi", 0, 0, tiled=True)
     (bias,) = call(
@@ -489,34 +548,49 @@
         scratch=[(n_cols,) + bias_block],
     )
     bias = trade([bias] * per_part, "gi")
-    pair = [block.reshape(-1, pair_width) for block in trade(pair, columns)]
     (msa_first,) = call(
         functools.partial(row_kernel, n_branch, n_gj, per_part, few),
         [(n_half, each, width)],
         me,
         msa,
-        *bias,
-        layernorm_scales,
-        horizontal_qkvg_kernel,
-        horizontal_final_kernel,
-        scratch=[(per_part, heads, residues, length)],
-    )
+        *[[block] for block in bias],
+        [layernorm_scales],
+        [horizontal_qkvg_kernel],
+        [horizontal_final_kernel],
+        scratch=[(per_part, heads, residues, length)]
+        + [w.shape for w in (layernorm_scales, horizontal_qkvg_kernel, horizontal_final_kernel)],
+        sems=[3 + per_part],
+    )
+    pair, msa_first = lax.optimization_barrier((pair_input_tensor, msa_first))
 
     msa_first = lax.all_to_all(msa_first, everyone, 0, 0, tiled=True, axis_index_groups=halves)
     count = n_half * each
-    left, right, *alignment = call(
-        functools.partial(column_kernel, n_branch, n_gj, few, heads),
-        [(outer_width, count), (n_gi, outer_width, count)] + [(per_part, each, width)] * n_cols,
-        me,
-        msa_first.reshape(count, width),
+    weights = (
         layernorm_scales,
         vertical_qkvg_kernel,
         vertical_final_kernel,
         feedforward_expand_kernel,
         feedforward_shrink_kernel,
         dyadic_sides_kernel.T,
-        scratch=[(n_cols, per_part, each, width)],
-    )
+    )
+    left, right, *alignment = call(
+        functools.partial(column_kernel, n_branch, n_gj, few, heads),
+        [[(outer_width, count)], [(n_gi, outer_width, count)]] + [(per_part, each, width)] * n_cols,
+        me,
+        msa_first.reshape(count, width),
+        *[[w] for w in weights],
+        scratch=[w.shape for w in weights]
+        + [(n_cols, per_part, each, width), (2 * outer_width, count)],
+        sems=[len(weights), 1 + n_gi],
+    )
+    pair = call(
+        functools.partial(pair_blocks_kernel, few, residues),
+        [(positions // n_cols, pair_width)] * n_cols,
+        me,
+        pair.reshape(positions, pair_width),
+        scratch=[(positions, pair_width)],
+    )
+    pair = trade(pair, columns)
     right = lax.all_to_all(right, "gi", 0, 0, tiled=True)
     left = trade([left] * n_cols, columns)
     alignment = [block.reshape(-1, width) for block in trade(alignment, columns)]
@@ -537,19 +611,21 @@
         [(slots, positions // lanes, 2 * share, lanes)]
         + [(2 * positions // n_cols, pair_width)] * n_cols,
         me,
-        *left,
-        *pair,
+        *[[block] for block in left + pair],
         right.reshape(n_gi * outer_width, count),
         pair_norm_gains[1][:, None],
-        matrix,
-        triangle,
+        [matrix],
+        [triangle],
         scratch=[
             (n_cols, outer_width, count),
             (positions, pair_width),
             (positions, pair_width),
             (positions, pair_width),
             (positions, pair_width),
+            matrix.shape,
+            triangle.shape,
         ],
+        sems=[2 * n_cols + 2],
     )
 
     first_gate = trade(first_gate, columns)

time: 112 us -> 117 us (1.045)
  starting transfers between devices: 38 us -> 41.3 us
  waiting for transfers between devices: 34.6 us -> 32 us
  Pallas kernels: 19.5 us -> 21.4 us
  local copies, waits for them, and re-layouts: 17.2 us -> 18.8 us
    all_to_all x1, waiting for transfers between devices: 3.86 us -> 0.84 us  [per_device(): lax.all_to_all(msa_first, everyone, 0, 0, tiled=True, axis_index_groups=h...]
    ppermute x18, waiting for transfers between devices: 18.4 us -> 21.3 us  [trade(): lax.ppermute(blocks[k], axes, [(t ^ k, t) for t in range(n) if t ^ k < n])]
    all_to_all x1, starting transfers between devices: 3.29 us -> 5.91 us  [per_device(): lax.all_to_all(tri, everyone, 0, 0, tiled=True, axis_index_groups=order)]
    all_to_all x1, waiting for transfers between devices: 2.65 us -> 0.2 us  [per_device(): right = lax.all_to_all(right, 'gi', 0, 0, tiled=True)]
    unnamed x75 -> x85, local copies, waits for them, and re-layouts: 14.1 us -> 16.3 us
    pallas_call x6 -> x7, Pallas kernels: 18.2 us -> 20.1 us  [call(): pl.pallas_call(kernel, out_shape=[jax.ShapeDtypeStruct(bare(out), f32) fo...]
  transfers between devices with their start and end apart: 23 -> 23, of which waited for: 11 -> 13; matrix products, arithmetic and copies ran while one was open for 4% -> 3% of each run, Pallas kernels for 8% -> 6%
where the time goes in v2:
time: 117 us; the launch traced here: 116 us
  starting transfers between devices  41.3 us (35%)
  waiting for transfers between devices  32 us (27%)
  Pallas kernels  21.4 us (18%)
  local copies, waits for them, and re-layouts  18.8 us (16%)
    ppermute x18, waiting for transfers between devices, trade(): lax.ppermute(blocks[k], axes, [(t ^ k, t) for t in range(n) if t ^ k < n])  21.3 us
    pallas_call x7, Pallas kernels, call(): pl.pallas_call(kernel, out_shape=[jax.ShapeDtypeStruct(bare(out), f32) fo...  20.1 us
    unnamed x85, local copies, waits for them, and re-layouts  16.3 us
    ppermute x18, starting transfers between devices, trade(): lax.ppermute(blocks[k], axes, [(t ^ k, t) for t in range(n) if t ^ k < n])  13.9 us
    all_to_all x1, waiting for transfers between devices, per_device(): lax.all_to_all(product, everyone, 0, 0, tiled=True, axis_index_groups=order)  9.7 us
    all_to_all x1, starting transfers between devices, per_device(): msa = lax.all_to_all(msa, 'gi', 0, 0, tiled=True)  7.42 us
    all_to_all x1, starting transfers between devices, per_device(): lax.all_to_all(tri, everyone, 0, 0, tiled=True, axis_index_groups=order)  5.91 us
    all_to_all x1, starting transfers between devices, per_device(): lax.all_to_all(product, everyone, 0, 0, tiled=True, axis_index_groups=order)  5.51 us
  transfers between devices with their start and end apart: 23, of which 13 were waited for; matrix products, arithmetic and copies ran while one was open for 3% of the time, Pallas kernels for 6%

profile of v2, /device:TPU:0, one launch (start us, length us, event | category | flops | bytes accessed | tf_op | source)
XLA Modules:
  0.0 115.6 jit_solution(5511683398347780672)
XLA Ops:
  4.6 7.4 %all-to-all-start = ((f32[16,16,256]{2,1,0:T(8,128)}), f32[16,16,256]{2,1,0:T(8,128)S(1)}, u32[]{:S(2)}, u32[]{:S(2)}) async-start(f32[16,16,256]{2,1,0:T(8,128)} %get-tuple-element.24), calls=%async_computation | async-start | bytes 524288 | tf_op jit(solution)/shard_map/all_to_all | solution.py:542
  12.1 1.5 %collective-permute-start = (f32[2,16,128]{2,1,0:T(8,128)S(1)}, f32[2,16,128]{2,1,0:T(8,128)S(1)}, u32[]{:S(2)}, u32[]{:S(2)}) collective-permute-start(f32[2,16,128]{2,1,0:T(8,128)S(1)} %get-tuple-element.25.rest_0_), channel_id=1, source_target_pairs={{1,0},{0,1},{17,16},{16,17},{3,2},{2,3},{19,18},{18,19},{5,4},{4,5... | collective-permute-start | bytes 49160 | tf_op jit(solution)/shard_map/ppermute | solution.py:510
  14.4 1.4 %collective-permute-done.rest_1_ = f32[2,16,128]{2,1,0:T(8,128)S(1)} collective-permute-done((f32[2,16,128]{2,1,0:T(8,128)S(1)}, f32[2,16,128]{2,1,0:T(8,128)S(1)}, u32[]{:S(2)}, u32[]{:S(2)}) %collective-permute-start) | collective-permute-done | bytes 16416 | tf_op jit(solution)/shard_map/ppermute | solution.py:510
  17.4 2.1 %collective-permute-start.3 = (f32[8,16,128]{2,1,0:T(8,128)S(1)}, f32[8,16,128]{2,1,0:T(8,128)S(1)}, u32[]{:S(2)}, u32[]{:S(2)}) collective-permute-start(f32[8,16,128]{2,1,0:T(8,128)S(1)} %shard_map.159.rest_0_), channel_id=1, source_target_pairs={{2,0},{0,2},{6,4},{4,6},{10,8},{8,10},{14,12},{12,14},{3,1},{1,3},... | collective-permute-start | bytes 196616 | tf_op jit(solution)/shard_map/ppermute | solution.py:510
  19.5 1.5 %collective-permute-start.4 = (f32[8,16,128]{2,1,0:T(8,128)S(1)}, f32[8,16,128]{2,1,0:T(8,128)S(1)}, u32[]{:S(2)}, u32[]{:S(2)}) collective-permute-start(f32[8,16,128]{2,1,0:T(8,128)S(1)} %shard_map.159.rest_0_), channel_id=1, source_target_pairs={{4,0},{6,2},{0,4},{2,6},{12,8},{14,10},{8,12},{10,14},{5,1},{7,3},... | collective-permute-start | bytes 196616 | tf_op jit(solution)/shard_map/ppermute | solution.py:510
  22.4 1.9 %collective-permute-done.4.rest_2_ = f32[8,16,128]{2,1,0:T(8,128)S(1)} collective-permute-done((f32[8,16,128]{2,1,0:T(8,128)S(1)}, f32[8,16,128]{2,1,0:T(8,128)S(1)}, u32[]{:S(2)}, u32[]{:S(2)}) %collective-permute-start.4) | collective-permute-done | bytes 65568 | tf_op jit(solution)/shard_map/ppermute | solution.py:510
  26.8 1.2 %copy-done.3 = f32[256,1024]{1,0:T(8,128)S(1)} copy-done((f32[256,1024]{1,0:T(8,128)S(1)}, f32[256,1024]{1,0:T(8,128)}, u32[]{:S(2)}) %copy-start.3) | copy-done | bytes 1048600
  30.6 4.2 %shard_map.160 = f32[16,8,256]{2,1,0:T(8,128)} custom-call(s32[3]{0:T(128)S(1)} %pad_add_fusion.me_ref, f32[16,16,256]{2,1,0:T(8,128)S(1)} %all-to-all-done.msa_ref, f32[8,16,128]{2,1,0:T(8,128)S(1)} %shard_map.159.rest_0_, f32[8,16,128]{2,1,0:T(8,128)S(1)} %collective-permute-done.3.rest_1_, f32[8,16,128]{2,1,0:T(8,128)S(1)} %copy-done.14, ...), custom_call_target="tpu_custom_call" | custom-call | tf_op jit(solution)/shard_map/pallas_call | solution.py:494
  34.8 3.5 %all-to-all-start.1 = ((f32[16,8,256]{2,1,0:T(8,128)}), f32[16,8,256]{2,1,0:T(8,128)S(1)}, u32[]{:S(2)}, u32[]{:S(2)}) async-start(f32[16,8,256]{2,1,0:T(8,128)} %shard_map.160), calls=%async_computation.1 | async-start | bytes 262144 | tf_op jit(solution)/shard_map/all_to_all | solution.py:566
  40.0 1.4 %shard_map.162 = (f32[128,128]{1,0:T(8,128)S(1)}, f32[128,128]{1,0:T(8,128)S(1)}, f32[128,128]{1,0:T(8,128)}, f32[128,128]{1,0:T(8,128)S(1)}) custom-call(s32[3]{0:T(128)S(1)} %pad_add_fusion.me_ref, f32[512,128]{1,0:T(8,128)S(1)} %bitcast.35), custom_call_target="tpu_custom_call" | custom-call | tf_op jit(solution)/shard_map/pallas_call | solution.py:494
  45.3 5.3 %shard_map.161 = (f32[32,128]{1,0:T(8,128)S(1)}, f32[8,32,128]{2,1,0:T(8,128)S(1)}, f32[4,8,256]{2,1,0:T(8,128)S(1)}, f32[4,8,256]{2,1,0:T(8,128)S(1)}, f32[4,8,...) custom-call(s32[3]{0:T(128)S(1)} %pad_add_fusion.me_ref, f32[128,256]{1,0:T(8,128)S(1)} %bitcast.38, f32[4,256]{1,0:T(4,128)S(1)} %copy-done.21, ...), custom_call_target="tpu_custom_call" | custom-call | tf_op jit(solution)/shard_map/pallas_call | solution.py:494
  54.3 5.0 %all-to-all-start.2 = ((f32[8,32,128]{2,1,0:T(8,128)}), f32[8,32,128]{2,1,0:T(8,128)S(1)}, u32[]{:S(2)}, u32[]{:S(2)}) async-start(f32[8,32,128]{2,1,0:T(8,128)} %copy-done.9), calls=%async_computation.2 | async-start | bytes 262144 | tf_op jit(solution)/shard_map/all_to_all | solution.py:594
  61.9 1.5 %collective-permute-start.6 = (f32[32,128]{1,0:T(8,128)S(1)}, f32[32,128]{1,0:T(8,128)S(1)}, u32[]{:S(2)}, u32[]{:S(2)}) collective-permute-start(f32[32,128]{1,0:T(8,128)S(1)} %copy-done.20), channel_id=1, source_target_pairs={{1,0},{0,1},{17,16},{16,17},{3,2},{2,3},{19,18},{18,19},{5,4},{4,5... | collective-permute-start | bytes 49160 | tf_op jit(solution)/shard_map/ppermute | solution.py:510
  64.8 1.4 %collective-permute-done.9.rest_5_ = f32[128,128]{1,0:T(8,128)S(1)} collective-permute-done((f32[128,128]{1,0:T(8,128)S(1)}, f32[128,128]{1,0:T(8,128)S(1)}, u32[]{:S(2)}, u32[]{:S(2)}) %collective-permute-start.9) | collective-permute-done | bytes 65568 | tf_op jit(solution)/shard_map/ppermute | solution.py:510
  66.8 5.5 %shard_map.163 = (f32[32,4,8,128]{3,2,1,0:T(8,128)}, f32[256,128]{1,0:T(8,128)S(1)}, f32[256,128]{1,0:T(8,128)S(1)}, f32[256,128]{1,0:T(8,128)S(1)}, f32[256,128]{1,0:T(8,128)S(1)}) custom-call(s32[3]{0:T(128)S(1)} %pad_add_fusion.me_ref, f32[32,128]{1,0:T(8,128)S(1)} %copy-done.20, f32[32,128]{1,0:T(8,128)S(1)} %collective-permute-done.6.rest_1_, ...), custom_call_target="tpu_custom_call" | custom-call | tf_op jit(solution)/shard_map/pallas_call | solution.py:494
  72.3 5.9 %all-to-all-start.3 = ((f32[32,4,8,128]{3,2,1,0:T(8,128)}), f32[32,4,8,128]{3,2,1,0:T(8,128)S(1)}, u32[]{:S(2)}, u32[]{:S(2)}) async-start(f32[32,4,8,128]{3,2,1,0:T(8,128)} %get-tuple-element.34), calls=%async_computation.3 | async-start | bytes 1048576 | tf_op jit(solution)/shard_map/all_to_all | solution.py:638
  78.3 1.8 %collective-permute-start.15 = (f32[256,128]{1,0:T(8,128)S(1)}, f32[256,128]{1,0:T(8,128)S(1)}, u32[]{:S(2)}, u32[]{:S(2)}) collective-permute-start(f32[256,128]{1,0:T(8,128)S(1)} %get-tuple-element.40), channel_id=1, source_target_pairs={{1,0},{0,1},{17,16},{16,17},{3,2},{2,3},{19,18},{18,19},{5,4},{4,5... | collective-permute-start | bytes 393224 | tf_op jit(solution)/shard_map/ppermute | solution.py:510
  80.5 1.8 %collective-permute-start.12 = (f32[4,8,256]{2,1,0:T(8,128)S(1)}, f32[4,8,256]{2,1,0:T(8,128)S(1)}, u32[]{:S(2)}, u32[]{:S(2)}) collective-permute-start(f32[4,8,256]{2,1,0:T(8,128)S(1)} %copy-done.34), channel_id=1, source_target_pairs={{1,0},{0,1},{17,16},{16,17},{3,2},{2,3},{19,18},{18,19},{5,4},{4,5... | collective-permute-start | bytes 98312 | tf_op jit(solution)/shard_map/ppermute | solution.py:510
  82.2 10.2 %collective-permute-done.12 = f32[4,8,256]{2,1,0:T(8,128)S(1)} collective-permute-done((f32[4,8,256]{2,1,0:T(8,128)S(1)}, f32[4,8,256]{2,1,0:T(8,128)S(1)}, u32[]{:S(2)}, u32[]{:S(2)}) %collective-permute-start.12) | collective-permute-done | bytes 32800 | tf_op jit(solution)/shard_map/ppermute | solution.py:510
  92.4 3.3 %collective-permute-done.14 = f32[4,8,256]{2,1,0:T(8,128)S(1)} collective-permute-done((f32[4,8,256]{2,1,0:T(8,128)S(1)}, f32[4,8,256]{2,1,0:T(8,128)S(1)}, u32[]{:S(2)}, u32[]{:S(2)}) %collective-permute-start.14) | collective-permute-done | bytes 32800 | tf_op jit(solution)/shard_map/ppermute | solution.py:510
  95.8 2.3 %shard_map.164 = (f32[32,16,128]{2,1,0:T(8,128)}, f32[8,16,256]{2,1,0:T(8,128)}, f32[1024,128]{1,0:T(8,128)S(1)}) custom-call(s32[3]{0:T(128)S(1)} %pad_add_fusion.me_ref, f32[1024,128]{1,0:T(8,128)S(1)} %bitcast.34, f32[32,256]{1,0:T(8,128)S(1)} %bitcast.41, f32[32,256]{1,0:T(8,128)S(1)} %bitcast.42, f32[32,256]{1,0:T(8,128)S(1)} %bitcast.43, ...), custom_call_target="tpu_custom_call" | custom-call | tf_op jit(solution)/shard_map/pallas_call | solution.py:494
  98.1 5.5 %all-to-all-start.4 = ((f32[32,16,128]{2,1,0:T(8,128)}), f32[32,16,128]{2,1,0:T(8,128)S(1)}, u32[]{:S(2)}, u32[]{:S(2)}) async-start(f32[32,16,128]{2,1,0:T(8,128)} %get-tuple-element.44), calls=%async_computation.4 | async-start | bytes 524288 | tf_op jit(solution)/shard_map/all_to_all | solution.py:648
  104.6 9.7 %all-to-all-done.4 = f32[32,16,128]{2,1,0:T(8,128)S(1)} async-done(((f32[32,16,128]{2,1,0:T(8,128)}), f32[32,16,128]{2,1,0:T(8,128)S(1)}, u32[]{:S(2)}, u32[]{:S(2)}) %all-to-all-start.4) | async-done | bytes 262176 | tf_op jit(solution)/shard_map/all_to_all | solution.py:648
  114.3 1.3 %shard_map.165 = f32[512,128]{1,0:T(8,128)} custom-call(f32[512,128]{1,0:T(8,128)S(1)} %bitcast.36, f32[1024,128]{1,0:T(8,128)S(1)} %get-tuple-element.45.pair_ref, f32[128,1]{1,0:T(8,128)S(1)} %broadcast_in_dim_reshape.4.gain_ref, f32[128,128]{1,0:T(8,128)S(1)} %bitcast.39), custom_call_target="tpu_custom_call" | custom-call | tf_op jit(solution)/shard_map/pallas_call | solution.py:671
  (131 shorter events, 28.0 us)
Async XLA Ops:
  4.6 22.1 %all-to-all-start = ((f32[16,16,256]{2,1,0:T(8,128)}), f32[16,16,256]{2,1,0:T(8,128)S(1)}, u32[]{:S(2)}, u32[]{:S(2)}) async-start(f32[16,16,256]{2,1,0:T(8,128)} %get-tuple-element.24), calls=%async_computation | async-start | bytes 524288 | tf_op jit(solution)/shard_map/all_to_all | solution.py:542
  12.1 3.7 %collective-permute-start = (f32[2,16,128]{2,1,0:T(8,128)S(1)}, f32[2,16,128]{2,1,0:T(8,128)S(1)}, u32[]{:S(2)}, u32[]{:S(2)}) collective-permute-start(f32[2,16,128]{2,1,0:T(8,128)S(1)} %get-tuple-element.25.rest_0_), channel_id=1, source_target_pairs={{1,0},{0,1},{17,16},{16,17},{3,2},{2,3},{19,18},{18,19},{5,4},{4,5... | collective-permute-start | bytes 49160 | tf_op jit(solution)/shard_map/ppermute | solution.py:510
  13.6 2.3 %collective-permute-start.1 = (f32[2,16,128]{2,1,0:T(8,128)S(1)}, f32[2,16,128]{2,1,0:T(8,128)S(1)}, u32[]{:S(2)}, u32[]{:S(2)}) collective-permute-start(f32[2,16,128]{2,1,0:T(8,128)S(1)} %get-tuple-element.25.rest_0_), channel_id=1, source_target_pairs={{16,0},{17,1},{0,16},{1,17},{18,2},{19,3},{2,18},{3,19},{20,4},{21... | collective-permute-start | bytes 49160 | tf_op jit(solution)/shard_map/ppermute | solution.py:510
  13.6 3.2 %collective-permute-start.2 = (f32[2,16,128]{2,1,0:T(8,128)S(1)}, f32[2,16,128]{2,1,0:T(8,128)S(1)}, u32[]{:S(2)}, u32[]{:S(2)}) collective-permute-start(f32[2,16,128]{2,1,0:T(8,128)S(1)} %get-tuple-element.25.rest_0_), channel_id=1, source_target_pairs={{17,0},{16,1},{1,16},{0,17},{19,2},{18,3},{3,18},{2,19},{21,4},{20... | collective-permute-start | bytes 49160 | tf_op jit(solution)/shard_map/ppermute | solution.py:510
  17.4 4.9 %collective-permute-start.3 = (f32[8,16,128]{2,1,0:T(8,128)S(1)}, f32[8,16,128]{2,1,0:T(8,128)S(1)}, u32[]{:S(2)}, u32[]{:S(2)}) collective-permute-start(f32[8,16,128]{2,1,0:T(8,128)S(1)} %shard_map.159.rest_0_), channel_id=1, source_target_pairs={{2,0},{0,2},{6,4},{4,6},{10,8},{8,10},{14,12},{12,14},{3,1},{1,3},... | collective-permute-start | bytes 196616 | tf_op jit(solution)/shard_map/ppermute | solution.py:510
  19.5 4.8 %collective-permute-start.4 = (f32[8,16,128]{2,1,0:T(8,128)S(1)}, f32[8,16,128]{2,1,0:T(8,128)S(1)}, u32[]{:S(2)}, u32[]{:S(2)}) collective-permute-start(f32[8,16,128]{2,1,0:T(8,128)S(1)} %shard_map.159.rest_0_), channel_id=1, source_target_pairs={{4,0},{6,2},{0,4},{2,6},{12,8},{14,10},{8,12},{10,14},{5,1},{7,3},... | collective-permute-start | bytes 196616 | tf_op jit(solution)/shard_map/ppermute | solution.py:510
  21.0 5.2 %collective-permute-start.5 = (f32[8,16,128]{2,1,0:T(8,128)S(1)}, f32[8,16,128]{2,1,0:T(8,128)S(1)}, u32[]{:S(2)}, u32[]{:S(2)}) collective-permute-start(f32[8,16,128]{2,1,0:T(8,128)S(1)} %shard_map.159.rest_0_), channel_id=1, source_target_pairs={{6,0},{4,2},{2,4},{0,6},{14,8},{12,10},{10,12},{8,14},{7,1},{5,3},... | collective-permute-start | bytes 196616 | tf_op jit(solution)/shard_map/ppermute | solution.py:510
  34.8 9.6 %all-to-all-start.1 = ((f32[16,8,256]{2,1,0:T(8,128)}), f32[16,8,256]{2,1,0:T(8,128)S(1)}, u32[]{:S(2)}, u32[]{:S(2)}) async-start(f32[16,8,256]{2,1,0:T(8,128)} %shard_map.160), calls=%async_computation.1 | async-start | bytes 262144 | tf_op jit(solution)/shard_map/all_to_all | solution.py:566
  43.3 20.1 %collective-permute-start.10 = (f32[128,128]{1,0:T(8,128)}, f32[128,128]{1,0:T(8,128)}, u32[]{:S(2)}, u32[]{:S(2)}) collective-permute-start(f32[128,128]{1,0:T(8,128)} %get-tuple-element.31), channel_id=1, source_target_pairs={{16,0},{17,1},{0,16},{1,17},{18,2},{19,3},{2,18},{3,19},{20,4},{21... | collective-permute-start | bytes 196616 | tf_op jit(solution)/shard_map/ppermute | solution.py:510
  54.3 12.5 %all-to-all-start.2 = ((f32[8,32,128]{2,1,0:T(8,128)}), f32[8,32,128]{2,1,0:T(8,128)S(1)}, u32[]{:S(2)}, u32[]{:S(2)}) async-start(f32[8,32,128]{2,1,0:T(8,128)} %copy-done.9), calls=%async_computation.2 | async-start | bytes 262144 | tf_op jit(solution)/shard_map/all_to_all | solution.py:594
  60.2 4.5 %collective-permute-start.11 = (f32[128,128]{1,0:T(8,128)S(1)}, f32[128,128]{1,0:T(8,128)S(1)}, u32[]{:S(2)}, u32[]{:S(2)}) collective-permute-start(f32[128,128]{1,0:T(8,128)S(1)} %copy-done.28), channel_id=1, source_target_pairs={{17,0},{16,1},{1,16},{0,17},{19,2},{18,3},{3,18},{2,19},{21,4},{20... | collective-permute-start | bytes 196616 | tf_op jit(solution)/shard_map/ppermute | solution.py:510
  61.4 4.8 %collective-permute-start.9 = (f32[128,128]{1,0:T(8,128)S(1)}, f32[128,128]{1,0:T(8,128)S(1)}, u32[]{:S(2)}, u32[]{:S(2)}) collective-permute-start(f32[128,128]{1,0:T(8,128)S(1)} %copy-done.26), channel_id=1, source_target_pairs={{1,0},{0,1},{17,16},{16,17},{3,2},{2,3},{19,18},{18,19},{5,4},{4,5... | collective-permute-start | bytes 196616 | tf_op jit(solution)/shard_map/ppermute | solution.py:510
  61.9 4.4 %collective-permute-start.6 = (f32[32,128]{1,0:T(8,128)S(1)}, f32[32,128]{1,0:T(8,128)S(1)}, u32[]{:S(2)}, u32[]{:S(2)}) collective-permute-start(f32[32,128]{1,0:T(8,128)S(1)} %copy-done.20), channel_id=1, source_target_pairs={{1,0},{0,1},{17,16},{16,17},{3,2},{2,3},{19,18},{18,19},{5,4},{4,5... | collective-permute-start | bytes 49160 | tf_op jit(solution)/shard_map/ppermute | solution.py:510
  63.4 3.0 %collective-permute-start.7 = (f32[32,128]{1,0:T(8,128)S(1)}, f32[32,128]{1,0:T(8,128)S(1)}, u32[]{:S(2)}, u32[]{:S(2)}) collective-permute-start(f32[32,128]{1,0:T(8,128)S(1)} %copy-done.20), channel_id=1, source_target_pairs={{16,0},{17,1},{0,16},{1,17},{18,2},{19,3},{2,18},{3,19},{20,4},{21... | collective-permute-start | bytes 49160 | tf_op jit(solution)/shard_map/ppermute | solution.py:510
  63.4 3.2 %collective-permute-start.8 = (f32[32,128]{1,0:T(8,128)S(1)}, f32[32,128]{1,0:T(8,128)S(1)}, u32[]{:S(2)}, u32[]{:S(2)}) collective-permute-start(f32[32,128]{1,0:T(8,128)S(1)} %copy-done.20), channel_id=1, source_target_pairs={{17,0},{16,1},{1,16},{0,17},{19,2},{18,3},{3,18},{2,19},{21,4},{20... | collective-permute-start | bytes 49160 | tf_op jit(solution)/shard_map/ppermute | solution.py:510
  72.3 23.5 %copy-start.18 = (f32[4,8,256]{2,1,0:T(8,128)S(1)}, f32[4,8,256]{2,1,0:T(8,128)}, u32[]{:S(2)}) copy-start(f32[4,8,256]{2,1,0:T(8,128)} %copy-done.17) | copy-start | bytes 98308
  72.3 23.4 %all-to-all-start.3 = ((f32[32,4,8,128]{3,2,1,0:T(8,128)}), f32[32,4,8,128]{3,2,1,0:T(8,128)S(1)}, u32[]{:S(2)}, u32[]{:S(2)}) async-start(f32[32,4,8,128]{3,2,1,0:T(8,128)} %get-tuple-element.34), calls=%async_computation.3 | async-start | bytes 1048576 | tf_op jit(solution)/shard_map/all_to_all | solution.py:638
  78.3 17.5 %collective-permute-start.15 = (f32[256,128]{1,0:T(8,128)S(1)}, f32[256,128]{1,0:T(8,128)S(1)}, u32[]{:S(2)}, u32[]{:S(2)}) collective-permute-start(f32[256,128]{1,0:T(8,128)S(1)} %get-tuple-element.40), channel_id=1, source_target_pairs={{1,0},{0,1},{17,16},{16,17},{3,2},{2,3},{19,18},{18,19},{5,4},{4,5... | collective-permute-start | bytes 393224 | tf_op jit(solution)/shard_map/ppermute | solution.py:510
  80.1 15.7 %collective-permute-start.16 = (f32[256,128]{1,0:T(8,128)S(1)}, f32[256,128]{1,0:T(8,128)S(1)}, u32[]{:S(2)}, u32[]{:S(2)}) collective-permute-start(f32[256,128]{1,0:T(8,128)S(1)} %get-tuple-element.41), channel_id=1, source_target_pairs={{16,0},{17,1},{0,16},{1,17},{18,2},{19,3},{2,18},{3,19},{20,4},{21... | collective-permute-start | bytes 393224 | tf_op jit(solution)/shard_map/ppermute | solution.py:510
  80.1 15.7 %collective-permute-start.17 = (f32[256,128]{1,0:T(8,128)S(1)}, f32[256,128]{1,0:T(8,128)S(1)}, u32[]{:S(2)}, u32[]{:S(2)}) collective-permute-start(f32[256,128]{1,0:T(8,128)S(1)} %get-tuple-element.42), channel_id=1, source_target_pairs={{17,0},{16,1},{1,16},{0,17},{19,2},{18,3},{3,18},{2,19},{21,4},{20... | collective-permute-start | bytes 393224 | tf_op jit(solution)/shard_map/ppermute | solution.py:510
  80.5 12.0 %collective-permute-start.12 = (f32[4,8,256]{2,1,0:T(8,128)S(1)}, f32[4,8,256]{2,1,0:T(8,128)S(1)}, u32[]{:S(2)}, u32[]{:S(2)}) collective-permute-start(f32[4,8,256]{2,1,0:T(8,128)S(1)} %copy-done.34), channel_id=1, source_target_pairs={{1,0},{0,1},{17,16},{16,17},{3,2},{2,3},{19,18},{18,19},{5,4},{4,5... | collective-permute-start | bytes 98312 | tf_op jit(solution)/shard_map/ppermute | solution.py:510
  82.2 10.2 %collective-permute-start.13 = (f32[4,8,256]{2,1,0:T(8,128)S(1)}, f32[4,8,256]{2,1,0:T(8,128)S(1)}, u32[]{:S(2)}, u32[]{:S(2)}) collective-permute-start(f32[4,8,256]{2,1,0:T(8,128)S(1)} %copy-done.32), channel_id=1, source_target_pairs={{16,0},{17,1},{0,16},{1,17},{18,2},{19,3},{2,18},{3,19},{20,4},{21... | collective-permute-start | bytes 98312 | tf_op jit(solution)/shard_map/ppermute | solution.py:510
  92.4 3.3 %collective-permute-start.14 = (f32[4,8,256]{2,1,0:T(8,128)S(1)}, f32[4,8,256]{2,1,0:T(8,128)S(1)}, u32[]{:S(2)}, u32[]{:S(2)}) collective-permute-start(f32[4,8,256]{2,1,0:T(8,128)S(1)} %copy-done.30), channel_id=1, source_target_pairs={{17,0},{16,1},{1,16},{0,17},{19,2},{18,3},{3,18},{2,19},{21,4},{20... | collective-permute-start | bytes 98312 | tf_op jit(solution)/shard_map/ppermute | solution.py:510
  98.1 16.2 %all-to-all-start.4 = ((f32[32,16,128]{2,1,0:T(8,128)}), f32[32,16,128]{2,1,0:T(8,128)S(1)}, u32[]{:S(2)}, u32[]{:S(2)}) async-start(f32[32,16,128]{2,1,0:T(8,128)} %get-tuple-element.44), calls=%async_computation.4 | async-start | bytes 524288 | tf_op jit(solution)/shard_map/all_to_all | solution.py:648
  (41 other events, 182.6 us)

commit v3 on v2

--- a/solution.py
+++ b/solution.py
@@ -13,10 +13,7 @@
 everyone = ("branch", "gi", "gj")
 columns = ("branch", "gj")
 lanes = 128
-vmem = pl.BlockSpec(memory_space=pltpu.VMEM)
-smem = pl.BlockSpec(memory_space=pltpu.SMEM)
-hbm = pl.BlockSpec(memory_space=pltpu.HBM)
-params = pltpu.CompilerParams(vmem_limit_bytes=16 * 1024 * 1024)
+far = pl.BlockSpec(memory_space=pl.ANY)
 
 
 def layer_normalise(values, norm_gain, axis=-1):
@@ -106,6 +103,44 @@
         copy.wait()
 
 
+def column_index():
+    return lax.axis_index("branch") * lax.axis_size("gj") + lax.axis_index("gj")
+
+
+def call(kernel, outs, *operands, scratch=(), sems=()):
+    def bare(item):
+        return item[0] if isinstance(item, list) else item
+
+    n_in, n_out = len(operands), len(outs)
+    near_in = [n for n, item in enumerate(operands) if not isinstance(item, list)]
+    near_out = [n for n, item in enumerate(outs) if not isinstance(item, list)]
+    shapes = [operands[n].shape for n in near_in] + [outs[n] for n in near_out]
+
+    def body(*refs):
+        inputs, results = list(refs[:n_in]), list(refs[n_in : n_in + n_out])
+        local = refs[n_in + n_out : n_in + n_out + len(shapes)]
+        rest, own_sems = refs[n_in + n_out + len(shapes) : -1], refs[-1]
+        pairs = list(zip([inputs[n] for n in near_in], local))
+        back = list(zip(local[len(near_in) :], [results[n] for n in near_out]))
+        for n, ref in zip(near_in, local):
+            inputs[n] = ref
+        for n, ref in zip(near_out, local[len(near_in) :]):
+            results[n] = ref
+        copies = start_copies(pairs, own_sems)
+        kernel(lambda: wait_all(copies), *inputs, *results, *rest)
+        wait_all(start_copies(back, own_sems))
+
+    return pl.pallas_call(
+        body,
+        out_shape=[jax.ShapeDtypeStruct(bare(out), jnp.float32) for out in outs],
+        in_specs=[far] * n_in,
+        out_specs=[far] * n_out,
+        scratch_shapes=[pltpu.VMEM(shape, jnp.float32) for shape in shapes + list(scratch)]
+        + [pltpu.SemaphoreType.DMA((n,)) for n in sems]
+        + [pltpu.SemaphoreType.DMA((max(len(near_in), len(near_out), 1),))],
+    )(*[bare(operand) for operand in operands])
+
+
 def spread(me, refs, slots):
     for k, ref in enumerate(refs):
         slots[me ^ k] = ref[...]
@@ -118,7 +153,7 @@
 
 
 def bias_kernel(
-    msa_far, pair_far, gains_far, matrix_far, copies_far, out_ref, pair_ref, gains_ref, matrix_ref, sems
+    ready, msa_far, pair_far, gains_far, matrix_far, copies_far, out_ref, pair_ref, gains_ref, matrix_ref, sems
 ):
     rows = msa_far.shape[0]
     repeats = copies_far.shape[0] // rows
@@ -130,6 +165,7 @@
     residues, pair_cols, _ = pair_ref.shape
     heads = matrix_ref.shape[0]
     per = lanes // pair_cols
+    ready()
     wait_all(copies[:3])
     normal = layer_normalise(pair_ref[...], gains_ref[0:1, :][None])
     for i in range(residues):
@@ -139,11 +175,13 @@
     wait_all(copies[3:])
 
 
-def pair_blocks_kernel(few, residues, me_ref, pair_ref, *rest):
+def pair_blocks_kernel(few, residues, ready, pair_ref, *rest):
     chunks, slots = rest[:-1], rest[-1]
     n_cols = len(chunks)
     block = chunks[0].shape[0]
     groups = block // (residues * few)
+    me = column_index()
+    ready()
     for c in range(n_cols):
         for o in range(groups):
             for f in range(few):
@@ -151,13 +189,14 @@
                 target = pl.ds(c * block + f * groups + o, residues, stride=few * groups)
                 slots[target, :] = pair_ref[source, :]
     for k in range(n_cols):
-        start = pl.multiple_of((me_ref[0] ^ k) * block, 8)
+        start = pl.multiple_of((me ^ k) * block, 8)
         chunks[k][...] = slots[pl.ds(start, block), :]
 
 
-def bias_rows_kernel(n_cols, me_ref, *rest):
+def bias_rows_kernel(n_cols, ready, *rest):
     blocks, (out_ref, slots) = rest[:n_cols], rest[n_cols:]
-    spread(me_ref[0], blocks, slots)
+    ready()
+    spread(column_index(), blocks, slots)
     count = slots.shape[1]
     per = out_ref.shape[0] // count
     for block in range(count):
@@ -170,14 +209,17 @@
             out_ref[block * per + k] = jnp.concatenate(tiles[k], axis=1)
 
 
-def row_kernel(n_branch, n_gj, per_part, few, me_ref, msa_ref, *rest):
+def row_kernel(n_branch, n_gj, per_part, few, ready, msa_ref, *rest):
     bias_refs, rest = rest[:per_part], rest[per_part:]
     gains_far, qkvg_far, final_far, out_ref, slots, gains_ref, qkvg_ref, final_ref, sems = rest
+    mine = lax.axis_index("gi")
+    me, part = lax.rem(mine, per_part), lax.div(mine, per_part)
     copies = start_copies(
         [(gains_far, gains_ref), (qkvg_far, qkvg_ref), (final_far, final_ref)]
-        + [(ref, slots.at[me_ref[1] ^ k]) for k, ref in enumerate(bias_refs)],
+        + [(ref, slots.at[me ^ k]) for k, ref in enumerate(bias_refs)],
         sems,
     )
+    ready()
     _, residues, width = msa_ref.shape
     _, heads, _, length = slots.shape
     n_gi = length // residues
@@ -187,7 +229,7 @@
     tokens = jnp.concatenate(
         [msa_ref[g * rows + r] for r in range(rows) for g in range(n_gi)], axis=0
     )
-    first = me_ref[2] * (per_part * rows)
+    first = part * (per_part * rows)
     asking = msa_ref[pl.ds(first, per_part * rows)]
     asking = jnp.concatenate(
         [asking[g * rows + r] for r in range(rows) for g in range(per_part)], axis=0
@@ -223,13 +265,14 @@
                 )
 
 
-def column_kernel(n_branch, n_gj, few, heads, me_ref, msa_ref, *rest):
+def column_kernel(n_branch, n_gj, few, heads, ready, msa_ref, *rest):
     n_cols = n_branch * n_gj
-    far, rest = rest[:6], rest[6:]
+    weights, rest = rest[:6], rest[6:]
     left_far, right_far, chunks, rest = rest[0], rest[1], rest[2 : 2 + n_cols], rest[2 + n_cols :]
     gains_ref, qkvg_ref, final_ref, expand_ref, shrink_ref, sides_ref = rest[:6]
     slots, factors_ref, sems, out_sems = rest[6:]
-    copies = start_copies(list(zip(far, rest[:6])), sems)
+    copies = start_copies(list(zip(weights, rest[:6])), sems)
+    ready()
     count, width = msa_ref.shape
     inner = final_ref.shape[0]
     half = sides_ref.shape[0] // 2
@@ -263,7 +306,7 @@
                 start = ((b * per_part + g) * n_gj + j) * each
                 slots[b * n_gj + j, g] = third[start : start + each]
     for k, chunk in enumerate(chunks):
-        chunk[...] = slots[me_ref[0] ^ k]
+        chunk[...] = slots[column_index() ^ k]
     wait_all(copies)
 
 
@@ -289,17 +332,19 @@
                 ]
 
 
-def gather_kernel(few, n_cols, me_ref, *rest):
-    gather_tiles(few, me_ref[0], rest[:n_cols], rest[n_cols : 2 * n_cols], *rest[2 * n_cols :])
-
-
-def triangle_kernel(few, n_cols, me_ref, tri_ref, *rest):
+def gather_kernel(few, n_cols, ready, *rest):
+    ready()
+    gather_tiles(few, column_index(), rest[:n_cols], rest[n_cols : 2 * n_cols], *rest[2 * n_cols :])
+
+
+def triangle_kernel(few, n_cols, ready, tri_ref, *rest):
     blocks, (out_ref, msa_out, pair_out, product_ref, msa_slots, slots) = (
         rest[: 2 * n_cols],
         rest[2 * n_cols :],
     )
+    ready()
     gather_tiles(
-        few, me_ref[0], blocks[:n_cols], blocks[n_cols:], msa_out, pair_out, msa_slots, slots
+        few, column_index(), blocks[:n_cols], blocks[n_cols:], msa_out, pair_out, msa_slots, slots
     )
     n_all, rows, _ = out_ref.shape
     n_gi = n_all // n_cols
@@ -352,7 +397,7 @@
 
 
 def pair_kernel(
-    few, n_gi, n_cols, me_ref, *rest
+    few, n_gi, n_cols, ready, *rest
 ):
     left_refs, pair_refs = rest[:n_cols], rest[n_cols : 2 * n_cols]
     right_ref, gain_ref, matrix_ref, triangle_ref, tri_ref = rest[2 * n_cols : 2 * n_cols + 5]
@@ -360,7 +405,7 @@
     chunks = rest[2 * n_cols + 5 : 3 * n_cols + 5]
     rest = rest[3 * n_cols + 5 :]
     left_ref, slots, pair_ref, first_ref, gate_ref, matrix_ref, triangle_ref, sems = rest
-    me = me_ref[0]
+    me = column_index()
     groups_j = n_gi // n_cols
     block = pair_refs[0].shape[0]
     pairs = [(ref, left_ref.at[me ^ k]) for k, ref in enumerate(left_refs)]
@@ -371,6 +416,7 @@
     copies = start_copies(pairs, sems)
     _, wide, count = left_ref.shape
     half = block // groups_j
+    ready()
     wait_all(copies[:n_cols])
     all_rows = count // few
     residues = n_cols * few
@@ -427,8 +473,11 @@
             chunks[k][pl.ds(block + o * half, half), :] = gate_ref[rows, :]
 
 
-def final_kernel(few, n_cols, residues, packed, product_ref, pair_ref, gain_ref, matrix_ref, out_ref):
+def final_kernel(
+    few, n_cols, residues, packed, ready, product_ref, pair_ref, gain_ref, matrix_ref, out_ref
+):
     positions = out_ref.shape[0]
+    ready()
     if packed:
         tiles = residues // few
         tall = product_ref.shape[0] // residues
@@ -482,27 +531,6 @@
     parts = 2
     per_part = n_gi // parts
     own_rows = rows // per_part
-    f32 = jnp.float32
-
-    def call(kernel, outs, *operands, scratch=(), sems=()):
-        def bare(item):
-            return item[0] if isinstance(item, list) else item
-
-        def spec(item):
-            return hbm if isinstance(item, list) else vmem
-
-        return pl.pallas_call(
-            kernel,
-            out_shape=[jax.ShapeDtypeStruct(bare(out), f32) for out in outs],
-            in_specs=[
-                smem if getattr(operand, "dtype", f32) == jnp.int32 else spec(operand)
-                for operand in operands
-            ],
-            out_specs=[spec(out) for out in outs],
-            scratch_shapes=[pltpu.VMEM(shape, f32) for shape in scratch]
-            + [pltpu.SemaphoreType.DMA((n,)) for n in sems],
-            compiler_params=params,
-        )(*[bare(operand) for operand in operands])
 
     def trade(blocks, axes):
         n = lax.axis_size(axes)
@@ -521,9 +549,6 @@
         for part in range(parts)
     ]
     n_half = n_cols * per_part
-    mine = lax.axis_index("gi")
-    me = jnp.stack([lax.axis_index(columns), mine % per_part, mine // per_part])
-    me = me.astype(jnp.int32)
     positions = residues * pair_cols
     each = own_rows * few
 
@@ -543,7 +568,6 @@
     (bias,) = call(
         functools.partial(bias_rows_kernel, n_cols),
         [(heads, residues, length)],
-        me,
         *trade([bias] * n_cols, columns),
         scratch=[(n_cols,) + bias_block],
     )
@@ -551,7 +575,6 @@
     (msa_first,) = call(
         functools.partial(row_kernel, n_branch, n_gj, per_part, few),
         [(n_half, each, width)],
-        me,
         msa,
         *[[block] for block in bias],
         [layernorm_scales],
@@ -576,7 +599,6 @@
     left, right, *alignment = call(
         functools.partial(column_kernel, n_branch, n_gj, few, heads),
         [[(outer_width, count)], [(n_gi, outer_width, count)]] + [(per_part, each, width)] * n_cols,
-        me,
         msa_first.reshape(count, width),
         *[[w] for w in weights],
         scratch=[w.shape for w in weights]
@@ -586,7 +608,6 @@
     pair = call(
         functools.partial(pair_blocks_kernel, few, residues),
         [(positions // n_cols, pair_width)] * n_cols,
-        me,
         pair.reshape(positions, pair_width),
         scratch=[(positions, pair_width)],
     )
@@ -610,7 +631,6 @@
         functools.partial(pair_kernel, few, n_gi, n_cols),
         [(slots, positions // lanes, 2 * share, lanes)]
         + [(2 * positions // n_cols, pair_width)] * n_cols,
-        me,
         *[[block] for block in left + pair],
         right.reshape(n_gi * outer_width, count),
         pair_norm_gains[1][:, None],
@@ -639,8 +659,7 @@
         product, alignment_output, first_gate = call(
             functools.partial(triangle_kernel, few, n_cols),
             [(n_all, residues, lanes)] + tiles,
-            me,
-            tri.reshape(-1, lanes),
+                tri.reshape(-1, lanes),
             *alignment,
             *first_gate,
             scratch=[(lanes, lanes)] + scratch,
@@ -653,8 +672,7 @@
         alignment_output, first_gate = call(
             functools.partial(gather_kernel, few, n_cols),
             tiles,
-            me,
-            *alignment,
+                *alignment,
             *first_gate,
             scratch=scratch,
         )
@@ -668,13 +686,14 @@
             tiled=True,
         ).reshape(groups, n_cols, few, residues, pair_width)
         product = jnp.transpose(product, (4, 3, 2, 0, 1)).reshape(pair_width, positions)
-    (pair_output_tensor,) = pl.pallas_call(
+    (pair_output_tensor,) = call(
         functools.partial(final_kernel, few, n_cols, residues, packed),
-        out_shape=[jax.ShapeDtypeStruct((positions, pair_width), f32)],
-        in_specs=[vmem] * 4,
-        out_specs=[vmem],
-        compiler_params=params,
-    )(product, first_gate, gain[:, None], last.T)
+        [(positions, pair_width)],
+        product,
+        first_gate,
+        gain[:, None],
+        last.T,
+    )
     return (
         alignment_output,
         pair_output_tensor.reshape(residues, pair_cols, pair_width),

time: 117 us -> 122 us (1.043)
  Pallas kernels: 21.4 us -> 36.5 us
  local copies, waits for them, and re-layouts: 18.8 us -> 10.2 us
  starting transfers between devices: 41.3 us -> 38.9 us
  waiting for transfers between devices: 32 us -> 33.4 us
    pallas_call x8, Pallas kernels: 21.4 us -> 36.5 us  [call(): pl.pallas_call(body, out_shape=[jax.ShapeDtypeStruct(bare(out), jnp.float...]
    unnamed x85 -> x75, local copies, waits for them, and re-layouts: 16.3 us -> 6.41 us
    all_to_all x1, waiting for transfers between devices: 0.84 us -> 3.09 us  [per_device(): lax.all_to_all(msa_first, everyone, 0, 0, tiled=True, axis_index_groups=h...]
  transfers between devices with their start and end apart: 23 -> 23, of which waited for: 13 -> 11; matrix products, arithmetic and copies ran while one was open for 3% -> 4% of each run, Pallas kernels for 6% -> 9%
where the time goes in v3:
time: 122 us; the launch traced here: 121 us
  starting transfers between devices  38.9 us (32%)
  Pallas kernels  36.5 us (30%)
  waiting for transfers between devices  33.4 us (27%)
  local copies, waits for them, and re-layouts  10.2 us (8%)
  between operations  1.22 us (1%)
    pallas_call x8, Pallas kernels, call(): pl.pallas_call(body, out_shape=[jax.ShapeDtypeStruct(bare(out), jnp.float...  36.5 us
    ppermute x18, waiting for transfers between devices, trade(): lax.ppermute(blocks[k], axes, [(t ^ k, t) for t in range(n) if t ^ k < n])  21.2 us
    ppermute x18, starting transfers between devices, trade(): lax.ppermute(blocks[k], axes, [(t ^ k, t) for t in range(n) if t ^ k < n])  13.3 us
    all_to_all x1, waiting for transfers between devices, per_device(): lax.all_to_all(product, everyone, 0, 0, tiled=True, axis_index_groups=order)  8.99 us
    all_to_all x1, starting transfers between devices, per_device(): msa = lax.all_to_all(msa, 'gi', 0, 0, tiled=True)  7.42 us
    unnamed x75, local copies, waits for them, and re-layouts  6.41 us
    all_to_all x1, starting transfers between devices, per_device(): lax.all_to_all(product, everyone, 0, 0, tiled=True, axis_index_groups=order)  5.52 us
    all_to_all x1, starting transfers between devices, per_device(): lax.all_to_all(tri, everyone, 0, 0, tiled=True, axis_index_groups=order)  5.3 us
  transfers between devices with their start and end apart: 23, of which 11 were waited for; matrix products, arithmetic and copies ran while one was open for 4% of the time, Pallas kernels for 9%

profile of v3, /device:TPU:0, one launch (start us, length us, event | category | flops | bytes accessed | tf_op | source)
XLA Modules:
  0.0 121.1 jit_solution(6824958004491473285)
XLA Ops:
  0.6 9.7 %shard_map.158 = (f32[16,16,256]{2,1,0:T(8,128)}, f32[2,16,128]{2,1,0:T(8,128)}) custom-call(f32[8,16,256]{2,1,0:T(8,128)} %refs_0_.1, f32[16,32,128]{2,1,0:T(8,128)} %refs_1_.2, f32[3,128]{1,0:T(4,128)} %refs_2_.2, f32[8,128]{1,0:T(8,128)} %bitcast.55), custom_call_target="tpu_custom_call" | custom-call | tf_op jit(solution)/shard_map/pallas_call | solution.py:133
  10.4 7.4 %all-to-all-start = ((f32[16,16,256]{2,1,0:T(8,128)}), f32[16,16,256]{2,1,0:T(8,128)S(1)}, u32[]{:S(2)}, u32[]{:S(2)}) async-start(f32[16,16,256]{2,1,0:T(8,128)} %get-tuple-element.24), calls=%async_computation | async-start | bytes 524288 | tf_op jit(solution)/shard_map/all_to_all | solution.py:567
  17.8 1.6 %collective-permute-start = (f32[2,16,128]{2,1,0:T(8,128)S(1)}, f32[2,16,128]{2,1,0:T(8,128)S(1)}, u32[]{:S(2)}, u32[]{:S(2)}) collective-permute-start(f32[2,16,128]{2,1,0:T(8,128)S(1)} %copy-done.24), channel_id=1, source_target_pairs={{1,0},{0,1},{17,16},{16,17},{3,2},{2,3},{19,18},{18,19},{5,4},{4,5... | collective-permute-start | bytes 49160 | tf_op jit(solution)/shard_map/ppermute | solution.py:538
  23.1 1.6 %shard_map.159.refs_1_ = f32[8,16,128]{2,1,0:T(8,128)} custom-call(f32[2,16,128]{2,1,0:T(8,128)} %get-tuple-element.25.refs_0_, f32[2,16,128]{2,1,0:T(8,128)} %copy-done.25, f32[2,16,128]{2,1,0:T(8,128)} %copy-done.26, f32[2,16,128]{2,1,0:T(8,128)} %copy-done.27), custom_call_target="tpu_custom_call" | custom-call | tf_op jit(solution)/shard_map/pallas_call | solution.py:133
  24.7 2.0 %collective-permute-start.3 = (f32[8,16,128]{2,1,0:T(8,128)}, f32[8,16,128]{2,1,0:T(8,128)S(1)}, u32[]{:S(2)}, u32[]{:S(2)}) collective-permute-start(f32[8,16,128]{2,1,0:T(8,128)} %shard_map.159.refs_1_), channel_id=1, source_target_pairs={{2,0},{0,2},{6,4},{4,6},{10,8},{8,10},{14,12},{12,14},{3,1},{1,3},... | collective-permute-start | bytes 196616 | tf_op jit(solution)/shard_map/ppermute | solution.py:538
  28.3 1.6 %collective-permute-done.3.refs_2_ = f32[8,16,128]{2,1,0:T(8,128)S(1)} collective-permute-done((f32[8,16,128]{2,1,0:T(8,128)}, f32[8,16,128]{2,1,0:T(8,128)S(1)}, u32[]{:S(2)}, u32[]{:S(2)}) %collective-permute-start.3) | collective-permute-done | bytes 65568 | tf_op jit(solution)/shard_map/ppermute | solution.py:538
  29.9 1.8 %collective-permute-done.4.refs_3_ = f32[8,16,128]{2,1,0:T(8,128)S(1)} collective-permute-done((f32[8,16,128]{2,1,0:T(8,128)}, f32[8,16,128]{2,1,0:T(8,128)S(1)}, u32[]{:S(2)}, u32[]{:S(2)}) %collective-permute-start.4) | collective-permute-done | bytes 65568 | tf_op jit(solution)/shard_map/ppermute | solution.py:538
  31.7 1.8 %collective-permute-done.5.refs_4_ = f32[8,16,128]{2,1,0:T(8,128)S(1)} collective-permute-done((f32[8,16,128]{2,1,0:T(8,128)}, f32[8,16,128]{2,1,0:T(8,128)S(1)}, u32[]{:S(2)}, u32[]{:S(2)}) %collective-permute-start.5) | collective-permute-done | bytes 65568 | tf_op jit(solution)/shard_map/ppermute | solution.py:538
  34.9 4.6 %shard_map.160 = f32[16,8,256]{2,1,0:T(8,128)} custom-call(f32[16,16,256]{2,1,0:T(8,128)} %copy-done.1, f32[8,16,128]{2,1,0:T(8,128)} %shard_map.159.refs_1_, f32[8,16,128]{2,1,0:T(8,128)} %copy-done.10, f32[8,16,128]{2,1,0:T(8,128)} %copy-done.11, f32[8,16,128]{2,1,0:T(8,128)} %copy-done.12, f32[4,256]{1,0:T(4,128)} %refs_1_.3, f32[256,1024]{1,0:T(8,128)} %refs_6_.1, ...), custom_call_target="tpu_custom_call" | custom-call | tf_op jit(solution)/shard_map/pallas_call | solution.py:133
  39.5 3.5 %all-to-all-start.1 = ((f32[16,8,256]{2,1,0:T(8,128)}), f32[16,8,256]{2,1,0:T(8,128)S(1)}, u32[]{:S(2)}, u32[]{:S(2)}) async-start(f32[16,8,256]{2,1,0:T(8,128)} %shard_map.160), calls=%async_computation.1 | async-start | bytes 262144 | tf_op jit(solution)/shard_map/all_to_all | solution.py:589
  43.8 1.9 %shard_map.162 = (f32[128,128]{1,0:T(8,128)}, f32[128,128]{1,0:T(8,128)}, f32[128,128]{1,0:T(8,128)}, f32[128,128]{1,0:T(8,128)}) custom-call(f32[512,128]{1,0:T(8,128)} %bitcast.34), custom_call_target="tpu_custom_call" | custom-call | tf_op jit(solution)/shard_map/pallas_call | solution.py:133
  46.0 3.1 %all-to-all-done.1 = f32[16,8,256]{2,1,0:T(8,128)S(1)} async-done(((f32[16,8,256]{2,1,0:T(8,128)}), f32[16,8,256]{2,1,0:T(8,128)S(1)}, u32[]{:S(2)}, u32[]{:S(2)}) %all-to-all-start.1) | async-done | bytes 131104 | tf_op jit(solution)/shard_map/all_to_all | solution.py:589
  49.8 7.5 %shard_map.161 = (f32[32,128]{1,0:T(8,128)}, f32[8,32,128]{2,1,0:T(8,128)}, f32[4,8,256]{2,1,0:T(8,128)}, f32[4,8,256]{2,1,0:T(8,128)}, f32[4,8,256]{2,1,0:T(8,128)}, /*index=5*/f32[4,8,256]{2,1,0:T(8,128)}) custom-call(f32[128,256]{1,0:T(8,128)} %bitcast.37, f32[4,256]{1,0:T(4,128)} %refs_1_.3, f32[256,1024]{1,0:T(8,128)} %refs_2_.3, f32[256,256]{1,0:T(8,128)} %refs_3_.1, ...), custom_call_target="tpu_custom_call" | custom-call | tf_op jit(solution)/shard_map/pallas_call | solution.py:133
  57.3 3.8 %all-to-all-start.2 = ((f32[8,32,128]{2,1,0:T(8,128)}), f32[8,32,128]{2,1,0:T(8,128)S(1)}, u32[]{:S(2)}, u32[]{:S(2)}) async-start(f32[8,32,128]{2,1,0:T(8,128)} %get-tuple-element.33), calls=%async_computation.2 | async-start | bytes 262144 | tf_op jit(solution)/shard_map/all_to_all | solution.py:615
  69.1 5.6 %shard_map.163 = (f32[32,4,8,128]{3,2,1,0:T(8,128)}, f32[256,128]{1,0:T(8,128)}, f32[256,128]{1,0:T(8,128)}, f32[256,128]{1,0:T(8,128)}, f32[256,128]{1,0:T(8,128)}) custom-call(f32[32,128]{1,0:T(8,128)} %get-tuple-element.27.refs_0_, f32[32,128]{1,0:T(8,128)} %copy-done.21, f32[32,128]{1,0:T(8,128)} %copy-done.22, f32[32,128]{1,0:T(8,128)} %copy-done.23, ...), custom_call_target="tpu_custom_call" | custom-call | tf_op jit(solution)/shard_map/pallas_call | solution.py:133
  74.8 5.3 %all-to-all-start.3 = ((f32[32,4,8,128]{3,2,1,0:T(8,128)}), f32[32,4,8,128]{3,2,1,0:T(8,128)S(1)}, u32[]{:S(2)}, u32[]{:S(2)}) async-start(f32[32,4,8,128]{3,2,1,0:T(8,128)} %get-tuple-element.34), calls=%async_computation.3 | async-start | bytes 1048576 | tf_op jit(solution)/shard_map/all_to_all | solution.py:658
  80.1 1.7 %collective-permute-start.15 = (f32[256,128]{1,0:T(8,128)S(1)}, f32[256,128]{1,0:T(8,128)S(1)}, u32[]{:S(2)}, u32[]{:S(2)}) collective-permute-start(f32[256,128]{1,0:T(8,128)S(1)} %copy-done.31), channel_id=1, source_target_pairs={{1,0},{0,1},{17,16},{16,17},{3,2},{2,3},{19,18},{18,19},{5,4},{4,5... | collective-permute-start | bytes 393224 | tf_op jit(solution)/shard_map/ppermute | solution.py:538
  82.3 1.6 %collective-permute-start.12 = (f32[4,8,256]{2,1,0:T(8,128)S(1)}, f32[4,8,256]{2,1,0:T(8,128)S(1)}, u32[]{:S(2)}, u32[]{:S(2)}) collective-permute-start(f32[4,8,256]{2,1,0:T(8,128)S(1)} %copy-done.36), channel_id=1, source_target_pairs={{1,0},{0,1},{17,16},{16,17},{3,2},{2,3},{19,18},{18,19},{5,4},{4,5... | collective-permute-start | bytes 98312 | tf_op jit(solution)/shard_map/ppermute | solution.py:538
  83.9 10.2 %collective-permute-done.12 = f32[4,8,256]{2,1,0:T(8,128)S(1)} collective-permute-done((f32[4,8,256]{2,1,0:T(8,128)S(1)}, f32[4,8,256]{2,1,0:T(8,128)S(1)}, u32[]{:S(2)}, u32[]{:S(2)}) %collective-permute-start.12) | collective-permute-done | bytes 32800 | tf_op jit(solution)/shard_map/ppermute | solution.py:538
  94.1 3.3 %collective-permute-done.14 = f32[4,8,256]{2,1,0:T(8,128)S(1)} collective-permute-done((f32[4,8,256]{2,1,0:T(8,128)S(1)}, f32[4,8,256]{2,1,0:T(8,128)S(1)}, u32[]{:S(2)}, u32[]{:S(2)}) %collective-permute-start.14) | collective-permute-done | bytes 32800 | tf_op jit(solution)/shard_map/ppermute | solution.py:538
  98.3 3.3 %shard_map.164 = (f32[32,16,128]{2,1,0:T(8,128)}, f32[8,16,256]{2,1,0:T(8,128)}, f32[1024,128]{1,0:T(8,128)}) custom-call(f32[1024,128]{1,0:T(8,128)} %bitcast.31, f32[32,256]{1,0:T(8,128)} %bitcast.51, f32[32,256]{1,0:T(8,128)} %bitcast.52, f32[32,256]{1,0:T(8,128)} %bitcast.53, f32[32,256]{1,0:T(8,128)} %bitcast.54, f32[256,128]{1,0:T(8,128)} %get-tuple-element.39.refs_5_, ...), custom_call_target="tpu_custom_call" | custom-call | tf_op jit(solution)/shard_map/pallas_call | solution.py:133
  101.6 5.5 %all-to-all-start.4 = ((f32[32,16,128]{2,1,0:T(8,128)}), f32[32,16,128]{2,1,0:T(8,128)S(1)}, u32[]{:S(2)}, u32[]{:S(2)}) async-start(f32[32,16,128]{2,1,0:T(8,128)} %get-tuple-element.44), calls=%async_computation.4 | async-start | bytes 524288 | tf_op jit(solution)/shard_map/all_to_all | solution.py:667
  108.8 9.0 %all-to-all-done.4 = f32[32,16,128]{2,1,0:T(8,128)S(1)} async-done(((f32[32,16,128]{2,1,0:T(8,128)}), f32[32,16,128]{2,1,0:T(8,128)S(1)}, u32[]{:S(2)}, u32[]{:S(2)}) %all-to-all-start.4) | async-done | bytes 262176 | tf_op jit(solution)/shard_map/all_to_all | solution.py:667
  118.5 2.5 %shard_map.165 = f32[512,128]{1,0:T(8,128)} custom-call(f32[512,128]{1,0:T(8,128)} %bitcast.35, f32[1024,128]{1,0:T(8,128)} %get-tuple-element.45.refs_1_, f32[128,1]{1,0:T(8,128)} %broadcast_in_dim_reshape.4.refs_2_, f32[128,128]{1,0:T(8,128)} %bitcast.41), custom_call_target="tpu_custom_call" | custom-call | tf_op jit(solution)/shard_map/pallas_call | solution.py:133
  (120 shorter events, 20.1 us)
Async XLA Ops:
  10.4 23.2 %all-to-all-start = ((f32[16,16,256]{2,1,0:T(8,128)}), f32[16,16,256]{2,1,0:T(8,128)S(1)}, u32[]{:S(2)}, u32[]{:S(2)}) async-start(f32[16,16,256]{2,1,0:T(8,128)} %get-tuple-element.24), calls=%async_computation | async-start | bytes 524288 | tf_op jit(solution)/shard_map/all_to_all | solution.py:567
  17.8 3.8 %collective-permute-start = (f32[2,16,128]{2,1,0:T(8,128)S(1)}, f32[2,16,128]{2,1,0:T(8,128)S(1)}, u32[]{:S(2)}, u32[]{:S(2)}) collective-permute-start(f32[2,16,128]{2,1,0:T(8,128)S(1)} %copy-done.24), channel_id=1, source_target_pairs={{1,0},{0,1},{17,16},{16,17},{3,2},{2,3},{19,18},{18,19},{5,4},{4,5... | collective-permute-start | bytes 49160 | tf_op jit(solution)/shard_map/ppermute | solution.py:538
  19.4 2.3 %collective-permute-start.1 = (f32[2,16,128]{2,1,0:T(8,128)S(1)}, f32[2,16,128]{2,1,0:T(8,128)S(1)}, u32[]{:S(2)}, u32[]{:S(2)}) collective-permute-start(f32[2,16,128]{2,1,0:T(8,128)S(1)} %copy-done.24), channel_id=1, source_target_pairs={{16,0},{17,1},{0,16},{1,17},{18,2},{19,3},{2,18},{3,19},{20,4},{21... | collective-permute-start | bytes 49160 | tf_op jit(solution)/shard_map/ppermute | solution.py:538
  19.4 3.2 %collective-permute-start.2 = (f32[2,16,128]{2,1,0:T(8,128)S(1)}, f32[2,16,128]{2,1,0:T(8,128)S(1)}, u32[]{:S(2)}, u32[]{:S(2)}) collective-permute-start(f32[2,16,128]{2,1,0:T(8,128)S(1)} %copy-done.24), channel_id=1, source_target_pairs={{17,0},{16,1},{1,16},{0,17},{19,2},{18,3},{3,18},{2,19},{21,4},{20... | collective-permute-start | bytes 49160 | tf_op jit(solution)/shard_map/ppermute | solution.py:538
  24.7 5.2 %collective-permute-start.3 = (f32[8,16,128]{2,1,0:T(8,128)}, f32[8,16,128]{2,1,0:T(8,128)S(1)}, u32[]{:S(2)}, u32[]{:S(2)}) collective-permute-start(f32[8,16,128]{2,1,0:T(8,128)} %shard_map.159.refs_1_), channel_id=1, source_target_pairs={{2,0},{0,2},{6,4},{4,6},{10,8},{8,10},{14,12},{12,14},{3,1},{1,3},... | collective-permute-start | bytes 196616 | tf_op jit(solution)/shard_map/ppermute | solution.py:538
  26.7 5.0 %collective-permute-start.4 = (f32[8,16,128]{2,1,0:T(8,128)}, f32[8,16,128]{2,1,0:T(8,128)S(1)}, u32[]{:S(2)}, u32[]{:S(2)}) collective-permute-start(f32[8,16,128]{2,1,0:T(8,128)} %shard_map.159.refs_1_), channel_id=1, source_target_pairs={{4,0},{6,2},{0,4},{2,6},{12,8},{14,10},{8,12},{10,14},{5,1},{7,3},... | collective-permute-start | bytes 196616 | tf_op jit(solution)/shard_map/ppermute | solution.py:538
  28.2 5.4 %collective-permute-start.5 = (f32[8,16,128]{2,1,0:T(8,128)}, f32[8,16,128]{2,1,0:T(8,128)S(1)}, u32[]{:S(2)}, u32[]{:S(2)}) collective-permute-start(f32[8,16,128]{2,1,0:T(8,128)} %shard_map.159.refs_1_), channel_id=1, source_target_pairs={{6,0},{4,2},{2,4},{0,6},{14,8},{12,10},{10,12},{8,14},{7,1},{5,3},... | collective-permute-start | bytes 196616 | tf_op jit(solution)/shard_map/ppermute | solution.py:538
  39.5 9.6 %all-to-all-start.1 = ((f32[16,8,256]{2,1,0:T(8,128)}), f32[16,8,256]{2,1,0:T(8,128)S(1)}, u32[]{:S(2)}, u32[]{:S(2)}) async-start(f32[16,8,256]{2,1,0:T(8,128)} %shard_map.160), calls=%async_computation.1 | async-start | bytes 262144 | tf_op jit(solution)/shard_map/all_to_all | solution.py:589
  45.6 18.5 %collective-permute-start.10 = (f32[128,128]{1,0:T(8,128)}, f32[128,128]{1,0:T(8,128)S(1)}, u32[]{:S(2)}, u32[]{:S(2)}) collective-permute-start(f32[128,128]{1,0:T(8,128)} %get-tuple-element.31), channel_id=1, source_target_pairs={{16,0},{17,1},{0,16},{1,17},{18,2},{19,3},{2,18},{3,19},{20,4},{21... | collective-permute-start | bytes 196616 | tf_op jit(solution)/shard_map/ppermute | solution.py:538
  57.3 11.2 %all-to-all-start.2 = ((f32[8,32,128]{2,1,0:T(8,128)}), f32[8,32,128]{2,1,0:T(8,128)S(1)}, u32[]{:S(2)}, u32[]{:S(2)}) async-start(f32[8,32,128]{2,1,0:T(8,128)} %get-tuple-element.33), calls=%async_computation.2 | async-start | bytes 262144 | tf_op jit(solution)/shard_map/all_to_all | solution.py:615
  61.9 6.2 %collective-permute-start.11 = (f32[128,128]{1,0:T(8,128)S(1)}, f32[128,128]{1,0:T(8,128)S(1)}, u32[]{:S(2)}, u32[]{:S(2)}) collective-permute-start(f32[128,128]{1,0:T(8,128)S(1)} %copy-done.33), channel_id=1, source_target_pairs={{17,0},{16,1},{1,16},{0,17},{19,2},{18,3},{3,18},{2,19},{21,4},{20... | collective-permute-start | bytes 196616 | tf_op jit(solution)/shard_map/ppermute | solution.py:538
  62.0 6.2 %collective-permute-start.9 = (f32[128,128]{1,0:T(8,128)S(1)}, f32[128,128]{1,0:T(8,128)S(1)}, u32[]{:S(2)}, u32[]{:S(2)}) collective-permute-start(f32[128,128]{1,0:T(8,128)S(1)} %copy-done.32), channel_id=1, source_target_pairs={{1,0},{0,1},{17,16},{16,17},{3,2},{2,3},{19,18},{18,19},{5,4},{4,5... | collective-permute-start | bytes 196616 | tf_op jit(solution)/shard_map/ppermute | solution.py:538
  63.2 4.9 %collective-permute-start.6 = (f32[32,128]{1,0:T(8,128)S(1)}, f32[32,128]{1,0:T(8,128)S(1)}, u32[]{:S(2)}, u32[]{:S(2)}) collective-permute-start(f32[32,128]{1,0:T(8,128)S(1)} %copy-done.20), channel_id=1, source_target_pairs={{1,0},{0,1},{17,16},{16,17},{3,2},{2,3},{19,18},{18,19},{5,4},{4,5... | collective-permute-start | bytes 49160 | tf_op jit(solution)/shard_map/ppermute | solution.py:538
  64.0 4.1 %collective-permute-start.7 = (f32[32,128]{1,0:T(8,128)S(1)}, f32[32,128]{1,0:T(8,128)S(1)}, u32[]{:S(2)}, u32[]{:S(2)}) collective-permute-start(f32[32,128]{1,0:T(8,128)S(1)} %copy-done.20), channel_id=1, source_target_pairs={{16,0},{17,1},{0,16},{1,17},{18,2},{19,3},{2,18},{3,19},{20,4},{21... | collective-permute-start | bytes 49160 | tf_op jit(solution)/shard_map/ppermute | solution.py:538
  64.2 4.1 %collective-permute-start.8 = (f32[32,128]{1,0:T(8,128)S(1)}, f32[32,128]{1,0:T(8,128)S(1)}, u32[]{:S(2)}, u32[]{:S(2)}) collective-permute-start(f32[32,128]{1,0:T(8,128)S(1)} %copy-done.20), channel_id=1, source_target_pairs={{17,0},{16,1},{1,16},{0,17},{19,2},{18,3},{3,18},{2,19},{21,4},{20... | collective-permute-start | bytes 49160 | tf_op jit(solution)/shard_map/ppermute | solution.py:538
  74.7 19.3 %copy-start.34 = (f32[4,8,256]{2,1,0:T(8,128)S(1)}, f32[4,8,256]{2,1,0:T(8,128)}, u32[]{:S(2)}) copy-start(f32[4,8,256]{2,1,0:T(8,128)} %get-tuple-element.38) | copy-start | bytes 98308
  74.8 22.7 %all-to-all-start.3 = ((f32[32,4,8,128]{3,2,1,0:T(8,128)}), f32[32,4,8,128]{3,2,1,0:T(8,128)S(1)}, u32[]{:S(2)}, u32[]{:S(2)}) async-start(f32[32,4,8,128]{3,2,1,0:T(8,128)} %get-tuple-element.34), calls=%async_computation.3 | async-start | bytes 1048576 | tf_op jit(solution)/shard_map/all_to_all | solution.py:658
  80.1 17.3 %collective-permute-start.15 = (f32[256,128]{1,0:T(8,128)S(1)}, f32[256,128]{1,0:T(8,128)S(1)}, u32[]{:S(2)}, u32[]{:S(2)}) collective-permute-start(f32[256,128]{1,0:T(8,128)S(1)} %copy-done.31), channel_id=1, source_target_pairs={{1,0},{0,1},{17,16},{16,17},{3,2},{2,3},{19,18},{18,19},{5,4},{4,5... | collective-permute-start | bytes 393224 | tf_op jit(solution)/shard_map/ppermute | solution.py:538
  81.7 15.7 %collective-permute-start.16 = (f32[256,128]{1,0:T(8,128)S(1)}, f32[256,128]{1,0:T(8,128)S(1)}, u32[]{:S(2)}, u32[]{:S(2)}) collective-permute-start(f32[256,128]{1,0:T(8,128)S(1)} %copy-done.30), channel_id=1, source_target_pairs={{16,0},{17,1},{0,16},{1,17},{18,2},{19,3},{2,18},{3,19},{20,4},{21... | collective-permute-start | bytes 393224 | tf_op jit(solution)/shard_map/ppermute | solution.py:538
  81.8 15.7 %collective-permute-start.17 = (f32[256,128]{1,0:T(8,128)S(1)}, f32[256,128]{1,0:T(8,128)S(1)}, u32[]{:S(2)}, u32[]{:S(2)}) collective-permute-start(f32[256,128]{1,0:T(8,128)S(1)} %copy-done.29), channel_id=1, source_target_pairs={{17,0},{16,1},{1,16},{0,17},{19,2},{18,3},{3,18},{2,19},{21,4},{20... | collective-permute-start | bytes 393224 | tf_op jit(solution)/shard_map/ppermute | solution.py:538
  82.3 11.8 %collective-permute-start.12 = (f32[4,8,256]{2,1,0:T(8,128)S(1)}, f32[4,8,256]{2,1,0:T(8,128)S(1)}, u32[]{:S(2)}, u32[]{:S(2)}) collective-permute-start(f32[4,8,256]{2,1,0:T(8,128)S(1)} %copy-done.36), channel_id=1, source_target_pairs={{1,0},{0,1},{17,16},{16,17},{3,2},{2,3},{19,18},{18,19},{5,4},{4,5... | collective-permute-start | bytes 98312 | tf_op jit(solution)/shard_map/ppermute | solution.py:538
  83.9 10.2 %collective-permute-start.13 = (f32[4,8,256]{2,1,0:T(8,128)S(1)}, f32[4,8,256]{2,1,0:T(8,128)S(1)}, u32[]{:S(2)}, u32[]{:S(2)}) collective-permute-start(f32[4,8,256]{2,1,0:T(8,128)S(1)} %copy-done.35), channel_id=1, source_target_pairs={{16,0},{17,1},{0,16},{1,17},{18,2},{19,3},{2,18},{3,19},{20,4},{21... | collective-permute-start | bytes 98312 | tf_op jit(solution)/shard_map/ppermute | solution.py:538
  94.1 3.3 %collective-permute-start.14 = (f32[4,8,256]{2,1,0:T(8,128)S(1)}, f32[4,8,256]{2,1,0:T(8,128)S(1)}, u32[]{:S(2)}, u32[]{:S(2)}) collective-permute-start(f32[4,8,256]{2,1,0:T(8,128)S(1)} %copy-done.34), channel_id=1, source_target_pairs={{17,0},{16,1},{1,16},{0,17},{19,2},{18,3},{3,18},{2,19},{21,4},{20... | collective-permute-start | bytes 98312 | tf_op jit(solution)/shard_map/ppermute | solution.py:538
  101.6 16.2 %all-to-all-start.4 = ((f32[32,16,128]{2,1,0:T(8,128)}), f32[32,16,128]{2,1,0:T(8,128)S(1)}, u32[]{:S(2)}, u32[]{:S(2)}) async-start(f32[32,16,128]{2,1,0:T(8,128)} %get-tuple-element.44), calls=%async_computation.4 | async-start | bytes 524288 | tf_op jit(solution)/shard_map/all_to_all | solution.py:667
  (36 other events, 91.0 us)

commit v4 on v3

--- a/solution.py
+++ b/solution.py
@@ -14,6 +14,8 @@
 columns = ("branch", "gj")
 lanes = 128
 far = pl.BlockSpec(memory_space=pl.ANY)
+vmem = pl.BlockSpec(memory_space=pltpu.VMEM)
+params = pltpu.CompilerParams(vmem_limit_bytes=16 * 1024 * 1024)
 
 
 def layer_normalise(values, norm_gain, axis=-1):
@@ -141,6 +143,17 @@
     )(*[bare(operand) for operand in operands])
 
 
+def call_near(kernel, outs, *operands, scratch=()):
+    return pl.pallas_call(
+        lambda *refs: kernel(lambda: None, *refs),
+        out_shape=[jax.ShapeDtypeStruct(out, jnp.float32) for out in outs],
+        in_specs=[vmem] * len(operands),
+        out_specs=[vmem] * len(outs),
+        scratch_shapes=[pltpu.VMEM(shape, jnp.float32) for shape in scratch],
+        compiler_params=params,
+    )(*operands)
+
+
 def spread(me, refs, slots):
     for k, ref in enumerate(refs):
         slots[me ^ k] = ref[...]
@@ -153,26 +166,29 @@
 
 
 def bias_kernel(
-    ready, msa_far, pair_far, gains_far, matrix_far, copies_far, out_ref, pair_ref, gains_ref, matrix_ref, sems
+    ready, msa_far, pair_far, gains_far, matrix_far, copies_far, out_ref, msa_ref, pair_ref,
+    gains_ref, matrix_ref, sems, out_sems
 ):
     rows = msa_far.shape[0]
     repeats = copies_far.shape[0] // rows
     copies = start_copies(
-        [(gains_far, gains_ref), (matrix_far, matrix_ref), (pair_far, pair_ref)]
-        + [(msa_far, copies_far.at[pl.ds(n * rows, rows)]) for n in range(repeats)],
+        [(msa_far, msa_ref), (gains_far, gains_ref), (matrix_far, matrix_ref), (pair_far, pair_ref)],
         sems,
     )
     residues, pair_cols, _ = pair_ref.shape
     heads = matrix_ref.shape[0]
     per = lanes // pair_cols
     ready()
-    wait_all(copies[:3])
+    wait_all(copies)
+    copies = start_copies(
+        [(msa_ref, copies_far.at[pl.ds(n * rows, rows)]) for n in range(repeats)], out_sems
+    )
     normal = layer_normalise(pair_ref[...], gains_ref[0:1, :][None])
     for i in range(residues):
         here = multiply(matrix_ref[...], normal[i], across=True)
         for h in range(heads):
             out_ref[h // per, i : i + 1, pl.ds(h % per * pair_cols, pair_cols)] = here[h : h + 1]
-    wait_all(copies[3:])
+    wait_all(copies)
 
 
 def pair_blocks_kernel(few, residues, ready, pair_ref, *rest):
@@ -265,21 +281,16 @@
                 )
 
 
-def column_kernel(n_branch, n_gj, few, heads, ready, msa_ref, *rest):
-    n_cols = n_branch * n_gj
-    weights, rest = rest[:6], rest[6:]
-    left_far, right_far, chunks, rest = rest[0], rest[1], rest[2 : 2 + n_cols], rest[2 + n_cols :]
-    gains_ref, qkvg_ref, final_ref, expand_ref, shrink_ref, sides_ref = rest[:6]
-    slots, factors_ref, sems, out_sems = rest[6:]
-    copies = start_copies(list(zip(weights, rest[:6])), sems)
+def column_kernel(
+    few, heads, ready, msa_ref, gains_ref, qkvg_ref, final_ref, expand_ref, shrink_ref, sides_ref,
+    left_ref, right_ref, out_ref
+):
     ready()
     count, width = msa_ref.shape
     inner = final_ref.shape[0]
     half = sides_ref.shape[0] // 2
     first = msa_ref[...]
-    normal = layer_normalise(first, 1.0)
-    wait_all(copies[:2])
-    projected = multiply(normal * gains_ref[1:2, :], qkvg_ref[...])
+    projected = multiply(layer_normalise(first, gains_ref[1:2, :]), qkvg_ref[...])
     query, key, value, gate = (projected[:, k * inner : (k + 1) * inner] for k in range(4))
     allowed = None
     if few > 1:
@@ -288,26 +299,27 @@
         holds = lax.broadcasted_iota(jnp.int32, shape, 1)
         allowed = lax.rem(asks, few) == lax.rem(holds, few)
     attended = attend(query, key, value, None, heads, allowed)
-    wait_all(copies[2:])
     second = first + multiply(sigmoid(gate) * attended, final_ref[...])
     expanded = multiply(layer_normalise(second, gains_ref[2:3, :]), expand_ref[...])
     third = second + multiply(jnp.maximum(expanded, 0.0), shrink_ref[...])
-    factors_ref[...] = multiply(
-        sides_ref[...], layer_normalise(third, gains_ref[3:4, :]), across=True
-    )
-    pairs = [(factors_ref.at[pl.ds(0, half)], left_far)]
-    for g in range(right_far.shape[0]):
-        pairs.append((factors_ref.at[pl.ds(half, half)], right_far.at[g]))
-    copies = start_copies(pairs, out_sems)
+    out_ref[...] = third
+    factors = multiply(sides_ref[...], layer_normalise(third, gains_ref[3:4, :]), across=True)
+    left_ref[...] = factors[:half]
+    for g in range(right_ref.shape[0]):
+        right_ref[g] = factors[half:]
+
+
+def msa_blocks_kernel(n_branch, n_gj, ready, msa_ref, *rest):
+    chunks, slots = rest[:-1], rest[-1]
     per_part, each = slots.shape[1:3]
+    ready()
     for b in range(n_branch):
         for g in range(per_part):
             for j in range(n_gj):
                 start = ((b * per_part + g) * n_gj + j) * each
-                slots[b * n_gj + j, g] = third[start : start + each]
+                slots[b * n_gj + j, g] = msa_ref[start : start + each]
     for k, chunk in enumerate(chunks):
         chunk[...] = slots[column_index() ^ k]
-    wait_all(copies)
 
 
 def gather_tiles(few, me, alignment_refs, pair_refs, msa_out, pair_out, msa_slots, slots):
@@ -337,7 +349,8 @@
     gather_tiles(few, column_index(), rest[:n_cols], rest[n_cols : 2 * n_cols], *rest[2 * n_cols :])
 
 
-def triangle_kernel(few, n_cols, ready, tri_ref, *rest):
+def triangle_kernel(few, n_branch, n_gj, ready, tri_ref, *rest):
+    n_cols = n_branch * n_gj
     blocks, (out_ref, msa_out, pair_out, product_ref, msa_slots, slots) = (
         rest[: 2 * n_cols],
         rest[2 * n_cols :],
@@ -357,10 +370,11 @@
     for q in range(share):
         left, right = [], []
         for c in range(n_cols):
-            base = c * n_gi * tiles * each
+            base = (c // n_gj * n_all // n_branch + c % n_gj) * tiles * each
+            step = n_gj * tiles * each
             here = jnp.concatenate(
                 [
-                    tri_ref[pl.ds(base + t * each + q, n_gi, stride=tiles * each), :]
+                    tri_ref[pl.ds(base + t * each + q, n_gi, stride=step), :]
                     for t in range(tiles)
                 ],
                 axis=0,
@@ -370,7 +384,13 @@
                     [jnp.where(group == i, here, 0.0) for i in range(few)], axis=0
                 )
             )
-            here = tri_ref[pl.ds(base + share + q, n_gi * tiles, stride=each), :]
+            here = jnp.concatenate(
+                [
+                    tri_ref[pl.ds(base + g * step + share + q, tiles, stride=each), :]
+                    for g in range(n_gi)
+                ],
+                axis=0,
+            )
             rolled = [here] + [pltpu.roll(here, k * wide, 1) for k in range(1, few)]
             copies = []
             for j in range(few):
@@ -393,7 +413,7 @@
     for c, product in enumerate(swap_lane_groups(products)):
         product_ref[...] = product
         for g in range(n_gi):
-            out_ref[c * n_gi + g] = product_ref[pl.ds(g, rows, stride=n_gi), :]
+            out_ref[(c // n_gj * n_gi + g) * n_gj + c % n_gj] = product_ref[pl.ds(g, rows, stride=n_gi), :]
 
 
 def pair_kernel(
@@ -401,23 +421,17 @@
 ):
     left_refs, pair_refs = rest[:n_cols], rest[n_cols : 2 * n_cols]
     right_ref, gain_ref, matrix_ref, triangle_ref, tri_ref = rest[2 * n_cols : 2 * n_cols + 5]
-    matrix_far, triangle_far = matrix_ref, triangle_ref
     chunks = rest[2 * n_cols + 5 : 3 * n_cols + 5]
     rest = rest[3 * n_cols + 5 :]
-    left_ref, slots, pair_ref, first_ref, gate_ref, matrix_ref, triangle_ref, sems = rest
+    left_ref, slots, pair_ref, first_ref, gate_ref = rest
     me = column_index()
     groups_j = n_gi // n_cols
     block = pair_refs[0].shape[0]
-    pairs = [(ref, left_ref.at[me ^ k]) for k, ref in enumerate(left_refs)]
-    for k, ref in enumerate(pair_refs):
-        start = pl.multiple_of((me ^ k) * block, 8)
-        pairs.append((ref, slots.at[pl.ds(start, block)]))
-    pairs += [(matrix_far, matrix_ref), (triangle_far, triangle_ref)]
-    copies = start_copies(pairs, sems)
+    ready()
+    spread(me, left_refs, left_ref)
+    spread_rows(me, pair_refs, slots)
     _, wide, count = left_ref.shape
     half = block // groups_j
-    ready()
-    wait_all(copies[:n_cols])
     all_rows = count // few
     residues = n_cols * few
     pair_cols = n_gi * few
@@ -451,7 +465,6 @@
             s[:, t * lanes : (t + 1) * lanes] for s in swapped for t in range(wide // per)
         ]
         outputs.append(jnp.concatenate(stacked, axis=0))
-    wait_all(copies[n_cols:])
     for c in range(n_cols):
         for o in range(groups_j):
             pair_ref[pl.ds(c * groups_j + o, half, stride=n_gi), :] = slots[
@@ -561,11 +574,16 @@
         [pair_input_tensor],
         [pair_norm_gains],
         [pair_bias_matrix.T],
-        scratch=[pair_input_tensor.shape, pair_norm_gains.shape, (heads, pair_width)],
-        sems=[3 + parts],
+        scratch=[
+            homolog_embedding.shape,
+            pair_input_tensor.shape,
+            pair_norm_gains.shape,
+            (heads, pair_width),
+        ],
+        sems=[4, parts],
     )
     msa = lax.all_to_all(msa, "gi", 0, 0, tiled=True)
-    (bias,) = call(
+    (bias,) = call_near(
         functools.partial(bias_rows_kernel, n_cols),
         [(heads, residues, length)],
         *trade([bias] * n_cols, columns),
@@ -596,16 +614,19 @@
         feedforward_shrink_kernel,
         dyadic_sides_kernel.T,
     )
-    left, right, *alignment = call(
-        functools.partial(column_kernel, n_branch, n_gj, few, heads),
-        [[(outer_width, count)], [(n_gi, outer_width, count)]] + [(per_part, each, width)] * n_cols,
+    left, right, alignment = call_near(
+        functools.partial(column_kernel, few, heads),
+        [(outer_width, count), (n_gi, outer_width, count), (count, width)],
         msa_first.reshape(count, width),
-        *[[w] for w in weights],
-        scratch=[w.shape for w in weights]
-        + [(n_cols, per_part, each, width), (2 * outer_width, count)],
-        sems=[len(weights), 1 + n_gi],
-    )
-    pair = call(
+        *weights,
+    )
+    alignment = call_near(
+        functools.partial(msa_blocks_kernel, n_branch, n_gj),
+        [(per_part, each, width)] * n_cols,
+        alignment,
+        scratch=[(n_cols, per_part, each, width)],
+    )
+    pair = call_near(
         functools.partial(pair_blocks_kernel, few, residues),
         [(positions // n_cols, pair_width)] * n_cols,
         pair.reshape(positions, pair_width),
@@ -627,25 +648,23 @@
     )
     matrix = outer_output_matrix.reshape(outer_width, outer_width // per, per, pair_width)
     matrix = jnp.transpose(matrix, (3, 2, 1, 0)).reshape(pair_width, -1)
-    tri, *first_gate = call(
+    tri, *first_gate = call_near(
         functools.partial(pair_kernel, few, n_gi, n_cols),
         [(slots, positions // lanes, 2 * share, lanes)]
         + [(2 * positions // n_cols, pair_width)] * n_cols,
-        *[[block] for block in left + pair],
+        *left,
+        *pair,
         right.reshape(n_gi * outer_width, count),
         pair_norm_gains[1][:, None],
-        [matrix],
-        [triangle],
+        matrix,
+        triangle,
         scratch=[
             (n_cols, outer_width, count),
             (positions, pair_width),
             (positions, pair_width),
             (positions, pair_width),
             (positions, pair_width),
-            matrix.shape,
-            triangle.shape,
         ],
-        sems=[2 * n_cols + 2],
     )
 
     first_gate = trade(first_gate, columns)
@@ -654,22 +673,21 @@
     packed = share * n_all == pair_width and share == few and few == per
     gain, last = pair_norm_gains[2], triangle_output_matrix
     if packed:
-        order = [[(c // n_gj * n_gi + g) * n_gj + c % n_gj for c in range(n_cols) for g in range(n_gi)]]
-        tri = lax.all_to_all(tri, everyone, 0, 0, tiled=True, axis_index_groups=order)
-        product, alignment_output, first_gate = call(
-            functools.partial(triangle_kernel, few, n_cols),
+        tri = lax.all_to_all(tri, everyone, 0, 0, tiled=True)
+        product, alignment_output, first_gate = call_near(
+            functools.partial(triangle_kernel, few, n_branch, n_gj),
             [(n_all, residues, lanes)] + tiles,
                 tri.reshape(-1, lanes),
             *alignment,
             *first_gate,
             scratch=[(lanes, lanes)] + scratch,
         )
-        product = lax.all_to_all(product, everyone, 0, 0, tiled=True, axis_index_groups=order)
+        product = lax.all_to_all(product, everyone, 0, 0, tiled=True)
         product = product.reshape(n_all * residues, lanes)
         gain = gain.reshape(n_all, share).T.reshape(-1)
         last = jnp.swapaxes(last.reshape(n_all, share, pair_width), 0, 1).reshape(last.shape)
     else:
-        alignment_output, first_gate = call(
+        alignment_output, first_gate = call_near(
             functools.partial(gather_kernel, few, n_cols),
             tiles,
                 *alignment,
@@ -686,7 +704,7 @@
             tiled=True,
         ).reshape(groups, n_cols, few, residues, pair_width)
         product = jnp.transpose(product, (4, 3, 2, 0, 1)).reshape(pair_width, positions)
-    (pair_output_tensor,) = call(
+    (pair_output_tensor,) = call_near(
         functools.partial(final_kernel, few, n_cols, residues, packed),
         [(positions, pair_width)],
         product,

time: 122 us -> 107 us (0.88)
  Pallas kernels: 36.5 us -> 20 us
  local copies, waits for them, and re-layouts: 10.2 us -> 11.7 us
  starting transfers between devices: 38.9 us -> 40.2 us
    pallas_call x8 -> x2, Pallas kernels: 36.5 us -> 6.98 us  [call(): pl.pallas_call(body, out_shape=[jax.ShapeDtypeStruct(bare(out), jnp.float...]
    pallas_call x0 -> x7, Pallas kernels: none -> 13 us  [call_near(): pl.pallas_call(lambda *refs: kernel(lambda: None, *refs), out_shape=[jax....]
    all_to_all x1, waiting for transfers between devices: 3.09 us -> 1.23 us  [per_device(): lax.all_to_all(msa_first, everyone, 0, 0, tiled=True, axis_index_groups=h...]
    unnamed x75 -> x63, local copies, waits for them, and re-layouts: 6.41 us -> 8.17 us
    all_to_all x2, waiting for transfers between devices: 8.99 us -> 10.3 us  [the longest x1 10.3 us: per_device(): product = lax.all_to_all(product, everyone, 0, 0, tiled=True)]
  transfers between devices with their start and end apart: 23 -> 23, of which waited for: 11 -> 13; matrix products, arithmetic and copies ran while one was open for 4% -> 4% of each run, Pallas kernels for 9% -> 5%
where the time goes in v4:
time: 107 us; the launch traced here: 106 us
  starting transfers between devices  40.2 us (38%)
  waiting for transfers between devices  33 us (31%)
  Pallas kernels  20 us (19%)
  local copies, waits for them, and re-layouts  11.7 us (11%)
    ppermute x18, waiting for transfers between devices, trade(): lax.ppermute(blocks[k], axes, [(t ^ k, t) for t in range(n) if t ^ k < n])  21.3 us
    ppermute x18, starting transfers between devices, trade(): lax.ppermute(blocks[k], axes, [(t ^ k, t) for t in range(n) if t ^ k < n])  14 us
    pallas_call x7, Pallas kernels, call_near(): pl.pallas_call(lambda *refs: kernel(lambda: None, *refs), out_shape=[jax....  13 us
    all_to_all x1, waiting for transfers between devices, per_device(): product = lax.all_to_all(product, everyone, 0, 0, tiled=True)  10.3 us
    unnamed x63, local copies, waits for them, and re-layouts  8.17 us
    all_to_all x1, starting transfers between devices, per_device(): msa = lax.all_to_all(msa, 'gi', 0, 0, tiled=True)  7.42 us
    pallas_call x2, Pallas kernels, call(): pl.pallas_call(body, out_shape=[jax.ShapeDtypeStruct(bare(out), jnp.float...  6.98 us
    all_to_all x1, starting transfers between devices, per_device(): tri = lax.all_to_all(tri, everyone, 0, 0, tiled=True)  5.86 us
  transfers between devices with their start and end apart: 23, of which 13 were waited for; matrix products, arithmetic and copies ran while one was open for 4% of the time, Pallas kernels for 5%

profile of v4, /device:TPU:0, one launch (start us, length us, event | category | flops | bytes accessed | tf_op | source)
XLA Modules:
  0.0 105.9 jit_solution(14789248925035802965)
XLA Ops:
  0.6 2.4 %shard_map.158 = (f32[16,16,256]{2,1,0:T(8,128)}, f32[2,16,128]{2,1,0:T(8,128)}) custom-call(f32[8,16,256]{2,1,0:T(8,128)} %refs_0_.1, f32[16,32,128]{2,1,0:T(8,128)} %refs_1_.2, f32[3,128]{1,0:T(4,128)} %refs_2_.2, f32[8,128]{1,0:T(8,128)} %bitcast.55), custom_call_target="tpu_custom_call" | custom-call | tf_op jit(solution)/shard_map/pallas_call | solution.py:135
  3.1 7.4 %all-to-all-start = ((f32[16,16,256]{2,1,0:T(8,128)}), f32[16,16,256]{2,1,0:T(8,128)S(1)}, u32[]{:S(2)}, u32[]{:S(2)}) async-start(f32[16,16,256]{2,1,0:T(8,128)} %get-tuple-element.25), calls=%async_computation | async-start | bytes 524288 | tf_op jit(solution)/shard_map/all_to_all | solution.py:585
  10.5 1.6 %collective-permute-start = (f32[2,16,128]{2,1,0:T(8,128)S(1)}, f32[2,16,128]{2,1,0:T(8,128)S(1)}, u32[]{:S(2)}, u32[]{:S(2)}) collective-permute-start(f32[2,16,128]{2,1,0:T(8,128)S(1)} %copy-done.12), channel_id=1, source_target_pairs={{1,0},{0,1},{17,16},{16,17},{3,2},{2,3},{19,18},{18,19},{5,4},{4,5... | collective-permute-start | bytes 49160 | tf_op jit(solution)/shard_map/ppermute | solution.py:551
  12.9 1.4 %collective-permute-done.refs_1_ = f32[2,16,128]{2,1,0:T(8,128)S(1)} collective-permute-done((f32[2,16,128]{2,1,0:T(8,128)S(1)}, f32[2,16,128]{2,1,0:T(8,128)S(1)}, u32[]{:S(2)}, u32[]{:S(2)}) %collective-permute-start) | collective-permute-done | bytes 16416 | tf_op jit(solution)/shard_map/ppermute | solution.py:551
  15.4 2.0 %collective-permute-start.3 = (f32[8,16,128]{2,1,0:T(8,128)S(1)}, f32[8,16,128]{2,1,0:T(8,128)S(1)}, u32[]{:S(2)}, u32[]{:S(2)}) collective-permute-start(f32[8,16,128]{2,1,0:T(8,128)S(1)} %shard_map.159.refs_1_), channel_id=1, source_target_pairs={{2,0},{0,2},{6,4},{4,6},{10,8},{8,10},{14,12},{12,14},{3,1},{1,3},... | collective-permute-start | bytes 196616 | tf_op jit(solution)/shard_map/ppermute | solution.py:551
  17.4 1.5 %collective-permute-start.4 = (f32[8,16,128]{2,1,0:T(8,128)S(1)}, f32[8,16,128]{2,1,0:T(8,128)S(1)}, u32[]{:S(2)}, u32[]{:S(2)}) collective-permute-start(f32[8,16,128]{2,1,0:T(8,128)S(1)} %shard_map.159.refs_1_), channel_id=1, source_target_pairs={{4,0},{6,2},{0,4},{2,6},{12,8},{14,10},{8,12},{10,14},{5,1},{7,3},... | collective-permute-start | bytes 196616 | tf_op jit(solution)/shard_map/ppermute | solution.py:551
  20.8 1.4 %collective-permute-done.4.refs_3_ = f32[8,16,128]{2,1,0:T(8,128)S(1)} collective-permute-done((f32[8,16,128]{2,1,0:T(8,128)S(1)}, f32[8,16,128]{2,1,0:T(8,128)S(1)}, u32[]{:S(2)}, u32[]{:S(2)}) %collective-permute-start.4) | collective-permute-done | bytes 65568 | tf_op jit(solution)/shard_map/ppermute | solution.py:551
  22.8 1.3 %collective-permute-done.5.refs_4_ = f32[8,16,128]{2,1,0:T(8,128)} collective-permute-done((f32[8,16,128]{2,1,0:T(8,128)S(1)}, f32[8,16,128]{2,1,0:T(8,128)}, u32[]{:S(2)}, u32[]{:S(2)}) %collective-permute-start.5) | collective-permute-done | bytes 65568 | tf_op jit(solution)/shard_map/ppermute | solution.py:551
  24.9 4.6 %shard_map.160 = f32[16,8,256]{2,1,0:T(8,128)} custom-call(f32[16,16,256]{2,1,0:T(8,128)} %copy-done.18, f32[8,16,128]{2,1,0:T(8,128)} %copy-done.4, f32[8,16,128]{2,1,0:T(8,128)} %copy-done.25, f32[8,16,128]{2,1,0:T(8,128)} %copy-done.26, f32[8,16,128]{2,1,0:T(8,128)} %collective-permute-done.5.refs_4_, f32[4,256]{1,0:T(4,128)} %refs_1_.3, ...), custom_call_target="tpu_custom_call" | custom-call | tf_op jit(solution)/shard_map/pallas_call | solution.py:135
  29.5 3.5 %all-to-all-start.1 = ((f32[16,8,256]{2,1,0:T(8,128)}), f32[16,8,256]{2,1,0:T(8,128)S(1)}, u32[]{:S(2)}, u32[]{:S(2)}) async-start(f32[16,8,256]{2,1,0:T(8,128)} %shard_map.160), calls=%async_computation.1 | async-start | bytes 262144 | tf_op jit(solution)/shard_map/all_to_all | solution.py:607
  37.8 1.2 %all-to-all-done.1 = f32[16,8,256]{2,1,0:T(8,128)S(1)} async-done(((f32[16,8,256]{2,1,0:T(8,128)}), f32[16,8,256]{2,1,0:T(8,128)S(1)}, u32[]{:S(2)}, u32[]{:S(2)}) %all-to-all-start.1) | async-done | bytes 131104 | tf_op jit(solution)/shard_map/all_to_all | solution.py:607
  40.6 4.0 %shard_map.161 = (f32[32,128]{1,0:T(8,128)S(1)}, f32[8,32,128]{2,1,0:T(8,128)S(1)}, f32[128,256]{1,0:T(8,128)S(1)}) custom-call(f32[128,256]{1,0:T(8,128)S(1)} %bitcast.34, f32[4,256]{1,0:T(4,128)S(1)} %copy-done.13, f32[256,1024]{1,0:T(8,128)S(1)} %copy-done.1, f32[256,256]{1,0:T(8,128)S(1)} %copy-done.5, f32[256,1024]{1,0:T(8,128)S(1)} %copy-done.2, ...), custom_call_target="tpu_custom_call" | custom-call | tf_op jit(solution)/shard_map/pallas_call | solution.py:147
  45.9 4.6 %all-to-all-start.2 = ((f32[8,32,128]{2,1,0:T(8,128)}), f32[8,32,128]{2,1,0:T(8,128)S(1)}, u32[]{:S(2)}, u32[]{:S(2)}) async-start(f32[8,32,128]{2,1,0:T(8,128)} %copy-done.8), calls=%async_computation.2 | async-start | bytes 262144 | tf_op jit(solution)/shard_map/all_to_all | solution.py:636
  53.1 1.5 %collective-permute-start.6 = (f32[32,128]{1,0:T(8,128)S(1)}, f32[32,128]{1,0:T(8,128)S(1)}, u32[]{:S(2)}, u32[]{:S(2)}) collective-permute-start(f32[32,128]{1,0:T(8,128)S(1)} %get-tuple-element.28.refs_0_), channel_id=1, source_target_pairs={{1,0},{0,1},{17,16},{16,17},{3,2},{2,3},{19,18},{18,19},{5,4},{4,5... | collective-permute-start | bytes 49160 | tf_op jit(solution)/shard_map/ppermute | solution.py:551
  58.0 5.0 %shard_map.163 = (f32[32,4,8,128]{3,2,1,0:T(8,128)}, f32[256,128]{1,0:T(8,128)S(1)}, f32[256,128]{1,0:T(8,128)S(1)}, f32[256,128]{1,0:T(8,128)S(1)}, f32[256,128]{1,0:T(8,128)S(1)}) custom-call(f32[32,128]{1,0:T(8,128)S(1)} %get-tuple-element.28.refs_0_, f32[32,128]{1,0:T(8,128)S(1)} %collective-permute-done.6.refs_1_, ...), custom_call_target="tpu_custom_call" | custom-call | tf_op jit(solution)/shard_map/pallas_call | solution.py:147
  62.9 5.9 %all-to-all-start.3 = ((f32[32,4,8,128]{3,2,1,0:T(8,128)}), f32[32,4,8,128]{3,2,1,0:T(8,128)S(1)}, u32[]{:S(2)}, u32[]{:S(2)}) async-start(f32[32,4,8,128]{3,2,1,0:T(8,128)} %get-tuple-element.35), calls=%async_computation.3 | async-start | bytes 1048576 | tf_op jit(solution)/shard_map/all_to_all | solution.py:676
  68.8 1.8 %collective-permute-start.15 = (f32[256,128]{1,0:T(8,128)S(1)}, f32[256,128]{1,0:T(8,128)S(1)}, u32[]{:S(2)}, u32[]{:S(2)}) collective-permute-start(f32[256,128]{1,0:T(8,128)S(1)} %get-tuple-element.42), channel_id=1, source_target_pairs={{1,0},{0,1},{17,16},{16,17},{3,2},{2,3},{19,18},{18,19},{5,4},{4,5... | collective-permute-start | bytes 393224 | tf_op jit(solution)/shard_map/ppermute | solution.py:551
  71.0 1.8 %collective-permute-start.12 = (f32[4,8,256]{2,1,0:T(8,128)S(1)}, f32[4,8,256]{2,1,0:T(8,128)S(1)}, u32[]{:S(2)}, u32[]{:S(2)}) collective-permute-start(f32[4,8,256]{2,1,0:T(8,128)S(1)} %get-tuple-element.38), channel_id=1, source_target_pairs={{1,0},{0,1},{17,16},{16,17},{3,2},{2,3},{19,18},{18,19},{5,4},{4,5... | collective-permute-start | bytes 98312 | tf_op jit(solution)/shard_map/ppermute | solution.py:551
  72.9 10.6 %collective-permute-done.12 = f32[4,8,256]{2,1,0:T(8,128)S(1)} collective-permute-done((f32[4,8,256]{2,1,0:T(8,128)S(1)}, f32[4,8,256]{2,1,0:T(8,128)S(1)}, u32[]{:S(2)}, u32[]{:S(2)}) %collective-permute-start.12) | collective-permute-done | bytes 32800 | tf_op jit(solution)/shard_map/ppermute | solution.py:551
  83.4 3.3 %collective-permute-done.14 = f32[4,8,256]{2,1,0:T(8,128)S(1)} collective-permute-done((f32[4,8,256]{2,1,0:T(8,128)S(1)}, f32[4,8,256]{2,1,0:T(8,128)S(1)}, u32[]{:S(2)}, u32[]{:S(2)}) %collective-permute-start.14) | collective-permute-done | bytes 32800 | tf_op jit(solution)/shard_map/ppermute | solution.py:551
  86.8 1.8 %shard_map.165 = (f32[32,16,128]{2,1,0:T(8,128)}, f32[8,16,256]{2,1,0:T(8,128)}, f32[1024,128]{1,0:T(8,128)S(1)}) custom-call(f32[1024,128]{1,0:T(8,128)S(1)} %bitcast.31, f32[32,256]{1,0:T(8,128)S(1)} %bitcast.38, f32[32,256]{1,0:T(8,128)S(1)} %bitcast.39, f32[32,256]{1,0:T(8,128)S(1)} %bitcast.40, f32[32,256]{1,0:T(8,128)S(1)} %bitcast.41, ...), custom_call_target="tpu_custom_call" | custom-call | tf_op jit(solution)/shard_map/pallas_call | solution.py:147
  88.6 4.8 %all-to-all-start.4 = ((f32[32,16,128]{2,1,0:T(8,128)}), f32[32,16,128]{2,1,0:T(8,128)S(1)}, u32[]{:S(2)}, u32[]{:S(2)}) async-start(f32[32,16,128]{2,1,0:T(8,128)} %get-tuple-element.46), calls=%async_computation.4 | async-start | bytes 524288 | tf_op jit(solution)/shard_map/all_to_all | solution.py:685
  94.3 10.3 %all-to-all-done.4 = f32[32,16,128]{2,1,0:T(8,128)S(1)} async-done(((f32[32,16,128]{2,1,0:T(8,128)}), f32[32,16,128]{2,1,0:T(8,128)S(1)}, u32[]{:S(2)}, u32[]{:S(2)}) %all-to-all-start.4) | async-done | bytes 262176 | tf_op jit(solution)/shard_map/all_to_all | solution.py:685
  104.6 1.3 %shard_map.166 = f32[512,128]{1,0:T(8,128)} custom-call(f32[512,128]{1,0:T(8,128)S(1)} %bitcast.33, f32[1024,128]{1,0:T(8,128)S(1)} %get-tuple-element.47.refs_1_, f32[128,1]{1,0:T(8,128)S(1)} %broadcast_in_dim_reshape.4.refs_2_, f32[128,128]{1,0:T(8,128)S(1)} %bitcast.36), custom_call_target="tpu_custom_call" | custom-call | tf_op jit(solution)/shard_map/pallas_call | solution.py:147
  (109 shorter events, 20.0 us)
Async XLA Ops:
  3.1 21.1 %all-to-all-start = ((f32[16,16,256]{2,1,0:T(8,128)}), f32[16,16,256]{2,1,0:T(8,128)S(1)}, u32[]{:S(2)}, u32[]{:S(2)}) async-start(f32[16,16,256]{2,1,0:T(8,128)} %get-tuple-element.25), calls=%async_computation | async-start | bytes 524288 | tf_op jit(solution)/shard_map/all_to_all | solution.py:585
  10.5 3.8 %collective-permute-start = (f32[2,16,128]{2,1,0:T(8,128)S(1)}, f32[2,16,128]{2,1,0:T(8,128)S(1)}, u32[]{:S(2)}, u32[]{:S(2)}) collective-permute-start(f32[2,16,128]{2,1,0:T(8,128)S(1)} %copy-done.12), channel_id=1, source_target_pairs={{1,0},{0,1},{17,16},{16,17},{3,2},{2,3},{19,18},{18,19},{5,4},{4,5... | collective-permute-start | bytes 49160 | tf_op jit(solution)/shard_map/ppermute | solution.py:551
  12.1 2.3 %collective-permute-start.1 = (f32[2,16,128]{2,1,0:T(8,128)S(1)}, f32[2,16,128]{2,1,0:T(8,128)S(1)}, u32[]{:S(2)}, u32[]{:S(2)}) collective-permute-start(f32[2,16,128]{2,1,0:T(8,128)S(1)} %copy-done.12), channel_id=1, source_target_pairs={{16,0},{17,1},{0,16},{1,17},{18,2},{19,3},{2,18},{3,19},{20,4},{21... | collective-permute-start | bytes 49160 | tf_op jit(solution)/shard_map/ppermute | solution.py:551
  12.1 3.2 %collective-permute-start.2 = (f32[2,16,128]{2,1,0:T(8,128)S(1)}, f32[2,16,128]{2,1,0:T(8,128)S(1)}, u32[]{:S(2)}, u32[]{:S(2)}) collective-permute-start(f32[2,16,128]{2,1,0:T(8,128)S(1)} %copy-done.12), channel_id=1, source_target_pairs={{17,0},{16,1},{1,16},{0,17},{19,2},{18,3},{3,18},{2,19},{21,4},{20... | collective-permute-start | bytes 49160 | tf_op jit(solution)/shard_map/ppermute | solution.py:551
  15.4 5.3 %collective-permute-start.3 = (f32[8,16,128]{2,1,0:T(8,128)S(1)}, f32[8,16,128]{2,1,0:T(8,128)S(1)}, u32[]{:S(2)}, u32[]{:S(2)}) collective-permute-start(f32[8,16,128]{2,1,0:T(8,128)S(1)} %shard_map.159.refs_1_), channel_id=1, source_target_pairs={{2,0},{0,2},{6,4},{4,6},{10,8},{8,10},{14,12},{12,14},{3,1},{1,3},... | collective-permute-start | bytes 196616 | tf_op jit(solution)/shard_map/ppermute | solution.py:551
  17.4 4.8 %collective-permute-start.4 = (f32[8,16,128]{2,1,0:T(8,128)S(1)}, f32[8,16,128]{2,1,0:T(8,128)S(1)}, u32[]{:S(2)}, u32[]{:S(2)}) collective-permute-start(f32[8,16,128]{2,1,0:T(8,128)S(1)} %shard_map.159.refs_1_), channel_id=1, source_target_pairs={{4,0},{6,2},{0,4},{2,6},{12,8},{14,10},{8,12},{10,14},{5,1},{7,3},... | collective-permute-start | bytes 196616 | tf_op jit(solution)/shard_map/ppermute | solution.py:551
  18.9 5.3 %collective-permute-start.5 = (f32[8,16,128]{2,1,0:T(8,128)S(1)}, f32[8,16,128]{2,1,0:T(8,128)}, u32[]{:S(2)}, u32[]{:S(2)}) collective-permute-start(f32[8,16,128]{2,1,0:T(8,128)S(1)} %shard_map.159.refs_1_), channel_id=1, source_target_pairs={{6,0},{4,2},{2,4},{0,6},{14,8},{12,10},{10,12},{8,14},{7,1},{5,3},... | collective-permute-start | bytes 196616 | tf_op jit(solution)/shard_map/ppermute | solution.py:551
  19.0 20.1 %copy-start.3 = (f32[1024,256]{1,0:T(8,128)S(1)}, f32[1024,256]{1,0:T(8,128)}, u32[]{:S(2)}) copy-start(f32[1024,256]{1,0:T(8,128)} %refs_5_.3) | copy-start | bytes 3145732
  29.5 9.6 %all-to-all-start.1 = ((f32[16,8,256]{2,1,0:T(8,128)}), f32[16,8,256]{2,1,0:T(8,128)S(1)}, u32[]{:S(2)}, u32[]{:S(2)}) async-start(f32[16,8,256]{2,1,0:T(8,128)} %shard_map.160), calls=%async_computation.1 | async-start | bytes 262144 | tf_op jit(solution)/shard_map/all_to_all | solution.py:607
  37.5 17.0 %collective-permute-start.10 = (f32[128,128]{1,0:T(8,128)}, f32[128,128]{1,0:T(8,128)}, u32[]{:S(2)}, u32[]{:S(2)}) collective-permute-start(f32[128,128]{1,0:T(8,128)} %get-tuple-element.32), channel_id=1, source_target_pairs={{16,0},{17,1},{0,16},{1,17},{18,2},{19,3},{2,18},{3,19},{20,4},{21... | collective-permute-start | bytes 196616 | tf_op jit(solution)/shard_map/ppermute | solution.py:551
  45.9 12.1 %all-to-all-start.2 = ((f32[8,32,128]{2,1,0:T(8,128)}), f32[8,32,128]{2,1,0:T(8,128)S(1)}, u32[]{:S(2)}, u32[]{:S(2)}) async-start(f32[8,32,128]{2,1,0:T(8,128)} %copy-done.8), calls=%async_computation.2 | async-start | bytes 262144 | tf_op jit(solution)/shard_map/all_to_all | solution.py:636
  51.4 5.2 %collective-permute-start.11 = (f32[128,128]{1,0:T(8,128)S(1)}, f32[128,128]{1,0:T(8,128)S(1)}, u32[]{:S(2)}, u32[]{:S(2)}) collective-permute-start(f32[128,128]{1,0:T(8,128)S(1)} %copy-done.17), channel_id=1, source_target_pairs={{17,0},{16,1},{1,16},{0,17},{19,2},{18,3},{3,18},{2,19},{21,4},{20... | collective-permute-start | bytes 196616 | tf_op jit(solution)/shard_map/ppermute | solution.py:551
  52.5 4.8 %collective-permute-start.9 = (f32[128,128]{1,0:T(8,128)S(1)}, f32[128,128]{1,0:T(8,128)S(1)}, u32[]{:S(2)}, u32[]{:S(2)}) collective-permute-start(f32[128,128]{1,0:T(8,128)S(1)} %copy-done.15), channel_id=1, source_target_pairs={{1,0},{0,1},{17,16},{16,17},{3,2},{2,3},{19,18},{18,19},{5,4},{4,5... | collective-permute-start | bytes 196616 | tf_op jit(solution)/shard_map/ppermute | solution.py:551
  53.1 4.4 %collective-permute-start.6 = (f32[32,128]{1,0:T(8,128)S(1)}, f32[32,128]{1,0:T(8,128)S(1)}, u32[]{:S(2)}, u32[]{:S(2)}) collective-permute-start(f32[32,128]{1,0:T(8,128)S(1)} %get-tuple-element.28.refs_0_), channel_id=1, source_target_pairs={{1,0},{0,1},{17,16},{16,17},{3,2},{2,3},{19,18},{18,19},{5,4},{4,5... | collective-permute-start | bytes 49160 | tf_op jit(solution)/shard_map/ppermute | solution.py:551
  54.5 3.0 %collective-permute-start.7 = (f32[32,128]{1,0:T(8,128)S(1)}, f32[32,128]{1,0:T(8,128)S(1)}, u32[]{:S(2)}, u32[]{:S(2)}) collective-permute-start(f32[32,128]{1,0:T(8,128)S(1)} %get-tuple-element.28.refs_0_), channel_id=1, source_target_pairs={{16,0},{17,1},{0,16},{1,17},{18,2},{19,3},{2,18},{3,19},{20,4},{21... | collective-permute-start | bytes 49160 | tf_op jit(solution)/shard_map/ppermute | solution.py:551
  54.5 3.2 %collective-permute-start.8 = (f32[32,128]{1,0:T(8,128)S(1)}, f32[32,128]{1,0:T(8,128)S(1)}, u32[]{:S(2)}, u32[]{:S(2)}) collective-permute-start(f32[32,128]{1,0:T(8,128)S(1)} %get-tuple-element.28.refs_0_), channel_id=1, source_target_pairs={{17,0},{16,1},{1,16},{0,17},{19,2},{18,3},{3,18},{2,19},{21,4},{20... | collective-permute-start | bytes 49160 | tf_op jit(solution)/shard_map/ppermute | solution.py:551
  62.9 23.8 %all-to-all-start.3 = ((f32[32,4,8,128]{3,2,1,0:T(8,128)}), f32[32,4,8,128]{3,2,1,0:T(8,128)S(1)}, u32[]{:S(2)}, u32[]{:S(2)}) async-start(f32[32,4,8,128]{3,2,1,0:T(8,128)} %get-tuple-element.35), calls=%async_computation.3 | async-start | bytes 1048576 | tf_op jit(solution)/shard_map/all_to_all | solution.py:676
  68.8 18.0 %collective-permute-start.15 = (f32[256,128]{1,0:T(8,128)S(1)}, f32[256,128]{1,0:T(8,128)S(1)}, u32[]{:S(2)}, u32[]{:S(2)}) collective-permute-start(f32[256,128]{1,0:T(8,128)S(1)} %get-tuple-element.42), channel_id=1, source_target_pairs={{1,0},{0,1},{17,16},{16,17},{3,2},{2,3},{19,18},{18,19},{5,4},{4,5... | collective-permute-start | bytes 393224 | tf_op jit(solution)/shard_map/ppermute | solution.py:551
  70.6 16.1 %collective-permute-start.16 = (f32[256,128]{1,0:T(8,128)S(1)}, f32[256,128]{1,0:T(8,128)S(1)}, u32[]{:S(2)}, u32[]{:S(2)}) collective-permute-start(f32[256,128]{1,0:T(8,128)S(1)} %get-tuple-element.43), channel_id=1, source_target_pairs={{16,0},{17,1},{0,16},{1,17},{18,2},{19,3},{2,18},{3,19},{20,4},{21... | collective-permute-start | bytes 393224 | tf_op jit(solution)/shard_map/ppermute | solution.py:551
  70.6 16.1 %collective-permute-start.17 = (f32[256,128]{1,0:T(8,128)S(1)}, f32[256,128]{1,0:T(8,128)S(1)}, u32[]{:S(2)}, u32[]{:S(2)}) collective-permute-start(f32[256,128]{1,0:T(8,128)S(1)} %get-tuple-element.44), channel_id=1, source_target_pairs={{17,0},{16,1},{1,16},{0,17},{19,2},{18,3},{3,18},{2,19},{21,4},{20... | collective-permute-start | bytes 393224 | tf_op jit(solution)/shard_map/ppermute | solution.py:551
  71.0 12.4 %collective-permute-start.12 = (f32[4,8,256]{2,1,0:T(8,128)S(1)}, f32[4,8,256]{2,1,0:T(8,128)S(1)}, u32[]{:S(2)}, u32[]{:S(2)}) collective-permute-start(f32[4,8,256]{2,1,0:T(8,128)S(1)} %get-tuple-element.38), channel_id=1, source_target_pairs={{1,0},{0,1},{17,16},{16,17},{3,2},{2,3},{19,18},{18,19},{5,4},{4,5... | collective-permute-start | bytes 98312 | tf_op jit(solution)/shard_map/ppermute | solution.py:551
  72.9 10.6 %collective-permute-start.13 = (f32[4,8,256]{2,1,0:T(8,128)S(1)}, f32[4,8,256]{2,1,0:T(8,128)S(1)}, u32[]{:S(2)}, u32[]{:S(2)}) collective-permute-start(f32[4,8,256]{2,1,0:T(8,128)S(1)} %get-tuple-element.39), channel_id=1, source_target_pairs={{16,0},{17,1},{0,16},{1,17},{18,2},{19,3},{2,18},{3,19},{20,4},{21... | collective-permute-start | bytes 98312 | tf_op jit(solution)/shard_map/ppermute | solution.py:551
  83.4 3.3 %collective-permute-start.14 = (f32[4,8,256]{2,1,0:T(8,128)S(1)}, f32[4,8,256]{2,1,0:T(8,128)S(1)}, u32[]{:S(2)}, u32[]{:S(2)}) collective-permute-start(f32[4,8,256]{2,1,0:T(8,128)S(1)} %get-tuple-element.40), channel_id=1, source_target_pairs={{17,0},{16,1},{1,16},{0,17},{19,2},{18,3},{3,18},{2,19},{21,4},{20... | collective-permute-start | bytes 98312 | tf_op jit(solution)/shard_map/ppermute | solution.py:551
  88.6 16.0 %all-to-all-start.4 = ((f32[32,16,128]{2,1,0:T(8,128)}), f32[32,16,128]{2,1,0:T(8,128)S(1)}, u32[]{:S(2)}, u32[]{:S(2)}) async-start(f32[32,16,128]{2,1,0:T(8,128)} %get-tuple-element.46), calls=%async_computation.4 | async-start | bytes 524288 | tf_op jit(solution)/shard_map/all_to_all | solution.py:685
  (30 other events, 119.1 us)

commit v5 on v4

--- a/solution.py
+++ b/solution.py
@@ -322,43 +322,41 @@
         chunk[...] = slots[column_index() ^ k]
 
 
-def gather_tiles(few, me, alignment_refs, pair_refs, msa_out, pair_out, msa_slots, slots):
-    n_cols = len(alignment_refs)
-    spread(me, alignment_refs, msa_slots)
-    for r in range(msa_out.shape[0]):
-        msa_out[r] = jnp.concatenate(
-            [msa_slots[c, r * few : (r + 1) * few] for c in range(n_cols)], axis=0
+def gather_msa(few, me, blocks, out_ref, slots):
+    n_cols = len(blocks)
+    spread(me, blocks, slots)
+    for r in range(out_ref.shape[0]):
+        out_ref[r] = jnp.concatenate(
+            [slots[c, r * few : (r + 1) * few] for c in range(n_cols)], axis=0
         )
-    spread_rows(me, pair_refs, slots)
-    block = pair_refs[0].shape[0]
-    positions = n_cols * block // 2
-    residues = msa_out.shape[1]
-    groups = positions // (residues * few * n_cols)
+
+
+def gather_msa_kernel(few, n_cols, ready, *rest):
+    ready()
+    gather_msa(few, column_index(), rest[:n_cols], *rest[n_cols:])
+
+
+def gather_pair_kernel(few, n_cols, residues, ready, gain_ref, matrix_ref, *rest):
+    blocks, (first_ref, gate_ref, slots) = rest[:n_cols], rest[n_cols:]
+    ready()
+    spread_rows(column_index(), blocks, slots)
+    block = blocks[0].shape[0]
     count = residues * few
+    groups = block // count
     for c in range(n_cols):
-        for part in range(2):
-            for o in range(groups):
-                start = part * positions + o * n_cols + c
-                pair_out[pl.ds(start, count, stride=groups * n_cols), :] = slots[
-                    pl.ds(c * block + (part * groups + o) * count, count), :
-                ]
-
-
-def gather_kernel(few, n_cols, ready, *rest):
-    ready()
-    gather_tiles(few, column_index(), rest[:n_cols], rest[n_cols : 2 * n_cols], *rest[2 * n_cols :])
+        for o in range(groups):
+            first_ref[pl.ds(o * n_cols + c, count, stride=groups * n_cols), :] = slots[
+                pl.ds(c * block + o * count, count), :
+            ]
+    normal = layer_normalise(first_ref[...], gain_ref[...])
+    gate_ref[...] = sigmoid(multiply(normal, matrix_ref[...]))
 
 
 def triangle_kernel(few, n_branch, n_gj, ready, tri_ref, *rest):
     n_cols = n_branch * n_gj
-    blocks, (out_ref, msa_out, pair_out, product_ref, msa_slots, slots) = (
-        rest[: 2 * n_cols],
-        rest[2 * n_cols :],
-    )
-    ready()
-    gather_tiles(
-        few, column_index(), blocks[:n_cols], blocks[n_cols:], msa_out, pair_out, msa_slots, slots
-    )
+    blocks, (out_ref, msa_out, product_ref, slots) = rest[:n_cols], rest[n_cols:]
+    ready()
+    gather_msa(few, column_index(), blocks, msa_out, slots)
     n_all, rows, _ = out_ref.shape
     n_gi = n_all // n_cols
     share = few
@@ -423,7 +421,7 @@
     right_ref, gain_ref, matrix_ref, triangle_ref, tri_ref = rest[2 * n_cols : 2 * n_cols + 5]
     chunks = rest[2 * n_cols + 5 : 3 * n_cols + 5]
     rest = rest[3 * n_cols + 5 :]
-    left_ref, slots, pair_ref, first_ref, gate_ref = rest
+    left_ref, slots, pair_ref, first_ref = rest
     me = column_index()
     groups_j = n_gi // n_cols
     block = pair_refs[0].shape[0]
@@ -478,16 +476,15 @@
     for g in range(groups):
         tri_ref[:, g] = tri[:, g * lanes : (g + 1) * lanes].reshape(slot_count, each, lanes)
     first_ref[...] = first.T
-    gate_ref[...] = sigmoid(projected[4 * width :]).T
     for k in range(n_cols):
         for o in range(groups_j):
             rows = pl.ds((me ^ k) * groups_j + o, half, stride=n_gi)
             chunks[k][pl.ds(o * half, half), :] = first_ref[rows, :]
-            chunks[k][pl.ds(block + o * half, half), :] = gate_ref[rows, :]
 
 
 def final_kernel(
-    few, n_cols, residues, packed, ready, product_ref, pair_ref, gain_ref, matrix_ref, out_ref
+    few, n_cols, residues, packed, ready, product_ref, first_ref, gate_ref, gain_ref, matrix_ref,
+    out_ref
 ):
     positions = out_ref.shape[0]
     ready()
@@ -504,7 +501,7 @@
     else:
         product = product_ref[...]
     update = multiply(matrix_ref[...], layer_normalise(product, gain_ref[...], axis=0))
-    result = pair_ref[pl.ds(0, positions), :] + pair_ref[pl.ds(positions, positions), :] * update.T
+    result = first_ref[...] + gate_ref[...] * update.T
     count = positions // (residues * few)
     for i in range(residues):
         for f in range(few):
@@ -582,13 +579,14 @@
         ],
         sems=[4, parts],
     )
-    msa = lax.all_to_all(msa, "gi", 0, 0, tiled=True)
     (bias,) = call_near(
         functools.partial(bias_rows_kernel, n_cols),
         [(heads, residues, length)],
         *trade([bias] * n_cols, columns),
         scratch=[(n_cols,) + bias_block],
     )
+    msa, bias = lax.optimization_barrier((msa, bias))
+    msa = lax.all_to_all(msa, "gi", 0, 0, tiled=True)
     bias = trade([bias] * per_part, "gi")
     (msa_first,) = call(
         functools.partial(row_kernel, n_branch, n_gj, per_part, few),
@@ -638,20 +636,16 @@
     alignment = [block.reshape(-1, width) for block in trade(alignment, columns)]
     share = max(pair_width // n_all, 1)
     slots = pair_width // share
-    triangle = triangle_input_matrix.T.reshape(5, slots, share, pair_width)
-    sides = jnp.stack([triangle[0], triangle[2]], axis=1)
-    gates = jnp.stack([triangle[1], triangle[3]], axis=1)
-    triangle = jnp.concatenate(
-        [side.reshape(2 * pair_width, pair_width) for side in (sides, gates)]
-        + [triangle[4].reshape(pair_width, pair_width)],
-        axis=0,
-    )
+    triangle = triangle_input_matrix[:, : 4 * pair_width].T.reshape(4, slots, share, pair_width)
+    triangle = jnp.stack(
+        [jnp.stack([triangle[n], triangle[n + 2]], axis=1) for n in range(2)]
+    ).reshape(4 * pair_width, pair_width)
     matrix = outer_output_matrix.reshape(outer_width, outer_width // per, per, pair_width)
     matrix = jnp.transpose(matrix, (3, 2, 1, 0)).reshape(pair_width, -1)
-    tri, *first_gate = call_near(
+    tri, *first = call_near(
         functools.partial(pair_kernel, few, n_gi, n_cols),
         [(slots, positions // lanes, 2 * share, lanes)]
-        + [(2 * positions // n_cols, pair_width)] * n_cols,
+        + [(positions // n_cols, pair_width)] * n_cols,
         *left,
         *pair,
         right.reshape(n_gi * outer_width, count),
@@ -663,23 +657,28 @@
             (positions, pair_width),
             (positions, pair_width),
             (positions, pair_width),
-            (positions, pair_width),
         ],
     )
 
-    first_gate = trade(first_gate, columns)
-    tiles = [(rows, residues, width), (2 * positions, pair_width)]
-    scratch = [(n_cols, rows * few, width), (2 * positions, pair_width)]
+    first, gate = call_near(
+        functools.partial(gather_pair_kernel, few, n_cols, residues),
+        [(positions, pair_width)] * 2,
+        pair_norm_gains[1:2],
+        triangle_input_matrix[:, 4 * pair_width :],
+        *trade(first, columns),
+        scratch=[(positions, pair_width)],
+    )
+    tile = (rows, residues, width)
+    scratch = [(n_cols, rows * few, width)]
     packed = share * n_all == pair_width and share == few and few == per
     gain, last = pair_norm_gains[2], triangle_output_matrix
     if packed:
         tri = lax.all_to_all(tri, everyone, 0, 0, tiled=True)
-        product, alignment_output, first_gate = call_near(
+        product, alignment_output = call_near(
             functools.partial(triangle_kernel, few, n_branch, n_gj),
-            [(n_all, residues, lanes)] + tiles,
-                tri.reshape(-1, lanes),
+            [(n_all, residues, lanes), tile],
+            tri.reshape(-1, lanes),
             *alignment,
-            *first_gate,
             scratch=[(lanes, lanes)] + scratch,
         )
         product = lax.all_to_all(product, everyone, 0, 0, tiled=True)
@@ -687,11 +686,10 @@
         gain = gain.reshape(n_all, share).T.reshape(-1)
         last = jnp.swapaxes(last.reshape(n_all, share, pair_width), 0, 1).reshape(last.shape)
     else:
-        alignment_output, first_gate = call_near(
-            functools.partial(gather_kernel, few, n_cols),
-            tiles,
-                *alignment,
-            *first_gate,
+        (alignment_output,) = call_near(
+            functools.partial(gather_msa_kernel, few, n_cols),
+            [tile],
+            *alignment,
             scratch=scratch,
         )
         tri = jnp.transpose(tri.reshape(slots, -1, 2, share, lanes), (2, 1, 4, 0, 3))
@@ -708,7 +706,8 @@
         functools.partial(final_kernel, few, n_cols, residues, packed),
         [(positions, pair_width)],
         product,
-        first_gate,
+        first,
+        gate,
         gain[:, None],
         last.T,
     )

time: 107 us -> 110 us (1.028)
  local copies, waits for them, and re-layouts: 11.7 us -> 16.3 us
  starting transfers between devices: 40.2 us -> 39 us
    all_to_all x1, waiting for transfers between devices: 0.01 us -> 10.2 us  [per_device(): tri = lax.all_to_all(tri, everyone, 0, 0, tiled=True)]
    all_to_all x1, waiting for transfers between devices: 10.3 us -> 3.07 us  [per_device(): product = lax.all_to_all(product, everyone, 0, 0, tiled=True)]
    unnamed x63 -> x65, local copies, waits for them, and re-layouts: 8.17 us -> 10.9 us
    slice x1 -> x3, local copies, waits for them, and re-layouts: 0.7 us -> 3.23 us  [the longest x1 1.67 us: per_device(): triangle_input_matrix[:, :4 * pair_width]]
    ppermute x18, waiting for transfers between devices: 21.3 us -> 18.9 us  [trade(): lax.ppermute(blocks[k], axes, [(t ^ k, t) for t in range(n) if t ^ k < n])]
    all_to_all x1, starting transfers between devices: 4.81 us -> 2.59 us  [per_device(): product = lax.all_to_all(product, everyone, 0, 0, tiled=True)]
    all_to_all x1, starting transfers between devices: 7.42 us -> 5.85 us  [per_device(): msa = lax.all_to_all(msa, 'gi', 0, 0, tiled=True)]
    ppermute x18, starting transfers between devices: 14 us -> 15.3 us  [trade(): lax.ppermute(blocks[k], axes, [(t ^ k, t) for t in range(n) if t ^ k < n])]
  transfers between devices with their start and end apart: 23 -> 23, of which waited for: 13 -> 14; matrix products, arithmetic and copies ran while one was open for 4% -> 6% of each run, Pallas kernels for 5% -> 5%
where the time goes in v5:
time: 110 us; the launch traced here: 109 us
  starting transfers between devices  39 us (35%)
  waiting for transfers between devices  32.4 us (29%)
  Pallas kernels  20.5 us (19%)
  local copies, waits for them, and re-layouts  16.3 us (15%)
    ppermute x18, waiting for transfers between devices, trade(): lax.ppermute(blocks[k], axes, [(t ^ k, t) for t in range(n) if t ^ k < n])  18.9 us
    ppermute x18, starting transfers between devices, trade(): lax.ppermute(blocks[k], axes, [(t ^ k, t) for t in range(n) if t ^ k < n])  15.3 us
    pallas_call x8, Pallas kernels, call_near(): pl.pallas_call(lambda *refs: kernel(lambda: None, *refs), out_shape=[jax....  13.4 us
    unnamed x65, local copies, waits for them, and re-layouts  10.9 us
    all_to_all x1, waiting for transfers between devices, per_device(): tri = lax.all_to_all(tri, everyone, 0, 0, tiled=True)  10.2 us
    pallas_call x2, Pallas kernels, call(): pl.pallas_call(body, out_shape=[jax.ShapeDtypeStruct(bare(out), jnp.float...  7.12 us
    all_to_all x1, starting transfers between devices, per_device(): msa = lax.all_to_all(msa, 'gi', 0, 0, tiled=True)  5.85 us
    all_to_all x1, starting transfers between devices, per_device(): tri = lax.all_to_all(tri, everyone, 0, 0, tiled=True)  5.83 us
  transfers between devices with their start and end apart: 23, of which 14 were waited for; matrix products, arithmetic and copies ran while one was open for 6% of the time, Pallas kernels for 5%

profile of v5, /device:TPU:0, one launch (start us, length us, event | category | flops | bytes accessed | tf_op | source)
XLA Modules:
  0.0 109.3 jit_solution(14222444873364051508)
XLA Ops:
  0.6 2.4 %shard_map.158 = (f32[16,16,256]{2,1,0:T(8,128)}, f32[2,16,128]{2,1,0:T(8,128)}) custom-call(f32[8,16,256]{2,1,0:T(8,128)} %refs_0_.1, f32[16,32,128]{2,1,0:T(8,128)} %refs_1_.2, f32[3,128]{1,0:T(4,128)} %refs_2_.2, f32[8,128]{1,0:T(8,128)} %bitcast.57), custom_call_target="tpu_custom_call" | custom-call | tf_op jit(solution)/shard_map/pallas_call | solution.py:135
  3.1 3.0 %collective-permute-start = (f32[2,16,128]{2,1,0:T(8,128)}, f32[2,16,128]{2,1,0:T(8,128)S(1)}, u32[]{:S(2)}, u32[]{:S(2)}) collective-permute-start(f32[2,16,128]{2,1,0:T(8,128)} %get-tuple-element.29.refs_0_), channel_id=1, source_target_pairs={{1,0},{0,1},{17,16},{16,17},{3,2},{2,3},{19,18},{18,19},{5,4},{4,5... | collective-permute-start | bytes 49160 | tf_op jit(solution)/shard_map/ppermute | solution.py:548
  6.3 1.7 %collective-permute-done.refs_1_ = f32[2,16,128]{2,1,0:T(8,128)S(1)} collective-permute-done((f32[2,16,128]{2,1,0:T(8,128)}, f32[2,16,128]{2,1,0:T(8,128)S(1)}, u32[]{:S(2)}, u32[]{:S(2)}) %collective-permute-start) | collective-permute-done | bytes 16416 | tf_op jit(solution)/shard_map/ppermute | solution.py:548
  10.3 5.8 %all-to-all-start = ((f32[16,16,256]{2,1,0:T(8,128)}), f32[16,16,256]{2,1,0:T(8,128)S(1)}, u32[]{:S(2)}, u32[]{:S(2)}) async-start(f32[16,16,256]{2,1,0:T(8,128)} %get-tuple-element.30), calls=%async_computation | async-start | bytes 524288 | tf_op jit(solution)/shard_map/all_to_all | solution.py:589
  16.2 2.0 %collective-permute-start.3 = (f32[8,16,128]{2,1,0:T(8,128)S(1)}, f32[8,16,128]{2,1,0:T(8,128)S(1)}, u32[]{:S(2)}, u32[]{:S(2)}) collective-permute-start(f32[8,16,128]{2,1,0:T(8,128)S(1)} %shard_map.159.refs_1_), channel_id=1, source_target_pairs={{2,0},{0,2},{6,4},{4,6},{10,8},{8,10},{14,12},{12,14},{3,1},{1,3},... | collective-permute-start | bytes 196616 | tf_op jit(solution)/shard_map/ppermute | solution.py:548
  19.7 2.6 %collective-permute-done.3.refs_2_ = f32[8,16,128]{2,1,0:T(8,128)S(1)} collective-permute-done((f32[8,16,128]{2,1,0:T(8,128)S(1)}, f32[8,16,128]{2,1,0:T(8,128)S(1)}, u32[]{:S(2)}, u32[]{:S(2)}) %collective-permute-start.3) | collective-permute-done | bytes 65568 | tf_op jit(solution)/shard_map/ppermute | solution.py:548
  22.3 3.0 %collective-permute-done.4.refs_3_ = f32[8,16,128]{2,1,0:T(8,128)S(1)} collective-permute-done((f32[8,16,128]{2,1,0:T(8,128)S(1)}, f32[8,16,128]{2,1,0:T(8,128)S(1)}, u32[]{:S(2)}, u32[]{:S(2)}) %collective-permute-start.4) | collective-permute-done | bytes 65568 | tf_op jit(solution)/shard_map/ppermute | solution.py:548
  25.3 1.8 %collective-permute-done.5.refs_4_ = f32[8,16,128]{2,1,0:T(8,128)S(1)} collective-permute-done((f32[8,16,128]{2,1,0:T(8,128)S(1)}, f32[8,16,128]{2,1,0:T(8,128)S(1)}, u32[]{:S(2)}, u32[]{:S(2)}) %collective-permute-start.5) | collective-permute-done | bytes 65568 | tf_op jit(solution)/shard_map/ppermute | solution.py:548
  28.5 4.7 %shard_map.160 = f32[16,8,256]{2,1,0:T(8,128)} custom-call(f32[16,16,256]{2,1,0:T(8,128)} %copy-done.19, f32[8,16,128]{2,1,0:T(8,128)} %copy-done.4, f32[8,16,128]{2,1,0:T(8,128)} %copy-done.25, f32[8,16,128]{2,1,0:T(8,128)} %copy-done.26, f32[8,16,128]{2,1,0:T(8,128)} %copy-done.27, f32[4,256]{1,0:T(4,128)} %refs_1_.3, f32[256,1024]{1,0:T(8,128)} %refs_6_.1, ...), custom_call_target="tpu_custom_call" | custom-call | tf_op jit(solution)/shard_map/pallas_call | solution.py:135
  33.2 3.7 %all-to-all-start.1 = ((f32[16,8,256]{2,1,0:T(8,128)}), f32[16,8,256]{2,1,0:T(8,128)S(1)}, u32[]{:S(2)}, u32[]{:S(2)}) async-start(f32[16,8,256]{2,1,0:T(8,128)} %shard_map.160), calls=%async_computation.1 | async-start | bytes 262144 | tf_op jit(solution)/shard_map/all_to_all | solution.py:605
  38.0 1.7 %slice.30 = f32[128,512]{1,0:T(8,128)} slice(f32[128,640]{1,0:T(8,128)} %param.28), slice={[0:128], [0:512]} | slice | bytes 524288 | tf_op jit(solution)/shard_map/slice | solution.py:639
  46.3 4.0 %shard_map.161 = (f32[32,128]{1,0:T(8,128)S(1)}, f32[8,32,128]{2,1,0:T(8,128)S(1)}, f32[128,256]{1,0:T(8,128)S(1)}) custom-call(f32[128,256]{1,0:T(8,128)S(1)} %bitcast.39, f32[4,256]{1,0:T(4,128)S(1)} %copy-done.13, f32[256,1024]{1,0:T(8,128)S(1)} %copy-done.1, f32[256,256]{1,0:T(8,128)S(1)} %copy-done.5, f32[256,1024]{1,0:T(8,128)S(1)} %copy-done.2, ...), custom_call_target="tpu_custom_call" | custom-call | tf_op jit(solution)/shard_map/pallas_call | solution.py:147
  51.6 5.8 %all-to-all-start.2 = ((f32[8,32,128]{2,1,0:T(8,128)}), f32[8,32,128]{2,1,0:T(8,128)S(1)}, u32[]{:S(2)}, u32[]{:S(2)}) async-start(f32[8,32,128]{2,1,0:T(8,128)} %copy-done.8), calls=%async_computation.2 | async-start | bytes 262144 | tf_op jit(solution)/shard_map/all_to_all | solution.py:634
  60.0 1.5 %collective-permute-start.6 = (f32[32,128]{1,0:T(8,128)S(1)}, f32[32,128]{1,0:T(8,128)S(1)}, u32[]{:S(2)}, u32[]{:S(2)}) collective-permute-start(f32[32,128]{1,0:T(8,128)S(1)} %get-tuple-element.33.refs_0_), channel_id=1, source_target_pairs={{1,0},{0,1},{17,16},{16,17},{3,2},{2,3},{19,18},{18,19},{5,4},{4,5... | collective-permute-start | bytes 49160 | tf_op jit(solution)/shard_map/ppermute | solution.py:548
  64.9 4.9 %shard_map.163 = (f32[32,4,8,128]{3,2,1,0:T(8,128)}, f32[128,128]{1,0:T(8,128)S(1)}, f32[128,128]{1,0:T(8,128)S(1)}, f32[128,128]{1,0:T(8,128)S(1)}, f32[128,128]{1,0:T(8,128)S(1)}) custom-call(f32[32,128]{1,0:T(8,128)S(1)} %get-tuple-element.33.refs_0_, f32[32,128]{1,0:T(8,128)S(1)} %collective-permute-done.6.refs_1_, ...), custom_call_target="tpu_custom_call" | custom-call | tf_op jit(solution)/shard_map/pallas_call | solution.py:147
  69.8 5.8 %all-to-all-start.3 = ((f32[32,4,8,128]{3,2,1,0:T(8,128)}), f32[32,4,8,128]{3,2,1,0:T(8,128)S(1)}, u32[]{:S(2)}, u32[]{:S(2)}) async-start(f32[32,4,8,128]{3,2,1,0:T(8,128)} %get-tuple-element.40), calls=%async_computation.3 | async-start | bytes 1048576 | tf_op jit(solution)/shard_map/all_to_all | solution.py:676
  75.7 1.8 %collective-permute-start.12 = (f32[4,8,256]{2,1,0:T(8,128)S(1)}, f32[4,8,256]{2,1,0:T(8,128)S(1)}, u32[]{:S(2)}, u32[]{:S(2)}) collective-permute-start(f32[4,8,256]{2,1,0:T(8,128)S(1)} %get-tuple-element.43), channel_id=1, source_target_pairs={{1,0},{0,1},{17,16},{16,17},{3,2},{2,3},{19,18},{18,19},{5,4},{4,5... | collective-permute-start | bytes 98312 | tf_op jit(solution)/shard_map/ppermute | solution.py:548
  77.9 4.3 %collective-permute-done.12 = f32[4,8,256]{2,1,0:T(8,128)S(1)} collective-permute-done((f32[4,8,256]{2,1,0:T(8,128)S(1)}, f32[4,8,256]{2,1,0:T(8,128)S(1)}, u32[]{:S(2)}, u32[]{:S(2)}) %collective-permute-start.12) | collective-permute-done | bytes 32800 | tf_op jit(solution)/shard_map/ppermute | solution.py:548
  82.2 10.2 %all-to-all-done.3 = f32[32,4,8,128]{3,2,1,0:T(8,128)S(1)} async-done(((f32[32,4,8,128]{3,2,1,0:T(8,128)}), f32[32,4,8,128]{3,2,1,0:T(8,128)S(1)}, u32[]{:S(2)}, u32[]{:S(2)}) %all-to-all-start.3) | async-done | bytes 524320 | tf_op jit(solution)/shard_map/all_to_all | solution.py:676
  92.4 1.7 %shard_map.165 = (f32[32,16,128]{2,1,0:T(8,128)}, f32[8,16,256]{2,1,0:T(8,128)}) custom-call(f32[1024,128]{1,0:T(8,128)S(1)} %bitcast.34, f32[32,256]{1,0:T(8,128)S(1)} %bitcast.42, f32[32,256]{1,0:T(8,128)S(1)} %bitcast.43, f32[32,256]{1,0:T(8,128)S(1)} %bitcast.44, f32[32,256]{1,0:T(8,128)S(1)} %bitcast.45), custom_call_target="tpu_custom_call" | custom-call | tf_op jit(solution)/shard_map/pallas_call | solution.py:147
  94.2 2.6 %all-to-all-start.4 = ((f32[32,16,128]{2,1,0:T(8,128)}), f32[32,16,128]{2,1,0:T(8,128)S(1)}, u32[]{:S(2)}, u32[]{:S(2)}) async-start(f32[32,16,128]{2,1,0:T(8,128)} %get-tuple-element.47), calls=%async_computation.4 | async-start | bytes 524288 | tf_op jit(solution)/shard_map/all_to_all | solution.py:684
  96.8 1.7 %collective-permute-start.15 = (f32[128,128]{1,0:T(8,128)S(1)}, f32[128,128]{1,0:T(8,128)S(1)}, u32[]{:S(2)}, u32[]{:S(2)}) collective-permute-start(f32[128,128]{1,0:T(8,128)S(1)} %get-tuple-element.49), channel_id=1, source_target_pairs={{1,0},{0,1},{17,16},{16,17},{3,2},{2,3},{19,18},{18,19},{5,4},{4,5... | collective-permute-start | bytes 196616 | tf_op jit(solution)/shard_map/ppermute | solution.py:548
  100.8 2.4 %collective-permute-done.15.refs_3_ = f32[128,128]{1,0:T(8,128)S(1)} collective-permute-done((f32[128,128]{1,0:T(8,128)S(1)}, f32[128,128]{1,0:T(8,128)S(1)}, u32[]{:S(2)}, u32[]{:S(2)}) %collective-permute-start.15) | collective-permute-done | bytes 65568 | tf_op jit(solution)/shard_map/ppermute | solution.py:548
  104.9 3.1 %all-to-all-done.4 = f32[32,16,128]{2,1,0:T(8,128)S(1)} async-done(((f32[32,16,128]{2,1,0:T(8,128)}), f32[32,16,128]{2,1,0:T(8,128)S(1)}, u32[]{:S(2)}, u32[]{:S(2)}) %all-to-all-start.4) | async-done | bytes 262176 | tf_op jit(solution)/shard_map/all_to_all | solution.py:684
  (112 shorter events, 26.0 us)
Async XLA Ops:
  3.1 4.9 %collective-permute-start = (f32[2,16,128]{2,1,0:T(8,128)}, f32[2,16,128]{2,1,0:T(8,128)S(1)}, u32[]{:S(2)}, u32[]{:S(2)}) collective-permute-start(f32[2,16,128]{2,1,0:T(8,128)} %get-tuple-element.29.refs_0_), channel_id=1, source_target_pairs={{1,0},{0,1},{17,16},{16,17},{3,2},{2,3},{19,18},{18,19},{5,4},{4,5... | collective-permute-start | bytes 49160 | tf_op jit(solution)/shard_map/ppermute | solution.py:548
  6.1 1.9 %collective-permute-start.1 = (f32[2,16,128]{2,1,0:T(8,128)}, f32[2,16,128]{2,1,0:T(8,128)S(1)}, u32[]{:S(2)}, u32[]{:S(2)}) collective-permute-start(f32[2,16,128]{2,1,0:T(8,128)} %get-tuple-element.29.refs_0_), channel_id=1, source_target_pairs={{16,0},{17,1},{0,16},{1,17},{18,2},{19,3},{2,18},{3,19},{20,4},{21... | collective-permute-start | bytes 49160 | tf_op jit(solution)/shard_map/ppermute | solution.py:548
  6.1 3.4 %collective-permute-start.2 = (f32[2,16,128]{2,1,0:T(8,128)}, f32[2,16,128]{2,1,0:T(8,128)S(1)}, u32[]{:S(2)}, u32[]{:S(2)}) collective-permute-start(f32[2,16,128]{2,1,0:T(8,128)} %get-tuple-element.29.refs_0_), channel_id=1, source_target_pairs={{17,0},{16,1},{1,16},{0,17},{19,2},{18,3},{3,18},{2,19},{21,4},{20... | collective-permute-start | bytes 49160 | tf_op jit(solution)/shard_map/ppermute | solution.py:548
  10.3 16.8 %all-to-all-start = ((f32[16,16,256]{2,1,0:T(8,128)}), f32[16,16,256]{2,1,0:T(8,128)S(1)}, u32[]{:S(2)}, u32[]{:S(2)}) async-start(f32[16,16,256]{2,1,0:T(8,128)} %get-tuple-element.30), calls=%async_computation | async-start | bytes 524288 | tf_op jit(solution)/shard_map/all_to_all | solution.py:589
  16.2 6.1 %collective-permute-start.3 = (f32[8,16,128]{2,1,0:T(8,128)S(1)}, f32[8,16,128]{2,1,0:T(8,128)S(1)}, u32[]{:S(2)}, u32[]{:S(2)}) collective-permute-start(f32[8,16,128]{2,1,0:T(8,128)S(1)} %shard_map.159.refs_1_), channel_id=1, source_target_pairs={{2,0},{0,2},{6,4},{4,6},{10,8},{8,10},{14,12},{12,14},{3,1},{1,3},... | collective-permute-start | bytes 196616 | tf_op jit(solution)/shard_map/ppermute | solution.py:548
  18.2 7.1 %collective-permute-start.4 = (f32[8,16,128]{2,1,0:T(8,128)S(1)}, f32[8,16,128]{2,1,0:T(8,128)S(1)}, u32[]{:S(2)}, u32[]{:S(2)}) collective-permute-start(f32[8,16,128]{2,1,0:T(8,128)S(1)} %shard_map.159.refs_1_), channel_id=1, source_target_pairs={{4,0},{6,2},{0,4},{2,6},{12,8},{14,10},{8,12},{10,14},{5,1},{7,3},... | collective-permute-start | bytes 196616 | tf_op jit(solution)/shard_map/ppermute | solution.py:548
  19.7 7.5 %collective-permute-start.5 = (f32[8,16,128]{2,1,0:T(8,128)S(1)}, f32[8,16,128]{2,1,0:T(8,128)S(1)}, u32[]{:S(2)}, u32[]{:S(2)}) collective-permute-start(f32[8,16,128]{2,1,0:T(8,128)S(1)} %shard_map.159.refs_1_), channel_id=1, source_target_pairs={{6,0},{4,2},{2,4},{0,6},{14,8},{12,10},{10,12},{8,14},{7,1},{5,3},... | collective-permute-start | bytes 196616 | tf_op jit(solution)/shard_map/ppermute | solution.py:548
  28.5 16.3 %copy-start.3 = (f32[1024,256]{1,0:T(8,128)S(1)}, f32[1024,256]{1,0:T(8,128)}, u32[]{:S(2)}) copy-start(f32[1024,256]{1,0:T(8,128)} %refs_5_.3) | copy-start | bytes 3145732
  33.2 11.6 %all-to-all-start.1 = ((f32[16,8,256]{2,1,0:T(8,128)}), f32[16,8,256]{2,1,0:T(8,128)S(1)}, u32[]{:S(2)}, u32[]{:S(2)}) async-start(f32[16,8,256]{2,1,0:T(8,128)} %shard_map.160), calls=%async_computation.1 | async-start | bytes 262144 | tf_op jit(solution)/shard_map/all_to_all | solution.py:605
  44.4 17.0 %collective-permute-start.10 = (f32[128,128]{1,0:T(8,128)}, f32[128,128]{1,0:T(8,128)}, u32[]{:S(2)}, u32[]{:S(2)}) collective-permute-start(f32[128,128]{1,0:T(8,128)} %get-tuple-element.37), channel_id=1, source_target_pairs={{16,0},{17,1},{0,16},{1,17},{18,2},{19,3},{2,18},{3,19},{20,4},{21... | collective-permute-start | bytes 196616 | tf_op jit(solution)/shard_map/ppermute | solution.py:548
  51.6 13.3 %all-to-all-start.2 = ((f32[8,32,128]{2,1,0:T(8,128)}), f32[8,32,128]{2,1,0:T(8,128)S(1)}, u32[]{:S(2)}, u32[]{:S(2)}) async-start(f32[8,32,128]{2,1,0:T(8,128)} %copy-done.8), calls=%async_computation.2 | async-start | bytes 262144 | tf_op jit(solution)/shard_map/all_to_all | solution.py:634
  58.3 5.4 %collective-permute-start.11 = (f32[128,128]{1,0:T(8,128)S(1)}, f32[128,128]{1,0:T(8,128)S(1)}, u32[]{:S(2)}, u32[]{:S(2)}) collective-permute-start(f32[128,128]{1,0:T(8,128)S(1)} %copy-done.18), channel_id=1, source_target_pairs={{17,0},{16,1},{1,16},{0,17},{19,2},{18,3},{3,18},{2,19},{21,4},{20... | collective-permute-start | bytes 196616 | tf_op jit(solution)/shard_map/ppermute | solution.py:548
  59.4 4.8 %collective-permute-start.9 = (f32[128,128]{1,0:T(8,128)S(1)}, f32[128,128]{1,0:T(8,128)S(1)}, u32[]{:S(2)}, u32[]{:S(2)}) collective-permute-start(f32[128,128]{1,0:T(8,128)S(1)} %copy-done.16), channel_id=1, source_target_pairs={{1,0},{0,1},{17,16},{16,17},{3,2},{2,3},{19,18},{18,19},{5,4},{4,5... | collective-permute-start | bytes 196616 | tf_op jit(solution)/shard_map/ppermute | solution.py:548
  60.0 4.5 %collective-permute-start.6 = (f32[32,128]{1,0:T(8,128)S(1)}, f32[32,128]{1,0:T(8,128)S(1)}, u32[]{:S(2)}, u32[]{:S(2)}) collective-permute-start(f32[32,128]{1,0:T(8,128)S(1)} %get-tuple-element.33.refs_0_), channel_id=1, source_target_pairs={{1,0},{0,1},{17,16},{16,17},{3,2},{2,3},{19,18},{18,19},{5,4},{4,5... | collective-permute-start | bytes 49160 | tf_op jit(solution)/shard_map/ppermute | solution.py:548
  61.5 3.0 %collective-permute-start.7 = (f32[32,128]{1,0:T(8,128)S(1)}, f32[32,128]{1,0:T(8,128)S(1)}, u32[]{:S(2)}, u32[]{:S(2)}) collective-permute-start(f32[32,128]{1,0:T(8,128)S(1)} %get-tuple-element.33.refs_0_), channel_id=1, source_target_pairs={{16,0},{17,1},{0,16},{1,17},{18,2},{19,3},{2,18},{3,19},{20,4},{21... | collective-permute-start | bytes 49160 | tf_op jit(solution)/shard_map/ppermute | solution.py:548
  61.5 3.2 %collective-permute-start.8 = (f32[32,128]{1,0:T(8,128)S(1)}, f32[32,128]{1,0:T(8,128)S(1)}, u32[]{:S(2)}, u32[]{:S(2)}) collective-permute-start(f32[32,128]{1,0:T(8,128)S(1)} %get-tuple-element.33.refs_0_), channel_id=1, source_target_pairs={{17,0},{16,1},{1,16},{0,17},{19,2},{18,3},{3,18},{2,19},{21,4},{20... | collective-permute-start | bytes 49160 | tf_op jit(solution)/shard_map/ppermute | solution.py:548
  69.8 22.7 %all-to-all-start.3 = ((f32[32,4,8,128]{3,2,1,0:T(8,128)}), f32[32,4,8,128]{3,2,1,0:T(8,128)S(1)}, u32[]{:S(2)}, u32[]{:S(2)}) async-start(f32[32,4,8,128]{3,2,1,0:T(8,128)} %get-tuple-element.40), calls=%async_computation.3 | async-start | bytes 1048576 | tf_op jit(solution)/shard_map/all_to_all | solution.py:676
  75.7 6.6 %collective-permute-start.12 = (f32[4,8,256]{2,1,0:T(8,128)S(1)}, f32[4,8,256]{2,1,0:T(8,128)S(1)}, u32[]{:S(2)}, u32[]{:S(2)}) collective-permute-start(f32[4,8,256]{2,1,0:T(8,128)S(1)} %get-tuple-element.43), channel_id=1, source_target_pairs={{1,0},{0,1},{17,16},{16,17},{3,2},{2,3},{19,18},{18,19},{5,4},{4,5... | collective-permute-start | bytes 98312 | tf_op jit(solution)/shard_map/ppermute | solution.py:548
  77.5 4.7 %collective-permute-start.13 = (f32[4,8,256]{2,1,0:T(8,128)S(1)}, f32[4,8,256]{2,1,0:T(8,128)S(1)}, u32[]{:S(2)}, u32[]{:S(2)}) collective-permute-start(f32[4,8,256]{2,1,0:T(8,128)S(1)} %get-tuple-element.44), channel_id=1, source_target_pairs={{16,0},{17,1},{0,16},{1,17},{18,2},{19,3},{2,18},{3,19},{20,4},{21... | collective-permute-start | bytes 98312 | tf_op jit(solution)/shard_map/ppermute | solution.py:548
  77.5 4.7 %collective-permute-start.14 = (f32[4,8,256]{2,1,0:T(8,128)S(1)}, f32[4,8,256]{2,1,0:T(8,128)S(1)}, u32[]{:S(2)}, u32[]{:S(2)}) collective-permute-start(f32[4,8,256]{2,1,0:T(8,128)S(1)} %get-tuple-element.45), channel_id=1, source_target_pairs={{17,0},{16,1},{1,16},{0,17},{19,2},{18,3},{3,18},{2,19},{21,4},{20... | collective-permute-start | bytes 98312 | tf_op jit(solution)/shard_map/ppermute | solution.py:548
  94.2 13.8 %all-to-all-start.4 = ((f32[32,16,128]{2,1,0:T(8,128)}), f32[32,16,128]{2,1,0:T(8,128)S(1)}, u32[]{:S(2)}, u32[]{:S(2)}) async-start(f32[32,16,128]{2,1,0:T(8,128)} %get-tuple-element.47), calls=%async_computation.4 | async-start | bytes 524288 | tf_op jit(solution)/shard_map/all_to_all | solution.py:684
  96.8 6.4 %collective-permute-start.15 = (f32[128,128]{1,0:T(8,128)S(1)}, f32[128,128]{1,0:T(8,128)S(1)}, u32[]{:S(2)}, u32[]{:S(2)}) collective-permute-start(f32[128,128]{1,0:T(8,128)S(1)} %get-tuple-element.49), channel_id=1, source_target_pairs={{1,0},{0,1},{17,16},{16,17},{3,2},{2,3},{19,18},{18,19},{5,4},{4,5... | collective-permute-start | bytes 196616 | tf_op jit(solution)/shard_map/ppermute | solution.py:548
  98.5 4.7 %collective-permute-start.16 = (f32[128,128]{1,0:T(8,128)S(1)}, f32[128,128]{1,0:T(8,128)S(1)}, u32[]{:S(2)}, u32[]{:S(2)}) collective-permute-start(f32[128,128]{1,0:T(8,128)S(1)} %get-tuple-element.50), channel_id=1, source_target_pairs={{16,0},{17,1},{0,16},{1,17},{18,2},{19,3},{2,18},{3,19},{20,4},{21... | collective-permute-start | bytes 196616 | tf_op jit(solution)/shard_map/ppermute | solution.py:548
  98.5 5.3 %collective-permute-start.17 = (f32[128,128]{1,0:T(8,128)S(1)}, f32[128,128]{1,0:T(8,128)S(1)}, u32[]{:S(2)}, u32[]{:S(2)}) collective-permute-start(f32[128,128]{1,0:T(8,128)S(1)} %get-tuple-element.51), channel_id=1, source_target_pairs={{17,0},{16,1},{1,16},{0,17},{19,2},{18,3},{3,18},{2,19},{21,4},{20... | collective-permute-start | bytes 196616 | tf_op jit(solution)/shard_map/ppermute | solution.py:548
  (31 other events, 101.4 us)

commit v6 on v5

--- a/solution.py
+++ b/solution.py
@@ -109,7 +109,7 @@
     return lax.axis_index("branch") * lax.axis_size("gj") + lax.axis_index("gj")
 
 
-def call(kernel, outs, *operands, scratch=(), sems=()):
+def call(kernel, outs, *operands, scratch=(), sems=(), grant=None):
     def bare(item):
         return item[0] if isinstance(item, list) else item
 
@@ -140,6 +140,7 @@
         scratch_shapes=[pltpu.VMEM(shape, jnp.float32) for shape in shapes + list(scratch)]
         + [pltpu.SemaphoreType.DMA((n,)) for n in sems]
         + [pltpu.SemaphoreType.DMA((max(len(near_in), len(near_out), 1),))],
+        compiler_params=pltpu.CompilerParams(vmem_limit_bytes=grant),
     )(*[bare(operand) for operand in operands])
 
 
@@ -165,30 +166,30 @@
         slots[pl.ds(pl.multiple_of((me ^ k) * count, 8), count), :] = ref[...]
 
 
-def bias_kernel(
-    ready, msa_far, pair_far, gains_far, matrix_far, copies_far, out_ref, msa_ref, pair_ref,
-    gains_ref, matrix_ref, sems, out_sems
-):
-    rows = msa_far.shape[0]
-    repeats = copies_far.shape[0] // rows
-    copies = start_copies(
-        [(msa_far, msa_ref), (gains_far, gains_ref), (matrix_far, matrix_ref), (pair_far, pair_ref)],
-        sems,
-    )
+def bias_kernel(ready, pair_ref, gains_ref, matrix_ref, out_ref):
     residues, pair_cols, _ = pair_ref.shape
     heads = matrix_ref.shape[0]
     per = lanes // pair_cols
     ready()
-    wait_all(copies)
-    copies = start_copies(
-        [(msa_ref, copies_far.at[pl.ds(n * rows, rows)]) for n in range(repeats)], out_sems
-    )
     normal = layer_normalise(pair_ref[...], gains_ref[0:1, :][None])
     for i in range(residues):
         here = multiply(matrix_ref[...], normal[i], across=True)
         for h in range(heads):
             out_ref[h // per, i : i + 1, pl.ds(h % per * pair_cols, pair_cols)] = here[h : h + 1]
-    wait_all(copies)
+
+
+def repeat_kernel(ready, msa_ref, copies_far, sems):
+    rows = msa_ref.shape[0]
+    ready()
+    wait_all(
+        start_copies(
+            [
+                (msa_ref, copies_far.at[pl.ds(n * rows, rows)])
+                for n in range(copies_far.shape[0] // rows)
+            ],
+            sems,
+        )
+    )
 
 
 def pair_blocks_kernel(few, residues, ready, pair_ref, *rest):
@@ -336,7 +337,7 @@
     gather_msa(few, column_index(), rest[:n_cols], *rest[n_cols:])
 
 
-def gather_pair_kernel(few, n_cols, residues, ready, gain_ref, matrix_ref, *rest):
+def gather_pair_kernel(few, n_cols, residues, ready, gains_ref, matrix_ref, *rest):
     blocks, (first_ref, gate_ref, slots) = rest[:n_cols], rest[n_cols:]
     ready()
     spread_rows(column_index(), blocks, slots)
@@ -348,8 +349,11 @@
             first_ref[pl.ds(o * n_cols + c, count, stride=groups * n_cols), :] = slots[
                 pl.ds(c * block + o * count, count), :
             ]
-    normal = layer_normalise(first_ref[...], gain_ref[...])
-    gate_ref[...] = sigmoid(multiply(normal, matrix_ref[...]))
+    width = first_ref.shape[1]
+    normal = layer_normalise(first_ref[...], gains_ref[1:2, :])
+    gate_ref[...] = sigmoid(
+        multiply(normal, matrix_ref[pl.ds(4 * width, width), :], across=True)
+    )
 
 
 def triangle_kernel(few, n_branch, n_gj, ready, tri_ref, *rest):
@@ -415,13 +419,13 @@
 
 
 def pair_kernel(
-    few, n_gi, n_cols, ready, *rest
+    few, n_gi, n_cols, share, ready, *rest
 ):
     left_refs, pair_refs = rest[:n_cols], rest[n_cols : 2 * n_cols]
-    right_ref, gain_ref, matrix_ref, triangle_ref, tri_ref = rest[2 * n_cols : 2 * n_cols + 5]
+    right_ref, gains_ref, matrix_ref, triangle_ref, tri_ref = rest[2 * n_cols : 2 * n_cols + 5]
     chunks = rest[2 * n_cols + 5 : 3 * n_cols + 5]
     rest = rest[3 * n_cols + 5 :]
-    left_ref, slots, pair_ref, first_ref = rest
+    left_ref, slots, pair_ref, first_ref, sides_ref = rest
     me = column_index()
     groups_j = n_gi // n_cols
     block = pair_refs[0].shape[0]
@@ -470,11 +474,18 @@
             ]
     update = multiply(matrix_ref[...], jnp.concatenate(outputs, axis=1))
     first = pair_ref[...].T + update
-    projected = multiply(triangle_ref[...], layer_normalise(first, gain_ref[...], axis=0))
-    tri = sigmoid(projected[2 * width : 4 * width]) * projected[: 2 * width]
-    slot_count, _, each, _ = tri_ref.shape
-    for g in range(groups):
-        tri_ref[:, g] = tri[:, g * lanes : (g + 1) * lanes].reshape(slot_count, each, lanes)
+    projected = multiply(
+        triangle_ref[pl.ds(0, 4 * width), :] * gains_ref[1:2, :],
+        layer_normalise(first, 1.0, axis=0),
+    )
+    for n in range(2):
+        value = projected[2 * n * width : (2 * n + 1) * width]
+        tri = sigmoid(projected[(2 * n + 1) * width : (2 * n + 2) * width]) * value
+        for g in range(groups):
+            sides_ref[...] = tri[:, g * lanes : (g + 1) * lanes]
+            for q in range(share):
+                rows = pl.ds(g * 2 * share + n * share + q, width // share, stride=2 * share * groups)
+                tri_ref[rows, :] = sides_ref[pl.ds(q, width // share, stride=share), :]
     first_ref[...] = first.T
     for k in range(n_cols):
         for o in range(groups_j):
@@ -483,8 +494,8 @@
 
 
 def final_kernel(
-    few, n_cols, residues, packed, ready, product_ref, first_ref, gate_ref, gain_ref, matrix_ref,
-    out_ref
+    few, residues, packed, ready, product_ref, first_ref, gate_ref, gains_ref, matrix_ref, out_ref,
+    channels_ref
 ):
     positions = out_ref.shape[0]
     ready()
@@ -496,12 +507,14 @@
             here = [
                 product_ref[pl.ds(i * tiles + t, tall, stride=residues), :] for i in range(few)
             ]
-            product.append(jnp.concatenate(swap_lane_groups(here), axis=0))
+            for q, piece in enumerate(swap_lane_groups(here)):
+                channels_ref[pl.ds(q, tall, stride=few), :] = piece
+            product.append(channels_ref[...])
         product = jnp.concatenate(product, axis=1)
     else:
         product = product_ref[...]
-    update = multiply(matrix_ref[...], layer_normalise(product, gain_ref[...], axis=0))
-    result = first_ref[...] + gate_ref[...] * update.T
+    normal = layer_normalise(product, 1.0, axis=0).T * gains_ref[2:3, :]
+    result = first_ref[...] + gate_ref[...] * multiply(normal, matrix_ref[...])
     count = positions // (residues * few)
     for i in range(residues):
         for f in range(few):
@@ -564,29 +577,18 @@
 
     per = lanes // pair_cols
     bias_block = (heads // per, residues, lanes)
-    msa, bias = call(
-        bias_kernel,
-        [[(parts * rows, residues, width)], bias_block],
-        [homolog_embedding],
-        [pair_input_tensor],
-        [pair_norm_gains],
-        [pair_bias_matrix.T],
-        scratch=[
-            homolog_embedding.shape,
-            pair_input_tensor.shape,
-            pair_norm_gains.shape,
-            (heads, pair_width),
-        ],
-        sems=[4, parts],
-    )
+    (bias,) = call(
+        bias_kernel, [bias_block], pair_input_tensor, pair_norm_gains, pair_bias_matrix.T
+    )
+    msa, bias = lax.optimization_barrier((homolog_embedding, bias))
+    (msa,) = call(repeat_kernel, [[(parts * rows, residues, width)]], msa, sems=[parts])
+    msa = lax.all_to_all(msa, "gi", 0, 0, tiled=True)
     (bias,) = call_near(
         functools.partial(bias_rows_kernel, n_cols),
         [(heads, residues, length)],
         *trade([bias] * n_cols, columns),
         scratch=[(n_cols,) + bias_block],
     )
-    msa, bias = lax.optimization_barrier((msa, bias))
-    msa = lax.all_to_all(msa, "gi", 0, 0, tiled=True)
     bias = trade([bias] * per_part, "gi")
     (msa_first,) = call(
         functools.partial(row_kernel, n_branch, n_gj, per_part, few),
@@ -599,6 +601,7 @@
         scratch=[(per_part, heads, residues, length)]
         + [w.shape for w in (layernorm_scales, horizontal_qkvg_kernel, horizontal_final_kernel)],
         sems=[3 + per_part],
+        grant=63 * 1024 * 1024,
     )
     pair, msa_first = lax.optimization_barrier((pair_input_tensor, msa_first))
 
@@ -636,44 +639,40 @@
     alignment = [block.reshape(-1, width) for block in trade(alignment, columns)]
     share = max(pair_width // n_all, 1)
     slots = pair_width // share
-    triangle = triangle_input_matrix[:, : 4 * pair_width].T.reshape(4, slots, share, pair_width)
-    triangle = jnp.stack(
-        [jnp.stack([triangle[n], triangle[n + 2]], axis=1) for n in range(2)]
-    ).reshape(4 * pair_width, pair_width)
     matrix = outer_output_matrix.reshape(outer_width, outer_width // per, per, pair_width)
     matrix = jnp.transpose(matrix, (3, 2, 1, 0)).reshape(pair_width, -1)
     tri, *first = call_near(
-        functools.partial(pair_kernel, few, n_gi, n_cols),
-        [(slots, positions // lanes, 2 * share, lanes)]
+        functools.partial(pair_kernel, few, n_gi, n_cols, share),
+        [(2 * pair_width * positions // lanes, lanes)]
         + [(positions // n_cols, pair_width)] * n_cols,
         *left,
         *pair,
         right.reshape(n_gi * outer_width, count),
-        pair_norm_gains[1][:, None],
+        pair_norm_gains,
         matrix,
-        triangle,
+        triangle_input_matrix.T,
         scratch=[
             (n_cols, outer_width, count),
             (positions, pair_width),
             (positions, pair_width),
             (positions, pair_width),
+            (pair_width, lanes),
         ],
     )
 
     first, gate = call_near(
         functools.partial(gather_pair_kernel, few, n_cols, residues),
         [(positions, pair_width)] * 2,
-        pair_norm_gains[1:2],
-        triangle_input_matrix[:, 4 * pair_width :],
+        pair_norm_gains,
+        triangle_input_matrix.T,
         *trade(first, columns),
         scratch=[(positions, pair_width)],
     )
     tile = (rows, residues, width)
     scratch = [(n_cols, rows * few, width)]
     packed = share * n_all == pair_width and share == few and few == per
-    gain, last = pair_norm_gains[2], triangle_output_matrix
     if packed:
-        tri = lax.all_to_all(tri, everyone, 0, 0, tiled=True)
+        tri = lax.all_to_all(tri.reshape(n_all, -1, lanes), everyone, 0, 0, tiled=True)
         product, alignment_output = call_near(
             functools.partial(triangle_kernel, few, n_branch, n_gj),
             [(n_all, residues, lanes), tile],
@@ -683,8 +682,6 @@
         )
         product = lax.all_to_all(product, everyone, 0, 0, tiled=True)
         product = product.reshape(n_all * residues, lanes)
-        gain = gain.reshape(n_all, share).T.reshape(-1)
-        last = jnp.swapaxes(last.reshape(n_all, share, pair_width), 0, 1).reshape(last.shape)
     else:
         (alignment_output,) = call_near(
             functools.partial(gather_msa_kernel, few, n_cols),
@@ -703,13 +700,14 @@
         ).reshape(groups, n_cols, few, residues, pair_width)
         product = jnp.transpose(product, (4, 3, 2, 0, 1)).reshape(pair_width, positions)
     (pair_output_tensor,) = call_near(
-        functools.partial(final_kernel, few, n_cols, residues, packed),
+        functools.partial(final_kernel, few, residues, packed),
         [(positions, pair_width)],
         product,
         first,
         gate,
-        gain[:, None],
-        last.T,
+        pair_norm_gains,
+        triangle_output_matrix,
+        scratch=[(pair_width, lanes)],
     )
     return (
         alignment_output,

time: 110 us -> 107 us (0.973)
  local copies, waits for them, and re-layouts: 16.3 us -> 6.37 us
  blocking collectives: 0 us -> 9.74 us
  starting transfers between devices: 39 us -> 32 us
  waiting for transfers between devices: 32.4 us -> 35.6 us
    all_to_all x0 -> x1, blocking collectives: none -> 9.74 us  [per_device(): lax.all_to_all(msa_first, everyone, 0, 0, tiled=True, axis_index_groups=h...]
    unnamed x65 -> x35, local copies, waits for them, and re-layouts: 10.9 us -> 5.87 us
    all_to_all x2 -> x1, starting transfers between devices: 9.49 us -> 5.07 us  [per_device(): lax.all_to_all(tri.reshape(n_all, -1, lanes), everyone, 0, 0, tiled=True)]
    slice x4 -> x0, local copies, waits for them, and re-layouts: 4.35 us -> none  [the longest x1 1.67 us: per_device(): triangle_input_matrix[:, :4 * pair_width]]
    ppermute x18, waiting for transfers between devices: 18.9 us -> 21.6 us  [trade(): lax.ppermute(blocks[k], axes, [(t ^ k, t) for t in range(n) if t ^ k < n])]
    ppermute x18, starting transfers between devices: 15.3 us -> 13.1 us  [trade(): lax.ppermute(blocks[k], axes, [(t ^ k, t) for t in range(n) if t ^ k < n])]
    all_to_all x1, starting transfers between devices: 5.79 us -> 3.96 us  [per_device(): right = lax.all_to_all(right, 'gi', 0, 0, tiled=True)]
    all_to_all x1, starting transfers between devices: 5.85 us -> 7.29 us  [per_device(): msa = lax.all_to_all(msa, 'gi', 0, 0, tiled=True)]
  transfers between devices with their start and end apart: 23 -> 22, of which waited for: 14 -> 12; matrix products, arithmetic and copies ran while one was open for 6% -> 1% of each run, Pallas kernels for 5% -> 1%
where the time goes in v6:
time: 107 us; the launch traced here: 106 us
  waiting for transfers between devices  35.6 us (33%)
  starting transfers between devices  32 us (30%)
  Pallas kernels  21.3 us (20%)
  blocking collectives  9.74 us (9%)
  local copies, waits for them, and re-layouts  6.37 us (6%)
    ppermute x18, waiting for transfers between devices, trade(): lax.ppermute(blocks[k], axes, [(t ^ k, t) for t in range(n) if t ^ k < n])  21.6 us
    ppermute x18, starting transfers between devices, trade(): lax.ppermute(blocks[k], axes, [(t ^ k, t) for t in range(n) if t ^ k < n])  13.1 us
    pallas_call x8, Pallas kernels, call_near(): pl.pallas_call(lambda *refs: kernel(lambda: None, *refs), out_shape=[jax....  12.9 us
    all_to_all x1, waiting for transfers between devices, per_device(): lax.all_to_all(tri.reshape(n_all, -1, lanes), everyone, 0, 0, tiled=True)  10.2 us
    all_to_all x1, blocking collectives, per_device(): lax.all_to_all(msa_first, everyone, 0, 0, tiled=True, axis_index_groups=h...  9.74 us
    pallas_call x3, Pallas kernels, call(): pl.pallas_call(body, out_shape=[jax.ShapeDtypeStruct(bare(out), jnp.float...  8.48 us
    all_to_all x1, starting transfers between devices, per_device(): msa = lax.all_to_all(msa, 'gi', 0, 0, tiled=True)  7.29 us
    unnamed x35, local copies, waits for them, and re-layouts  5.87 us
  transfers between devices with their start and end apart: 22, of which 12 were waited for; matrix products, arithmetic and copies ran while one was open for 1% of the time, Pallas kernels for 1%

profile of v6, /device:TPU:0, one launch (start us, length us, event | category | flops | bytes accessed | tf_op | source)
XLA Modules:
  0.0 105.9 jit_solution(4147369226638156994)
XLA Ops:
  0.6 2.3 %shard_map.158.refs_0_ = f32[2,16,128]{2,1,0:T(8,128)} custom-call(f32[16,32,128]{2,1,0:T(8,128)} %refs_0_.2, f32[3,128]{1,0:T(4,128)} %refs_3_.3, f32[8,128]{1,0:T(8,128)} %bitcast.33), custom_call_target="tpu_custom_call" | custom-call | tf_op jit(solution)/shard_map/pallas_call | solution.py:135
  2.9 1.6 %shard_map.159 = f32[16,16,256]{2,1,0:T(8,128)} custom-call(f32[8,16,256]{2,1,0:T(8,128)} %refs_0_.3), custom_call_target="tpu_custom_call" | custom-call | tf_op jit(solution)/shard_map/pallas_call | solution.py:135
  4.5 7.3 %all-to-all-start = ((f32[16,16,256]{2,1,0:T(8,128)}), f32[16,16,256]{2,1,0:T(8,128)S(1)}, u32[]{:S(2)}, u32[]{:S(2)}) async-start(f32[16,16,256]{2,1,0:T(8,128)} %shard_map.159), calls=%async_computation | async-start | bytes 524288 | tf_op jit(solution)/shard_map/all_to_all | solution.py:585
  15.2 2.1 %collective-permute-done.refs_1_ = f32[2,16,128]{2,1,0:T(8,128)S(1)} collective-permute-done((f32[2,16,128]{2,1,0:T(8,128)S(1)}, f32[2,16,128]{2,1,0:T(8,128)S(1)}, u32[]{:S(2)}, u32[]{:S(2)}) %collective-permute-start) | collective-permute-done | bytes 16416 | tf_op jit(solution)/shard_map/ppermute | solution.py:561
  17.4 2.9 %collective-permute-start.5 = (f32[8,16,128]{2,1,0:T(8,128)S(1)}, f32[8,16,128]{2,1,0:T(8,128)S(1)}, u32[]{:S(2)}, u32[]{:S(2)}) collective-permute-start(f32[8,16,128]{2,1,0:T(8,128)S(1)} %shard_map.160.refs_1_), channel_id=1, source_target_pairs={{6,0},{4,2},{2,4},{0,6},{14,8},{12,10},{10,12},{8,14},{7,1},{5,3},... | collective-permute-start | bytes 196616 | tf_op jit(solution)/shard_map/ppermute | solution.py:561
  21.0 2.3 %collective-permute-done.5.refs_4_ = f32[8,16,128]{2,1,0:T(8,128)S(1)} collective-permute-done((f32[8,16,128]{2,1,0:T(8,128)S(1)}, f32[8,16,128]{2,1,0:T(8,128)S(1)}, u32[]{:S(2)}, u32[]{:S(2)}) %collective-permute-start.5) | collective-permute-done | bytes 65568 | tf_op jit(solution)/shard_map/ppermute | solution.py:561
  23.3 1.3 %collective-permute-done.4.refs_3_ = f32[8,16,128]{2,1,0:T(8,128)S(1)} collective-permute-done((f32[8,16,128]{2,1,0:T(8,128)S(1)}, f32[8,16,128]{2,1,0:T(8,128)S(1)}, u32[]{:S(2)}, u32[]{:S(2)}) %collective-permute-start.4) | collective-permute-done | bytes 65568 | tf_op jit(solution)/shard_map/ppermute | solution.py:561
  26.5 4.6 %shard_map.161 = f32[16,8,256]{2,1,0:T(8,128)} custom-call(f32[16,16,256]{2,1,0:T(8,128)} %copy-done.11, f32[8,16,128]{2,1,0:T(8,128)} %copy-done.4, f32[8,16,128]{2,1,0:T(8,128)} %copy-done.16, f32[8,16,128]{2,1,0:T(8,128)} %copy-done.15, f32[8,16,128]{2,1,0:T(8,128)} %copy-done.14, f32[4,256]{1,0:T(4,128)} %refs_1_.3, f32[256,1024]{1,0:T(8,128)} %refs_6_.1, ...), custom_call_target="tpu_custom_call" | custom-call | tf_op jit(solution)/shard_map/pallas_call | solution.py:135
  31.1 9.7 %all_to_all.25 = f32[16,8,256]{2,1,0:T(8,128)S(1)} all-to-all(f32[16,8,256]{2,1,0:T(8,128)} %shard_map.161), channel_id=1, replica_groups={{0,1,2,3,4,5,6,7,16,17,18,19,20,21,22,23},{8,9,10,11,12,13,14,15,24,25,..., dimensions={0} | all-to-all | bytes 262144 | tf_op jit(solution)/shard_map/all_to_all | solution.py:608
  44.6 4.6 %shard_map.162 = (f32[32,128]{1,0:T(8,128)S(1)}, f32[8,32,128]{2,1,0:T(8,128)}, f32[128,256]{1,0:T(8,128)S(1)}) custom-call(f32[128,256]{1,0:T(8,128)S(1)} %bitcast.24, f32[4,256]{1,0:T(4,128)S(1)} %copy-done.10, f32[256,1024]{1,0:T(8,128)S(1)} %copy-done.1, f32[256,256]{1,0:T(8,128)S(1)} %copy-done.5, f32[256,1024]{1,0:T(8,128)S(1)} %copy-done.2, ...), custom_call_target="tpu_custom_call" | custom-call | tf_op jit(solution)/shard_map/pallas_call | solution.py:148
  49.2 4.0 %all-to-all-start.2 = ((f32[8,32,128]{2,1,0:T(8,128)}), f32[8,32,128]{2,1,0:T(8,128)S(1)}, u32[]{:S(2)}, u32[]{:S(2)}) async-start(f32[8,32,128]{2,1,0:T(8,128)} %get-tuple-element.35), calls=%async_computation.2 | async-start | bytes 262144 | tf_op jit(solution)/shard_map/all_to_all | solution.py:637
  54.1 1.5 %collective-permute-start.11 = (f32[128,128]{1,0:T(8,128)S(1)}, f32[128,128]{1,0:T(8,128)S(1)}, u32[]{:S(2)}, u32[]{:S(2)}) collective-permute-start(f32[128,128]{1,0:T(8,128)S(1)} %get-tuple-element.34), channel_id=1, source_target_pairs={{17,0},{16,1},{1,16},{0,17},{19,2},{18,3},{3,18},{2,19},{21,4},{20... | collective-permute-start | bytes 196616 | tf_op jit(solution)/shard_map/ppermute | solution.py:561
  56.3 2.1 %collective-permute-done.9.refs_5_ = f32[128,128]{1,0:T(8,128)S(1)} collective-permute-done((f32[128,128]{1,0:T(8,128)S(1)}, f32[128,128]{1,0:T(8,128)S(1)}, u32[]{:S(2)}, u32[]{:S(2)}) %collective-permute-start.9) | collective-permute-done | bytes 65568 | tf_op jit(solution)/shard_map/ppermute | solution.py:561
  59.1 3.0 %collective-permute-done.6.refs_1_ = f32[32,128]{1,0:T(8,128)S(1)} collective-permute-done((f32[32,128]{1,0:T(8,128)S(1)}, f32[32,128]{1,0:T(8,128)S(1)}, u32[]{:S(2)}, u32[]{:S(2)}) %collective-permute-start.6) | collective-permute-done | bytes 16416 | tf_op jit(solution)/shard_map/ppermute | solution.py:561
  62.8 4.3 %shard_map.164 = (f32[1024,128]{1,0:T(8,128)}, f32[128,128]{1,0:T(8,128)S(1)}, f32[128,128]{1,0:T(8,128)S(1)}, f32[128,128]{1,0:T(8,128)S(1)}, f32[128,128]{1,0:T(8,128)S(1)}) custom-call(f32[32,128]{1,0:T(8,128)S(1)} %get-tuple-element.29.refs_0_, f32[32,128]{1,0:T(8,128)S(1)} %collective-permute-done.6.refs_1_, ...), custom_call_target="tpu_custom_call" | custom-call | tf_op jit(solution)/shard_map/pallas_call | solution.py:148
  67.1 5.1 %all-to-all-start.3 = ((f32[32,32,128]{2,1,0:T(8,128)}), f32[32,32,128]{2,1,0:T(8,128)S(1)}, u32[]{:S(2)}, u32[]{:S(2)}) async-start(f32[32,32,128]{2,1,0:T(8,128)} %bitcast.9), calls=%async_computation.3 | async-start | bytes 1048576 | tf_op jit(solution)/shard_map/all_to_all | solution.py:675
  72.2 1.8 %collective-permute-start.12 = (f32[4,8,256]{2,1,0:T(8,128)S(1)}, f32[4,8,256]{2,1,0:T(8,128)S(1)}, u32[]{:S(2)}, u32[]{:S(2)}) collective-permute-start(f32[4,8,256]{2,1,0:T(8,128)S(1)} %get-tuple-element.39), channel_id=1, source_target_pairs={{1,0},{0,1},{17,16},{16,17},{3,2},{2,3},{19,18},{18,19},{5,4},{4,5... | collective-permute-start | bytes 98312 | tf_op jit(solution)/shard_map/ppermute | solution.py:561
  74.4 4.4 %collective-permute-done.12 = f32[4,8,256]{2,1,0:T(8,128)S(1)} collective-permute-done((f32[4,8,256]{2,1,0:T(8,128)S(1)}, f32[4,8,256]{2,1,0:T(8,128)S(1)}, u32[]{:S(2)}, u32[]{:S(2)}) %collective-permute-start.12) | collective-permute-done | bytes 32800 | tf_op jit(solution)/shard_map/ppermute | solution.py:561
  78.8 10.2 %all-to-all-done.3 = f32[32,32,128]{2,1,0:T(8,128)S(1)} async-done(((f32[32,32,128]{2,1,0:T(8,128)}), f32[32,32,128]{2,1,0:T(8,128)S(1)}, u32[]{:S(2)}, u32[]{:S(2)}) %all-to-all-start.3) | async-done | bytes 524320 | tf_op jit(solution)/shard_map/all_to_all | solution.py:675
  89.0 1.7 %shard_map.166 = (f32[32,16,128]{2,1,0:T(8,128)}, f32[8,16,256]{2,1,0:T(8,128)}) custom-call(f32[1024,128]{1,0:T(8,128)S(1)} %bitcast.20, f32[32,256]{1,0:T(8,128)S(1)} %bitcast.26, f32[32,256]{1,0:T(8,128)S(1)} %bitcast.27, f32[32,256]{1,0:T(8,128)S(1)} %bitcast.28, f32[32,256]{1,0:T(8,128)S(1)} %bitcast.29), custom_call_target="tpu_custom_call" | custom-call | tf_op jit(solution)/shard_map/pallas_call | solution.py:148
  90.8 2.6 %all-to-all-start.4 = ((f32[32,16,128]{2,1,0:T(8,128)}), f32[32,16,128]{2,1,0:T(8,128)S(1)}, u32[]{:S(2)}, u32[]{:S(2)}) async-start(f32[32,16,128]{2,1,0:T(8,128)} %get-tuple-element.43), calls=%async_computation.4 | async-start | bytes 524288 | tf_op jit(solution)/shard_map/all_to_all | solution.py:683
  93.4 1.7 %collective-permute-start.15 = (f32[128,128]{1,0:T(8,128)S(1)}, f32[128,128]{1,0:T(8,128)S(1)}, u32[]{:S(2)}, u32[]{:S(2)}) collective-permute-start(f32[128,128]{1,0:T(8,128)S(1)} %get-tuple-element.45), channel_id=1, source_target_pairs={{1,0},{0,1},{17,16},{16,17},{3,2},{2,3},{19,18},{18,19},{5,4},{4,5... | collective-permute-start | bytes 196616 | tf_op jit(solution)/shard_map/ppermute | solution.py:561
  95.6 4.2 %collective-permute-done.15.refs_3_ = f32[128,128]{1,0:T(8,128)S(1)} collective-permute-done((f32[128,128]{1,0:T(8,128)S(1)}, f32[128,128]{1,0:T(8,128)S(1)}, u32[]{:S(2)}, u32[]{:S(2)}) %collective-permute-start.15) | collective-permute-done | bytes 65568 | tf_op jit(solution)/shard_map/ppermute | solution.py:561
  100.9 3.7 %all-to-all-done.4 = f32[32,16,128]{2,1,0:T(8,128)S(1)} async-done(((f32[32,16,128]{2,1,0:T(8,128)}), f32[32,16,128]{2,1,0:T(8,128)S(1)}, u32[]{:S(2)}, u32[]{:S(2)}) %all-to-all-start.4) | async-done | bytes 262176 | tf_op jit(solution)/shard_map/all_to_all | solution.py:683
  (69 shorter events, 16.0 us)
Async XLA Ops:
  4.5 20.7 %all-to-all-start = ((f32[16,16,256]{2,1,0:T(8,128)}), f32[16,16,256]{2,1,0:T(8,128)S(1)}, u32[]{:S(2)}, u32[]{:S(2)}) async-start(f32[16,16,256]{2,1,0:T(8,128)} %shard_map.159), calls=%async_computation | async-start | bytes 524288 | tf_op jit(solution)/shard_map/all_to_all | solution.py:585
  11.8 3.4 %collective-permute-start.2 = (f32[2,16,128]{2,1,0:T(8,128)S(1)}, f32[2,16,128]{2,1,0:T(8,128)S(1)}, u32[]{:S(2)}, u32[]{:S(2)}) collective-permute-start(f32[2,16,128]{2,1,0:T(8,128)S(1)} %copy-done.8), channel_id=1, source_target_pairs={{17,0},{16,1},{1,16},{0,17},{19,2},{18,3},{3,18},{2,19},{21,4},{20... | collective-permute-start | bytes 49160 | tf_op jit(solution)/shard_map/ppermute | solution.py:561
  12.6 2.6 %collective-permute-start.1 = (f32[2,16,128]{2,1,0:T(8,128)S(1)}, f32[2,16,128]{2,1,0:T(8,128)S(1)}, u32[]{:S(2)}, u32[]{:S(2)}) collective-permute-start(f32[2,16,128]{2,1,0:T(8,128)S(1)} %copy-done.8), channel_id=1, source_target_pairs={{16,0},{17,1},{0,16},{1,17},{18,2},{19,3},{2,18},{3,19},{20,4},{21... | collective-permute-start | bytes 49160 | tf_op jit(solution)/shard_map/ppermute | solution.py:561
  13.5 3.7 %collective-permute-start = (f32[2,16,128]{2,1,0:T(8,128)S(1)}, f32[2,16,128]{2,1,0:T(8,128)S(1)}, u32[]{:S(2)}, u32[]{:S(2)}) collective-permute-start(f32[2,16,128]{2,1,0:T(8,128)S(1)} %copy-done.8), channel_id=1, source_target_pairs={{1,0},{0,1},{17,16},{16,17},{3,2},{2,3},{19,18},{18,19},{5,4},{4,5... | collective-permute-start | bytes 49160 | tf_op jit(solution)/shard_map/ppermute | solution.py:561
  17.4 5.9 %collective-permute-start.5 = (f32[8,16,128]{2,1,0:T(8,128)S(1)}, f32[8,16,128]{2,1,0:T(8,128)S(1)}, u32[]{:S(2)}, u32[]{:S(2)}) collective-permute-start(f32[8,16,128]{2,1,0:T(8,128)S(1)} %shard_map.160.refs_1_), channel_id=1, source_target_pairs={{6,0},{4,2},{2,4},{0,6},{14,8},{12,10},{10,12},{8,14},{7,1},{5,3},... | collective-permute-start | bytes 196616 | tf_op jit(solution)/shard_map/ppermute | solution.py:561
  20.4 4.3 %collective-permute-start.4 = (f32[8,16,128]{2,1,0:T(8,128)S(1)}, f32[8,16,128]{2,1,0:T(8,128)S(1)}, u32[]{:S(2)}, u32[]{:S(2)}) collective-permute-start(f32[8,16,128]{2,1,0:T(8,128)S(1)} %shard_map.160.refs_1_), channel_id=1, source_target_pairs={{4,0},{6,2},{0,4},{2,6},{12,8},{14,10},{8,12},{10,14},{5,1},{7,3},... | collective-permute-start | bytes 196616 | tf_op jit(solution)/shard_map/ppermute | solution.py:561
  20.9 4.3 %collective-permute-start.3 = (f32[8,16,128]{2,1,0:T(8,128)S(1)}, f32[8,16,128]{2,1,0:T(8,128)S(1)}, u32[]{:S(2)}, u32[]{:S(2)}) collective-permute-start(f32[8,16,128]{2,1,0:T(8,128)S(1)} %shard_map.160.refs_1_), channel_id=1, source_target_pairs={{2,0},{0,2},{6,4},{4,6},{10,8},{8,10},{14,12},{12,14},{3,1},{1,3},... | collective-permute-start | bytes 196616 | tf_op jit(solution)/shard_map/ppermute | solution.py:561
  26.5 14.4 %copy-start.6 = (f32[256,64]{0,1:T(8,128)S(1)}, f32[256,64]{0,1:T(8,128)}, u32[]{:S(2)}) copy-start(f32[256,64]{0,1:T(8,128)} %param.26) | copy-start | bytes 196612
  26.5 14.4 %copy-start.10 = (f32[4,256]{1,0:T(4,128)S(1)}, f32[4,256]{1,0:T(4,128)}, u32[]{:S(2)}) copy-start(f32[4,256]{1,0:T(4,128)} %refs_1_.3) | copy-start | bytes 12292
  49.2 12.9 %all-to-all-start.2 = ((f32[8,32,128]{2,1,0:T(8,128)}), f32[8,32,128]{2,1,0:T(8,128)S(1)}, u32[]{:S(2)}, u32[]{:S(2)}) async-start(f32[8,32,128]{2,1,0:T(8,128)} %get-tuple-element.35), calls=%async_computation.2 | async-start | bytes 262144 | tf_op jit(solution)/shard_map/all_to_all | solution.py:637
  53.4 5.0 %collective-permute-start.9 = (f32[128,128]{1,0:T(8,128)S(1)}, f32[128,128]{1,0:T(8,128)S(1)}, u32[]{:S(2)}, u32[]{:S(2)}) collective-permute-start(f32[128,128]{1,0:T(8,128)S(1)} %get-tuple-element.32), channel_id=1, source_target_pairs={{1,0},{0,1},{17,16},{16,17},{3,2},{2,3},{19,18},{18,19},{5,4},{4,5... | collective-permute-start | bytes 196616 | tf_op jit(solution)/shard_map/ppermute | solution.py:561
  54.1 5.0 %collective-permute-start.10 = (f32[128,128]{1,0:T(8,128)S(1)}, f32[128,128]{1,0:T(8,128)S(1)}, u32[]{:S(2)}, u32[]{:S(2)}) collective-permute-start(f32[128,128]{1,0:T(8,128)S(1)} %get-tuple-element.33), channel_id=1, source_target_pairs={{16,0},{17,1},{0,16},{1,17},{18,2},{19,3},{2,18},{3,19},{20,4},{21... | collective-permute-start | bytes 196616 | tf_op jit(solution)/shard_map/ppermute | solution.py:561
  54.1 5.0 %collective-permute-start.11 = (f32[128,128]{1,0:T(8,128)S(1)}, f32[128,128]{1,0:T(8,128)S(1)}, u32[]{:S(2)}, u32[]{:S(2)}) collective-permute-start(f32[128,128]{1,0:T(8,128)S(1)} %get-tuple-element.34), channel_id=1, source_target_pairs={{17,0},{16,1},{1,16},{0,17},{19,2},{18,3},{3,18},{2,19},{21,4},{20... | collective-permute-start | bytes 196616 | tf_op jit(solution)/shard_map/ppermute | solution.py:561
  55.6 3.5 %collective-permute-start.8 = (f32[32,128]{1,0:T(8,128)S(1)}, f32[32,128]{1,0:T(8,128)S(1)}, u32[]{:S(2)}, u32[]{:S(2)}) collective-permute-start(f32[32,128]{1,0:T(8,128)S(1)} %get-tuple-element.29.refs_0_), channel_id=1, source_target_pairs={{17,0},{16,1},{1,16},{0,17},{19,2},{18,3},{3,18},{2,19},{21,4},{20... | collective-permute-start | bytes 49160 | tf_op jit(solution)/shard_map/ppermute | solution.py:561
  55.8 3.3 %collective-permute-start.7 = (f32[32,128]{1,0:T(8,128)S(1)}, f32[32,128]{1,0:T(8,128)S(1)}, u32[]{:S(2)}, u32[]{:S(2)}) collective-permute-start(f32[32,128]{1,0:T(8,128)S(1)} %get-tuple-element.29.refs_0_), channel_id=1, source_target_pairs={{16,0},{17,1},{0,16},{1,17},{18,2},{19,3},{2,18},{3,19},{20,4},{21... | collective-permute-start | bytes 49160 | tf_op jit(solution)/shard_map/ppermute | solution.py:561
  58.4 3.7 %collective-permute-start.6 = (f32[32,128]{1,0:T(8,128)S(1)}, f32[32,128]{1,0:T(8,128)S(1)}, u32[]{:S(2)}, u32[]{:S(2)}) collective-permute-start(f32[32,128]{1,0:T(8,128)S(1)} %get-tuple-element.29.refs_0_), channel_id=1, source_target_pairs={{1,0},{0,1},{17,16},{16,17},{3,2},{2,3},{19,18},{18,19},{5,4},{4,5... | collective-permute-start | bytes 49160 | tf_op jit(solution)/shard_map/ppermute | solution.py:561
  67.1 21.9 %all-to-all-start.3 = ((f32[32,32,128]{2,1,0:T(8,128)}), f32[32,32,128]{2,1,0:T(8,128)S(1)}, u32[]{:S(2)}, u32[]{:S(2)}) async-start(f32[32,32,128]{2,1,0:T(8,128)} %bitcast.9), calls=%async_computation.3 | async-start | bytes 1048576 | tf_op jit(solution)/shard_map/all_to_all | solution.py:675
  72.2 6.6 %collective-permute-start.12 = (f32[4,8,256]{2,1,0:T(8,128)S(1)}, f32[4,8,256]{2,1,0:T(8,128)S(1)}, u32[]{:S(2)}, u32[]{:S(2)}) collective-permute-start(f32[4,8,256]{2,1,0:T(8,128)S(1)} %get-tuple-element.39), channel_id=1, source_target_pairs={{1,0},{0,1},{17,16},{16,17},{3,2},{2,3},{19,18},{18,19},{5,4},{4,5... | collective-permute-start | bytes 98312 | tf_op jit(solution)/shard_map/ppermute | solution.py:561
  74.1 4.7 %collective-permute-start.13 = (f32[4,8,256]{2,1,0:T(8,128)S(1)}, f32[4,8,256]{2,1,0:T(8,128)S(1)}, u32[]{:S(2)}, u32[]{:S(2)}) collective-permute-start(f32[4,8,256]{2,1,0:T(8,128)S(1)} %get-tuple-element.40), channel_id=1, source_target_pairs={{16,0},{17,1},{0,16},{1,17},{18,2},{19,3},{2,18},{3,19},{20,4},{21... | collective-permute-start | bytes 98312 | tf_op jit(solution)/shard_map/ppermute | solution.py:561
  74.1 4.7 %collective-permute-start.14 = (f32[4,8,256]{2,1,0:T(8,128)S(1)}, f32[4,8,256]{2,1,0:T(8,128)S(1)}, u32[]{:S(2)}, u32[]{:S(2)}) collective-permute-start(f32[4,8,256]{2,1,0:T(8,128)S(1)} %get-tuple-element.41), channel_id=1, source_target_pairs={{17,0},{16,1},{1,16},{0,17},{19,2},{18,3},{3,18},{2,19},{21,4},{20... | collective-permute-start | bytes 98312 | tf_op jit(solution)/shard_map/ppermute | solution.py:561
  90.8 13.8 %all-to-all-start.4 = ((f32[32,16,128]{2,1,0:T(8,128)}), f32[32,16,128]{2,1,0:T(8,128)S(1)}, u32[]{:S(2)}, u32[]{:S(2)}) async-start(f32[32,16,128]{2,1,0:T(8,128)} %get-tuple-element.43), calls=%async_computation.4 | async-start | bytes 524288 | tf_op jit(solution)/shard_map/all_to_all | solution.py:683
  93.4 6.4 %collective-permute-start.15 = (f32[128,128]{1,0:T(8,128)S(1)}, f32[128,128]{1,0:T(8,128)S(1)}, u32[]{:S(2)}, u32[]{:S(2)}) collective-permute-start(f32[128,128]{1,0:T(8,128)S(1)} %get-tuple-element.45), channel_id=1, source_target_pairs={{1,0},{0,1},{17,16},{16,17},{3,2},{2,3},{19,18},{18,19},{5,4},{4,5... | collective-permute-start | bytes 196616 | tf_op jit(solution)/shard_map/ppermute | solution.py:561
  95.1 4.7 %collective-permute-start.16 = (f32[128,128]{1,0:T(8,128)S(1)}, f32[128,128]{1,0:T(8,128)S(1)}, u32[]{:S(2)}, u32[]{:S(2)}) collective-permute-start(f32[128,128]{1,0:T(8,128)S(1)} %get-tuple-element.46), channel_id=1, source_target_pairs={{16,0},{17,1},{0,16},{1,17},{18,2},{19,3},{2,18},{3,19},{20,4},{21... | collective-permute-start | bytes 196616 | tf_op jit(solution)/shard_map/ppermute | solution.py:561
  95.1 5.3 %collective-permute-start.17 = (f32[128,128]{1,0:T(8,128)S(1)}, f32[128,128]{1,0:T(8,128)S(1)}, u32[]{:S(2)}, u32[]{:S(2)}) collective-permute-start(f32[128,128]{1,0:T(8,128)S(1)} %get-tuple-element.47), channel_id=1, source_target_pairs={{17,0},{16,1},{1,16},{0,17},{19,2},{18,3},{3,18},{2,19},{21,4},{20... | collective-permute-start | bytes 196616 | tf_op jit(solution)/shard_map/ppermute | solution.py:561
  (15 other events, 60.4 us)

commit v7 on v6

--- a/solution.py
+++ b/solution.py
@@ -44,7 +44,8 @@
     def one(a, b):
         return lax.dot_general(a, b, numbers, preferred_element_type=jnp.float32)
 
-    (lh, ll), (rh, rl) = split(left), split(right)
+    lh, ll = left if isinstance(left, tuple) else split(left)
+    rh, rl = right if isinstance(right, tuple) else split(right)
     return one(lh, rh) + (one(lh, rl) + one(ll, rh))
 
 
@@ -147,7 +148,10 @@
 def call_near(kernel, outs, *operands, scratch=()):
     return pl.pallas_call(
         lambda *refs: kernel(lambda: None, *refs),
-        out_shape=[jax.ShapeDtypeStruct(out, jnp.float32) for out in outs],
+        out_shape=[
+            out if hasattr(out, "dtype") else jax.ShapeDtypeStruct(out, jnp.float32)
+            for out in outs
+        ],
         in_specs=[vmem] * len(operands),
         out_specs=[vmem] * len(outs),
         scratch_shapes=[pltpu.VMEM(shape, jnp.float32) for shape in scratch],
@@ -166,39 +170,46 @@
         slots[pl.ds(pl.multiple_of((me ^ k) * count, 8), count), :] = ref[...]
 
 
-def bias_kernel(ready, pair_ref, gains_ref, matrix_ref, out_ref):
+def bias_kernel(
+    ready, msa_far, pair_far, gains_far, matrix_far, copies_far, out_ref, msa_ref, pair_ref,
+    gains_ref, matrix_ref, sems, out_sems
+):
+    rows = msa_far.shape[0]
+    repeats = copies_far.shape[0] // rows
+    copies = start_copies(
+        [(msa_far, msa_ref), (gains_far, gains_ref), (matrix_far, matrix_ref), (pair_far, pair_ref)],
+        sems,
+    )
     residues, pair_cols, _ = pair_ref.shape
     heads = matrix_ref.shape[0]
     per = lanes // pair_cols
     ready()
+    wait_all(copies)
+    copies = start_copies(
+        [(msa_ref, copies_far.at[pl.ds(n * rows, rows)]) for n in range(repeats)], out_sems
+    )
     normal = layer_normalise(pair_ref[...], gains_ref[0:1, :][None])
     for i in range(residues):
         here = multiply(matrix_ref[...], normal[i], across=True)
         for h in range(heads):
             out_ref[h // per, i : i + 1, pl.ds(h % per * pair_cols, pair_cols)] = here[h : h + 1]
-
-
-def repeat_kernel(ready, msa_ref, copies_far, sems):
-    rows = msa_ref.shape[0]
-    ready()
-    wait_all(
-        start_copies(
-            [
-                (msa_ref, copies_far.at[pl.ds(n * rows, rows)])
-                for n in range(copies_far.shape[0] // rows)
-            ],
-            sems,
-        )
-    )
-
-
-def pair_blocks_kernel(few, residues, ready, pair_ref, *rest):
-    chunks, slots = rest[:-1], rest[-1]
-    n_cols = len(chunks)
+    wait_all(copies)
+
+
+def store_pair(value, high_ref, low_ref):
+    high_ref[...], low_ref[...] = split(value)
+
+
+def column_stage_kernel(few, residues, n_cols, ready, gains_ref, *rest):
+    weights, pair_ref, gains_out, rest = rest[:5], rest[5], rest[6], rest[7:]
+    pairs, chunks, slots = rest[:10], rest[10 : 10 + n_cols], rest[-1]
+    ready()
+    gains_out[...] = gains_ref[...]
+    for n, ref in enumerate(weights):
+        store_pair(ref[...], pairs[2 * n], pairs[2 * n + 1])
     block = chunks[0].shape[0]
     groups = block // (residues * few)
     me = column_index()
-    ready()
     for c in range(n_cols):
         for o in range(groups):
             for f in range(few):
@@ -208,6 +219,18 @@
     for k in range(n_cols):
         start = pl.multiple_of((me ^ k) * block, 8)
         chunks[k][...] = slots[pl.ds(start, block), :]
+
+
+def pair_stage_kernel(wide, per, ready, gains_ref, matrix_ref, triangle_ref, *pairs):
+    ready()
+    width = triangle_ref.shape[0]
+    rows = [
+        matrix_ref[pl.ds(t * per + d, wide, stride=wide), :]
+        for d in range(per)
+        for t in range(wide // per)
+    ]
+    store_pair(jnp.concatenate(rows, axis=0).T, *pairs[:2])
+    store_pair(triangle_ref[:, : 4 * width].T * gains_ref[1:2, :], *pairs[2:])
 
 
 def bias_rows_kernel(n_cols, ready, *rest):
@@ -282,16 +305,17 @@
                 )
 
 
-def column_kernel(
-    few, heads, ready, msa_ref, gains_ref, qkvg_ref, final_ref, expand_ref, shrink_ref, sides_ref,
-    left_ref, right_ref, out_ref
-):
+def column_kernel(few, heads, ready, msa_ref, gains_ref, *rest):
+    left_ref, right_ref, out_ref = rest[10:]
+    qkvg, final, expand, shrink, sides = (
+        (rest[2 * n][...], rest[2 * n + 1][...]) for n in range(5)
+    )
     ready()
     count, width = msa_ref.shape
-    inner = final_ref.shape[0]
-    half = sides_ref.shape[0] // 2
+    inner = final[0].shape[0]
+    half = sides[0].shape[0] // 2
     first = msa_ref[...]
-    projected = multiply(layer_normalise(first, gains_ref[1:2, :]), qkvg_ref[...])
+    projected = multiply(layer_normalise(first, gains_ref[1:2, :]), qkvg)
     query, key, value, gate = (projected[:, k * inner : (k + 1) * inner] for k in range(4))
     allowed = None
     if few > 1:
@@ -300,11 +324,11 @@
         holds = lax.broadcasted_iota(jnp.int32, shape, 1)
         allowed = lax.rem(asks, few) == lax.rem(holds, few)
     attended = attend(query, key, value, None, heads, allowed)
-    second = first + multiply(sigmoid(gate) * attended, final_ref[...])
-    expanded = multiply(layer_normalise(second, gains_ref[2:3, :]), expand_ref[...])
-    third = second + multiply(jnp.maximum(expanded, 0.0), shrink_ref[...])
+    second = first + multiply(sigmoid(gate) * attended, final)
+    expanded = multiply(layer_normalise(second, gains_ref[2:3, :]), expand)
+    third = second + multiply(jnp.maximum(expanded, 0.0), shrink)
     out_ref[...] = third
-    factors = multiply(sides_ref[...], layer_normalise(third, gains_ref[3:4, :]), across=True)
+    factors = multiply(sides, layer_normalise(third, gains_ref[3:4, :]), across=True)
     left_ref[...] = factors[:half]
     for g in range(right_ref.shape[0]):
         right_ref[g] = factors[half:]
@@ -352,7 +376,7 @@
     width = first_ref.shape[1]
     normal = layer_normalise(first_ref[...], gains_ref[1:2, :])
     gate_ref[...] = sigmoid(
-        multiply(normal, matrix_ref[pl.ds(4 * width, width), :], across=True)
+        multiply(normal, matrix_ref[:, 4 * width :])
     )
 
 
@@ -422,9 +446,8 @@
     few, n_gi, n_cols, share, ready, *rest
 ):
     left_refs, pair_refs = rest[:n_cols], rest[n_cols : 2 * n_cols]
-    right_ref, gains_ref, matrix_ref, triangle_ref, tri_ref = rest[2 * n_cols : 2 * n_cols + 5]
-    chunks = rest[2 * n_cols + 5 : 3 * n_cols + 5]
-    rest = rest[3 * n_cols + 5 :]
+    right_ref, *staged, tri_ref = rest[2 * n_cols : 2 * n_cols + 6]
+    chunks, rest = rest[2 * n_cols + 6 : 3 * n_cols + 6], rest[3 * n_cols + 6 :]
     left_ref, slots, pair_ref, first_ref, sides_ref = rest
     me = column_index()
     groups_j = n_gi // n_cols
@@ -472,12 +495,10 @@
             pair_ref[pl.ds(c * groups_j + o, half, stride=n_gi), :] = slots[
                 pl.ds(c * block + o, half, stride=groups_j), :
             ]
-    update = multiply(matrix_ref[...], jnp.concatenate(outputs, axis=1))
+    matrix, triangle = ((staged[n][...], staged[n + 1][...]) for n in (0, 2))
+    update = multiply(matrix, jnp.concatenate(outputs, axis=1))
     first = pair_ref[...].T + update
-    projected = multiply(
-        triangle_ref[pl.ds(0, 4 * width), :] * gains_ref[1:2, :],
-        layer_normalise(first, 1.0, axis=0),
-    )
+    projected = multiply(triangle, layer_normalise(first, 1.0, axis=0))
     for n in range(2):
         value = projected[2 * n * width : (2 * n + 1) * width]
         tri = sigmoid(projected[(2 * n + 1) * width : (2 * n + 2) * width]) * value
@@ -577,11 +598,21 @@
 
     per = lanes // pair_cols
     bias_block = (heads // per, residues, lanes)
-    (bias,) = call(
-        bias_kernel, [bias_block], pair_input_tensor, pair_norm_gains, pair_bias_matrix.T
-    )
-    msa, bias = lax.optimization_barrier((homolog_embedding, bias))
-    (msa,) = call(repeat_kernel, [[(parts * rows, residues, width)]], msa, sems=[parts])
+    msa, bias = call(
+        bias_kernel,
+        [[(parts * rows, residues, width)], bias_block],
+        [homolog_embedding],
+        [pair_input_tensor],
+        [pair_norm_gains],
+        [pair_bias_matrix.T],
+        scratch=[
+            homolog_embedding.shape,
+            pair_input_tensor.shape,
+            pair_norm_gains.shape,
+            (heads, pair_width),
+        ],
+        sems=[4, parts],
+    )
     msa = lax.all_to_all(msa, "gi", 0, 0, tiled=True)
     (bias,) = call_near(
         functools.partial(bias_rows_kernel, n_cols),
@@ -604,21 +635,31 @@
         grant=63 * 1024 * 1024,
     )
     pair, msa_first = lax.optimization_barrier((pair_input_tensor, msa_first))
-
     msa_first = lax.all_to_all(msa_first, everyone, 0, 0, tiled=True, axis_index_groups=halves)
     count = n_half * each
     weights = (
-        layernorm_scales,
         vertical_qkvg_kernel,
         vertical_final_kernel,
         feedforward_expand_kernel,
         feedforward_shrink_kernel,
         dyadic_sides_kernel.T,
     )
+    gains, *weights = call_near(
+        functools.partial(column_stage_kernel, few, residues, n_cols),
+        [layernorm_scales.shape]
+        + [jax.ShapeDtypeStruct(w.shape, jnp.bfloat16) for w in weights for _ in range(2)]
+        + [(positions // n_cols, pair_width)] * n_cols,
+        layernorm_scales,
+        *weights,
+        pair.reshape(positions, pair_width),
+        scratch=[(positions, pair_width)],
+    )
+    weights, pair = weights[:-n_cols], trade(weights[-n_cols:], columns)
     left, right, alignment = call_near(
         functools.partial(column_kernel, few, heads),
         [(outer_width, count), (n_gi, outer_width, count), (count, width)],
         msa_first.reshape(count, width),
+        gains,
         *weights,
     )
     alignment = call_near(
@@ -627,20 +668,23 @@
         alignment,
         scratch=[(n_cols, per_part, each, width)],
     )
-    pair = call_near(
-        functools.partial(pair_blocks_kernel, few, residues),
-        [(positions // n_cols, pair_width)] * n_cols,
-        pair.reshape(positions, pair_width),
-        scratch=[(positions, pair_width)],
-    )
-    pair = trade(pair, columns)
     right = lax.all_to_all(right, "gi", 0, 0, tiled=True)
     left = trade([left] * n_cols, columns)
     alignment = [block.reshape(-1, width) for block in trade(alignment, columns)]
     share = max(pair_width // n_all, 1)
     slots = pair_width // share
-    matrix = outer_output_matrix.reshape(outer_width, outer_width // per, per, pair_width)
-    matrix = jnp.transpose(matrix, (3, 2, 1, 0)).reshape(pair_width, -1)
+    matrix, left[0] = lax.optimization_barrier((outer_output_matrix, left[0]))
+    staged = call_near(
+        functools.partial(pair_stage_kernel, outer_width, per),
+        [
+            jax.ShapeDtypeStruct(shape, jnp.bfloat16)
+            for shape in (matrix.shape[::-1], (4 * pair_width, pair_width))
+            for _ in range(2)
+        ],
+        pair_norm_gains,
+        matrix,
+        triangle_input_matrix,
+    )
     tri, *first = call_near(
         functools.partial(pair_kernel, few, n_gi, n_cols, share),
         [(2 * pair_width * positions // lanes, lanes)]
@@ -648,9 +692,7 @@
         *left,
         *pair,
         right.reshape(n_gi * outer_width, count),
-        pair_norm_gains,
-        matrix,
-        triangle_input_matrix.T,
+        *staged,
         scratch=[
             (n_cols, outer_width, count),
             (positions, pair_width),
@@ -664,7 +706,7 @@
         functools.partial(gather_pair_kernel, few, n_cols, residues),
         [(positions, pair_width)] * 2,
         pair_norm_gains,
-        triangle_input_matrix.T,
+        triangle_input_matrix,
         *trade(first, columns),
         scratch=[(positions, pair_width)],
     )

time: 107 us -> 116 us (1.084)
  local copies, waits for them, and re-layouts: 6.37 us -> 18.7 us
  starting transfers between devices: 32 us -> 42.1 us
  blocking collectives: 9.74 us -> 0 us
  waiting for transfers between devices: 35.6 us -> 32.1 us
    unnamed x35 -> x78, local copies, waits for them, and re-layouts: 5.87 us -> 18.7 us
    all_to_all x1 -> x0, blocking collectives: 9.74 us -> none  [per_device(): lax.all_to_all(msa_first, everyone, 0, 0, tiled=True, axis_index_groups=h...]
    all_to_all x0 -> x1, starting transfers between devices: none -> 3.66 us  [per_device(): lax.all_to_all(msa_first, everyone, 0, 0, tiled=True, axis_index_groups=h...]
    ppermute x18, waiting for transfers between devices: 21.6 us -> 18.1 us  [trade(): lax.ppermute(blocks[k], axes, [(t ^ k, t) for t in range(n) if t ^ k < n])]
    ppermute x18, starting transfers between devices: 13.1 us -> 16.1 us  [trade(): lax.ppermute(blocks[k], axes, [(t ^ k, t) for t in range(n) if t ^ k < n])]
    all_to_all x1, starting transfers between devices: 3.96 us -> 5.8 us  [per_device(): right = lax.all_to_all(right, 'gi', 0, 0, tiled=True)]
    all_to_all x1, starting transfers between devices: 5.07 us -> 6.65 us  [per_device(): lax.all_to_all(tri.reshape(n_all, -1, lanes), everyone, 0, 0, tiled=True)]
    pallas_call x3 -> x2, Pallas kernels: 8.48 us -> 7.01 us  [call(): pl.pallas_call(body, out_shape=[jax.ShapeDtypeStruct(bare(out), jnp.float...]
  transfers between devices with their start and end apart: 22 -> 23, of which waited for: 12 -> 12; matrix products, arithmetic and copies ran while one was open for 1% -> 0% of each run, Pallas kernels for 1% -> 2%
where the time goes in v7:
time: 116 us; the launch traced here: 115 us
  starting transfers between devices  42.1 us (36%)
  waiting for transfers between devices  32.1 us (28%)
  Pallas kernels  21.2 us (18%)
  local copies, waits for them, and re-layouts  18.7 us (16%)
    unnamed x78, local copies, waits for them, and re-layouts  18.7 us
    ppermute x18, waiting for transfers between devices, trade(): lax.ppermute(blocks[k], axes, [(t ^ k, t) for t in range(n) if t ^ k < n])  18.1 us
    ppermute x18, starting transfers between devices, trade(): lax.ppermute(blocks[k], axes, [(t ^ k, t) for t in range(n) if t ^ k < n])  16.1 us
    pallas_call x9, Pallas kernels, call_near(): pl.pallas_call(lambda *refs: kernel(lambda: None, *refs), out_shape=[out...  14.2 us
    all_to_all x1, waiting for transfers between devices, per_device(): lax.all_to_all(tri.reshape(n_all, -1, lanes), everyone, 0, 0, tiled=True)  10.2 us
    all_to_all x1, starting transfers between devices, per_device(): msa = lax.all_to_all(msa, 'gi', 0, 0, tiled=True)  7.29 us
    pallas_call x2, Pallas kernels, call(): pl.pallas_call(body, out_shape=[jax.ShapeDtypeStruct(bare(out), jnp.float...  7.01 us
    all_to_all x1, starting transfers between devices, per_device(): lax.all_to_all(tri.reshape(n_all, -1, lanes), everyone, 0, 0, tiled=True)  6.65 us
  transfers between devices with their start and end apart: 23, of which 12 were waited for; matrix products, arithmetic and copies ran while one was open for 0% of the time, Pallas kernels for 2%

profile of v7, /device:TPU:0, one launch (start us, length us, event | category | flops | bytes accessed | tf_op | source)
XLA Modules:
  0.0 114.9 jit_solution(9488600916684265982)
XLA Ops:
  0.6 2.4 %shard_map.158 = (f32[16,16,256]{2,1,0:T(8,128)}, f32[2,16,128]{2,1,0:T(8,128)}) custom-call(f32[8,16,256]{2,1,0:T(8,128)} %refs_0_.4, f32[16,32,128]{2,1,0:T(8,128)} %refs_1_.3, f32[3,128]{1,0:T(4,128)} %refs_3_.3, f32[8,128]{1,0:T(8,128)} %bitcast.24), custom_call_target="tpu_custom_call" | custom-call | tf_op jit(solution)/shard_map/pallas_call | solution.py:136
  3.1 7.3 %all-to-all-start = ((f32[16,16,256]{2,1,0:T(8,128)}), f32[16,16,256]{2,1,0:T(8,128)S(1)}, u32[]{:S(2)}, u32[]{:S(2)}) async-start(f32[16,16,256]{2,1,0:T(8,128)} %get-tuple-element.43), calls=%async_computation | async-start | bytes 524288 | tf_op jit(solution)/shard_map/all_to_all | solution.py:616
  13.7 2.1 %collective-permute-done.refs_1_ = f32[2,16,128]{2,1,0:T(8,128)S(1)} collective-permute-done((f32[2,16,128]{2,1,0:T(8,128)S(1)}, f32[2,16,128]{2,1,0:T(8,128)S(1)}, u32[]{:S(2)}, u32[]{:S(2)}) %collective-permute-start) | collective-permute-done | bytes 16416 | tf_op jit(solution)/shard_map/ppermute | solution.py:582
  16.0 2.9 %collective-permute-start.5 = (f32[8,16,128]{2,1,0:T(8,128)S(1)}, f32[8,16,128]{2,1,0:T(8,128)S(1)}, u32[]{:S(2)}, u32[]{:S(2)}) collective-permute-start(f32[8,16,128]{2,1,0:T(8,128)S(1)} %shard_map.159.refs_1_), channel_id=1, source_target_pairs={{6,0},{4,2},{2,4},{0,6},{14,8},{12,10},{10,12},{8,14},{7,1},{5,3},... | collective-permute-start | bytes 196616 | tf_op jit(solution)/shard_map/ppermute | solution.py:582
  19.5 2.3 %collective-permute-done.5.refs_4_ = f32[8,16,128]{2,1,0:T(8,128)S(1)} collective-permute-done((f32[8,16,128]{2,1,0:T(8,128)S(1)}, f32[8,16,128]{2,1,0:T(8,128)S(1)}, u32[]{:S(2)}, u32[]{:S(2)}) %collective-permute-start.5) | collective-permute-done | bytes 65568 | tf_op jit(solution)/shard_map/ppermute | solution.py:582
  21.9 1.3 %collective-permute-done.4.refs_3_ = f32[8,16,128]{2,1,0:T(8,128)S(1)} collective-permute-done((f32[8,16,128]{2,1,0:T(8,128)S(1)}, f32[8,16,128]{2,1,0:T(8,128)S(1)}, u32[]{:S(2)}, u32[]{:S(2)}) %collective-permute-start.4) | collective-permute-done | bytes 65568 | tf_op jit(solution)/shard_map/ppermute | solution.py:582
  25.0 4.6 %shard_map.160 = f32[16,8,256]{2,1,0:T(8,128)} custom-call(f32[16,16,256]{2,1,0:T(8,128)} %copy-done.35, f32[8,16,128]{2,1,0:T(8,128)} %copy-done.11, f32[8,16,128]{2,1,0:T(8,128)} %copy-done.38, f32[8,16,128]{2,1,0:T(8,128)} %copy-done.37, f32[8,16,128]{2,1,0:T(8,128)} %copy-done.36, f32[4,256]{1,0:T(4,128)} %refs_0_.5, f32[256,1024]{1,0:T(8,128)} %refs_6_.1, ...), custom_call_target="tpu_custom_call" | custom-call | tf_op jit(solution)/shard_map/pallas_call | solution.py:136
  29.6 3.7 %all-to-all-start.1 = ((f32[16,8,256]{2,1,0:T(8,128)}), f32[16,8,256]{2,1,0:T(8,128)S(1)}, u32[]{:S(2)}, u32[]{:S(2)}) async-start(f32[16,8,256]{2,1,0:T(8,128)} %shard_map.160), calls=%async_computation.1 | async-start | bytes 262144 | tf_op jit(solution)/shard_map/all_to_all | solution.py:638
  51.2 4.6 %shard_map.162 = (f32[32,128]{1,0:T(8,128)S(1)}, f32[8,32,128]{2,1,0:T(8,128)}, f32[128,256]{1,0:T(8,128)S(1)}) custom-call(f32[128,256]{1,0:T(8,128)S(1)} %bitcast.17, f32[4,256]{1,0:T(4,128)S(1)} %get-tuple-element.47.refs_1_, bf16[256,1024]{1,0:T(8,128)(2,1)S(1)} %get-tuple-element.48.refs_2_, bf16[256,1024]{1,0:T(8,128)(2,1)S(1)} %get-tuple-element.49.refs_3_, ...), custom_call_target="tpu_custom_call" | custom-call | tf_op jit(solution)/shard_map/pallas_call | solution.py:149
  56.5 5.8 %all-to-all-start.2 = ((f32[8,32,128]{2,1,0:T(8,128)}), f32[8,32,128]{2,1,0:T(8,128)S(1)}, u32[]{:S(2)}, u32[]{:S(2)}) async-start(f32[8,32,128]{2,1,0:T(8,128)} %get-tuple-element.64), calls=%async_computation.2 | async-start | bytes 262144 | tf_op jit(solution)/shard_map/all_to_all | solution.py:671
  62.3 1.5 %collective-permute-start.9 = (f32[128,128]{1,0:T(8,128)S(1)}, f32[128,128]{1,0:T(8,128)S(1)}, u32[]{:S(2)}, u32[]{:S(2)}) collective-permute-start(f32[128,128]{1,0:T(8,128)S(1)} %copy-done.34), channel_id=1, source_target_pairs={{1,0},{0,1},{17,16},{16,17},{3,2},{2,3},{19,18},{18,19},{5,4},{4,5... | collective-permute-start | bytes 196616 | tf_op jit(solution)/shard_map/ppermute | solution.py:582
  66.6 2.1 %collective-permute-start.6 = (f32[32,128]{1,0:T(8,128)S(1)}, f32[32,128]{1,0:T(8,128)S(1)}, u32[]{:S(2)}, u32[]{:S(2)}) collective-permute-start(f32[32,128]{1,0:T(8,128)S(1)} %get-tuple-element.59.refs_0_), channel_id=1, source_target_pairs={{1,0},{0,1},{17,16},{16,17},{3,2},{2,3},{19,18},{18,19},{5,4},{4,5... | collective-permute-start | bytes 49160 | tf_op jit(solution)/shard_map/ppermute | solution.py:582
  69.2 1.2 %collective-permute-done.6.refs_1_ = f32[32,128]{1,0:T(8,128)S(1)} collective-permute-done((f32[32,128]{1,0:T(8,128)S(1)}, f32[32,128]{1,0:T(8,128)S(1)}, u32[]{:S(2)}, u32[]{:S(2)}) %collective-permute-start.6) | collective-permute-done | bytes 16416 | tf_op jit(solution)/shard_map/ppermute | solution.py:582
  70.4 4.3 %shard_map.164 = (f32[1024,128]{1,0:T(8,128)}, f32[128,128]{1,0:T(8,128)S(1)}, f32[128,128]{1,0:T(8,128)S(1)}, f32[128,128]{1,0:T(8,128)S(1)}, f32[128,128]{1,0:T(8,128)S(1)}) custom-call(f32[32,128]{1,0:T(8,128)S(1)} %get-tuple-element.59.refs_0_, f32[32,128]{1,0:T(8,128)S(1)} %collective-permute-done.6.refs_1_, ...), custom_call_target="tpu_custom_call" | custom-call | tf_op jit(solution)/shard_map/pallas_call | solution.py:149
  74.8 6.7 %all-to-all-start.3 = ((f32[32,32,128]{2,1,0:T(8,128)}), f32[32,32,128]{2,1,0:T(8,128)S(1)}, u32[]{:S(2)}, u32[]{:S(2)}) async-start(f32[32,32,128]{2,1,0:T(8,128)} %bitcast.5), calls=%async_computation.3 | async-start | bytes 1048576 | tf_op jit(solution)/shard_map/all_to_all | solution.py:717
  81.5 1.7 %collective-permute-start.12 = (f32[4,8,256]{2,1,0:T(8,128)S(1)}, f32[4,8,256]{2,1,0:T(8,128)S(1)}, u32[]{:S(2)}, u32[]{:S(2)}) collective-permute-start(f32[4,8,256]{2,1,0:T(8,128)S(1)} %get-tuple-element.73), channel_id=1, source_target_pairs={{1,0},{0,1},{17,16},{16,17},{3,2},{2,3},{19,18},{18,19},{5,4},{4,5... | collective-permute-start | bytes 98312 | tf_op jit(solution)/shard_map/ppermute | solution.py:582
  83.7 4.2 %collective-permute-done.12 = f32[4,8,256]{2,1,0:T(8,128)S(1)} collective-permute-done((f32[4,8,256]{2,1,0:T(8,128)S(1)}, f32[4,8,256]{2,1,0:T(8,128)S(1)}, u32[]{:S(2)}, u32[]{:S(2)}) %collective-permute-start.12) | collective-permute-done | bytes 32800 | tf_op jit(solution)/shard_map/ppermute | solution.py:582
  87.8 10.2 %all-to-all-done.3 = f32[32,32,128]{2,1,0:T(8,128)S(1)} async-done(((f32[32,32,128]{2,1,0:T(8,128)}), f32[32,32,128]{2,1,0:T(8,128)S(1)}, u32[]{:S(2)}, u32[]{:S(2)}) %all-to-all-start.3) | async-done | bytes 524320 | tf_op jit(solution)/shard_map/all_to_all | solution.py:717
  98.1 1.7 %shard_map.166 = (f32[32,16,128]{2,1,0:T(8,128)}, f32[8,16,256]{2,1,0:T(8,128)}) custom-call(f32[1024,128]{1,0:T(8,128)S(1)} %bitcast.13, f32[32,256]{1,0:T(8,128)S(1)} %bitcast.19, f32[32,256]{1,0:T(8,128)S(1)} %bitcast.20, f32[32,256]{1,0:T(8,128)S(1)} %bitcast.21, f32[32,256]{1,0:T(8,128)S(1)} %bitcast.22), custom_call_target="tpu_custom_call" | custom-call | tf_op jit(solution)/shard_map/pallas_call | solution.py:149
  99.8 2.6 %all-to-all-start.4 = ((f32[32,16,128]{2,1,0:T(8,128)}), f32[32,16,128]{2,1,0:T(8,128)S(1)}, u32[]{:S(2)}, u32[]{:S(2)}) async-start(f32[32,16,128]{2,1,0:T(8,128)} %get-tuple-element.77), calls=%async_computation.4 | async-start | bytes 524288 | tf_op jit(solution)/shard_map/all_to_all | solution.py:725
  102.4 1.7 %collective-permute-start.15 = (f32[128,128]{1,0:T(8,128)S(1)}, f32[128,128]{1,0:T(8,128)S(1)}, u32[]{:S(2)}, u32[]{:S(2)}) collective-permute-start(f32[128,128]{1,0:T(8,128)S(1)} %get-tuple-element.79), channel_id=1, source_target_pairs={{1,0},{0,1},{17,16},{16,17},{3,2},{2,3},{19,18},{18,19},{5,4},{4,5... | collective-permute-start | bytes 196616 | tf_op jit(solution)/shard_map/ppermute | solution.py:582
  104.6 4.2 %collective-permute-done.15.refs_3_ = f32[128,128]{1,0:T(8,128)S(1)} collective-permute-done((f32[128,128]{1,0:T(8,128)S(1)}, f32[128,128]{1,0:T(8,128)S(1)}, u32[]{:S(2)}, u32[]{:S(2)}) %collective-permute-start.15) | collective-permute-done | bytes 65568 | tf_op jit(solution)/shard_map/ppermute | solution.py:582
  109.9 3.7 %all-to-all-done.4 = f32[32,16,128]{2,1,0:T(8,128)S(1)} async-done(((f32[32,16,128]{2,1,0:T(8,128)}), f32[32,16,128]{2,1,0:T(8,128)S(1)}, u32[]{:S(2)}, u32[]{:S(2)}) %all-to-all-start.4) | async-done | bytes 262176 | tf_op jit(solution)/shard_map/all_to_all | solution.py:725
  113.6 1.3 %shard_map.168 = f32[512,128]{1,0:T(8,128)} custom-call(f32[512,128]{1,0:T(8,128)S(1)} %bitcast.15, f32[512,128]{1,0:T(8,128)S(1)} %get-tuple-element.82.refs_1_, f32[512,128]{1,0:T(8,128)S(1)} %get-tuple-element.83.refs_2_, f32[3,128]{1,0:T(4,128)S(1)} %copy-done.26, f32[128,128]{1,0:T(8,128)S(1)} %copy-done.19), custom_call_target="tpu_custom_call" | custom-call | tf_op jit(solution)/shard_map/pallas_call | solution.py:149
  (111 shorter events, 29.9 us)
Async XLA Ops:
  3.1 20.7 %all-to-all-start = ((f32[16,16,256]{2,1,0:T(8,128)}), f32[16,16,256]{2,1,0:T(8,128)S(1)}, u32[]{:S(2)}, u32[]{:S(2)}) async-start(f32[16,16,256]{2,1,0:T(8,128)} %get-tuple-element.43), calls=%async_computation | async-start | bytes 524288 | tf_op jit(solution)/shard_map/all_to_all | solution.py:616
  10.4 3.4 %collective-permute-start.2 = (f32[2,16,128]{2,1,0:T(8,128)S(1)}, f32[2,16,128]{2,1,0:T(8,128)S(1)}, u32[]{:S(2)}, u32[]{:S(2)}) collective-permute-start(f32[2,16,128]{2,1,0:T(8,128)S(1)} %copy-done.27), channel_id=1, source_target_pairs={{17,0},{16,1},{1,16},{0,17},{19,2},{18,3},{3,18},{2,19},{21,4},{20... | collective-permute-start | bytes 49160 | tf_op jit(solution)/shard_map/ppermute | solution.py:582
  11.1 2.6 %collective-permute-start.1 = (f32[2,16,128]{2,1,0:T(8,128)S(1)}, f32[2,16,128]{2,1,0:T(8,128)S(1)}, u32[]{:S(2)}, u32[]{:S(2)}) collective-permute-start(f32[2,16,128]{2,1,0:T(8,128)S(1)} %copy-done.27), channel_id=1, source_target_pairs={{16,0},{17,1},{0,16},{1,17},{18,2},{19,3},{2,18},{3,19},{20,4},{21... | collective-permute-start | bytes 49160 | tf_op jit(solution)/shard_map/ppermute | solution.py:582
  12.0 3.7 %collective-permute-start = (f32[2,16,128]{2,1,0:T(8,128)S(1)}, f32[2,16,128]{2,1,0:T(8,128)S(1)}, u32[]{:S(2)}, u32[]{:S(2)}) collective-permute-start(f32[2,16,128]{2,1,0:T(8,128)S(1)} %copy-done.27), channel_id=1, source_target_pairs={{1,0},{0,1},{17,16},{16,17},{3,2},{2,3},{19,18},{18,19},{5,4},{4,5... | collective-permute-start | bytes 49160 | tf_op jit(solution)/shard_map/ppermute | solution.py:582
  16.0 5.9 %collective-permute-start.5 = (f32[8,16,128]{2,1,0:T(8,128)S(1)}, f32[8,16,128]{2,1,0:T(8,128)S(1)}, u32[]{:S(2)}, u32[]{:S(2)}) collective-permute-start(f32[8,16,128]{2,1,0:T(8,128)S(1)} %shard_map.159.refs_1_), channel_id=1, source_target_pairs={{6,0},{4,2},{2,4},{0,6},{14,8},{12,10},{10,12},{8,14},{7,1},{5,3},... | collective-permute-start | bytes 196616 | tf_op jit(solution)/shard_map/ppermute | solution.py:582
  18.9 4.3 %collective-permute-start.4 = (f32[8,16,128]{2,1,0:T(8,128)S(1)}, f32[8,16,128]{2,1,0:T(8,128)S(1)}, u32[]{:S(2)}, u32[]{:S(2)}) collective-permute-start(f32[8,16,128]{2,1,0:T(8,128)S(1)} %shard_map.159.refs_1_), channel_id=1, source_target_pairs={{4,0},{6,2},{0,4},{2,6},{12,8},{14,10},{8,12},{10,14},{5,1},{7,3},... | collective-permute-start | bytes 196616 | tf_op jit(solution)/shard_map/ppermute | solution.py:582
  19.4 4.3 %collective-permute-start.3 = (f32[8,16,128]{2,1,0:T(8,128)S(1)}, f32[8,16,128]{2,1,0:T(8,128)S(1)}, u32[]{:S(2)}, u32[]{:S(2)}) collective-permute-start(f32[8,16,128]{2,1,0:T(8,128)S(1)} %shard_map.159.refs_1_), channel_id=1, source_target_pairs={{2,0},{0,2},{6,4},{4,6},{10,8},{8,10},{14,12},{12,14},{3,1},{1,3},... | collective-permute-start | bytes 196616 | tf_op jit(solution)/shard_map/ppermute | solution.py:582
  29.6 16.1 %all-to-all-start.1 = ((f32[16,8,256]{2,1,0:T(8,128)}), f32[16,8,256]{2,1,0:T(8,128)S(1)}, u32[]{:S(2)}, u32[]{:S(2)}) async-start(f32[16,8,256]{2,1,0:T(8,128)} %shard_map.160), calls=%async_computation.1 | async-start | bytes 262144 | tf_op jit(solution)/shard_map/all_to_all | solution.py:638
  51.2 17.5 %copy-start.5 = (f32[1024,128]{1,0:T(8,128)S(1)}, f32[1024,128]{1,0:T(8,128)}, u32[]{:S(2)}) copy-start(f32[1024,128]{1,0:T(8,128)} %refs_1_.5) | copy-start | bytes 1572868
  56.5 14.0 %all-to-all-start.2 = ((f32[8,32,128]{2,1,0:T(8,128)}), f32[8,32,128]{2,1,0:T(8,128)S(1)}, u32[]{:S(2)}, u32[]{:S(2)}) async-start(f32[8,32,128]{2,1,0:T(8,128)} %get-tuple-element.64), calls=%async_computation.2 | async-start | bytes 262144 | tf_op jit(solution)/shard_map/all_to_all | solution.py:671
  62.3 4.3 %collective-permute-start.9 = (f32[128,128]{1,0:T(8,128)S(1)}, f32[128,128]{1,0:T(8,128)S(1)}, u32[]{:S(2)}, u32[]{:S(2)}) collective-permute-start(f32[128,128]{1,0:T(8,128)S(1)} %copy-done.34), channel_id=1, source_target_pairs={{1,0},{0,1},{17,16},{16,17},{3,2},{2,3},{19,18},{18,19},{5,4},{4,5... | collective-permute-start | bytes 196616 | tf_op jit(solution)/shard_map/ppermute | solution.py:582
  63.8 5.4 %collective-permute-start.10 = (f32[128,128]{1,0:T(8,128)S(1)}, f32[128,128]{1,0:T(8,128)S(1)}, u32[]{:S(2)}, u32[]{:S(2)}) collective-permute-start(f32[128,128]{1,0:T(8,128)S(1)} %copy-done.32), channel_id=1, source_target_pairs={{16,0},{17,1},{0,16},{1,17},{18,2},{19,3},{2,18},{3,19},{20,4},{21... | collective-permute-start | bytes 196616 | tf_op jit(solution)/shard_map/ppermute | solution.py:582
  63.8 5.4 %collective-permute-start.11 = (f32[128,128]{1,0:T(8,128)S(1)}, f32[128,128]{1,0:T(8,128)S(1)}, u32[]{:S(2)}, u32[]{:S(2)}) collective-permute-start(f32[128,128]{1,0:T(8,128)S(1)} %copy-done.30), channel_id=1, source_target_pairs={{17,0},{16,1},{1,16},{0,17},{19,2},{18,3},{3,18},{2,19},{21,4},{20... | collective-permute-start | bytes 196616 | tf_op jit(solution)/shard_map/ppermute | solution.py:582
  64.5 4.7 %collective-permute-start.8 = (f32[32,128]{1,0:T(8,128)S(1)}, f32[32,128]{1,0:T(8,128)S(1)}, u32[]{:S(2)}, u32[]{:S(2)}) collective-permute-start(f32[32,128]{1,0:T(8,128)S(1)} %get-tuple-element.59.refs_0_), channel_id=1, source_target_pairs={{17,0},{16,1},{1,16},{0,17},{19,2},{18,3},{3,18},{2,19},{21,4},{20... | collective-permute-start | bytes 49160 | tf_op jit(solution)/shard_map/ppermute | solution.py:582
  65.6 3.6 %collective-permute-start.7 = (f32[32,128]{1,0:T(8,128)S(1)}, f32[32,128]{1,0:T(8,128)S(1)}, u32[]{:S(2)}, u32[]{:S(2)}) collective-permute-start(f32[32,128]{1,0:T(8,128)S(1)} %get-tuple-element.59.refs_0_), channel_id=1, source_target_pairs={{16,0},{17,1},{0,16},{1,17},{18,2},{19,3},{2,18},{3,19},{20,4},{21... | collective-permute-start | bytes 49160 | tf_op jit(solution)/shard_map/ppermute | solution.py:582
  66.6 3.8 %collective-permute-start.6 = (f32[32,128]{1,0:T(8,128)S(1)}, f32[32,128]{1,0:T(8,128)S(1)}, u32[]{:S(2)}, u32[]{:S(2)}) collective-permute-start(f32[32,128]{1,0:T(8,128)S(1)} %get-tuple-element.59.refs_0_), channel_id=1, source_target_pairs={{1,0},{0,1},{17,16},{16,17},{3,2},{2,3},{19,18},{18,19},{5,4},{4,5... | collective-permute-start | bytes 49160 | tf_op jit(solution)/shard_map/ppermute | solution.py:582
  74.8 23.3 %all-to-all-start.3 = ((f32[32,32,128]{2,1,0:T(8,128)}), f32[32,32,128]{2,1,0:T(8,128)S(1)}, u32[]{:S(2)}, u32[]{:S(2)}) async-start(f32[32,32,128]{2,1,0:T(8,128)} %bitcast.5), calls=%async_computation.3 | async-start | bytes 1048576 | tf_op jit(solution)/shard_map/all_to_all | solution.py:717
  81.5 6.4 %collective-permute-start.12 = (f32[4,8,256]{2,1,0:T(8,128)S(1)}, f32[4,8,256]{2,1,0:T(8,128)S(1)}, u32[]{:S(2)}, u32[]{:S(2)}) collective-permute-start(f32[4,8,256]{2,1,0:T(8,128)S(1)} %get-tuple-element.73), channel_id=1, source_target_pairs={{1,0},{0,1},{17,16},{16,17},{3,2},{2,3},{19,18},{18,19},{5,4},{4,5... | collective-permute-start | bytes 98312 | tf_op jit(solution)/shard_map/ppermute | solution.py:582
  83.1 4.7 %collective-permute-start.13 = (f32[4,8,256]{2,1,0:T(8,128)S(1)}, f32[4,8,256]{2,1,0:T(8,128)S(1)}, u32[]{:S(2)}, u32[]{:S(2)}) collective-permute-start(f32[4,8,256]{2,1,0:T(8,128)S(1)} %get-tuple-element.74), channel_id=1, source_target_pairs={{16,0},{17,1},{0,16},{1,17},{18,2},{19,3},{2,18},{3,19},{20,4},{21... | collective-permute-start | bytes 98312 | tf_op jit(solution)/shard_map/ppermute | solution.py:582
  83.1 4.7 %collective-permute-start.14 = (f32[4,8,256]{2,1,0:T(8,128)S(1)}, f32[4,8,256]{2,1,0:T(8,128)S(1)}, u32[]{:S(2)}, u32[]{:S(2)}) collective-permute-start(f32[4,8,256]{2,1,0:T(8,128)S(1)} %get-tuple-element.75), channel_id=1, source_target_pairs={{17,0},{16,1},{1,16},{0,17},{19,2},{18,3},{3,18},{2,19},{21,4},{20... | collective-permute-start | bytes 98312 | tf_op jit(solution)/shard_map/ppermute | solution.py:582
  99.8 13.8 %all-to-all-start.4 = ((f32[32,16,128]{2,1,0:T(8,128)}), f32[32,16,128]{2,1,0:T(8,128)S(1)}, u32[]{:S(2)}, u32[]{:S(2)}) async-start(f32[32,16,128]{2,1,0:T(8,128)} %get-tuple-element.77), calls=%async_computation.4 | async-start | bytes 524288 | tf_op jit(solution)/shard_map/all_to_all | solution.py:725
  102.4 6.4 %collective-permute-start.15 = (f32[128,128]{1,0:T(8,128)S(1)}, f32[128,128]{1,0:T(8,128)S(1)}, u32[]{:S(2)}, u32[]{:S(2)}) collective-permute-start(f32[128,128]{1,0:T(8,128)S(1)} %get-tuple-element.79), channel_id=1, source_target_pairs={{1,0},{0,1},{17,16},{16,17},{3,2},{2,3},{19,18},{18,19},{5,4},{4,5... | collective-permute-start | bytes 196616 | tf_op jit(solution)/shard_map/ppermute | solution.py:582
  104.1 4.7 %collective-permute-start.16 = (f32[128,128]{1,0:T(8,128)S(1)}, f32[128,128]{1,0:T(8,128)S(1)}, u32[]{:S(2)}, u32[]{:S(2)}) collective-permute-start(f32[128,128]{1,0:T(8,128)S(1)} %get-tuple-element.80), channel_id=1, source_target_pairs={{16,0},{17,1},{0,16},{1,17},{18,2},{19,3},{2,18},{3,19},{20,4},{21... | collective-permute-start | bytes 196616 | tf_op jit(solution)/shard_map/ppermute | solution.py:582
  104.1 5.3 %collective-permute-start.17 = (f32[128,128]{1,0:T(8,128)S(1)}, f32[128,128]{1,0:T(8,128)S(1)}, u32[]{:S(2)}, u32[]{:S(2)}) collective-permute-start(f32[128,128]{1,0:T(8,128)S(1)} %get-tuple-element.81), channel_id=1, source_target_pairs={{17,0},{16,1},{1,16},{0,17},{19,2},{18,3},{3,18},{2,19},{21,4},{20... | collective-permute-start | bytes 196616 | tf_op jit(solution)/shard_map/ppermute | solution.py:582
  (38 other events, 118.3 us)

commit v8 on v5

--- a/solution.py
+++ b/solution.py
@@ -209,27 +209,17 @@
         chunks[k][...] = slots[pl.ds(start, block), :]
 
 
-def bias_rows_kernel(n_cols, ready, *rest):
-    blocks, (out_ref, slots) = rest[:n_cols], rest[n_cols:]
-    ready()
-    spread(column_index(), blocks, slots)
-    count = slots.shape[1]
-    per = out_ref.shape[0] // count
-    for block in range(count):
-        tiles = [[] for _ in range(per)]
-        for tile in range(n_cols // per):
-            group = [slots[c, block] for c in range(tile * per, (tile + 1) * per)]
-            for k, piece in enumerate(swap_lane_groups(group)):
-                tiles[k].append(piece)
-        for k in range(per):
-            out_ref[block * per + k] = jnp.concatenate(tiles[k], axis=1)
+def bias_part_kernel(per_part, ready, *rest):
+    blocks, (out_ref,) = rest[:per_part], rest[per_part:]
+    ready()
+    spread(lax.rem(lax.axis_index("gi"), per_part), blocks, out_ref)
 
 
 def row_kernel(n_branch, n_gj, per_part, few, ready, msa_ref, *rest):
-    bias_refs, rest = rest[:per_part], rest[per_part:]
+    n_cols = n_branch * n_gj
+    bias_refs, rest = rest[:n_cols], rest[n_cols:]
     gains_far, qkvg_far, final_far, out_ref, slots, gains_ref, qkvg_ref, final_ref, sems = rest
-    mine = lax.axis_index("gi")
-    me, part = lax.rem(mine, per_part), lax.div(mine, per_part)
+    me, part = column_index(), lax.div(lax.axis_index("gi"), per_part)
     copies = start_copies(
         [(gains_far, gains_ref), (qkvg_far, qkvg_ref), (final_far, final_ref)]
         + [(ref, slots.at[me ^ k]) for k, ref in enumerate(bias_refs)],
@@ -237,8 +227,11 @@
     )
     ready()
     _, residues, width = msa_ref.shape
-    _, heads, _, length = slots.shape
-    n_gi = length // residues
+    blocks = slots.shape[2]
+    n_gi = lax.axis_size("gi")
+    length = n_gi * residues
+    per = lanes * n_cols // length
+    heads = blocks * per
     rows = msa_ref.shape[0] // n_gi
     inner = final_ref.shape[0]
     queries = per_part * residues
@@ -259,9 +252,17 @@
     query = multiply(normal, qkvg_ref[:, :inner])
     gate = multiply(normal, qkvg_ref[:, 3 * inner :])
     wait_all(copies[2:])
-    bias = jnp.concatenate(
-        [slots[g, h] for h in range(heads) for g in range(per_part)], axis=0
-    )
+    pieces = [[] for _ in range(heads)]
+    for block in range(blocks):
+        for g in range(per_part):
+            tiles = [[] for _ in range(per)]
+            for tile in range(n_cols // per):
+                group = [slots[c, g, block] for c in range(tile * per, (tile + 1) * per)]
+                for k, piece in enumerate(swap_lane_groups(group)):
+                    tiles[k].append(piece)
+            for k in range(per):
+                pieces[block * per + k].append(jnp.concatenate(tiles[k], axis=1))
+    bias = jnp.concatenate([piece for head in pieces for piece in head], axis=0)
     attended = []
     for r in range(rows):
         keys = key_value[r * length : (r + 1) * length, :inner]
@@ -336,7 +337,7 @@
     gather_msa(few, column_index(), rest[:n_cols], *rest[n_cols:])
 
 
-def gather_pair_kernel(few, n_cols, residues, ready, gain_ref, matrix_ref, *rest):
+def gather_pair_kernel(few, n_cols, residues, ready, gains_ref, matrix_ref, *rest):
     blocks, (first_ref, gate_ref, slots) = rest[:n_cols], rest[n_cols:]
     ready()
     spread_rows(column_index(), blocks, slots)
@@ -348,8 +349,9 @@
             first_ref[pl.ds(o * n_cols + c, count, stride=groups * n_cols), :] = slots[
                 pl.ds(c * block + o * count, count), :
             ]
-    normal = layer_normalise(first_ref[...], gain_ref[...])
-    gate_ref[...] = sigmoid(multiply(normal, matrix_ref[...]))
+    width = first_ref.shape[1]
+    normal = layer_normalise(first_ref[...], gains_ref[1:2, :])
+    gate_ref[...] = sigmoid(multiply(normal, matrix_ref[:, 4 * width :]))
 
 
 def triangle_kernel(few, n_branch, n_gj, ready, tri_ref, *rest):
@@ -470,7 +472,9 @@
             ]
     update = multiply(matrix_ref[...], jnp.concatenate(outputs, axis=1))
     first = pair_ref[...].T + update
-    projected = multiply(triangle_ref[...], layer_normalise(first, gain_ref[...], axis=0))
+    projected = multiply(
+        triangle_ref[pl.ds(0, 4 * width), :], layer_normalise(first, gain_ref[...], axis=0)
+    )
     tri = sigmoid(projected[2 * width : 4 * width]) * projected[: 2 * width]
     slot_count, _, each, _ = tri_ref.shape
     for g in range(groups):
@@ -483,8 +487,8 @@
 
 
 def final_kernel(
-    few, n_cols, residues, packed, ready, product_ref, first_ref, gate_ref, gain_ref, matrix_ref,
-    out_ref
+    few, residues, packed, ready, product_ref, first_ref, gate_ref, gains_ref, matrix_ref, out_ref,
+    channels_ref
 ):
     positions = out_ref.shape[0]
     ready()
@@ -496,12 +500,14 @@
             here = [
                 product_ref[pl.ds(i * tiles + t, tall, stride=residues), :] for i in range(few)
             ]
-            product.append(jnp.concatenate(swap_lane_groups(here), axis=0))
+            for q, piece in enumerate(swap_lane_groups(here)):
+                channels_ref[pl.ds(q, tall, stride=few), :] = piece
+            product.append(channels_ref[...])
         product = jnp.concatenate(product, axis=1)
     else:
         product = product_ref[...]
-    update = multiply(matrix_ref[...], layer_normalise(product, gain_ref[...], axis=0))
-    result = first_ref[...] + gate_ref[...] * update.T
+    normal = layer_normalise(product, 1.0, axis=0).T * gains_ref[2:3, :]
+    result = first_ref[...] + gate_ref[...] * multiply(normal, matrix_ref[...])
     count = positions // (residues * few)
     for i in range(residues):
         for f in range(few):
@@ -579,15 +585,13 @@
         ],
         sems=[4, parts],
     )
+    msa = lax.all_to_all(msa, "gi", 0, 0, tiled=True)
     (bias,) = call_near(
-        functools.partial(bias_rows_kernel, n_cols),
-        [(heads, residues, length)],
-        *trade([bias] * n_cols, columns),
-        scratch=[(n_cols,) + bias_block],
-    )
-    msa, bias = lax.optimization_barrier((msa, bias))
-    msa = lax.all_to_all(msa, "gi", 0, 0, tiled=True)
-    bias = trade([bias] * per_part, "gi")
+        functools.partial(bias_part_kernel, per_part),
+        [(per_part,) + bias_block],
+        *trade([bias] * per_part, "gi"),
+    )
+    bias = trade([bias] * n_cols, columns)
     (msa_first,) = call(
         functools.partial(row_kernel, n_branch, n_gj, per_part, few),
         [(n_half, each, width)],
@@ -596,9 +600,9 @@
         [layernorm_scales],
         [horizontal_qkvg_kernel],
         [horizontal_final_kernel],
-        scratch=[(per_part, heads, residues, length)]
+        scratch=[(n_cols, per_part) + bias_block]
         + [w.shape for w in (layernorm_scales, horizontal_qkvg_kernel, horizontal_final_kernel)],
-        sems=[3 + per_part],
+        sems=[3 + n_cols],
     )
     pair, msa_first = lax.optimization_barrier((pair_input_tensor, msa_first))
 
@@ -636,10 +640,14 @@
     alignment = [block.reshape(-1, width) for block in trade(alignment, columns)]
     share = max(pair_width // n_all, 1)
     slots = pair_width // share
-    triangle = triangle_input_matrix[:, : 4 * pair_width].T.reshape(4, slots, share, pair_width)
-    triangle = jnp.stack(
-        [jnp.stack([triangle[n], triangle[n + 2]], axis=1) for n in range(2)]
-    ).reshape(4 * pair_width, pair_width)
+    triangle = triangle_input_matrix.T.reshape(5, slots, share, pair_width)
+    sides = jnp.stack([triangle[0], triangle[2]], axis=1)
+    gates = jnp.stack([triangle[1], triangle[3]], axis=1)
+    triangle = jnp.concatenate(
+        [side.reshape(2 * pair_width, pair_width) for side in (sides, gates)]
+        + [triangle[4].reshape(pair_width, pair_width)],
+        axis=0,
+    )
     matrix = outer_output_matrix.reshape(outer_width, outer_width // per, per, pair_width)
     matrix = jnp.transpose(matrix, (3, 2, 1, 0)).reshape(pair_width, -1)
     tri, *first = call_near(
@@ -663,15 +671,14 @@
     first, gate = call_near(
         functools.partial(gather_pair_kernel, few, n_cols, residues),
         [(positions, pair_width)] * 2,
-        pair_norm_gains[1:2],
-        triangle_input_matrix[:, 4 * pair_width :],
+        pair_norm_gains,
+        triangle_input_matrix,
         *trade(first, columns),
         scratch=[(positions, pair_width)],
     )
     tile = (rows, residues, width)
     scratch = [(n_cols, rows * few, width)]
     packed = share * n_all == pair_width and share == few and few == per
-    gain, last = pair_norm_gains[2], triangle_output_matrix
     if packed:
         tri = lax.all_to_all(tri, everyone, 0, 0, tiled=True)
         product, alignment_output = call_near(
@@ -683,8 +690,6 @@
         )
         product = lax.all_to_all(product, everyone, 0, 0, tiled=True)
         product = product.reshape(n_all * residues, lanes)
-        gain = gain.reshape(n_all, share).T.reshape(-1)
-        last = jnp.swapaxes(last.reshape(n_all, share, pair_width), 0, 1).reshape(last.shape)
     else:
         (alignment_output,) = call_near(
             functools.partial(gather_msa_kernel, few, n_cols),
@@ -703,13 +708,14 @@
         ).reshape(groups, n_cols, few, residues, pair_width)
         product = jnp.transpose(product, (4, 3, 2, 0, 1)).reshape(pair_width, positions)
     (pair_output_tensor,) = call_near(
-        functools.partial(final_kernel, few, n_cols, residues, packed),
+        functools.partial(final_kernel, few, residues, packed),
         [(positions, pair_width)],
         product,
         first,
         gate,
-        gain[:, None],
-        last.T,
+        pair_norm_gains,
+        triangle_output_matrix,
+        scratch=[(pair_width, lanes)],
     )
     return (
         alignment_output,

time: 110 us -> 99.9 us (0.908)
  local copies, waits for them, and re-layouts: 16.3 us -> 4.94 us
  waiting for transfers between devices: 32.4 us -> 36.5 us
  starting transfers between devices: 39 us -> 37.1 us
    unnamed x65 -> x39, local copies, waits for them, and re-layouts: 10.9 us -> 2.97 us
    slice x4 -> x1, local copies, waits for them, and re-layouts: 4.35 us -> 0.64 us  [per_device(): sides = jnp.stack([triangle[0], triangle[2]], axis=1)]
    all_to_all x1, waiting for transfers between devices: 0.01 us -> 3.07 us  [per_device(): lax.all_to_all(msa_first, everyone, 0, 0, tiled=True, axis_index_groups=h...]
    all_to_all x1, starting transfers between devices: 5.83 us -> 3.92 us  [per_device(): tri = lax.all_to_all(tri, everyone, 0, 0, tiled=True)]
    all_to_all x1, starting transfers between devices: 5.85 us -> 7.42 us  [per_device(): msa = lax.all_to_all(msa, 'gi', 0, 0, tiled=True)]
  transfers between devices with their start and end apart: 23 -> 23, of which waited for: 14 -> 15; matrix products, arithmetic and copies ran while one was open for 6% -> 2% of each run, Pallas kernels for 5% -> 5%
where the time goes in v8:
time: 99.9 us; the launch traced here: 99.2 us
  starting transfers between devices  37.1 us (37%)
  waiting for transfers between devices  36.5 us (37%)
  Pallas kernels  19.7 us (20%)
  local copies, waits for them, and re-layouts  4.94 us (5%)
    ppermute x18, waiting for transfers between devices, trade(): lax.ppermute(blocks[k], axes, [(t ^ k, t) for t in range(n) if t ^ k < n])  18.3 us
    ppermute x18, starting transfers between devices, trade(): lax.ppermute(blocks[k], axes, [(t ^ k, t) for t in range(n) if t ^ k < n])  14.9 us
    pallas_call x8, Pallas kernels, call_near(): pl.pallas_call(lambda *refs: kernel(lambda: None, *refs), out_shape=[jax....  12.5 us
    all_to_all x1, waiting for transfers between devices, per_device(): tri = lax.all_to_all(tri, everyone, 0, 0, tiled=True)  10.2 us
    all_to_all x1, starting transfers between devices, per_device(): msa = lax.all_to_all(msa, 'gi', 0, 0, tiled=True)  7.42 us
    pallas_call x2, Pallas kernels, call(): pl.pallas_call(body, out_shape=[jax.ShapeDtypeStruct(bare(out), jnp.float...  7.22 us
    all_to_all x1, starting transfers between devices, per_device(): right = lax.all_to_all(right, 'gi', 0, 0, tiled=True)  4.76 us
    all_to_all x1, starting transfers between devices, per_device(): tri = lax.all_to_all(tri, everyone, 0, 0, tiled=True)  3.92 us
  transfers between devices with their start and end apart: 23, of which 15 were waited for; matrix products, arithmetic and copies ran while one was open for 2% of the time, Pallas kernels for 5%

profile of v8, /device:TPU:0, one launch (start us, length us, event | category | flops | bytes accessed | tf_op | source)
XLA Modules:
  0.0 99.2 jit_solution(12421054969336352794)
XLA Ops:
  0.6 2.4 %shard_map.158 = (f32[16,16,256]{2,1,0:T(8,128)}, f32[2,16,128]{2,1,0:T(8,128)}) custom-call(f32[8,16,256]{2,1,0:T(8,128)} %refs_0_.2, f32[16,32,128]{2,1,0:T(8,128)} %refs_1_.3, f32[3,128]{1,0:T(4,128)} %refs_3_.3, f32[8,128]{1,0:T(8,128)} %bitcast.45), custom_call_target="tpu_custom_call" | custom-call | tf_op jit(solution)/shard_map/pallas_call | solution.py:135
  3.1 7.4 %all-to-all-start = ((f32[16,16,256]{2,1,0:T(8,128)}), f32[16,16,256]{2,1,0:T(8,128)S(1)}, u32[]{:S(2)}, u32[]{:S(2)}) async-start(f32[16,16,256]{2,1,0:T(8,128)} %get-tuple-element.26), calls=%async_computation | async-start | bytes 524288 | tf_op jit(solution)/shard_map/all_to_all | solution.py:588
  10.5 2.9 %collective-permute-start.2 = (f32[2,16,128]{2,1,0:T(8,128)S(1)}, f32[2,16,128]{2,1,0:T(8,128)S(1)}, u32[]{:S(2)}, u32[]{:S(2)}) collective-permute-start(f32[2,16,128]{2,1,0:T(8,128)S(1)} %copy-done.10), channel_id=1, source_target_pairs={{6,0},{4,2},{2,4},{0,6},{14,8},{12,10},{10,12},{8,14},{7,1},{5,3},... | collective-permute-start | bytes 49160 | tf_op jit(solution)/shard_map/ppermute | solution.py:554
  14.2 1.9 %collective-permute-done.2.refs_3_ = f32[2,16,128]{2,1,0:T(8,128)S(1)} collective-permute-done((f32[2,16,128]{2,1,0:T(8,128)S(1)}, f32[2,16,128]{2,1,0:T(8,128)S(1)}, u32[]{:S(2)}, u32[]{:S(2)}) %collective-permute-start.2) | collective-permute-done | bytes 16416 | tf_op jit(solution)/shard_map/ppermute | solution.py:554
  17.9 1.6 %collective-permute-start.4 = (f32[4,2,16,128]{3,2,1,0:T(8,128)S(1)}, f32[4,2,16,128]{3,2,1,0:T(8,128)S(1)}, u32[]{:S(2)}, u32[]{:S(2)}) collective-permute-start(f32[4,2,16,128]{3,2,1,0:T(8,128)S(1)} %shard_map.159.refs_1_), channel_id=1, source_target_pairs={{16,0},{17,1},{0,16},{1,17},{18,2},{19,3},{2,18},{3,19},{20,4},{21... | collective-permute-start | bytes 196616 | tf_op jit(solution)/shard_map/ppermute | solution.py:554
  20.6 1.6 %collective-permute-done.5.refs_4_ = f32[4,2,16,128]{3,2,1,0:T(8,128)S(1)} collective-permute-done((f32[4,2,16,128]{3,2,1,0:T(8,128)S(1)}, f32[4,2,16,128]{3,2,1,0:T(8,128)S(1)}, u32[]{:S(2)}, u32[]{:S(2)}) %collective-permute-start.5) | collective-permute-done | bytes 65568 | tf_op jit(solution)/shard_map/ppermute | solution.py:554
  22.2 1.5 %collective-permute-done.3.refs_2_ = f32[4,2,16,128]{3,2,1,0:T(8,128)S(1)} collective-permute-done((f32[4,2,16,128]{3,2,1,0:T(8,128)S(1)}, f32[4,2,16,128]{3,2,1,0:T(8,128)S(1)}, u32[]{:S(2)}, u32[]{:S(2)}) %collective-permute-start.3) | collective-permute-done | bytes 65568 | tf_op jit(solution)/shard_map/ppermute | solution.py:554
  25.0 4.8 %shard_map.160 = f32[16,8,256]{2,1,0:T(8,128)} custom-call(f32[16,16,256]{2,1,0:T(8,128)} %copy-done.12, f32[4,2,16,128]{3,2,1,0:T(8,128)} %copy-done.5, f32[4,2,16,128]{3,2,1,0:T(8,128)} %copy-done.18, f32[4,2,16,128]{3,2,1,0:T(8,128)} %copy-done.17, f32[4,2,16,128]{3,2,1,0:T(8,128)} %copy-done.16, f32[4,256]{1,0:T(4,128)} %refs_1_.4, f32[256,1024]{1,0:T(8,128)} %refs_6_.1, ...), custom_call_target="tpu_custom_call" | custom-call | tf_op jit(solution)/shard_map/pallas_call | solution.py:135
  29.9 3.5 %all-to-all-start.1 = ((f32[16,8,256]{2,1,0:T(8,128)}), f32[16,8,256]{2,1,0:T(8,128)S(1)}, u32[]{:S(2)}, u32[]{:S(2)}) async-start(f32[16,8,256]{2,1,0:T(8,128)} %shard_map.160), calls=%async_computation.1 | async-start | bytes 262144 | tf_op jit(solution)/shard_map/all_to_all | solution.py:609
  34.6 1.9 %collective-permute-start.9 = (f32[128,128]{1,0:T(8,128)S(1)}, f32[128,128]{1,0:T(8,128)S(1)}, u32[]{:S(2)}, u32[]{:S(2)}) collective-permute-start(f32[128,128]{1,0:T(8,128)S(1)} %get-tuple-element.32), channel_id=1, source_target_pairs={{1,0},{0,1},{17,16},{16,17},{3,2},{2,3},{19,18},{18,19},{5,4},{4,5... | collective-permute-start | bytes 196616 | tf_op jit(solution)/shard_map/ppermute | solution.py:554
  36.4 3.1 %all-to-all-done.1 = f32[16,8,256]{2,1,0:T(8,128)S(1)} async-done(((f32[16,8,256]{2,1,0:T(8,128)}), f32[16,8,256]{2,1,0:T(8,128)S(1)}, u32[]{:S(2)}, u32[]{:S(2)}) %all-to-all-start.1) | async-done | bytes 131104 | tf_op jit(solution)/shard_map/all_to_all | solution.py:609
  40.8 4.7 %shard_map.161 = (f32[32,128]{1,0:T(8,128)S(1)}, f32[8,32,128]{2,1,0:T(8,128)}, f32[128,256]{1,0:T(8,128)S(1)}) custom-call(f32[128,256]{1,0:T(8,128)S(1)} %bitcast.28, f32[4,256]{1,0:T(4,128)S(1)} %copy-done.11, f32[256,1024]{1,0:T(8,128)S(1)} %copy-done.2, f32[256,256]{1,0:T(8,128)S(1)} %copy-done.6, f32[256,1024]{1,0:T(8,128)S(1)} %copy-done.3, ...), custom_call_target="tpu_custom_call" | custom-call | tf_op jit(solution)/shard_map/pallas_call | solution.py:147
  45.4 4.8 %all-to-all-start.2 = ((f32[8,32,128]{2,1,0:T(8,128)}), f32[8,32,128]{2,1,0:T(8,128)S(1)}, u32[]{:S(2)}, u32[]{:S(2)}) async-start(f32[8,32,128]{2,1,0:T(8,128)} %get-tuple-element.35), calls=%async_computation.2 | async-start | bytes 262144 | tf_op jit(solution)/shard_map/all_to_all | solution.py:638
  54.6 1.8 %collective-permute-done.6.refs_1_ = f32[32,128]{1,0:T(8,128)S(1)} collective-permute-done((f32[32,128]{1,0:T(8,128)S(1)}, f32[32,128]{1,0:T(8,128)S(1)}, u32[]{:S(2)}, u32[]{:S(2)}) %collective-permute-start.6) | collective-permute-done | bytes 16416 | tf_op jit(solution)/shard_map/ppermute | solution.py:554
  57.5 4.1 %shard_map.163 = (f32[32,4,8,128]{3,2,1,0:T(8,128)}, f32[128,128]{1,0:T(8,128)S(1)}, f32[128,128]{1,0:T(8,128)S(1)}, f32[128,128]{1,0:T(8,128)S(1)}, f32[128,128]{1,0:T(8,128)S(1)}) custom-call(f32[32,128]{1,0:T(8,128)S(1)} %get-tuple-element.29.refs_0_, f32[32,128]{1,0:T(8,128)S(1)} %collective-permute-done.6.refs_1_, ...), custom_call_target="tpu_custom_call" | custom-call | tf_op jit(solution)/shard_map/pallas_call | solution.py:147
  61.6 3.9 %all-to-all-start.3 = ((f32[32,4,8,128]{3,2,1,0:T(8,128)}), f32[32,4,8,128]{3,2,1,0:T(8,128)S(1)}, u32[]{:S(2)}, u32[]{:S(2)}) async-start(f32[32,4,8,128]{3,2,1,0:T(8,128)} %get-tuple-element.36), calls=%async_computation.3 | async-start | bytes 1048576 | tf_op jit(solution)/shard_map/all_to_all | solution.py:683
  65.6 1.8 %collective-permute-start.12 = (f32[4,8,256]{2,1,0:T(8,128)S(1)}, f32[4,8,256]{2,1,0:T(8,128)S(1)}, u32[]{:S(2)}, u32[]{:S(2)}) collective-permute-start(f32[4,8,256]{2,1,0:T(8,128)S(1)} %get-tuple-element.39), channel_id=1, source_target_pairs={{1,0},{0,1},{17,16},{16,17},{3,2},{2,3},{19,18},{18,19},{5,4},{4,5... | collective-permute-start | bytes 98312 | tf_op jit(solution)/shard_map/ppermute | solution.py:554
  67.8 4.4 %collective-permute-done.12 = f32[4,8,256]{2,1,0:T(8,128)S(1)} collective-permute-done((f32[4,8,256]{2,1,0:T(8,128)S(1)}, f32[4,8,256]{2,1,0:T(8,128)S(1)}, u32[]{:S(2)}, u32[]{:S(2)}) %collective-permute-start.12) | collective-permute-done | bytes 32800 | tf_op jit(solution)/shard_map/ppermute | solution.py:554
  72.1 10.2 %all-to-all-done.3 = f32[32,4,8,128]{3,2,1,0:T(8,128)S(1)} async-done(((f32[32,4,8,128]{3,2,1,0:T(8,128)}), f32[32,4,8,128]{3,2,1,0:T(8,128)S(1)}, u32[]{:S(2)}, u32[]{:S(2)}) %all-to-all-start.3) | async-done | bytes 524320 | tf_op jit(solution)/shard_map/all_to_all | solution.py:683
  82.4 1.7 %shard_map.165 = (f32[32,16,128]{2,1,0:T(8,128)}, f32[8,16,256]{2,1,0:T(8,128)}) custom-call(f32[1024,128]{1,0:T(8,128)S(1)} %bitcast.25, f32[32,256]{1,0:T(8,128)S(1)} %bitcast.31, f32[32,256]{1,0:T(8,128)S(1)} %bitcast.32, f32[32,256]{1,0:T(8,128)S(1)} %bitcast.33, f32[32,256]{1,0:T(8,128)S(1)} %bitcast.34), custom_call_target="tpu_custom_call" | custom-call | tf_op jit(solution)/shard_map/pallas_call | solution.py:147
  84.1 2.6 %all-to-all-start.4 = ((f32[32,16,128]{2,1,0:T(8,128)}), f32[32,16,128]{2,1,0:T(8,128)S(1)}, u32[]{:S(2)}, u32[]{:S(2)}) async-start(f32[32,16,128]{2,1,0:T(8,128)} %get-tuple-element.43), calls=%async_computation.4 | async-start | bytes 524288 | tf_op jit(solution)/shard_map/all_to_all | solution.py:691
  86.7 1.7 %collective-permute-start.15 = (f32[128,128]{1,0:T(8,128)S(1)}, f32[128,128]{1,0:T(8,128)S(1)}, u32[]{:S(2)}, u32[]{:S(2)}) collective-permute-start(f32[128,128]{1,0:T(8,128)S(1)} %get-tuple-element.45), channel_id=1, source_target_pairs={{1,0},{0,1},{17,16},{16,17},{3,2},{2,3},{19,18},{18,19},{5,4},{4,5... | collective-permute-start | bytes 196616 | tf_op jit(solution)/shard_map/ppermute | solution.py:554
  88.9 4.2 %collective-permute-done.15.refs_3_ = f32[128,128]{1,0:T(8,128)S(1)} collective-permute-done((f32[128,128]{1,0:T(8,128)S(1)}, f32[128,128]{1,0:T(8,128)S(1)}, u32[]{:S(2)}, u32[]{:S(2)}) %collective-permute-start.15) | collective-permute-done | bytes 65568 | tf_op jit(solution)/shard_map/ppermute | solution.py:554
  94.2 3.7 %all-to-all-done.4 = f32[32,16,128]{2,1,0:T(8,128)S(1)} async-done(((f32[32,16,128]{2,1,0:T(8,128)}), f32[32,16,128]{2,1,0:T(8,128)S(1)}, u32[]{:S(2)}, u32[]{:S(2)}) %all-to-all-start.4) | async-done | bytes 262176 | tf_op jit(solution)/shard_map/all_to_all | solution.py:691
  (81 shorter events, 16.2 us)
Async XLA Ops:
  3.1 20.6 %all-to-all-start = ((f32[16,16,256]{2,1,0:T(8,128)}), f32[16,16,256]{2,1,0:T(8,128)S(1)}, u32[]{:S(2)}, u32[]{:S(2)}) async-start(f32[16,16,256]{2,1,0:T(8,128)} %get-tuple-element.26), calls=%async_computation | async-start | bytes 524288 | tf_op jit(solution)/shard_map/all_to_all | solution.py:588
  10.5 5.6 %collective-permute-start.2 = (f32[2,16,128]{2,1,0:T(8,128)S(1)}, f32[2,16,128]{2,1,0:T(8,128)S(1)}, u32[]{:S(2)}, u32[]{:S(2)}) collective-permute-start(f32[2,16,128]{2,1,0:T(8,128)S(1)} %copy-done.10), channel_id=1, source_target_pairs={{6,0},{4,2},{2,4},{0,6},{14,8},{12,10},{10,12},{8,14},{7,1},{5,3},... | collective-permute-start | bytes 49160 | tf_op jit(solution)/shard_map/ppermute | solution.py:554
  13.4 3.9 %collective-permute-start.1 = (f32[2,16,128]{2,1,0:T(8,128)S(1)}, f32[2,16,128]{2,1,0:T(8,128)S(1)}, u32[]{:S(2)}, u32[]{:S(2)}) collective-permute-start(f32[2,16,128]{2,1,0:T(8,128)S(1)} %copy-done.10), channel_id=1, source_target_pairs={{4,0},{6,2},{0,4},{2,6},{12,8},{14,10},{8,12},{10,14},{5,1},{7,3},... | collective-permute-start | bytes 49160 | tf_op jit(solution)/shard_map/ppermute | solution.py:554
  14.0 3.8 %collective-permute-start = (f32[2,16,128]{2,1,0:T(8,128)S(1)}, f32[2,16,128]{2,1,0:T(8,128)S(1)}, u32[]{:S(2)}, u32[]{:S(2)}) collective-permute-start(f32[2,16,128]{2,1,0:T(8,128)S(1)} %copy-done.10), channel_id=1, source_target_pairs={{2,0},{0,2},{6,4},{4,6},{10,8},{8,10},{14,12},{12,14},{3,1},{1,3},... | collective-permute-start | bytes 49160 | tf_op jit(solution)/shard_map/ppermute | solution.py:554
  17.8 4.4 %collective-permute-start.5 = (f32[4,2,16,128]{3,2,1,0:T(8,128)S(1)}, f32[4,2,16,128]{3,2,1,0:T(8,128)S(1)}, u32[]{:S(2)}, u32[]{:S(2)}) collective-permute-start(f32[4,2,16,128]{3,2,1,0:T(8,128)S(1)} %shard_map.159.refs_1_), channel_id=1, source_target_pairs={{17,0},{16,1},{1,16},{0,17},{19,2},{18,3},{3,18},{2,19},{21,4},{20... | collective-permute-start | bytes 196616 | tf_op jit(solution)/shard_map/ppermute | solution.py:554
  17.9 4.3 %collective-permute-start.4 = (f32[4,2,16,128]{3,2,1,0:T(8,128)S(1)}, f32[4,2,16,128]{3,2,1,0:T(8,128)S(1)}, u32[]{:S(2)}, u32[]{:S(2)}) collective-permute-start(f32[4,2,16,128]{3,2,1,0:T(8,128)S(1)} %shard_map.159.refs_1_), channel_id=1, source_target_pairs={{16,0},{17,1},{0,16},{1,17},{18,2},{19,3},{2,18},{3,19},{20,4},{21... | collective-permute-start | bytes 196616 | tf_op jit(solution)/shard_map/ppermute | solution.py:554
  19.5 4.3 %collective-permute-start.3 = (f32[4,2,16,128]{3,2,1,0:T(8,128)S(1)}, f32[4,2,16,128]{3,2,1,0:T(8,128)S(1)}, u32[]{:S(2)}, u32[]{:S(2)}) collective-permute-start(f32[4,2,16,128]{3,2,1,0:T(8,128)S(1)} %shard_map.159.refs_1_), channel_id=1, source_target_pairs={{1,0},{0,1},{17,16},{16,17},{3,2},{2,3},{19,18},{18,19},{5,4},{4,5... | collective-permute-start | bytes 196616 | tf_op jit(solution)/shard_map/ppermute | solution.py:554
  20.6 18.9 %copy-start.3 = (f32[256,1024]{1,0:T(8,128)S(1)}, f32[256,1024]{1,0:T(8,128)}, u32[]{:S(2)}) copy-start(f32[256,1024]{1,0:T(8,128)} %refs_4_.2) | copy-start | bytes 3145732
  29.9 9.7 %all-to-all-start.1 = ((f32[16,8,256]{2,1,0:T(8,128)}), f32[16,8,256]{2,1,0:T(8,128)S(1)}, u32[]{:S(2)}, u32[]{:S(2)}) async-start(f32[16,8,256]{2,1,0:T(8,128)} %shard_map.160), calls=%async_computation.1 | async-start | bytes 262144 | tf_op jit(solution)/shard_map/all_to_all | solution.py:609
  34.6 18.1 %collective-permute-start.9 = (f32[128,128]{1,0:T(8,128)S(1)}, f32[128,128]{1,0:T(8,128)S(1)}, u32[]{:S(2)}, u32[]{:S(2)}) collective-permute-start(f32[128,128]{1,0:T(8,128)S(1)} %get-tuple-element.32), channel_id=1, source_target_pairs={{1,0},{0,1},{17,16},{16,17},{3,2},{2,3},{19,18},{18,19},{5,4},{4,5... | collective-permute-start | bytes 196616 | tf_op jit(solution)/shard_map/ppermute | solution.py:554
  45.4 12.1 %all-to-all-start.2 = ((f32[8,32,128]{2,1,0:T(8,128)}), f32[8,32,128]{2,1,0:T(8,128)S(1)}, u32[]{:S(2)}, u32[]{:S(2)}) async-start(f32[8,32,128]{2,1,0:T(8,128)} %get-tuple-element.35), calls=%async_computation.2 | async-start | bytes 262144 | tf_op jit(solution)/shard_map/all_to_all | solution.py:638
  50.3 3.5 %collective-permute-start.10 = (f32[128,128]{1,0:T(8,128)S(1)}, f32[128,128]{1,0:T(8,128)S(1)}, u32[]{:S(2)}, u32[]{:S(2)}) collective-permute-start(f32[128,128]{1,0:T(8,128)S(1)} %get-tuple-element.33), channel_id=1, source_target_pairs={{16,0},{17,1},{0,16},{1,17},{18,2},{19,3},{2,18},{3,19},{20,4},{21... | collective-permute-start | bytes 196616 | tf_op jit(solution)/shard_map/ppermute | solution.py:554
  50.4 3.9 %collective-permute-start.11 = (f32[128,128]{1,0:T(8,128)S(1)}, f32[128,128]{1,0:T(8,128)S(1)}, u32[]{:S(2)}, u32[]{:S(2)}) collective-permute-start(f32[128,128]{1,0:T(8,128)S(1)} %get-tuple-element.34), channel_id=1, source_target_pairs={{17,0},{16,1},{1,16},{0,17},{19,2},{18,3},{3,18},{2,19},{21,4},{20... | collective-permute-start | bytes 196616 | tf_op jit(solution)/shard_map/ppermute | solution.py:554
  51.0 3.6 %collective-permute-start.8 = (f32[32,128]{1,0:T(8,128)S(1)}, f32[32,128]{1,0:T(8,128)S(1)}, u32[]{:S(2)}, u32[]{:S(2)}) collective-permute-start(f32[32,128]{1,0:T(8,128)S(1)} %get-tuple-element.29.refs_0_), channel_id=1, source_target_pairs={{17,0},{16,1},{1,16},{0,17},{19,2},{18,3},{3,18},{2,19},{21,4},{20... | collective-permute-start | bytes 49160 | tf_op jit(solution)/shard_map/ppermute | solution.py:554
  52.2 2.4 %collective-permute-start.7 = (f32[32,128]{1,0:T(8,128)S(1)}, f32[32,128]{1,0:T(8,128)S(1)}, u32[]{:S(2)}, u32[]{:S(2)}) collective-permute-start(f32[32,128]{1,0:T(8,128)S(1)} %get-tuple-element.29.refs_0_), channel_id=1, source_target_pairs={{16,0},{17,1},{0,16},{1,17},{18,2},{19,3},{2,18},{3,19},{20,4},{21... | collective-permute-start | bytes 49160 | tf_op jit(solution)/shard_map/ppermute | solution.py:554
  52.6 3.7 %collective-permute-start.6 = (f32[32,128]{1,0:T(8,128)S(1)}, f32[32,128]{1,0:T(8,128)S(1)}, u32[]{:S(2)}, u32[]{:S(2)}) collective-permute-start(f32[32,128]{1,0:T(8,128)S(1)} %get-tuple-element.29.refs_0_), channel_id=1, source_target_pairs={{1,0},{0,1},{17,16},{16,17},{3,2},{2,3},{19,18},{18,19},{5,4},{4,5... | collective-permute-start | bytes 49160 | tf_op jit(solution)/shard_map/ppermute | solution.py:554
  61.6 20.8 %all-to-all-start.3 = ((f32[32,4,8,128]{3,2,1,0:T(8,128)}), f32[32,4,8,128]{3,2,1,0:T(8,128)S(1)}, u32[]{:S(2)}, u32[]{:S(2)}) async-start(f32[32,4,8,128]{3,2,1,0:T(8,128)} %get-tuple-element.36), calls=%async_computation.3 | async-start | bytes 1048576 | tf_op jit(solution)/shard_map/all_to_all | solution.py:683
  65.6 6.6 %collective-permute-start.12 = (f32[4,8,256]{2,1,0:T(8,128)S(1)}, f32[4,8,256]{2,1,0:T(8,128)S(1)}, u32[]{:S(2)}, u32[]{:S(2)}) collective-permute-start(f32[4,8,256]{2,1,0:T(8,128)S(1)} %get-tuple-element.39), channel_id=1, source_target_pairs={{1,0},{0,1},{17,16},{16,17},{3,2},{2,3},{19,18},{18,19},{5,4},{4,5... | collective-permute-start | bytes 98312 | tf_op jit(solution)/shard_map/ppermute | solution.py:554
  67.4 4.7 %collective-permute-start.13 = (f32[4,8,256]{2,1,0:T(8,128)S(1)}, f32[4,8,256]{2,1,0:T(8,128)S(1)}, u32[]{:S(2)}, u32[]{:S(2)}) collective-permute-start(f32[4,8,256]{2,1,0:T(8,128)S(1)} %get-tuple-element.40), channel_id=1, source_target_pairs={{16,0},{17,1},{0,16},{1,17},{18,2},{19,3},{2,18},{3,19},{20,4},{21... | collective-permute-start | bytes 98312 | tf_op jit(solution)/shard_map/ppermute | solution.py:554
  67.4 4.7 %collective-permute-start.14 = (f32[4,8,256]{2,1,0:T(8,128)S(1)}, f32[4,8,256]{2,1,0:T(8,128)S(1)}, u32[]{:S(2)}, u32[]{:S(2)}) collective-permute-start(f32[4,8,256]{2,1,0:T(8,128)S(1)} %get-tuple-element.41), channel_id=1, source_target_pairs={{17,0},{16,1},{1,16},{0,17},{19,2},{18,3},{3,18},{2,19},{21,4},{20... | collective-permute-start | bytes 98312 | tf_op jit(solution)/shard_map/ppermute | solution.py:554
  84.1 13.8 %all-to-all-start.4 = ((f32[32,16,128]{2,1,0:T(8,128)}), f32[32,16,128]{2,1,0:T(8,128)S(1)}, u32[]{:S(2)}, u32[]{:S(2)}) async-start(f32[32,16,128]{2,1,0:T(8,128)} %get-tuple-element.43), calls=%async_computation.4 | async-start | bytes 524288 | tf_op jit(solution)/shard_map/all_to_all | solution.py:691
  86.7 6.4 %collective-permute-start.15 = (f32[128,128]{1,0:T(8,128)S(1)}, f32[128,128]{1,0:T(8,128)S(1)}, u32[]{:S(2)}, u32[]{:S(2)}) collective-permute-start(f32[128,128]{1,0:T(8,128)S(1)} %get-tuple-element.45), channel_id=1, source_target_pairs={{1,0},{0,1},{17,16},{16,17},{3,2},{2,3},{19,18},{18,19},{5,4},{4,5... | collective-permute-start | bytes 196616 | tf_op jit(solution)/shard_map/ppermute | solution.py:554
  88.4 4.7 %collective-permute-start.16 = (f32[128,128]{1,0:T(8,128)S(1)}, f32[128,128]{1,0:T(8,128)S(1)}, u32[]{:S(2)}, u32[]{:S(2)}) collective-permute-start(f32[128,128]{1,0:T(8,128)S(1)} %get-tuple-element.46), channel_id=1, source_target_pairs={{16,0},{17,1},{0,16},{1,17},{18,2},{19,3},{2,18},{3,19},{20,4},{21... | collective-permute-start | bytes 196616 | tf_op jit(solution)/shard_map/ppermute | solution.py:554
  88.4 5.3 %collective-permute-start.17 = (f32[128,128]{1,0:T(8,128)S(1)}, f32[128,128]{1,0:T(8,128)S(1)}, u32[]{:S(2)}, u32[]{:S(2)}) collective-permute-start(f32[128,128]{1,0:T(8,128)S(1)} %get-tuple-element.47), channel_id=1, source_target_pairs={{17,0},{16,1},{1,16},{0,17},{19,2},{18,3},{3,18},{2,19},{21,4},{20... | collective-permute-start | bytes 196616 | tf_op jit(solution)/shard_map/ppermute | solution.py:554
  (18 other events, 78.7 us)

commit v9 on v8

--- a/solution.py
+++ b/solution.py
@@ -109,6 +109,25 @@
     return lax.axis_index("branch") * lax.axis_size("gj") + lax.axis_index("gj")
 
 
+def cost(kernel):
+    name = getattr(kernel, "func", kernel).__name__
+    work = {
+        "bias_kernel": 2.0,
+        "bias_part_kernel": 0.2,
+        "row_kernel": 4.5,
+        "pair_blocks_kernel": 3.0,
+        "column_kernel": 4.5,
+        "msa_blocks_kernel": 0.5,
+        "pair_kernel": 4.0,
+        "triangle_kernel": 2.0,
+        "gather_pair_kernel": 1.0,
+        "final_kernel": 1.3,
+    }.get(name, 1.0)
+    return pl.CostEstimate(
+        flops=int(work * 1.1e9), bytes_accessed=int(work * 3.6e6), transcendentals=0
+    )
+
+
 def call(kernel, outs, *operands, scratch=(), sems=()):
     def bare(item):
         return item[0] if isinstance(item, list) else item
@@ -140,6 +159,7 @@
         scratch_shapes=[pltpu.VMEM(shape, jnp.float32) for shape in shapes + list(scratch)]
         + [pltpu.SemaphoreType.DMA((n,)) for n in sems]
         + [pltpu.SemaphoreType.DMA((max(len(near_in), len(near_out), 1),))],
+        cost_estimate=cost(kernel),
     )(*[bare(operand) for operand in operands])
 
 
@@ -151,6 +171,7 @@
         out_specs=[vmem] * len(outs),
         scratch_shapes=[pltpu.VMEM(shape, jnp.float32) for shape in scratch],
         compiler_params=params,
+        cost_estimate=cost(kernel),
     )(*operands)
 
 
@@ -219,9 +240,13 @@
     n_cols = n_branch * n_gj
     bias_refs, rest = rest[:n_cols], rest[n_cols:]
     gains_far, qkvg_far, final_far, out_ref, slots, gains_ref, qkvg_ref, final_ref, sems = rest
-    me, part = column_index(), lax.div(lax.axis_index("gi"), per_part)
+    me, half = column_index(), lax.div(lax.axis_index("gi"), per_part)
+    inner = final_ref.shape[0]
+    parts = [pl.ds(n * inner, inner) for n in (1, 2, 0, 3)]
     copies = start_copies(
-        [(gains_far, gains_ref), (qkvg_far, qkvg_ref), (final_far, final_ref)]
+        [(gains_far, gains_ref)]
+        + [(qkvg_far.at[:, part], qkvg_ref.at[:, part]) for part in parts]
+        + [(final_far, final_ref)]
         + [(ref, slots.at[me ^ k]) for k, ref in enumerate(bias_refs)],
         sems,
     )
@@ -238,20 +263,21 @@
     tokens = jnp.concatenate(
         [msa_ref[g * rows + r] for r in range(rows) for g in range(n_gi)], axis=0
     )
-    first = part * (per_part * rows)
+    first = half * (per_part * rows)
     asking = msa_ref[pl.ds(first, per_part * rows)]
     asking = jnp.concatenate(
         [asking[g * rows + r] for r in range(rows) for g in range(per_part)], axis=0
     )
     tokens = layer_normalise(tokens, 1.0)
     normal = layer_normalise(asking, 1.0)
-    wait_all(copies[:2])
+    wait_all(copies[:3])
     gain = gains_ref[0:1, :]
     key_value = multiply(tokens * gain, qkvg_ref[:, inner : 3 * inner])
     normal = normal * gain
+    wait_all(copies[3:5])
     query = multiply(normal, qkvg_ref[:, :inner])
     gate = multiply(normal, qkvg_ref[:, 3 * inner :])
-    wait_all(copies[2:])
+    wait_all(copies[5:])
     pieces = [[] for _ in range(heads)]
     for block in range(blocks):
         for g in range(per_part):
@@ -602,7 +628,7 @@
         [horizontal_final_kernel],
         scratch=[(n_cols, per_part) + bias_block]
         + [w.shape for w in (layernorm_scales, horizontal_qkvg_kernel, horizontal_final_kernel)],
-        sems=[3 + n_cols],
+        sems=[6 + n_cols],
     )
     pair, msa_first = lax.optimization_barrier((pair_input_tensor, msa_first))
 

time: 99.9 us -> 98.4 us (0.985)
  waiting for transfers between devices: 36.5 us -> 35.3 us
    ppermute x18, waiting for transfers between devices: 18.3 us -> 14.9 us  [trade(): lax.ppermute(blocks[k], axes, [(t ^ k, t) for t in range(n) if t ^ k < n])]
    all_to_all x1, waiting for transfers between devices: 0.01 us -> 1.32 us  [per_device(): msa = lax.all_to_all(msa, 'gi', 0, 0, tiled=True)]
    all_to_all x1, starting transfers between devices: 7.42 us -> 6.15 us  [per_device(): msa = lax.all_to_all(msa, 'gi', 0, 0, tiled=True)]
    ppermute x18, starting transfers between devices: 14.9 us -> 15.9 us  [trade(): lax.ppermute(blocks[k], axes, [(t ^ k, t) for t in range(n) if t ^ k < n])]
    unnamed x39 -> x47, local copies, waits for them, and re-layouts: 2.97 us -> 2.83 us
  transfers between devices with their start and end apart: 23 -> 23, of which waited for: 15 -> 13; matrix products, arithmetic and copies ran while one was open for 2% -> 2% of each run, Pallas kernels for 5% -> 6%
where the time goes in v9:
time: 98.4 us; the launch traced here: 97.7 us
  starting transfers between devices  36.6 us (37%)
  waiting for transfers between devices  35.3 us (36%)
  Pallas kernels  19.9 us (20%)
  local copies, waits for them, and re-layouts  4.85 us (5%)
  between operations  1 us (1%)
    ppermute x18, starting transfers between devices, trade(): lax.ppermute(blocks[k], axes, [(t ^ k, t) for t in range(n) if t ^ k < n])  15.9 us
    ppermute x18, waiting for transfers between devices, trade(): lax.ppermute(blocks[k], axes, [(t ^ k, t) for t in range(n) if t ^ k < n])  14.9 us
    pallas_call x8, Pallas kernels, call_near(): pl.pallas_call(lambda *refs: kernel(lambda: None, *refs), out_shape=[jax....  12.5 us
    all_to_all x1, waiting for transfers between devices, per_device(): tri = lax.all_to_all(tri, everyone, 0, 0, tiled=True)  10.2 us
    pallas_call x2, Pallas kernels, call(): pl.pallas_call(body, out_shape=[jax.ShapeDtypeStruct(bare(out), jnp.float...  7.42 us
    all_to_all x1, starting transfers between devices, per_device(): msa = lax.all_to_all(msa, 'gi', 0, 0, tiled=True)  6.15 us
    all_to_all x1, starting transfers between devices, per_device(): right = lax.all_to_all(right, 'gi', 0, 0, tiled=True)  4.14 us
    all_to_all x1, waiting for transfers between devices, per_device(): lax.all_to_all(msa_first, everyone, 0, 0, tiled=True, axis_index_groups=h...  3.93 us
  transfers between devices with their start and end apart: 23, of which 13 were waited for; matrix products, arithmetic and copies ran while one was open for 2% of the time, Pallas kernels for 6%

profile of v9, /device:TPU:0, one launch (start us, length us, event | category | flops | bytes accessed | tf_op | source)
XLA Modules:
  0.0 97.7 jit_solution(1248766305229086047)
XLA Ops:
  0.6 2.4 %shard_map.158 = (f32[16,16,256]{2,1,0:T(8,128)}, f32[2,16,128]{2,1,0:T(8,128)}) custom-call(f32[8,16,256]{2,1,0:T(8,128)} %refs_0_.2, f32[16,32,128]{2,1,0:T(8,128)} %refs_1_.3, f32[3,128]{1,0:T(4,128)} %refs_3_.3, f32[8,128]{1,0:T(8,128)} %bitcast.44), custom_call_target="tpu_custom_call" | custom-call | flops 2200000000 | bytes 7200000 | tf_op jit(solution)/shard_map/pallas_call | solution.py:154
  3.1 4.0 %collective-permute-start.2 = (f32[2,16,128]{2,1,0:T(8,128)}, f32[2,16,128]{2,1,0:T(8,128)S(1)}, u32[]{:S(2)}, u32[]{:S(2)}) collective-permute-start(f32[2,16,128]{2,1,0:T(8,128)} %get-tuple-element.27.refs_0_), channel_id=1, source_target_pairs={{6,0},{4,2},{2,4},{0,6},{14,8},{12,10},{10,12},{8,14},{7,1},{5,3},... | collective-permute-start | bytes 49160 | tf_op jit(solution)/shard_map/ppermute | solution.py:580
  7.8 6.1 %all-to-all-start = ((f32[16,16,256]{2,1,0:T(8,128)}), f32[16,16,256]{2,1,0:T(8,128)S(1)}, u32[]{:S(2)}, u32[]{:S(2)}) async-start(f32[16,16,256]{2,1,0:T(8,128)} %get-tuple-element.26), calls=%async_computation | async-start | bytes 524288 | tf_op jit(solution)/shard_map/all_to_all | solution.py:614
  14.9 1.6 %collective-permute-start.4 = (f32[4,2,16,128]{3,2,1,0:T(8,128)S(1)}, f32[4,2,16,128]{3,2,1,0:T(8,128)S(1)}, u32[]{:S(2)}, u32[]{:S(2)}) collective-permute-start(f32[4,2,16,128]{3,2,1,0:T(8,128)S(1)} %shard_map.159.refs_1_), channel_id=1, source_target_pairs={{16,0},{17,1},{0,16},{1,17},{18,2},{19,3},{2,18},{3,19},{20,4},{21... | collective-permute-start | bytes 196616 | tf_op jit(solution)/shard_map/ppermute | solution.py:580
  17.8 1.5 %collective-permute-done.5.refs_4_ = f32[4,2,16,128]{3,2,1,0:T(8,128)S(1)} collective-permute-done((f32[4,2,16,128]{3,2,1,0:T(8,128)S(1)}, f32[4,2,16,128]{3,2,1,0:T(8,128)S(1)}, u32[]{:S(2)}, u32[]{:S(2)}) %collective-permute-start.5) | collective-permute-done | bytes 65568 | tf_op jit(solution)/shard_map/ppermute | solution.py:580
  19.3 1.5 %collective-permute-done.3.refs_2_ = f32[4,2,16,128]{3,2,1,0:T(8,128)S(1)} collective-permute-done((f32[4,2,16,128]{3,2,1,0:T(8,128)S(1)}, f32[4,2,16,128]{3,2,1,0:T(8,128)S(1)}, u32[]{:S(2)}, u32[]{:S(2)}) %collective-permute-start.3) | collective-permute-done | bytes 65568 | tf_op jit(solution)/shard_map/ppermute | solution.py:580
  22.8 5.0 %shard_map.160 = f32[16,8,256]{2,1,0:T(8,128)} custom-call(f32[16,16,256]{2,1,0:T(8,128)} %copy-done.17, f32[4,2,16,128]{3,2,1,0:T(8,128)} %copy-done.8, f32[4,2,16,128]{3,2,1,0:T(8,128)} %copy-done.22, f32[4,2,16,128]{3,2,1,0:T(8,128)} %copy-done.21, f32[4,2,16,128]{3,2,1,0:T(8,128)} %copy-done.20, f32[4,256]{1,0:T(4,128)} %refs_1_.4, f32[256,1024]{1,0:T(8,128)} %refs_6_.1, ...), custom_call_target="tpu_custom_call" | custom-call | flops 4950000128 | bytes 16200000 | tf_op jit(solution)/shard_map/pallas_call | solution.py:154
  27.9 3.9 %all-to-all-start.1 = ((f32[16,8,256]{2,1,0:T(8,128)}), f32[16,8,256]{2,1,0:T(8,128)S(1)}, u32[]{:S(2)}, u32[]{:S(2)}) async-start(f32[16,8,256]{2,1,0:T(8,128)} %shard_map.160), calls=%async_computation.1 | async-start | bytes 262144 | tf_op jit(solution)/shard_map/all_to_all | solution.py:635
  32.0 2.0 %collective-permute-start.9 = (f32[128,128]{1,0:T(8,128)S(1)}, f32[128,128]{1,0:T(8,128)S(1)}, u32[]{:S(2)}, u32[]{:S(2)}) collective-permute-start(f32[128,128]{1,0:T(8,128)S(1)} %get-tuple-element.32), channel_id=1, source_target_pairs={{1,0},{0,1},{17,16},{16,17},{3,2},{2,3},{19,18},{18,19},{5,4},{4,5... | collective-permute-start | bytes 196616 | tf_op jit(solution)/shard_map/ppermute | solution.py:580
  34.0 3.9 %all-to-all-done.1 = f32[16,8,256]{2,1,0:T(8,128)S(1)} async-done(((f32[16,8,256]{2,1,0:T(8,128)}), f32[16,8,256]{2,1,0:T(8,128)S(1)}, u32[]{:S(2)}, u32[]{:S(2)}) %all-to-all-start.1) | async-done | bytes 131104 | tf_op jit(solution)/shard_map/all_to_all | solution.py:635
  39.2 4.7 %shard_map.161 = (f32[32,128]{1,0:T(8,128)S(1)}, f32[8,32,128]{2,1,0:T(8,128)}, f32[128,256]{1,0:T(8,128)S(1)}) custom-call(f32[128,256]{1,0:T(8,128)S(1)} %bitcast.28, f32[4,256]{1,0:T(4,128)S(1)} %copy-done.10, f32[256,1024]{1,0:T(8,128)S(1)} %copy-done.1, f32[256,256]{1,0:T(8,128)S(1)} %copy-done.5, f32[256,1024]{1,0:T(8,128)S(1)} %copy-done.2, ...), custom_call_target="tpu_custom_call" | custom-call | flops 4950000128 | bytes 16200000 | tf_op jit(solution)/shard_map/pallas_call | solution.py:167
  44.6 4.1 %all-to-all-start.2 = ((f32[8,32,128]{2,1,0:T(8,128)}), f32[8,32,128]{2,1,0:T(8,128)S(1)}, u32[]{:S(2)}, u32[]{:S(2)}) async-start(f32[8,32,128]{2,1,0:T(8,128)} %get-tuple-element.35), calls=%async_computation.2 | async-start | bytes 262144 | tf_op jit(solution)/shard_map/all_to_all | solution.py:664
  49.3 1.4 %collective-permute-start.8 = (f32[32,128]{1,0:T(8,128)S(1)}, f32[32,128]{1,0:T(8,128)S(1)}, u32[]{:S(2)}, u32[]{:S(2)}) collective-permute-start(f32[32,128]{1,0:T(8,128)S(1)} %get-tuple-element.29.refs_0_), channel_id=1, source_target_pairs={{17,0},{16,1},{1,16},{0,17},{19,2},{18,3},{3,18},{2,19},{21,4},{20... | collective-permute-start | bytes 49160 | tf_op jit(solution)/shard_map/ppermute | solution.py:580
  53.1 1.8 %collective-permute-done.6.refs_1_ = f32[32,128]{1,0:T(8,128)S(1)} collective-permute-done((f32[32,128]{1,0:T(8,128)S(1)}, f32[32,128]{1,0:T(8,128)S(1)}, u32[]{:S(2)}, u32[]{:S(2)}) %collective-permute-start.6) | collective-permute-done | bytes 16416 | tf_op jit(solution)/shard_map/ppermute | solution.py:580
  56.0 4.1 %shard_map.163 = (f32[32,4,8,128]{3,2,1,0:T(8,128)}, f32[128,128]{1,0:T(8,128)S(1)}, f32[128,128]{1,0:T(8,128)S(1)}, f32[128,128]{1,0:T(8,128)S(1)}, f32[128,128]{1,0:T(8,128)S(1)}) custom-call(f32[32,128]{1,0:T(8,128)S(1)} %get-tuple-element.29.refs_0_, f32[32,128]{1,0:T(8,128)S(1)} %collective-permute-done.6.refs_1_, ...), custom_call_target="tpu_custom_call" | custom-call | flops 4400000000 | bytes 14400000 | tf_op jit(solution)/shard_map/pallas_call | solution.py:167
  60.1 3.9 %all-to-all-start.3 = ((f32[32,4,8,128]{3,2,1,0:T(8,128)}), f32[32,4,8,128]{3,2,1,0:T(8,128)S(1)}, u32[]{:S(2)}, u32[]{:S(2)}) async-start(f32[32,4,8,128]{3,2,1,0:T(8,128)} %get-tuple-element.36), calls=%async_computation.3 | async-start | bytes 1048576 | tf_op jit(solution)/shard_map/all_to_all | solution.py:709
  64.1 1.8 %collective-permute-start.12 = (f32[4,8,256]{2,1,0:T(8,128)S(1)}, f32[4,8,256]{2,1,0:T(8,128)S(1)}, u32[]{:S(2)}, u32[]{:S(2)}) collective-permute-start(f32[4,8,256]{2,1,0:T(8,128)S(1)} %get-tuple-element.39), channel_id=1, source_target_pairs={{1,0},{0,1},{17,16},{16,17},{3,2},{2,3},{19,18},{18,19},{5,4},{4,5... | collective-permute-start | bytes 98312 | tf_op jit(solution)/shard_map/ppermute | solution.py:580
  66.3 4.3 %collective-permute-done.12 = f32[4,8,256]{2,1,0:T(8,128)S(1)} collective-permute-done((f32[4,8,256]{2,1,0:T(8,128)S(1)}, f32[4,8,256]{2,1,0:T(8,128)S(1)}, u32[]{:S(2)}, u32[]{:S(2)}) %collective-permute-start.12) | collective-permute-done | bytes 32800 | tf_op jit(solution)/shard_map/ppermute | solution.py:580
  70.6 10.2 %all-to-all-done.3 = f32[32,4,8,128]{3,2,1,0:T(8,128)S(1)} async-done(((f32[32,4,8,128]{3,2,1,0:T(8,128)}), f32[32,4,8,128]{3,2,1,0:T(8,128)S(1)}, u32[]{:S(2)}, u32[]{:S(2)}) %all-to-all-start.3) | async-done | bytes 524320 | tf_op jit(solution)/shard_map/all_to_all | solution.py:709
  80.9 1.8 %shard_map.165 = (f32[32,16,128]{2,1,0:T(8,128)}, f32[8,16,256]{2,1,0:T(8,128)}) custom-call(f32[1024,128]{1,0:T(8,128)S(1)} %bitcast.25, f32[32,256]{1,0:T(8,128)S(1)} %bitcast.34, f32[32,256]{1,0:T(8,128)S(1)} %bitcast.31, f32[32,256]{1,0:T(8,128)S(1)} %bitcast.32, f32[32,256]{1,0:T(8,128)S(1)} %bitcast.33), custom_call_target="tpu_custom_call" | custom-call | flops 2200000000 | bytes 7200000 | tf_op jit(solution)/shard_map/pallas_call | solution.py:167
  82.6 2.6 %all-to-all-start.4 = ((f32[32,16,128]{2,1,0:T(8,128)}), f32[32,16,128]{2,1,0:T(8,128)S(1)}, u32[]{:S(2)}, u32[]{:S(2)}) async-start(f32[32,16,128]{2,1,0:T(8,128)} %get-tuple-element.43), calls=%async_computation.4 | async-start | bytes 524288 | tf_op jit(solution)/shard_map/all_to_all | solution.py:717
  85.2 1.7 %collective-permute-start.15 = (f32[128,128]{1,0:T(8,128)S(1)}, f32[128,128]{1,0:T(8,128)S(1)}, u32[]{:S(2)}, u32[]{:S(2)}) collective-permute-start(f32[128,128]{1,0:T(8,128)S(1)} %get-tuple-element.45), channel_id=1, source_target_pairs={{1,0},{0,1},{17,16},{16,17},{3,2},{2,3},{19,18},{18,19},{5,4},{4,5... | collective-permute-start | bytes 196616 | tf_op jit(solution)/shard_map/ppermute | solution.py:580
  87.4 4.2 %collective-permute-done.15.refs_3_ = f32[128,128]{1,0:T(8,128)S(1)} collective-permute-done((f32[128,128]{1,0:T(8,128)S(1)}, f32[128,128]{1,0:T(8,128)S(1)}, u32[]{:S(2)}, u32[]{:S(2)}) %collective-permute-start.15) | collective-permute-done | bytes 65568 | tf_op jit(solution)/shard_map/ppermute | solution.py:580
  92.7 3.7 %all-to-all-done.4 = f32[32,16,128]{2,1,0:T(8,128)S(1)} async-done(((f32[32,16,128]{2,1,0:T(8,128)}), f32[32,16,128]{2,1,0:T(8,128)S(1)}, u32[]{:S(2)}, u32[]{:S(2)}) %all-to-all-start.4) | async-done | bytes 262176 | tf_op jit(solution)/shard_map/all_to_all | solution.py:717
  (89 shorter events, 14.4 us)
Async XLA Ops:
  3.1 10.9 %copy-start = (f32[128,640]{1,0:T(8,128)S(1)}, f32[128,640]{1,0:T(8,128)}, u32[]{:S(2)}) copy-start(f32[128,640]{1,0:T(8,128)} %refs_1_.5) | copy-start | bytes 983044
  3.1 11.7 %collective-permute-start.2 = (f32[2,16,128]{2,1,0:T(8,128)}, f32[2,16,128]{2,1,0:T(8,128)S(1)}, u32[]{:S(2)}, u32[]{:S(2)}) collective-permute-start(f32[2,16,128]{2,1,0:T(8,128)} %get-tuple-element.27.refs_0_), channel_id=1, source_target_pairs={{6,0},{4,2},{2,4},{0,6},{14,8},{12,10},{10,12},{8,14},{7,1},{5,3},... | collective-permute-start | bytes 49160 | tf_op jit(solution)/shard_map/ppermute | solution.py:580
  7.1 7.7 %collective-permute-start.1 = (f32[2,16,128]{2,1,0:T(8,128)}, f32[2,16,128]{2,1,0:T(8,128)S(1)}, u32[]{:S(2)}, u32[]{:S(2)}) collective-permute-start(f32[2,16,128]{2,1,0:T(8,128)} %get-tuple-element.27.refs_0_), channel_id=1, source_target_pairs={{4,0},{6,2},{0,4},{2,6},{12,8},{14,10},{8,12},{10,14},{5,1},{7,3},... | collective-permute-start | bytes 49160 | tf_op jit(solution)/shard_map/ppermute | solution.py:580
  7.6 7.3 %collective-permute-start = (f32[2,16,128]{2,1,0:T(8,128)}, f32[2,16,128]{2,1,0:T(8,128)S(1)}, u32[]{:S(2)}, u32[]{:S(2)}) collective-permute-start(f32[2,16,128]{2,1,0:T(8,128)} %get-tuple-element.27.refs_0_), channel_id=1, source_target_pairs={{2,0},{0,2},{6,4},{4,6},{10,8},{8,10},{14,12},{12,14},{3,1},{1,3},... | collective-permute-start | bytes 49160 | tf_op jit(solution)/shard_map/ppermute | solution.py:580
  7.8 14.4 %all-to-all-start = ((f32[16,16,256]{2,1,0:T(8,128)}), f32[16,16,256]{2,1,0:T(8,128)S(1)}, u32[]{:S(2)}, u32[]{:S(2)}) async-start(f32[16,16,256]{2,1,0:T(8,128)} %get-tuple-element.26), calls=%async_computation | async-start | bytes 524288 | tf_op jit(solution)/shard_map/all_to_all | solution.py:614
  14.9 4.4 %collective-permute-start.5 = (f32[4,2,16,128]{3,2,1,0:T(8,128)S(1)}, f32[4,2,16,128]{3,2,1,0:T(8,128)S(1)}, u32[]{:S(2)}, u32[]{:S(2)}) collective-permute-start(f32[4,2,16,128]{3,2,1,0:T(8,128)S(1)} %shard_map.159.refs_1_), channel_id=1, source_target_pairs={{17,0},{16,1},{1,16},{0,17},{19,2},{18,3},{3,18},{2,19},{21,4},{20... | collective-permute-start | bytes 196616 | tf_op jit(solution)/shard_map/ppermute | solution.py:580
  14.9 4.3 %collective-permute-start.4 = (f32[4,2,16,128]{3,2,1,0:T(8,128)S(1)}, f32[4,2,16,128]{3,2,1,0:T(8,128)S(1)}, u32[]{:S(2)}, u32[]{:S(2)}) collective-permute-start(f32[4,2,16,128]{3,2,1,0:T(8,128)S(1)} %shard_map.159.refs_1_), channel_id=1, source_target_pairs={{16,0},{17,1},{0,16},{1,17},{18,2},{19,3},{2,18},{3,19},{20,4},{21... | collective-permute-start | bytes 196616 | tf_op jit(solution)/shard_map/ppermute | solution.py:580
  16.5 4.3 %collective-permute-start.3 = (f32[4,2,16,128]{3,2,1,0:T(8,128)S(1)}, f32[4,2,16,128]{3,2,1,0:T(8,128)S(1)}, u32[]{:S(2)}, u32[]{:S(2)}) collective-permute-start(f32[4,2,16,128]{3,2,1,0:T(8,128)S(1)} %shard_map.159.refs_1_), channel_id=1, source_target_pairs={{1,0},{0,1},{17,16},{16,17},{3,2},{2,3},{19,18},{18,19},{5,4},{4,5... | collective-permute-start | bytes 196616 | tf_op jit(solution)/shard_map/ppermute | solution.py:580
  27.9 10.1 %all-to-all-start.1 = ((f32[16,8,256]{2,1,0:T(8,128)}), f32[16,8,256]{2,1,0:T(8,128)S(1)}, u32[]{:S(2)}, u32[]{:S(2)}) async-start(f32[16,8,256]{2,1,0:T(8,128)} %shard_map.160), calls=%async_computation.1 | async-start | bytes 262144 | tf_op jit(solution)/shard_map/all_to_all | solution.py:635
  32.0 19.1 %collective-permute-start.9 = (f32[128,128]{1,0:T(8,128)S(1)}, f32[128,128]{1,0:T(8,128)S(1)}, u32[]{:S(2)}, u32[]{:S(2)}) collective-permute-start(f32[128,128]{1,0:T(8,128)S(1)} %get-tuple-element.32), channel_id=1, source_target_pairs={{1,0},{0,1},{17,16},{16,17},{3,2},{2,3},{19,18},{18,19},{5,4},{4,5... | collective-permute-start | bytes 196616 | tf_op jit(solution)/shard_map/ppermute | solution.py:580
  44.6 11.5 %all-to-all-start.2 = ((f32[8,32,128]{2,1,0:T(8,128)}), f32[8,32,128]{2,1,0:T(8,128)S(1)}, u32[]{:S(2)}, u32[]{:S(2)}) async-start(f32[8,32,128]{2,1,0:T(8,128)} %get-tuple-element.35), calls=%async_computation.2 | async-start | bytes 262144 | tf_op jit(solution)/shard_map/all_to_all | solution.py:664
  48.8 3.3 %collective-permute-start.10 = (f32[128,128]{1,0:T(8,128)S(1)}, f32[128,128]{1,0:T(8,128)S(1)}, u32[]{:S(2)}, u32[]{:S(2)}) collective-permute-start(f32[128,128]{1,0:T(8,128)S(1)} %get-tuple-element.33), channel_id=1, source_target_pairs={{16,0},{17,1},{0,16},{1,17},{18,2},{19,3},{2,18},{3,19},{20,4},{21... | collective-permute-start | bytes 196616 | tf_op jit(solution)/shard_map/ppermute | solution.py:580
  48.9 3.9 %collective-permute-start.11 = (f32[128,128]{1,0:T(8,128)S(1)}, f32[128,128]{1,0:T(8,128)S(1)}, u32[]{:S(2)}, u32[]{:S(2)}) collective-permute-start(f32[128,128]{1,0:T(8,128)S(1)} %get-tuple-element.34), channel_id=1, source_target_pairs={{17,0},{16,1},{1,16},{0,17},{19,2},{18,3},{3,18},{2,19},{21,4},{20... | collective-permute-start | bytes 196616 | tf_op jit(solution)/shard_map/ppermute | solution.py:580
  49.3 3.8 %collective-permute-start.8 = (f32[32,128]{1,0:T(8,128)S(1)}, f32[32,128]{1,0:T(8,128)S(1)}, u32[]{:S(2)}, u32[]{:S(2)}) collective-permute-start(f32[32,128]{1,0:T(8,128)S(1)} %get-tuple-element.29.refs_0_), channel_id=1, source_target_pairs={{17,0},{16,1},{1,16},{0,17},{19,2},{18,3},{3,18},{2,19},{21,4},{20... | collective-permute-start | bytes 49160 | tf_op jit(solution)/shard_map/ppermute | solution.py:580
  50.7 2.4 %collective-permute-start.7 = (f32[32,128]{1,0:T(8,128)S(1)}, f32[32,128]{1,0:T(8,128)S(1)}, u32[]{:S(2)}, u32[]{:S(2)}) collective-permute-start(f32[32,128]{1,0:T(8,128)S(1)} %get-tuple-element.29.refs_0_), channel_id=1, source_target_pairs={{16,0},{17,1},{0,16},{1,17},{18,2},{19,3},{2,18},{3,19},{20,4},{21... | collective-permute-start | bytes 49160 | tf_op jit(solution)/shard_map/ppermute | solution.py:580
  51.2 3.7 %collective-permute-start.6 = (f32[32,128]{1,0:T(8,128)S(1)}, f32[32,128]{1,0:T(8,128)S(1)}, u32[]{:S(2)}, u32[]{:S(2)}) collective-permute-start(f32[32,128]{1,0:T(8,128)S(1)} %get-tuple-element.29.refs_0_), channel_id=1, source_target_pairs={{1,0},{0,1},{17,16},{16,17},{3,2},{2,3},{19,18},{18,19},{5,4},{4,5... | collective-permute-start | bytes 49160 | tf_op jit(solution)/shard_map/ppermute | solution.py:580
  60.1 20.8 %all-to-all-start.3 = ((f32[32,4,8,128]{3,2,1,0:T(8,128)}), f32[32,4,8,128]{3,2,1,0:T(8,128)S(1)}, u32[]{:S(2)}, u32[]{:S(2)}) async-start(f32[32,4,8,128]{3,2,1,0:T(8,128)} %get-tuple-element.36), calls=%async_computation.3 | async-start | bytes 1048576 | tf_op jit(solution)/shard_map/all_to_all | solution.py:709
  64.1 6.6 %collective-permute-start.12 = (f32[4,8,256]{2,1,0:T(8,128)S(1)}, f32[4,8,256]{2,1,0:T(8,128)S(1)}, u32[]{:S(2)}, u32[]{:S(2)}) collective-permute-start(f32[4,8,256]{2,1,0:T(8,128)S(1)} %get-tuple-element.39), channel_id=1, source_target_pairs={{1,0},{0,1},{17,16},{16,17},{3,2},{2,3},{19,18},{18,19},{5,4},{4,5... | collective-permute-start | bytes 98312 | tf_op jit(solution)/shard_map/ppermute | solution.py:580
  65.9 4.7 %collective-permute-start.13 = (f32[4,8,256]{2,1,0:T(8,128)S(1)}, f32[4,8,256]{2,1,0:T(8,128)S(1)}, u32[]{:S(2)}, u32[]{:S(2)}) collective-permute-start(f32[4,8,256]{2,1,0:T(8,128)S(1)} %get-tuple-element.40), channel_id=1, source_target_pairs={{16,0},{17,1},{0,16},{1,17},{18,2},{19,3},{2,18},{3,19},{20,4},{21... | collective-permute-start | bytes 98312 | tf_op jit(solution)/shard_map/ppermute | solution.py:580
  65.9 4.7 %collective-permute-start.14 = (f32[4,8,256]{2,1,0:T(8,128)S(1)}, f32[4,8,256]{2,1,0:T(8,128)S(1)}, u32[]{:S(2)}, u32[]{:S(2)}) collective-permute-start(f32[4,8,256]{2,1,0:T(8,128)S(1)} %get-tuple-element.41), channel_id=1, source_target_pairs={{17,0},{16,1},{1,16},{0,17},{19,2},{18,3},{3,18},{2,19},{21,4},{20... | collective-permute-start | bytes 98312 | tf_op jit(solution)/shard_map/ppermute | solution.py:580
  82.6 13.8 %all-to-all-start.4 = ((f32[32,16,128]{2,1,0:T(8,128)}), f32[32,16,128]{2,1,0:T(8,128)S(1)}, u32[]{:S(2)}, u32[]{:S(2)}) async-start(f32[32,16,128]{2,1,0:T(8,128)} %get-tuple-element.43), calls=%async_computation.4 | async-start | bytes 524288 | tf_op jit(solution)/shard_map/all_to_all | solution.py:717
  85.2 6.4 %collective-permute-start.15 = (f32[128,128]{1,0:T(8,128)S(1)}, f32[128,128]{1,0:T(8,128)S(1)}, u32[]{:S(2)}, u32[]{:S(2)}) collective-permute-start(f32[128,128]{1,0:T(8,128)S(1)} %get-tuple-element.45), channel_id=1, source_target_pairs={{1,0},{0,1},{17,16},{16,17},{3,2},{2,3},{19,18},{18,19},{5,4},{4,5... | collective-permute-start | bytes 196616 | tf_op jit(solution)/shard_map/ppermute | solution.py:580
  86.9 4.7 %collective-permute-start.16 = (f32[128,128]{1,0:T(8,128)S(1)}, f32[128,128]{1,0:T(8,128)S(1)}, u32[]{:S(2)}, u32[]{:S(2)}) collective-permute-start(f32[128,128]{1,0:T(8,128)S(1)} %get-tuple-element.46), channel_id=1, source_target_pairs={{16,0},{17,1},{0,16},{1,17},{18,2},{19,3},{2,18},{3,19},{20,4},{21... | collective-permute-start | bytes 196616 | tf_op jit(solution)/shard_map/ppermute | solution.py:580
  86.9 5.3 %collective-permute-start.17 = (f32[128,128]{1,0:T(8,128)S(1)}, f32[128,128]{1,0:T(8,128)S(1)}, u32[]{:S(2)}, u32[]{:S(2)}) collective-permute-start(f32[128,128]{1,0:T(8,128)S(1)} %get-tuple-element.47), channel_id=1, source_target_pairs={{17,0},{16,1},{1,16},{0,17},{19,2},{18,3},{3,18},{2,19},{21,4},{20... | collective-permute-start | bytes 196616 | tf_op jit(solution)/shard_map/ppermute | solution.py:580
  (22 other events, 78.7 us)

commit v10 on v9

--- a/solution.py
+++ b/solution.py
@@ -15,7 +15,6 @@
 lanes = 128
 far = pl.BlockSpec(memory_space=pl.ANY)
 vmem = pl.BlockSpec(memory_space=pltpu.VMEM)
-params = pltpu.CompilerParams(vmem_limit_bytes=16 * 1024 * 1024)
 
 
 def layer_normalise(values, norm_gain, axis=-1):
@@ -128,7 +127,7 @@
     )
 
 
-def call(kernel, outs, *operands, scratch=(), sems=()):
+def call(kernel, outs, *operands, scratch=(), sems=(), grant=None):
     def bare(item):
         return item[0] if isinstance(item, list) else item
 
@@ -160,19 +159,21 @@
         + [pltpu.SemaphoreType.DMA((n,)) for n in sems]
         + [pltpu.SemaphoreType.DMA((max(len(near_in), len(near_out), 1),))],
         cost_estimate=cost(kernel),
+        compiler_params=pltpu.CompilerParams(vmem_limit_bytes=grant),
     )(*[bare(operand) for operand in operands])
 
 
-def call_near(kernel, outs, *operands, scratch=()):
+def call_near(kernel, outs, *operands, scratch=(), sems=(), grant=16 * 1024 * 1024):
     return pl.pallas_call(
         lambda *refs: kernel(lambda: None, *refs),
         out_shape=[jax.ShapeDtypeStruct(out, jnp.float32) for out in outs],
-        in_specs=[vmem] * len(operands),
+        in_specs=[far if isinstance(operand, list) else vmem for operand in operands],
         out_specs=[vmem] * len(outs),
-        scratch_shapes=[pltpu.VMEM(shape, jnp.float32) for shape in scratch],
-        compiler_params=params,
+        scratch_shapes=[pltpu.VMEM(shape, jnp.float32) for shape in scratch]
+        + [pltpu.SemaphoreType.DMA((n,)) for n in sems],
+        compiler_params=pltpu.CompilerParams(vmem_limit_bytes=grant),
         cost_estimate=cost(kernel),
-    )(*operands)
+    )(*[operand[0] if isinstance(operand, list) else operand for operand in operands])
 
 
 def spread(me, refs, slots):
@@ -309,9 +310,10 @@
 
 
 def column_kernel(
-    few, heads, ready, msa_ref, gains_ref, qkvg_ref, final_ref, expand_ref, shrink_ref, sides_ref,
-    left_ref, right_ref, out_ref
+    few, heads, ready, msa_ref, gains_ref, qkvg_ref, final_ref, expand_ref, shrink_far, sides_ref,
+    left_ref, right_ref, out_ref, shrink_ref, sems
 ):
+    copies = start_copies([(shrink_far, shrink_ref)], sems)
     ready()
     count, width = msa_ref.shape
     inner = final_ref.shape[0]
@@ -328,6 +330,7 @@
     attended = attend(query, key, value, None, heads, allowed)
     second = first + multiply(sigmoid(gate) * attended, final_ref[...])
     expanded = multiply(layer_normalise(second, gains_ref[2:3, :]), expand_ref[...])
+    wait_all(copies)
     third = second + multiply(jnp.maximum(expanded, 0.0), shrink_ref[...])
     out_ref[...] = third
     factors = multiply(sides_ref[...], layer_normalise(third, gains_ref[3:4, :]), across=True)
@@ -629,6 +632,7 @@
         scratch=[(n_cols, per_part) + bias_block]
         + [w.shape for w in (layernorm_scales, horizontal_qkvg_kernel, horizontal_final_kernel)],
         sems=[6 + n_cols],
+        grant=60 * 1024 * 1024,
     )
     pair, msa_first = lax.optimization_barrier((pair_input_tensor, msa_first))
 
@@ -639,7 +643,7 @@
         vertical_qkvg_kernel,
         vertical_final_kernel,
         feedforward_expand_kernel,
-        feedforward_shrink_kernel,
+        [feedforward_shrink_kernel],
         dyadic_sides_kernel.T,
     )
     left, right, alignment = call_near(
@@ -647,6 +651,9 @@
         [(outer_width, count), (n_gi, outer_width, count), (count, width)],
         msa_first.reshape(count, width),
         *weights,
+        scratch=[feedforward_shrink_kernel.shape],
+        sems=[1],
+        grant=60 * 1024 * 1024,
     )
     alignment = call_near(
         functools.partial(msa_blocks_kernel, n_branch, n_gj),

time: 98.4 us -> 98.9 us (level)
  local copies, waits for them, and re-layouts: 4.85 us -> 3.03 us
  Pallas kernels: 19.9 us -> 21.7 us
    pallas_call x8, Pallas kernels: 12.5 us -> 14.3 us  [call_near(): pl.pallas_call(lambda *refs: kernel(lambda: None, *refs), out_shape=[jax....]
    unnamed x47 -> x29, local copies, waits for them, and re-layouts: 2.83 us -> 2.34 us
  transfers between devices with their start and end apart: 23 -> 23, of which waited for: 13 -> 13; matrix products, arithmetic and copies ran while one was open for 2% -> 1% of each run, Pallas kernels for 6% -> 7%
where the time goes in v10:
time: 98.9 us; the launch traced here: 98.2 us
  starting transfers between devices  36.5 us (37%)
  waiting for transfers between devices  35.9 us (36%)
  Pallas kernels  21.7 us (22%)
  local copies, waits for them, and re-layouts  3.03 us (3%)
    ppermute x18, starting transfers between devices, trade(): lax.ppermute(blocks[k], axes, [(t ^ k, t) for t in range(n) if t ^ k < n])  16 us
    ppermute x18, waiting for transfers between devices, trade(): lax.ppermute(blocks[k], axes, [(t ^ k, t) for t in range(n) if t ^ k < n])  15.4 us
    pallas_call x8, Pallas kernels, call_near(): pl.pallas_call(lambda *refs: kernel(lambda: None, *refs), out_shape=[jax....  14.3 us
    all_to_all x1, waiting for transfers between devices, per_device(): tri = lax.all_to_all(tri, everyone, 0, 0, tiled=True)  10.2 us
    pallas_call x2, Pallas kernels, call(): pl.pallas_call(body, out_shape=[jax.ShapeDtypeStruct(bare(out), jnp.float...  7.42 us
    all_to_all x1, starting transfers between devices, per_device(): msa = lax.all_to_all(msa, 'gi', 0, 0, tiled=True)  6.15 us
    all_to_all x1, starting transfers between devices, per_device(): right = lax.all_to_all(right, 'gi', 0, 0, tiled=True)  4.06 us
    all_to_all x1, waiting for transfers between devices, per_device(): lax.all_to_all(msa_first, everyone, 0, 0, tiled=True, axis_index_groups=h...  3.99 us
  transfers between devices with their start and end apart: 23, of which 13 were waited for; matrix products, arithmetic and copies ran while one was open for 1% of the time, Pallas kernels for 7%

profile of v10, /device:TPU:0, one launch (start us, length us, event | category | flops | bytes accessed | tf_op | source)
XLA Modules:
  0.0 98.2 jit_solution(8613831963873038139)
XLA Ops:
  0.6 2.4 %shard_map.158 = (f32[16,16,256]{2,1,0:T(8,128)}, f32[2,16,128]{2,1,0:T(8,128)}) custom-call(f32[8,16,256]{2,1,0:T(8,128)} %refs_0_.2, f32[16,32,128]{2,1,0:T(8,128)} %refs_1_.3, f32[3,128]{1,0:T(4,128)} %refs_3_.3, f32[8,128]{1,0:T(8,128)} %bitcast.44), custom_call_target="tpu_custom_call" | custom-call | flops 2200000000 | bytes 7200000 | tf_op jit(solution)/shard_map/pallas_call | solution.py:153
  3.1 4.0 %collective-permute-start.2 = (f32[2,16,128]{2,1,0:T(8,128)}, f32[2,16,128]{2,1,0:T(8,128)S(1)}, u32[]{:S(2)}, u32[]{:S(2)}) collective-permute-start(f32[2,16,128]{2,1,0:T(8,128)} %get-tuple-element.27.refs_0_), channel_id=1, source_target_pairs={{6,0},{4,2},{2,4},{0,6},{14,8},{12,10},{10,12},{8,14},{7,1},{5,3},... | collective-permute-start | bytes 49160 | tf_op jit(solution)/shard_map/ppermute | solution.py:583
  7.8 6.1 %all-to-all-start = ((f32[16,16,256]{2,1,0:T(8,128)}), f32[16,16,256]{2,1,0:T(8,128)S(1)}, u32[]{:S(2)}, u32[]{:S(2)}) async-start(f32[16,16,256]{2,1,0:T(8,128)} %get-tuple-element.26), calls=%async_computation | async-start | bytes 524288 | tf_op jit(solution)/shard_map/all_to_all | solution.py:617
  14.9 1.6 %collective-permute-start.4 = (f32[4,2,16,128]{3,2,1,0:T(8,128)S(1)}, f32[4,2,16,128]{3,2,1,0:T(8,128)S(1)}, u32[]{:S(2)}, u32[]{:S(2)}) collective-permute-start(f32[4,2,16,128]{3,2,1,0:T(8,128)S(1)} %shard_map.159.refs_1_), channel_id=1, source_target_pairs={{16,0},{17,1},{0,16},{1,17},{18,2},{19,3},{2,18},{3,19},{20,4},{21... | collective-permute-start | bytes 196616 | tf_op jit(solution)/shard_map/ppermute | solution.py:583
  17.1 2.1 %collective-permute-done.5.refs_4_ = f32[4,2,16,128]{3,2,1,0:T(8,128)S(1)} collective-permute-done((f32[4,2,16,128]{3,2,1,0:T(8,128)S(1)}, f32[4,2,16,128]{3,2,1,0:T(8,128)S(1)}, u32[]{:S(2)}, u32[]{:S(2)}) %collective-permute-start.5) | collective-permute-done | bytes 65568 | tf_op jit(solution)/shard_map/ppermute | solution.py:583
  19.2 1.5 %collective-permute-done.3.refs_2_ = f32[4,2,16,128]{3,2,1,0:T(8,128)S(1)} collective-permute-done((f32[4,2,16,128]{3,2,1,0:T(8,128)S(1)}, f32[4,2,16,128]{3,2,1,0:T(8,128)S(1)}, u32[]{:S(2)}, u32[]{:S(2)}) %collective-permute-start.3) | collective-permute-done | bytes 65568 | tf_op jit(solution)/shard_map/ppermute | solution.py:583
  20.8 1.4 %all-to-all-done.refs_0_ = f32[16,16,256]{2,1,0:T(8,128)S(1)} async-done(((f32[16,16,256]{2,1,0:T(8,128)}), f32[16,16,256]{2,1,0:T(8,128)S(1)}, u32[]{:S(2)}, u32[]{:S(2)}) %all-to-all-start) | async-done | bytes 262176 | tf_op jit(solution)/shard_map/all_to_all | solution.py:617
  22.8 5.0 %shard_map.160 = f32[16,8,256]{2,1,0:T(8,128)} custom-call(f32[16,16,256]{2,1,0:T(8,128)} %copy-done.9, f32[4,2,16,128]{3,2,1,0:T(8,128)} %copy-done.3, f32[4,2,16,128]{3,2,1,0:T(8,128)} %copy-done.13, f32[4,2,16,128]{3,2,1,0:T(8,128)} %copy-done.12, f32[4,2,16,128]{3,2,1,0:T(8,128)} %copy-done.11, f32[4,256]{1,0:T(4,128)} %refs_1_.4, f32[256,1024]{1,0:T(8,128)} %refs_6_.1, ...), custom_call_target="tpu_custom_call" | custom-call | flops 4950000128 | bytes 16200000 | tf_op jit(solution)/shard_map/pallas_call | solution.py:153
  27.9 3.9 %all-to-all-start.1 = ((f32[16,8,256]{2,1,0:T(8,128)}), f32[16,8,256]{2,1,0:T(8,128)S(1)}, u32[]{:S(2)}, u32[]{:S(2)}) async-start(f32[16,8,256]{2,1,0:T(8,128)} %shard_map.160), calls=%async_computation.1 | async-start | bytes 262144 | tf_op jit(solution)/shard_map/all_to_all | solution.py:639
  32.0 2.0 %collective-permute-start.9 = (f32[128,128]{1,0:T(8,128)S(1)}, f32[128,128]{1,0:T(8,128)S(1)}, u32[]{:S(2)}, u32[]{:S(2)}) collective-permute-start(f32[128,128]{1,0:T(8,128)S(1)} %get-tuple-element.32), channel_id=1, source_target_pairs={{1,0},{0,1},{17,16},{16,17},{3,2},{2,3},{19,18},{18,19},{5,4},{4,5... | collective-permute-start | bytes 196616 | tf_op jit(solution)/shard_map/ppermute | solution.py:583
  33.9 4.0 %all-to-all-done.1 = f32[16,8,256]{2,1,0:T(8,128)S(1)} async-done(((f32[16,8,256]{2,1,0:T(8,128)}), f32[16,8,256]{2,1,0:T(8,128)S(1)}, u32[]{:S(2)}, u32[]{:S(2)}) %all-to-all-start.1) | async-done | bytes 131104 | tf_op jit(solution)/shard_map/all_to_all | solution.py:639
  38.6 6.5 %shard_map.161 = (f32[32,128]{1,0:T(8,128)}, f32[8,32,128]{2,1,0:T(8,128)}, f32[128,256]{1,0:T(8,128)}) custom-call(f32[128,256]{1,0:T(8,128)} %bitcast.42, f32[4,256]{1,0:T(4,128)} %refs_1_.4, f32[256,1024]{1,0:T(8,128)} %refs_2_.3, f32[256,256]{1,0:T(8,128)} %refs_3_.2, f32[256,1024]{1,0:T(8,128)} %refs_4_.2, f32[1024,256]{1,0:T(8,128)} %refs_5_.3, ...), custom_call_target="tpu_custom_call" | custom-call | flops 4950000128 | bytes 16200000 | tf_op jit(solution)/shard_map/pallas_call | solution.py:167
  45.1 4.1 %all-to-all-start.2 = ((f32[8,32,128]{2,1,0:T(8,128)}), f32[8,32,128]{2,1,0:T(8,128)S(1)}, u32[]{:S(2)}, u32[]{:S(2)}) async-start(f32[8,32,128]{2,1,0:T(8,128)} %get-tuple-element.35), calls=%async_computation.2 | async-start | bytes 262144 | tf_op jit(solution)/shard_map/all_to_all | solution.py:671
  53.6 1.8 %collective-permute-done.6.refs_1_ = f32[32,128]{1,0:T(8,128)S(1)} collective-permute-done((f32[32,128]{1,0:T(8,128)S(1)}, f32[32,128]{1,0:T(8,128)S(1)}, u32[]{:S(2)}, u32[]{:S(2)}) %collective-permute-start.6) | collective-permute-done | bytes 16416 | tf_op jit(solution)/shard_map/ppermute | solution.py:583
  56.5 4.1 %shard_map.163 = (f32[32,4,8,128]{3,2,1,0:T(8,128)}, f32[128,128]{1,0:T(8,128)S(1)}, f32[128,128]{1,0:T(8,128)S(1)}, f32[128,128]{1,0:T(8,128)S(1)}, f32[128,128]{1,0:T(8,128)S(1)}) custom-call(f32[32,128]{1,0:T(8,128)S(1)} %copy-done.4, f32[32,128]{1,0:T(8,128)S(1)} %collective-permute-done.6.refs_1_, f32[32,128]{1,0:T(8,128)S(1)} %collective-permute-done.7.refs_2_, ...), custom_call_target="tpu_custom_call" | custom-call | flops 4400000000 | bytes 14400000 | tf_op jit(solution)/shard_map/pallas_call | solution.py:167
  60.6 3.9 %all-to-all-start.3 = ((f32[32,4,8,128]{3,2,1,0:T(8,128)}), f32[32,4,8,128]{3,2,1,0:T(8,128)S(1)}, u32[]{:S(2)}, u32[]{:S(2)}) async-start(f32[32,4,8,128]{3,2,1,0:T(8,128)} %get-tuple-element.36), calls=%async_computation.3 | async-start | bytes 1048576 | tf_op jit(solution)/shard_map/all_to_all | solution.py:716
  64.5 1.8 %collective-permute-start.12 = (f32[4,8,256]{2,1,0:T(8,128)S(1)}, f32[4,8,256]{2,1,0:T(8,128)S(1)}, u32[]{:S(2)}, u32[]{:S(2)}) collective-permute-start(f32[4,8,256]{2,1,0:T(8,128)S(1)} %get-tuple-element.39), channel_id=1, source_target_pairs={{1,0},{0,1},{17,16},{16,17},{3,2},{2,3},{19,18},{18,19},{5,4},{4,5... | collective-permute-start | bytes 98312 | tf_op jit(solution)/shard_map/ppermute | solution.py:583
  66.7 4.3 %collective-permute-done.12 = f32[4,8,256]{2,1,0:T(8,128)S(1)} collective-permute-done((f32[4,8,256]{2,1,0:T(8,128)S(1)}, f32[4,8,256]{2,1,0:T(8,128)S(1)}, u32[]{:S(2)}, u32[]{:S(2)}) %collective-permute-start.12) | collective-permute-done | bytes 32800 | tf_op jit(solution)/shard_map/ppermute | solution.py:583
  71.1 10.2 %all-to-all-done.3 = f32[32,4,8,128]{3,2,1,0:T(8,128)S(1)} async-done(((f32[32,4,8,128]{3,2,1,0:T(8,128)}), f32[32,4,8,128]{3,2,1,0:T(8,128)S(1)}, u32[]{:S(2)}, u32[]{:S(2)}) %all-to-all-start.3) | async-done | bytes 524320 | tf_op jit(solution)/shard_map/all_to_all | solution.py:716
  81.3 1.7 %shard_map.165 = (f32[32,16,128]{2,1,0:T(8,128)}, f32[8,16,256]{2,1,0:T(8,128)}) custom-call(f32[1024,128]{1,0:T(8,128)S(1)} %bitcast.25, f32[32,256]{1,0:T(8,128)S(1)} %bitcast.32, f32[32,256]{1,0:T(8,128)S(1)} %bitcast.29, f32[32,256]{1,0:T(8,128)S(1)} %bitcast.30, f32[32,256]{1,0:T(8,128)S(1)} %bitcast.31), custom_call_target="tpu_custom_call" | custom-call | flops 2200000000 | bytes 7200000 | tf_op jit(solution)/shard_map/pallas_call | solution.py:167
  83.1 2.6 %all-to-all-start.4 = ((f32[32,16,128]{2,1,0:T(8,128)}), f32[32,16,128]{2,1,0:T(8,128)S(1)}, u32[]{:S(2)}, u32[]{:S(2)}) async-start(f32[32,16,128]{2,1,0:T(8,128)} %get-tuple-element.43), calls=%async_computation.4 | async-start | bytes 524288 | tf_op jit(solution)/shard_map/all_to_all | solution.py:724
  85.7 1.7 %collective-permute-start.15 = (f32[128,128]{1,0:T(8,128)S(1)}, f32[128,128]{1,0:T(8,128)S(1)}, u32[]{:S(2)}, u32[]{:S(2)}) collective-permute-start(f32[128,128]{1,0:T(8,128)S(1)} %get-tuple-element.45), channel_id=1, source_target_pairs={{1,0},{0,1},{17,16},{16,17},{3,2},{2,3},{19,18},{18,19},{5,4},{4,5... | collective-permute-start | bytes 196616 | tf_op jit(solution)/shard_map/ppermute | solution.py:583
  87.9 4.2 %collective-permute-done.15.refs_3_ = f32[128,128]{1,0:T(8,128)S(1)} collective-permute-done((f32[128,128]{1,0:T(8,128)S(1)}, f32[128,128]{1,0:T(8,128)S(1)}, u32[]{:S(2)}, u32[]{:S(2)}) %collective-permute-start.15) | collective-permute-done | bytes 65568 | tf_op jit(solution)/shard_map/ppermute | solution.py:583
  93.2 3.7 %all-to-all-done.4 = f32[32,16,128]{2,1,0:T(8,128)S(1)} async-done(((f32[32,16,128]{2,1,0:T(8,128)}), f32[32,16,128]{2,1,0:T(8,128)S(1)}, u32[]{:S(2)}, u32[]{:S(2)}) %all-to-all-start.4) | async-done | bytes 262176 | tf_op jit(solution)/shard_map/all_to_all | solution.py:724
  (71 shorter events, 12.5 us)
Async XLA Ops:
  3.1 10.9 %copy-start = (f32[128,640]{1,0:T(8,128)S(1)}, f32[128,640]{1,0:T(8,128)}, u32[]{:S(2)}) copy-start(f32[128,640]{1,0:T(8,128)} %refs_1_.5) | copy-start | bytes 983044
  3.1 11.7 %collective-permute-start.2 = (f32[2,16,128]{2,1,0:T(8,128)}, f32[2,16,128]{2,1,0:T(8,128)S(1)}, u32[]{:S(2)}, u32[]{:S(2)}) collective-permute-start(f32[2,16,128]{2,1,0:T(8,128)} %get-tuple-element.27.refs_0_), channel_id=1, source_target_pairs={{6,0},{4,2},{2,4},{0,6},{14,8},{12,10},{10,12},{8,14},{7,1},{5,3},... | collective-permute-start | bytes 49160 | tf_op jit(solution)/shard_map/ppermute | solution.py:583
  7.1 7.7 %collective-permute-start.1 = (f32[2,16,128]{2,1,0:T(8,128)}, f32[2,16,128]{2,1,0:T(8,128)S(1)}, u32[]{:S(2)}, u32[]{:S(2)}) collective-permute-start(f32[2,16,128]{2,1,0:T(8,128)} %get-tuple-element.27.refs_0_), channel_id=1, source_target_pairs={{4,0},{6,2},{0,4},{2,6},{12,8},{14,10},{8,12},{10,14},{5,1},{7,3},... | collective-permute-start | bytes 49160 | tf_op jit(solution)/shard_map/ppermute | solution.py:583
  7.6 7.2 %collective-permute-start = (f32[2,16,128]{2,1,0:T(8,128)}, f32[2,16,128]{2,1,0:T(8,128)S(1)}, u32[]{:S(2)}, u32[]{:S(2)}) collective-permute-start(f32[2,16,128]{2,1,0:T(8,128)} %get-tuple-element.27.refs_0_), channel_id=1, source_target_pairs={{2,0},{0,2},{6,4},{4,6},{10,8},{8,10},{14,12},{12,14},{3,1},{1,3},... | collective-permute-start | bytes 49160 | tf_op jit(solution)/shard_map/ppermute | solution.py:583
  7.8 14.4 %all-to-all-start = ((f32[16,16,256]{2,1,0:T(8,128)}), f32[16,16,256]{2,1,0:T(8,128)S(1)}, u32[]{:S(2)}, u32[]{:S(2)}) async-start(f32[16,16,256]{2,1,0:T(8,128)} %get-tuple-element.26), calls=%async_computation | async-start | bytes 524288 | tf_op jit(solution)/shard_map/all_to_all | solution.py:617
  14.8 4.4 %collective-permute-start.5 = (f32[4,2,16,128]{3,2,1,0:T(8,128)S(1)}, f32[4,2,16,128]{3,2,1,0:T(8,128)S(1)}, u32[]{:S(2)}, u32[]{:S(2)}) collective-permute-start(f32[4,2,16,128]{3,2,1,0:T(8,128)S(1)} %shard_map.159.refs_1_), channel_id=1, source_target_pairs={{17,0},{16,1},{1,16},{0,17},{19,2},{18,3},{3,18},{2,19},{21,4},{20... | collective-permute-start | bytes 196616 | tf_op jit(solution)/shard_map/ppermute | solution.py:583
  14.9 4.3 %collective-permute-start.4 = (f32[4,2,16,128]{3,2,1,0:T(8,128)S(1)}, f32[4,2,16,128]{3,2,1,0:T(8,128)S(1)}, u32[]{:S(2)}, u32[]{:S(2)}) collective-permute-start(f32[4,2,16,128]{3,2,1,0:T(8,128)S(1)} %shard_map.159.refs_1_), channel_id=1, source_target_pairs={{16,0},{17,1},{0,16},{1,17},{18,2},{19,3},{2,18},{3,19},{20,4},{21... | collective-permute-start | bytes 196616 | tf_op jit(solution)/shard_map/ppermute | solution.py:583
  16.5 4.3 %collective-permute-start.3 = (f32[4,2,16,128]{3,2,1,0:T(8,128)S(1)}, f32[4,2,16,128]{3,2,1,0:T(8,128)S(1)}, u32[]{:S(2)}, u32[]{:S(2)}) collective-permute-start(f32[4,2,16,128]{3,2,1,0:T(8,128)S(1)} %shard_map.159.refs_1_), channel_id=1, source_target_pairs={{1,0},{0,1},{17,16},{16,17},{3,2},{2,3},{19,18},{18,19},{5,4},{4,5... | collective-permute-start | bytes 196616 | tf_op jit(solution)/shard_map/ppermute | solution.py:583
  27.9 10.1 %all-to-all-start.1 = ((f32[16,8,256]{2,1,0:T(8,128)}), f32[16,8,256]{2,1,0:T(8,128)S(1)}, u32[]{:S(2)}, u32[]{:S(2)}) async-start(f32[16,8,256]{2,1,0:T(8,128)} %shard_map.160), calls=%async_computation.1 | async-start | bytes 262144 | tf_op jit(solution)/shard_map/all_to_all | solution.py:639
  32.0 19.6 %collective-permute-start.9 = (f32[128,128]{1,0:T(8,128)S(1)}, f32[128,128]{1,0:T(8,128)S(1)}, u32[]{:S(2)}, u32[]{:S(2)}) collective-permute-start(f32[128,128]{1,0:T(8,128)S(1)} %get-tuple-element.32), channel_id=1, source_target_pairs={{1,0},{0,1},{17,16},{16,17},{3,2},{2,3},{19,18},{18,19},{5,4},{4,5... | collective-permute-start | bytes 196616 | tf_op jit(solution)/shard_map/ppermute | solution.py:583
  45.1 11.4 %all-to-all-start.2 = ((f32[8,32,128]{2,1,0:T(8,128)}), f32[8,32,128]{2,1,0:T(8,128)S(1)}, u32[]{:S(2)}, u32[]{:S(2)}) async-start(f32[8,32,128]{2,1,0:T(8,128)} %get-tuple-element.35), calls=%async_computation.2 | async-start | bytes 262144 | tf_op jit(solution)/shard_map/all_to_all | solution.py:671
  49.3 3.5 %collective-permute-start.10 = (f32[128,128]{1,0:T(8,128)S(1)}, f32[128,128]{1,0:T(8,128)S(1)}, u32[]{:S(2)}, u32[]{:S(2)}) collective-permute-start(f32[128,128]{1,0:T(8,128)S(1)} %get-tuple-element.33), channel_id=1, source_target_pairs={{16,0},{17,1},{0,16},{1,17},{18,2},{19,3},{2,18},{3,19},{20,4},{21... | collective-permute-start | bytes 196616 | tf_op jit(solution)/shard_map/ppermute | solution.py:583
  49.3 3.9 %collective-permute-start.11 = (f32[128,128]{1,0:T(8,128)S(1)}, f32[128,128]{1,0:T(8,128)S(1)}, u32[]{:S(2)}, u32[]{:S(2)}) collective-permute-start(f32[128,128]{1,0:T(8,128)S(1)} %get-tuple-element.34), channel_id=1, source_target_pairs={{17,0},{16,1},{1,16},{0,17},{19,2},{18,3},{3,18},{2,19},{21,4},{20... | collective-permute-start | bytes 196616 | tf_op jit(solution)/shard_map/ppermute | solution.py:583
  49.9 3.7 %collective-permute-start.8 = (f32[32,128]{1,0:T(8,128)S(1)}, f32[32,128]{1,0:T(8,128)S(1)}, u32[]{:S(2)}, u32[]{:S(2)}) collective-permute-start(f32[32,128]{1,0:T(8,128)S(1)} %copy-done.4), channel_id=1, source_target_pairs={{17,0},{16,1},{1,16},{0,17},{19,2},{18,3},{3,18},{2,19},{21,4},{20... | collective-permute-start | bytes 49160 | tf_op jit(solution)/shard_map/ppermute | solution.py:583
  51.1 2.4 %collective-permute-start.7 = (f32[32,128]{1,0:T(8,128)S(1)}, f32[32,128]{1,0:T(8,128)S(1)}, u32[]{:S(2)}, u32[]{:S(2)}) collective-permute-start(f32[32,128]{1,0:T(8,128)S(1)} %copy-done.4), channel_id=1, source_target_pairs={{16,0},{17,1},{0,16},{1,17},{18,2},{19,3},{2,18},{3,19},{20,4},{21... | collective-permute-start | bytes 49160 | tf_op jit(solution)/shard_map/ppermute | solution.py:583
  51.6 3.7 %collective-permute-start.6 = (f32[32,128]{1,0:T(8,128)S(1)}, f32[32,128]{1,0:T(8,128)S(1)}, u32[]{:S(2)}, u32[]{:S(2)}) collective-permute-start(f32[32,128]{1,0:T(8,128)S(1)} %copy-done.4), channel_id=1, source_target_pairs={{1,0},{0,1},{17,16},{16,17},{3,2},{2,3},{19,18},{18,19},{5,4},{4,5... | collective-permute-start | bytes 49160 | tf_op jit(solution)/shard_map/ppermute | solution.py:583
  60.6 20.8 %all-to-all-start.3 = ((f32[32,4,8,128]{3,2,1,0:T(8,128)}), f32[32,4,8,128]{3,2,1,0:T(8,128)S(1)}, u32[]{:S(2)}, u32[]{:S(2)}) async-start(f32[32,4,8,128]{3,2,1,0:T(8,128)} %get-tuple-element.36), calls=%async_computation.3 | async-start | bytes 1048576 | tf_op jit(solution)/shard_map/all_to_all | solution.py:716
  64.5 6.6 %collective-permute-start.12 = (f32[4,8,256]{2,1,0:T(8,128)S(1)}, f32[4,8,256]{2,1,0:T(8,128)S(1)}, u32[]{:S(2)}, u32[]{:S(2)}) collective-permute-start(f32[4,8,256]{2,1,0:T(8,128)S(1)} %get-tuple-element.39), channel_id=1, source_target_pairs={{1,0},{0,1},{17,16},{16,17},{3,2},{2,3},{19,18},{18,19},{5,4},{4,5... | collective-permute-start | bytes 98312 | tf_op jit(solution)/shard_map/ppermute | solution.py:583
  66.4 4.7 %collective-permute-start.13 = (f32[4,8,256]{2,1,0:T(8,128)S(1)}, f32[4,8,256]{2,1,0:T(8,128)S(1)}, u32[]{:S(2)}, u32[]{:S(2)}) collective-permute-start(f32[4,8,256]{2,1,0:T(8,128)S(1)} %get-tuple-element.40), channel_id=1, source_target_pairs={{16,0},{17,1},{0,16},{1,17},{18,2},{19,3},{2,18},{3,19},{20,4},{21... | collective-permute-start | bytes 98312 | tf_op jit(solution)/shard_map/ppermute | solution.py:583
  66.4 4.7 %collective-permute-start.14 = (f32[4,8,256]{2,1,0:T(8,128)S(1)}, f32[4,8,256]{2,1,0:T(8,128)S(1)}, u32[]{:S(2)}, u32[]{:S(2)}) collective-permute-start(f32[4,8,256]{2,1,0:T(8,128)S(1)} %get-tuple-element.41), channel_id=1, source_target_pairs={{17,0},{16,1},{1,16},{0,17},{19,2},{18,3},{3,18},{2,19},{21,4},{20... | collective-permute-start | bytes 98312 | tf_op jit(solution)/shard_map/ppermute | solution.py:583
  83.1 13.8 %all-to-all-start.4 = ((f32[32,16,128]{2,1,0:T(8,128)}), f32[32,16,128]{2,1,0:T(8,128)S(1)}, u32[]{:S(2)}, u32[]{:S(2)}) async-start(f32[32,16,128]{2,1,0:T(8,128)} %get-tuple-element.43), calls=%async_computation.4 | async-start | bytes 524288 | tf_op jit(solution)/shard_map/all_to_all | solution.py:724
  85.7 6.4 %collective-permute-start.15 = (f32[128,128]{1,0:T(8,128)S(1)}, f32[128,128]{1,0:T(8,128)S(1)}, u32[]{:S(2)}, u32[]{:S(2)}) collective-permute-start(f32[128,128]{1,0:T(8,128)S(1)} %get-tuple-element.45), channel_id=1, source_target_pairs={{1,0},{0,1},{17,16},{16,17},{3,2},{2,3},{19,18},{18,19},{5,4},{4,5... | collective-permute-start | bytes 196616 | tf_op jit(solution)/shard_map/ppermute | solution.py:583
  87.4 4.7 %collective-permute-start.16 = (f32[128,128]{1,0:T(8,128)S(1)}, f32[128,128]{1,0:T(8,128)S(1)}, u32[]{:S(2)}, u32[]{:S(2)}) collective-permute-start(f32[128,128]{1,0:T(8,128)S(1)} %get-tuple-element.46), channel_id=1, source_target_pairs={{16,0},{17,1},{0,16},{1,17},{18,2},{19,3},{2,18},{3,19},{20,4},{21... | collective-permute-start | bytes 196616 | tf_op jit(solution)/shard_map/ppermute | solution.py:583
  87.4 5.3 %collective-permute-start.17 = (f32[128,128]{1,0:T(8,128)S(1)}, f32[128,128]{1,0:T(8,128)S(1)}, u32[]{:S(2)}, u32[]{:S(2)}) collective-permute-start(f32[128,128]{1,0:T(8,128)S(1)} %get-tuple-element.47), channel_id=1, source_target_pairs={{17,0},{16,1},{1,16},{0,17},{19,2},{18,3},{3,18},{2,19},{21,4},{20... | collective-permute-start | bytes 196616 | tf_op jit(solution)/shard_map/ppermute | solution.py:583
  (13 other events, 27.9 us)

commit v11 on v9

--- a/solution.py
+++ b/solution.py
@@ -113,9 +113,9 @@
     name = getattr(kernel, "func", kernel).__name__
     work = {
         "bias_kernel": 2.0,
-        "bias_part_kernel": 0.2,
+        "bias_part_kernel": 6.0,
         "row_kernel": 4.5,
-        "pair_blocks_kernel": 3.0,
+        "pair_blocks_kernel": 8.0,
         "column_kernel": 4.5,
         "msa_blocks_kernel": 0.5,
         "pair_kernel": 4.0,
@@ -238,18 +238,8 @@
 
 def row_kernel(n_branch, n_gj, per_part, few, ready, msa_ref, *rest):
     n_cols = n_branch * n_gj
-    bias_refs, rest = rest[:n_cols], rest[n_cols:]
-    gains_far, qkvg_far, final_far, out_ref, slots, gains_ref, qkvg_ref, final_ref, sems = rest
-    me, half = column_index(), lax.div(lax.axis_index("gi"), per_part)
-    inner = final_ref.shape[0]
-    parts = [pl.ds(n * inner, inner) for n in (1, 2, 0, 3)]
-    copies = start_copies(
-        [(gains_far, gains_ref)]
-        + [(qkvg_far.at[:, part], qkvg_ref.at[:, part]) for part in parts]
-        + [(final_far, final_ref)]
-        + [(ref, slots.at[me ^ k]) for k, ref in enumerate(bias_refs)],
-        sems,
-    )
+    bias_refs, (gains_ref, qkvg_ref, final_ref, out_ref, slots) = rest[:n_cols], rest[n_cols:]
+    half = lax.div(lax.axis_index("gi"), per_part)
     ready()
     _, residues, width = msa_ref.shape
     blocks = slots.shape[2]
@@ -270,14 +260,12 @@
     )
     tokens = layer_normalise(tokens, 1.0)
     normal = layer_normalise(asking, 1.0)
-    wait_all(copies[:3])
     gain = gains_ref[0:1, :]
     key_value = multiply(tokens * gain, qkvg_ref[:, inner : 3 * inner])
     normal = normal * gain
-    wait_all(copies[3:5])
     query = multiply(normal, qkvg_ref[:, :inner])
     gate = multiply(normal, qkvg_ref[:, 3 * inner :])
-    wait_all(copies[5:])
+    spread(column_index(), bias_refs, slots)
     pieces = [[] for _ in range(heads)]
     for block in range(blocks):
         for g in range(per_part):
@@ -618,17 +606,15 @@
         *trade([bias] * per_part, "gi"),
     )
     bias = trade([bias] * n_cols, columns)
-    (msa_first,) = call(
+    (msa_first,) = call_near(
         functools.partial(row_kernel, n_branch, n_gj, per_part, few),
         [(n_half, each, width)],
         msa,
-        *[[block] for block in bias],
-        [layernorm_scales],
-        [horizontal_qkvg_kernel],
-        [horizontal_final_kernel],
-        scratch=[(n_cols, per_part) + bias_block]
-        + [w.shape for w in (layernorm_scales, horizontal_qkvg_kernel, horizontal_final_kernel)],
-        sems=[6 + n_cols],
+        *bias,
+        layernorm_scales,
+        horizontal_qkvg_kernel,
+        horizontal_final_kernel,
+        scratch=[(n_cols, per_part) + bias_block],
     )
     pair, msa_first = lax.optimization_barrier((pair_input_tensor, msa_first))
 

time: 98.4 us -> 95 us (0.965)
  Pallas kernels: 19.9 us -> 17.9 us
    pallas_call x2 -> x1, Pallas kernels: 7.42 us -> 2.41 us  [call(): pl.pallas_call(body, out_shape=[jax.ShapeDtypeStruct(bare(out), jnp.float...]
    pallas_call x8 -> x9, Pallas kernels: 12.5 us -> 15.5 us  [call_near(): pl.pallas_call(lambda *refs: kernel(lambda: None, *refs), out_shape=[jax....]
    unnamed x47 -> x41, local copies, waits for them, and re-layouts: 2.83 us -> 2.12 us
where the time goes in v11:
time: 95 us; the launch traced here: 94.4 us
  starting transfers between devices  36.1 us (38%)
  waiting for transfers between devices  35.2 us (37%)
  Pallas kernels  17.9 us (19%)
  local copies, waits for them, and re-layouts  4.14 us (4%)
    ppermute x18, starting transfers between devices, trade(): lax.ppermute(blocks[k], axes, [(t ^ k, t) for t in range(n) if t ^ k < n])  16 us
    pallas_call x9, Pallas kernels, call_near(): pl.pallas_call(lambda *refs: kernel(lambda: None, *refs), out_shape=[jax....  15.5 us
    ppermute x18, waiting for transfers between devices, trade(): lax.ppermute(blocks[k], axes, [(t ^ k, t) for t in range(n) if t ^ k < n])  14.8 us
    all_to_all x1, waiting for transfers between devices, per_device(): tri = lax.all_to_all(tri, everyone, 0, 0, tiled=True)  10.2 us
    all_to_all x1, starting transfers between devices, per_device(): msa = lax.all_to_all(msa, 'gi', 0, 0, tiled=True)  6.15 us
    all_to_all x1, waiting for transfers between devices, per_device(): lax.all_to_all(msa_first, everyone, 0, 0, tiled=True, axis_index_groups=h...  3.94 us
    all_to_all x1, starting transfers between devices, per_device(): tri = lax.all_to_all(tri, everyone, 0, 0, tiled=True)  3.92 us
    all_to_all x1, starting transfers between devices, per_device(): lax.all_to_all(msa_first, everyone, 0, 0, tiled=True, axis_index_groups=h...  3.86 us
  transfers between devices with their start and end apart: 23, of which 13 were waited for; matrix products, arithmetic and copies ran while one was open for 2% of the time, Pallas kernels for 6%

profile of v11, /device:TPU:0, one launch (start us, length us, event | category | flops | bytes accessed | tf_op | source)
XLA Modules:
  0.0 94.4 jit_solution(14412770179428107817)
XLA Ops:
  0.6 2.4 %shard_map.158 = (f32[16,16,256]{2,1,0:T(8,128)}, f32[2,16,128]{2,1,0:T(8,128)}) custom-call(f32[8,16,256]{2,1,0:T(8,128)} %refs_0_.2, f32[16,32,128]{2,1,0:T(8,128)} %refs_1_.3, f32[3,128]{1,0:T(4,128)} %refs_3_.3, f32[8,128]{1,0:T(8,128)} %bitcast.44), custom_call_target="tpu_custom_call" | custom-call | flops 2200000000 | bytes 7200000 | tf_op jit(solution)/shard_map/pallas_call | solution.py:154
  3.1 4.0 %collective-permute-start.2 = (f32[2,16,128]{2,1,0:T(8,128)}, f32[2,16,128]{2,1,0:T(8,128)S(1)}, u32[]{:S(2)}, u32[]{:S(2)}) collective-permute-start(f32[2,16,128]{2,1,0:T(8,128)} %get-tuple-element.27.refs_0_), channel_id=1, source_target_pairs={{6,0},{4,2},{2,4},{0,6},{14,8},{12,10},{10,12},{8,14},{7,1},{5,3},... | collective-permute-start | bytes 49160 | tf_op jit(solution)/shard_map/ppermute | solution.py:568
  7.8 6.1 %all-to-all-start = ((f32[16,16,256]{2,1,0:T(8,128)}), f32[16,16,256]{2,1,0:T(8,128)S(1)}, u32[]{:S(2)}, u32[]{:S(2)}) async-start(f32[16,16,256]{2,1,0:T(8,128)} %get-tuple-element.26), calls=%async_computation | async-start | bytes 524288 | tf_op jit(solution)/shard_map/all_to_all | solution.py:602
  14.9 1.6 %collective-permute-start.4 = (f32[4,2,16,128]{3,2,1,0:T(8,128)S(1)}, f32[4,2,16,128]{3,2,1,0:T(8,128)S(1)}, u32[]{:S(2)}, u32[]{:S(2)}) collective-permute-start(f32[4,2,16,128]{3,2,1,0:T(8,128)S(1)} %shard_map.159.refs_1_), channel_id=1, source_target_pairs={{16,0},{17,1},{0,16},{1,17},{18,2},{19,3},{2,18},{3,19},{20,4},{21... | collective-permute-start | bytes 196616 | tf_op jit(solution)/shard_map/ppermute | solution.py:568
  17.8 1.5 %collective-permute-done.5.refs_4_ = f32[4,2,16,128]{3,2,1,0:T(8,128)S(1)} collective-permute-done((f32[4,2,16,128]{3,2,1,0:T(8,128)S(1)}, f32[4,2,16,128]{3,2,1,0:T(8,128)S(1)}, u32[]{:S(2)}, u32[]{:S(2)}) %collective-permute-start.5) | collective-permute-done | bytes 65568 | tf_op jit(solution)/shard_map/ppermute | solution.py:568
  19.3 1.5 %collective-permute-done.3.refs_2_ = f32[4,2,16,128]{3,2,1,0:T(8,128)S(1)} collective-permute-done((f32[4,2,16,128]{3,2,1,0:T(8,128)S(1)}, f32[4,2,16,128]{3,2,1,0:T(8,128)S(1)}, u32[]{:S(2)}, u32[]{:S(2)}) %collective-permute-start.3) | collective-permute-done | bytes 65568 | tf_op jit(solution)/shard_map/ppermute | solution.py:568
  20.8 1.3 %all-to-all-done.refs_0_ = f32[16,16,256]{2,1,0:T(8,128)S(1)} async-done(((f32[16,16,256]{2,1,0:T(8,128)}), f32[16,16,256]{2,1,0:T(8,128)S(1)}, u32[]{:S(2)}, u32[]{:S(2)}) %all-to-all-start) | async-done | bytes 262176 | tf_op jit(solution)/shard_map/all_to_all | solution.py:602
  22.1 3.1 %shard_map.160 = f32[16,8,256]{2,1,0:T(8,128)} custom-call(f32[16,16,256]{2,1,0:T(8,128)S(1)} %all-to-all-done.refs_0_, f32[4,2,16,128]{3,2,1,0:T(8,128)S(1)} %shard_map.159.refs_1_, f32[4,2,16,128]{3,2,1,0:T(8,128)S(1)} %collective-permute-done.3.refs_2_, f32[4,2,16,128]{3,2,1,0:T(8,128)S(1)} %collective-permute-done.4.refs_3_, ...), custom_call_target="tpu_custom_call" | custom-call | flops 4950000128 | bytes 16200000 | tf_op jit(solution)/shard_map/pallas_call | solution.py:167
  25.2 3.9 %all-to-all-start.1 = ((f32[16,8,256]{2,1,0:T(8,128)}), f32[16,8,256]{2,1,0:T(8,128)S(1)}, u32[]{:S(2)}, u32[]{:S(2)}) async-start(f32[16,8,256]{2,1,0:T(8,128)} %shard_map.160), calls=%async_computation.1 | async-start | bytes 262144 | tf_op jit(solution)/shard_map/all_to_all | solution.py:621
  29.4 2.0 %collective-permute-start.9 = (f32[128,128]{1,0:T(8,128)S(1)}, f32[128,128]{1,0:T(8,128)S(1)}, u32[]{:S(2)}, u32[]{:S(2)}) collective-permute-start(f32[128,128]{1,0:T(8,128)S(1)} %get-tuple-element.32), channel_id=1, source_target_pairs={{1,0},{0,1},{17,16},{16,17},{3,2},{2,3},{19,18},{18,19},{5,4},{4,5... | collective-permute-start | bytes 196616 | tf_op jit(solution)/shard_map/ppermute | solution.py:568
  31.3 3.9 %all-to-all-done.1 = f32[16,8,256]{2,1,0:T(8,128)S(1)} async-done(((f32[16,8,256]{2,1,0:T(8,128)}), f32[16,8,256]{2,1,0:T(8,128)S(1)}, u32[]{:S(2)}, u32[]{:S(2)}) %all-to-all-start.1) | async-done | bytes 131104 | tf_op jit(solution)/shard_map/all_to_all | solution.py:621
  36.5 4.6 %shard_map.161 = (f32[32,128]{1,0:T(8,128)S(1)}, f32[8,32,128]{2,1,0:T(8,128)}, f32[128,256]{1,0:T(8,128)S(1)}) custom-call(f32[128,256]{1,0:T(8,128)S(1)} %bitcast.28, f32[4,256]{1,0:T(4,128)S(1)} %copy-done.11, f32[256,1024]{1,0:T(8,128)S(1)} %copy-done.2, f32[256,256]{1,0:T(8,128)S(1)} %copy-done.7, f32[256,1024]{1,0:T(8,128)S(1)} %copy-done.3, ...), custom_call_target="tpu_custom_call" | custom-call | flops 4950000128 | bytes 16200000 | tf_op jit(solution)/shard_map/pallas_call | solution.py:167
  41.8 3.6 %all-to-all-start.2 = ((f32[8,32,128]{2,1,0:T(8,128)}), f32[8,32,128]{2,1,0:T(8,128)S(1)}, u32[]{:S(2)}, u32[]{:S(2)}) async-start(f32[8,32,128]{2,1,0:T(8,128)} %get-tuple-element.35), calls=%async_computation.2 | async-start | bytes 262144 | tf_op jit(solution)/shard_map/all_to_all | solution.py:650
  49.8 1.8 %collective-permute-done.6.refs_1_ = f32[32,128]{1,0:T(8,128)S(1)} collective-permute-done((f32[32,128]{1,0:T(8,128)S(1)}, f32[32,128]{1,0:T(8,128)S(1)}, u32[]{:S(2)}, u32[]{:S(2)}) %collective-permute-start.6) | collective-permute-done | bytes 16416 | tf_op jit(solution)/shard_map/ppermute | solution.py:568
  52.7 4.0 %shard_map.163 = (f32[32,4,8,128]{3,2,1,0:T(8,128)}, f32[128,128]{1,0:T(8,128)S(1)}, f32[128,128]{1,0:T(8,128)S(1)}, f32[128,128]{1,0:T(8,128)S(1)}, f32[128,128]{1,0:T(8,128)S(1)}) custom-call(f32[32,128]{1,0:T(8,128)S(1)} %get-tuple-element.29.refs_0_, f32[32,128]{1,0:T(8,128)S(1)} %collective-permute-done.6.refs_1_, ...), custom_call_target="tpu_custom_call" | custom-call | flops 4400000000 | bytes 14400000 | tf_op jit(solution)/shard_map/pallas_call | solution.py:167
  56.8 3.9 %all-to-all-start.3 = ((f32[32,4,8,128]{3,2,1,0:T(8,128)}), f32[32,4,8,128]{3,2,1,0:T(8,128)S(1)}, u32[]{:S(2)}, u32[]{:S(2)}) async-start(f32[32,4,8,128]{3,2,1,0:T(8,128)} %get-tuple-element.36), calls=%async_computation.3 | async-start | bytes 1048576 | tf_op jit(solution)/shard_map/all_to_all | solution.py:695
  60.7 1.8 %collective-permute-start.12 = (f32[4,8,256]{2,1,0:T(8,128)S(1)}, f32[4,8,256]{2,1,0:T(8,128)S(1)}, u32[]{:S(2)}, u32[]{:S(2)}) collective-permute-start(f32[4,8,256]{2,1,0:T(8,128)S(1)} %get-tuple-element.39), channel_id=1, source_target_pairs={{1,0},{0,1},{17,16},{16,17},{3,2},{2,3},{19,18},{18,19},{5,4},{4,5... | collective-permute-start | bytes 98312 | tf_op jit(solution)/shard_map/ppermute | solution.py:568
  62.9 4.3 %collective-permute-done.12 = f32[4,8,256]{2,1,0:T(8,128)S(1)} collective-permute-done((f32[4,8,256]{2,1,0:T(8,128)S(1)}, f32[4,8,256]{2,1,0:T(8,128)S(1)}, u32[]{:S(2)}, u32[]{:S(2)}) %collective-permute-start.12) | collective-permute-done | bytes 32800 | tf_op jit(solution)/shard_map/ppermute | solution.py:568
  67.3 10.2 %all-to-all-done.3 = f32[32,4,8,128]{3,2,1,0:T(8,128)S(1)} async-done(((f32[32,4,8,128]{3,2,1,0:T(8,128)}), f32[32,4,8,128]{3,2,1,0:T(8,128)S(1)}, u32[]{:S(2)}, u32[]{:S(2)}) %all-to-all-start.3) | async-done | bytes 524320 | tf_op jit(solution)/shard_map/all_to_all | solution.py:695
  77.5 1.7 %shard_map.165 = (f32[32,16,128]{2,1,0:T(8,128)}, f32[8,16,256]{2,1,0:T(8,128)}) custom-call(f32[1024,128]{1,0:T(8,128)S(1)} %bitcast.25, f32[32,256]{1,0:T(8,128)S(1)} %bitcast.34, f32[32,256]{1,0:T(8,128)S(1)} %bitcast.31, f32[32,256]{1,0:T(8,128)S(1)} %bitcast.32, f32[32,256]{1,0:T(8,128)S(1)} %bitcast.33), custom_call_target="tpu_custom_call" | custom-call | flops 2200000000 | bytes 7200000 | tf_op jit(solution)/shard_map/pallas_call | solution.py:167
  79.3 2.6 %all-to-all-start.4 = ((f32[32,16,128]{2,1,0:T(8,128)}), f32[32,16,128]{2,1,0:T(8,128)S(1)}, u32[]{:S(2)}, u32[]{:S(2)}) async-start(f32[32,16,128]{2,1,0:T(8,128)} %get-tuple-element.43), calls=%async_computation.4 | async-start | bytes 524288 | tf_op jit(solution)/shard_map/all_to_all | solution.py:703
  81.9 1.7 %collective-permute-start.15 = (f32[128,128]{1,0:T(8,128)S(1)}, f32[128,128]{1,0:T(8,128)S(1)}, u32[]{:S(2)}, u32[]{:S(2)}) collective-permute-start(f32[128,128]{1,0:T(8,128)S(1)} %get-tuple-element.45), channel_id=1, source_target_pairs={{1,0},{0,1},{17,16},{16,17},{3,2},{2,3},{19,18},{18,19},{5,4},{4,5... | collective-permute-start | bytes 196616 | tf_op jit(solution)/shard_map/ppermute | solution.py:568
  84.1 4.2 %collective-permute-done.15.refs_3_ = f32[128,128]{1,0:T(8,128)S(1)} collective-permute-done((f32[128,128]{1,0:T(8,128)S(1)}, f32[128,128]{1,0:T(8,128)S(1)}, u32[]{:S(2)}, u32[]{:S(2)}) %collective-permute-start.15) | collective-permute-done | bytes 65568 | tf_op jit(solution)/shard_map/ppermute | solution.py:568
  89.3 3.7 %all-to-all-done.4 = f32[32,16,128]{2,1,0:T(8,128)S(1)} async-done(((f32[32,16,128]{2,1,0:T(8,128)}), f32[32,16,128]{2,1,0:T(8,128)S(1)}, u32[]{:S(2)}, u32[]{:S(2)}) %all-to-all-start.4) | async-done | bytes 262176 | tf_op jit(solution)/shard_map/all_to_all | solution.py:703
  (83 shorter events, 13.7 us)
Async XLA Ops:
  3.1 11.7 %collective-permute-start.2 = (f32[2,16,128]{2,1,0:T(8,128)}, f32[2,16,128]{2,1,0:T(8,128)S(1)}, u32[]{:S(2)}, u32[]{:S(2)}) collective-permute-start(f32[2,16,128]{2,1,0:T(8,128)} %get-tuple-element.27.refs_0_), channel_id=1, source_target_pairs={{6,0},{4,2},{2,4},{0,6},{14,8},{12,10},{10,12},{8,14},{7,1},{5,3},... | collective-permute-start | bytes 49160 | tf_op jit(solution)/shard_map/ppermute | solution.py:568
  7.1 7.7 %collective-permute-start.1 = (f32[2,16,128]{2,1,0:T(8,128)}, f32[2,16,128]{2,1,0:T(8,128)S(1)}, u32[]{:S(2)}, u32[]{:S(2)}) collective-permute-start(f32[2,16,128]{2,1,0:T(8,128)} %get-tuple-element.27.refs_0_), channel_id=1, source_target_pairs={{4,0},{6,2},{0,4},{2,6},{12,8},{14,10},{8,12},{10,14},{5,1},{7,3},... | collective-permute-start | bytes 49160 | tf_op jit(solution)/shard_map/ppermute | solution.py:568
  7.6 7.3 %collective-permute-start = (f32[2,16,128]{2,1,0:T(8,128)}, f32[2,16,128]{2,1,0:T(8,128)S(1)}, u32[]{:S(2)}, u32[]{:S(2)}) collective-permute-start(f32[2,16,128]{2,1,0:T(8,128)} %get-tuple-element.27.refs_0_), channel_id=1, source_target_pairs={{2,0},{0,2},{6,4},{4,6},{10,8},{8,10},{14,12},{12,14},{3,1},{1,3},... | collective-permute-start | bytes 49160 | tf_op jit(solution)/shard_map/ppermute | solution.py:568
  7.8 14.4 %all-to-all-start = ((f32[16,16,256]{2,1,0:T(8,128)}), f32[16,16,256]{2,1,0:T(8,128)S(1)}, u32[]{:S(2)}, u32[]{:S(2)}) async-start(f32[16,16,256]{2,1,0:T(8,128)} %get-tuple-element.26), calls=%async_computation | async-start | bytes 524288 | tf_op jit(solution)/shard_map/all_to_all | solution.py:602
  14.9 4.4 %collective-permute-start.5 = (f32[4,2,16,128]{3,2,1,0:T(8,128)S(1)}, f32[4,2,16,128]{3,2,1,0:T(8,128)S(1)}, u32[]{:S(2)}, u32[]{:S(2)}) collective-permute-start(f32[4,2,16,128]{3,2,1,0:T(8,128)S(1)} %shard_map.159.refs_1_), channel_id=1, source_target_pairs={{17,0},{16,1},{1,16},{0,17},{19,2},{18,3},{3,18},{2,19},{21,4},{20... | collective-permute-start | bytes 196616 | tf_op jit(solution)/shard_map/ppermute | solution.py:568
  14.9 4.3 %collective-permute-start.4 = (f32[4,2,16,128]{3,2,1,0:T(8,128)S(1)}, f32[4,2,16,128]{3,2,1,0:T(8,128)S(1)}, u32[]{:S(2)}, u32[]{:S(2)}) collective-permute-start(f32[4,2,16,128]{3,2,1,0:T(8,128)S(1)} %shard_map.159.refs_1_), channel_id=1, source_target_pairs={{16,0},{17,1},{0,16},{1,17},{18,2},{19,3},{2,18},{3,19},{20,4},{21... | collective-permute-start | bytes 196616 | tf_op jit(solution)/shard_map/ppermute | solution.py:568
  16.5 4.3 %collective-permute-start.3 = (f32[4,2,16,128]{3,2,1,0:T(8,128)S(1)}, f32[4,2,16,128]{3,2,1,0:T(8,128)S(1)}, u32[]{:S(2)}, u32[]{:S(2)}) collective-permute-start(f32[4,2,16,128]{3,2,1,0:T(8,128)S(1)} %shard_map.159.refs_1_), channel_id=1, source_target_pairs={{1,0},{0,1},{17,16},{16,17},{3,2},{2,3},{19,18},{18,19},{5,4},{4,5... | collective-permute-start | bytes 196616 | tf_op jit(solution)/shard_map/ppermute | solution.py:568
  25.2 10.1 %all-to-all-start.1 = ((f32[16,8,256]{2,1,0:T(8,128)}), f32[16,8,256]{2,1,0:T(8,128)S(1)}, u32[]{:S(2)}, u32[]{:S(2)}) async-start(f32[16,8,256]{2,1,0:T(8,128)} %shard_map.160), calls=%async_computation.1 | async-start | bytes 262144 | tf_op jit(solution)/shard_map/all_to_all | solution.py:621
  29.4 18.5 %collective-permute-start.9 = (f32[128,128]{1,0:T(8,128)S(1)}, f32[128,128]{1,0:T(8,128)S(1)}, u32[]{:S(2)}, u32[]{:S(2)}) collective-permute-start(f32[128,128]{1,0:T(8,128)S(1)} %get-tuple-element.32), channel_id=1, source_target_pairs={{1,0},{0,1},{17,16},{16,17},{3,2},{2,3},{19,18},{18,19},{5,4},{4,5... | collective-permute-start | bytes 196616 | tf_op jit(solution)/shard_map/ppermute | solution.py:568
  36.5 11.7 %copy-start.17 = (f32[128,128]{1,0:T(8,128)S(1)}, f32[128,128]{1,0:T(8,128)}, u32[]{:S(2)}) copy-start(f32[128,128]{1,0:T(8,128)} %get-tuple-element.51) | copy-start | bytes 196612
  41.8 10.9 %all-to-all-start.2 = ((f32[8,32,128]{2,1,0:T(8,128)}), f32[8,32,128]{2,1,0:T(8,128)S(1)}, u32[]{:S(2)}, u32[]{:S(2)}) async-start(f32[8,32,128]{2,1,0:T(8,128)} %get-tuple-element.35), calls=%async_computation.2 | async-start | bytes 262144 | tf_op jit(solution)/shard_map/all_to_all | solution.py:650
  45.5 3.4 %collective-permute-start.10 = (f32[128,128]{1,0:T(8,128)S(1)}, f32[128,128]{1,0:T(8,128)S(1)}, u32[]{:S(2)}, u32[]{:S(2)}) collective-permute-start(f32[128,128]{1,0:T(8,128)S(1)} %get-tuple-element.33), channel_id=1, source_target_pairs={{16,0},{17,1},{0,16},{1,17},{18,2},{19,3},{2,18},{3,19},{20,4},{21... | collective-permute-start | bytes 196616 | tf_op jit(solution)/shard_map/ppermute | solution.py:568
  45.6 3.9 %collective-permute-start.11 = (f32[128,128]{1,0:T(8,128)S(1)}, f32[128,128]{1,0:T(8,128)S(1)}, u32[]{:S(2)}, u32[]{:S(2)}) collective-permute-start(f32[128,128]{1,0:T(8,128)S(1)} %get-tuple-element.34), channel_id=1, source_target_pairs={{17,0},{16,1},{1,16},{0,17},{19,2},{18,3},{3,18},{2,19},{21,4},{20... | collective-permute-start | bytes 196616 | tf_op jit(solution)/shard_map/ppermute | solution.py:568
  46.1 3.7 %collective-permute-start.8 = (f32[32,128]{1,0:T(8,128)S(1)}, f32[32,128]{1,0:T(8,128)S(1)}, u32[]{:S(2)}, u32[]{:S(2)}) collective-permute-start(f32[32,128]{1,0:T(8,128)S(1)} %get-tuple-element.29.refs_0_), channel_id=1, source_target_pairs={{17,0},{16,1},{1,16},{0,17},{19,2},{18,3},{3,18},{2,19},{21,4},{20... | collective-permute-start | bytes 49160 | tf_op jit(solution)/shard_map/ppermute | solution.py:568
  47.4 2.4 %collective-permute-start.7 = (f32[32,128]{1,0:T(8,128)S(1)}, f32[32,128]{1,0:T(8,128)S(1)}, u32[]{:S(2)}, u32[]{:S(2)}) collective-permute-start(f32[32,128]{1,0:T(8,128)S(1)} %get-tuple-element.29.refs_0_), channel_id=1, source_target_pairs={{16,0},{17,1},{0,16},{1,17},{18,2},{19,3},{2,18},{3,19},{20,4},{21... | collective-permute-start | bytes 49160 | tf_op jit(solution)/shard_map/ppermute | solution.py:568
  47.8 3.7 %collective-permute-start.6 = (f32[32,128]{1,0:T(8,128)S(1)}, f32[32,128]{1,0:T(8,128)S(1)}, u32[]{:S(2)}, u32[]{:S(2)}) collective-permute-start(f32[32,128]{1,0:T(8,128)S(1)} %get-tuple-element.29.refs_0_), channel_id=1, source_target_pairs={{1,0},{0,1},{17,16},{16,17},{3,2},{2,3},{19,18},{18,19},{5,4},{4,5... | collective-permute-start | bytes 49160 | tf_op jit(solution)/shard_map/ppermute | solution.py:568
  56.8 20.8 %all-to-all-start.3 = ((f32[32,4,8,128]{3,2,1,0:T(8,128)}), f32[32,4,8,128]{3,2,1,0:T(8,128)S(1)}, u32[]{:S(2)}, u32[]{:S(2)}) async-start(f32[32,4,8,128]{3,2,1,0:T(8,128)} %get-tuple-element.36), calls=%async_computation.3 | async-start | bytes 1048576 | tf_op jit(solution)/shard_map/all_to_all | solution.py:695
  60.7 6.6 %collective-permute-start.12 = (f32[4,8,256]{2,1,0:T(8,128)S(1)}, f32[4,8,256]{2,1,0:T(8,128)S(1)}, u32[]{:S(2)}, u32[]{:S(2)}) collective-permute-start(f32[4,8,256]{2,1,0:T(8,128)S(1)} %get-tuple-element.39), channel_id=1, source_target_pairs={{1,0},{0,1},{17,16},{16,17},{3,2},{2,3},{19,18},{18,19},{5,4},{4,5... | collective-permute-start | bytes 98312 | tf_op jit(solution)/shard_map/ppermute | solution.py:568
  62.6 4.7 %collective-permute-start.13 = (f32[4,8,256]{2,1,0:T(8,128)S(1)}, f32[4,8,256]{2,1,0:T(8,128)S(1)}, u32[]{:S(2)}, u32[]{:S(2)}) collective-permute-start(f32[4,8,256]{2,1,0:T(8,128)S(1)} %get-tuple-element.40), channel_id=1, source_target_pairs={{16,0},{17,1},{0,16},{1,17},{18,2},{19,3},{2,18},{3,19},{20,4},{21... | collective-permute-start | bytes 98312 | tf_op jit(solution)/shard_map/ppermute | solution.py:568
  62.6 4.7 %collective-permute-start.14 = (f32[4,8,256]{2,1,0:T(8,128)S(1)}, f32[4,8,256]{2,1,0:T(8,128)S(1)}, u32[]{:S(2)}, u32[]{:S(2)}) collective-permute-start(f32[4,8,256]{2,1,0:T(8,128)S(1)} %get-tuple-element.41), channel_id=1, source_target_pairs={{17,0},{16,1},{1,16},{0,17},{19,2},{18,3},{3,18},{2,19},{21,4},{20... | collective-permute-start | bytes 98312 | tf_op jit(solution)/shard_map/ppermute | solution.py:568
  79.3 13.8 %all-to-all-start.4 = ((f32[32,16,128]{2,1,0:T(8,128)}), f32[32,16,128]{2,1,0:T(8,128)S(1)}, u32[]{:S(2)}, u32[]{:S(2)}) async-start(f32[32,16,128]{2,1,0:T(8,128)} %get-tuple-element.43), calls=%async_computation.4 | async-start | bytes 524288 | tf_op jit(solution)/shard_map/all_to_all | solution.py:703
  81.9 6.4 %collective-permute-start.15 = (f32[128,128]{1,0:T(8,128)S(1)}, f32[128,128]{1,0:T(8,128)S(1)}, u32[]{:S(2)}, u32[]{:S(2)}) collective-permute-start(f32[128,128]{1,0:T(8,128)S(1)} %get-tuple-element.45), channel_id=1, source_target_pairs={{1,0},{0,1},{17,16},{16,17},{3,2},{2,3},{19,18},{18,19},{5,4},{4,5... | collective-permute-start | bytes 196616 | tf_op jit(solution)/shard_map/ppermute | solution.py:568
  83.6 4.7 %collective-permute-start.16 = (f32[128,128]{1,0:T(8,128)S(1)}, f32[128,128]{1,0:T(8,128)S(1)}, u32[]{:S(2)}, u32[]{:S(2)}) collective-permute-start(f32[128,128]{1,0:T(8,128)S(1)} %get-tuple-element.46), channel_id=1, source_target_pairs={{16,0},{17,1},{0,16},{1,17},{18,2},{19,3},{2,18},{3,19},{20,4},{21... | collective-permute-start | bytes 196616 | tf_op jit(solution)/shard_map/ppermute | solution.py:568
  83.6 5.3 %collective-permute-start.17 = (f32[128,128]{1,0:T(8,128)S(1)}, f32[128,128]{1,0:T(8,128)S(1)}, u32[]{:S(2)}, u32[]{:S(2)}) collective-permute-start(f32[128,128]{1,0:T(8,128)S(1)} %get-tuple-element.47), channel_id=1, source_target_pairs={{17,0},{16,1},{1,16},{0,17},{19,2},{18,3},{3,18},{2,19},{21,4},{20... | collective-permute-start | bytes 196616 | tf_op jit(solution)/shard_map/ppermute | solution.py:568
  (19 other events, 82.5 us)

commit v12 on v11

--- a/solution.py
+++ b/solution.py
@@ -297,13 +297,13 @@
 
 
 def column_kernel(
-    few, heads, ready, msa_ref, gains_ref, qkvg_ref, final_ref, expand_ref, shrink_ref, sides_ref,
-    left_ref, right_ref, out_ref
+    few, heads, ready, msa_ref, gains_ref, qkvg_ref, joined_ref, expand_ref, shrink_ref, left_ref,
+    right_ref, out_ref
 ):
     ready()
     count, width = msa_ref.shape
-    inner = final_ref.shape[0]
-    half = sides_ref.shape[0] // 2
+    inner = qkvg_ref.shape[1] // 4
+    half = (joined_ref.shape[0] - inner) // 2
     first = msa_ref[...]
     projected = multiply(layer_normalise(first, gains_ref[1:2, :]), qkvg_ref[...])
     query, key, value, gate = (projected[:, k * inner : (k + 1) * inner] for k in range(4))
@@ -314,11 +314,11 @@
         holds = lax.broadcasted_iota(jnp.int32, shape, 1)
         allowed = lax.rem(asks, few) == lax.rem(holds, few)
     attended = attend(query, key, value, None, heads, allowed)
-    second = first + multiply(sigmoid(gate) * attended, final_ref[...])
+    second = first + multiply(sigmoid(gate) * attended, joined_ref[:inner])
     expanded = multiply(layer_normalise(second, gains_ref[2:3, :]), expand_ref[...])
     third = second + multiply(jnp.maximum(expanded, 0.0), shrink_ref[...])
     out_ref[...] = third
-    factors = multiply(sides_ref[...], layer_normalise(third, gains_ref[3:4, :]), across=True)
+    factors = multiply(joined_ref[inner:], layer_normalise(third, gains_ref[3:4, :]), across=True)
     left_ref[...] = factors[:half]
     for g in range(right_ref.shape[0]):
         right_ref[g] = factors[half:]
@@ -623,10 +623,9 @@
     weights = (
         layernorm_scales,
         vertical_qkvg_kernel,
-        vertical_final_kernel,
+        jnp.concatenate([vertical_final_kernel, dyadic_sides_kernel.T], axis=0),
         feedforward_expand_kernel,
         feedforward_shrink_kernel,
-        dyadic_sides_kernel.T,
     )
     left, right, alignment = call_near(
         functools.partial(column_kernel, few, heads),
@@ -648,6 +647,7 @@
     )
     pair = trade(pair, columns)
     right = lax.all_to_all(right, "gi", 0, 0, tiled=True)
+    right, *alignment = lax.optimization_barrier((right, *alignment))
     left = trade([left] * n_cols, columns)
     alignment = [block.reshape(-1, width) for block in trade(alignment, columns)]
     share = max(pair_width // n_all, 1)

time: 95 us -> 97.9 us (1.031)
  other arithmetic: 0.08 us -> 1.62 us
  local copies, waits for them, and re-layouts: 4.14 us -> 5.32 us
    ppermute x18, starting transfers between devices: 16 us -> 14.5 us  [trade(): lax.ppermute(blocks[k], axes, [(t ^ k, t) for t in range(n) if t ^ k < n])]
    all_to_all x1, starting transfers between devices: 3.92 us -> 5.07 us  [per_device(): tri = lax.all_to_all(tri, everyone, 0, 0, tiled=True)]
    unnamed x41 -> x31, local copies, waits for them, and re-layouts: 2.12 us -> 3.06 us
  transfers between devices with their start and end apart: 23 -> 23, of which waited for: 13 -> 12; matrix products, arithmetic and copies ran while one was open for 2% -> 4% of each run, Pallas kernels for 6% -> 1%
where the time goes in v12:
time: 97.9 us; the launch traced here: 97.2 us
  starting transfers between devices  36.5 us (37%)
  waiting for transfers between devices  35 us (36%)
  Pallas kernels  17.9 us (18%)
  local copies, waits for them, and re-layouts  5.32 us (5%)
  other arithmetic  1.62 us (2%)
    pallas_call x9, Pallas kernels, call_near(): pl.pallas_call(lambda *refs: kernel(lambda: None, *refs), out_shape=[jax....  15.5 us
    ppermute x18, waiting for transfers between devices, trade(): lax.ppermute(blocks[k], axes, [(t ^ k, t) for t in range(n) if t ^ k < n])  15 us
    ppermute x18, starting transfers between devices, trade(): lax.ppermute(blocks[k], axes, [(t ^ k, t) for t in range(n) if t ^ k < n])  14.5 us
    all_to_all x1, waiting for transfers between devices, per_device(): tri = lax.all_to_all(tri, everyone, 0, 0, tiled=True)  10.2 us
    all_to_all x1, starting transfers between devices, per_device(): msa = lax.all_to_all(msa, 'gi', 0, 0, tiled=True)  6.15 us
    all_to_all x1, starting transfers between devices, per_device(): tri = lax.all_to_all(tri, everyone, 0, 0, tiled=True)  5.07 us
    all_to_all x1, starting transfers between devices, per_device(): lax.all_to_all(msa_first, everyone, 0, 0, tiled=True, axis_index_groups=h...  4.24 us
    all_to_all x1, starting transfers between devices, per_device(): right = lax.all_to_all(right, 'gi', 0, 0, tiled=True)  3.94 us
  transfers between devices with their start and end apart: 23, of which 12 were waited for; matrix products, arithmetic and copies ran while one was open for 4% of the time, Pallas kernels for 1%

profile of v12, /device:TPU:0, one launch (start us, length us, event | category | flops | bytes accessed | tf_op | source)
XLA Modules:
  0.0 97.2 jit_solution(7675403276118541150)
XLA Ops:
  0.6 2.4 %shard_map.158 = (f32[16,16,256]{2,1,0:T(8,128)}, f32[2,16,128]{2,1,0:T(8,128)}) custom-call(f32[8,16,256]{2,1,0:T(8,128)} %refs_0_.2, f32[16,32,128]{2,1,0:T(8,128)} %refs_1_.3, f32[3,128]{1,0:T(4,128)} %refs_3_.1, f32[8,128]{1,0:T(8,128)} %bitcast.44), custom_call_target="tpu_custom_call" | custom-call | flops 2200000000 | bytes 7200000 | tf_op jit(solution)/shard_map/pallas_call | solution.py:154
  3.1 4.0 %collective-permute-start.2 = (f32[2,16,128]{2,1,0:T(8,128)}, f32[2,16,128]{2,1,0:T(8,128)S(1)}, u32[]{:S(2)}, u32[]{:S(2)}) collective-permute-start(f32[2,16,128]{2,1,0:T(8,128)} %get-tuple-element.32.refs_0_), channel_id=1, source_target_pairs={{6,0},{4,2},{2,4},{0,6},{14,8},{12,10},{10,12},{8,14},{7,1},{5,3},... | collective-permute-start | bytes 49160 | tf_op jit(solution)/shard_map/ppermute | solution.py:568
  7.8 6.1 %all-to-all-start = ((f32[16,16,256]{2,1,0:T(8,128)}), f32[16,16,256]{2,1,0:T(8,128)S(1)}, u32[]{:S(2)}, u32[]{:S(2)}) async-start(f32[16,16,256]{2,1,0:T(8,128)} %get-tuple-element.31), calls=%async_computation | async-start | bytes 524288 | tf_op jit(solution)/shard_map/all_to_all | solution.py:602
  15.9 1.6 %collective-permute-start.4 = (f32[4,2,16,128]{3,2,1,0:T(8,128)S(1)}, f32[4,2,16,128]{3,2,1,0:T(8,128)S(1)}, u32[]{:S(2)}, u32[]{:S(2)}) collective-permute-start(f32[4,2,16,128]{3,2,1,0:T(8,128)S(1)} %shard_map.159.refs_1_), channel_id=1, source_target_pairs={{16,0},{17,1},{0,16},{1,17},{18,2},{19,3},{2,18},{3,19},{20,4},{21... | collective-permute-start | bytes 196616 | tf_op jit(solution)/shard_map/ppermute | solution.py:568
  18.7 1.5 %collective-permute-done.5.refs_4_ = f32[4,2,16,128]{3,2,1,0:T(8,128)S(1)} collective-permute-done((f32[4,2,16,128]{3,2,1,0:T(8,128)S(1)}, f32[4,2,16,128]{3,2,1,0:T(8,128)S(1)}, u32[]{:S(2)}, u32[]{:S(2)}) %collective-permute-start.5) | collective-permute-done | bytes 65568 | tf_op jit(solution)/shard_map/ppermute | solution.py:568
  20.3 1.5 %collective-permute-done.3.refs_2_ = f32[4,2,16,128]{3,2,1,0:T(8,128)S(1)} collective-permute-done((f32[4,2,16,128]{3,2,1,0:T(8,128)S(1)}, f32[4,2,16,128]{3,2,1,0:T(8,128)S(1)}, u32[]{:S(2)}, u32[]{:S(2)}) %collective-permute-start.3) | collective-permute-done | bytes 65568 | tf_op jit(solution)/shard_map/ppermute | solution.py:568
  22.1 3.1 %shard_map.160 = f32[16,8,256]{2,1,0:T(8,128)} custom-call(f32[16,16,256]{2,1,0:T(8,128)S(1)} %all-to-all-done.refs_0_, f32[4,2,16,128]{3,2,1,0:T(8,128)S(1)} %shard_map.159.refs_1_, f32[4,2,16,128]{3,2,1,0:T(8,128)S(1)} %collective-permute-done.3.refs_2_, f32[4,2,16,128]{3,2,1,0:T(8,128)S(1)} %collective-permute-done.4.refs_3_, ...), custom_call_target="tpu_custom_call" | custom-call | flops 4950000128 | bytes 16200000 | tf_op jit(solution)/shard_map/pallas_call | solution.py:167
  25.2 4.2 %all-to-all-start.1 = ((f32[16,8,256]{2,1,0:T(8,128)}), f32[16,8,256]{2,1,0:T(8,128)S(1)}, u32[]{:S(2)}, u32[]{:S(2)}) async-start(f32[16,8,256]{2,1,0:T(8,128)} %shard_map.160), calls=%async_computation.1 | async-start | bytes 262144 | tf_op jit(solution)/shard_map/all_to_all | solution.py:621
  32.0 3.6 %all-to-all-done.1 = f32[16,8,256]{2,1,0:T(8,128)S(1)} async-done(((f32[16,8,256]{2,1,0:T(8,128)}), f32[16,8,256]{2,1,0:T(8,128)S(1)}, u32[]{:S(2)}, u32[]{:S(2)}) %all-to-all-start.1) | async-done | bytes 131104 | tf_op jit(solution)/shard_map/all_to_all | solution.py:621
  36.9 4.6 %shard_map.161 = (f32[32,128]{1,0:T(8,128)S(1)}, f32[8,32,128]{2,1,0:T(8,128)}, f32[128,256]{1,0:T(8,128)S(1)}) custom-call(f32[128,256]{1,0:T(8,128)S(1)} %bitcast.28, f32[4,256]{1,0:T(4,128)S(1)} %copy-done.9, f32[256,1024]{1,0:T(8,128)S(1)} %copy-done.2, f32[320,256]{1,0:T(8,128)S(1)} %pad_maximum_fusion.refs_3_, f32[256,1024]{1,0:T(8,128)S(1)} %copy-done.3, ...), custom_call_target="tpu_custom_call" | custom-call | flops 4950000128 | bytes 16200000 | tf_op jit(solution)/shard_map/pallas_call | solution.py:167
  41.5 3.9 %all-to-all-start.2 = ((f32[8,32,128]{2,1,0:T(8,128)}), f32[8,32,128]{2,1,0:T(8,128)S(1)}, u32[]{:S(2)}, u32[]{:S(2)}) async-start(f32[8,32,128]{2,1,0:T(8,128)} %get-tuple-element.40), calls=%async_computation.2 | async-start | bytes 262144 | tf_op jit(solution)/shard_map/all_to_all | solution.py:649
  46.4 1.5 %collective-permute-start.11 = (f32[128,128]{1,0:T(8,128)S(1)}, f32[128,128]{1,0:T(8,128)S(1)}, u32[]{:S(2)}, u32[]{:S(2)}) collective-permute-start(f32[128,128]{1,0:T(8,128)S(1)} %get-tuple-element.39), channel_id=1, source_target_pairs={{17,0},{16,1},{1,16},{0,17},{19,2},{18,3},{3,18},{2,19},{21,4},{20... | collective-permute-start | bytes 196616 | tf_op jit(solution)/shard_map/ppermute | solution.py:568
  50.8 2.0 %all-to-all-done.2 = f32[8,32,128]{2,1,0:T(8,128)S(1)} async-done(((f32[8,32,128]{2,1,0:T(8,128)}), f32[8,32,128]{2,1,0:T(8,128)S(1)}, u32[]{:S(2)}, u32[]{:S(2)}) %all-to-all-start.2) | async-done | bytes 131104 | tf_op jit(solution)/shard_map/all_to_all | solution.py:649
  52.8 1.5 %collective-permute-done.6.refs_1_ = f32[32,128]{1,0:T(8,128)S(1)} collective-permute-done((f32[32,128]{1,0:T(8,128)S(1)}, f32[32,128]{1,0:T(8,128)S(1)}, u32[]{:S(2)}, u32[]{:S(2)}) %collective-permute-start.6) | collective-permute-done | bytes 16416 | tf_op jit(solution)/shard_map/ppermute | solution.py:568
  54.4 4.0 %shard_map.164 = (f32[32,4,8,128]{3,2,1,0:T(8,128)}, f32[128,128]{1,0:T(8,128)S(1)}, f32[128,128]{1,0:T(8,128)S(1)}, f32[128,128]{1,0:T(8,128)S(1)}, f32[128,128]{1,0:T(8,128)S(1)}) custom-call(f32[32,128]{1,0:T(8,128)S(1)} %get-tuple-element.34.refs_0_, f32[32,128]{1,0:T(8,128)S(1)} %collective-permute-done.6.refs_1_, ...), custom_call_target="tpu_custom_call" | custom-call | flops 4400000000 | bytes 14400000 | tf_op jit(solution)/shard_map/pallas_call | solution.py:167
  58.4 5.1 %all-to-all-start.3 = ((f32[32,4,8,128]{3,2,1,0:T(8,128)}), f32[32,4,8,128]{3,2,1,0:T(8,128)S(1)}, u32[]{:S(2)}, u32[]{:S(2)}) async-start(f32[32,4,8,128]{3,2,1,0:T(8,128)} %get-tuple-element.47), calls=%async_computation.3 | async-start | bytes 1048576 | tf_op jit(solution)/shard_map/all_to_all | solution.py:695
  63.5 1.8 %collective-permute-start.12 = (f32[4,8,256]{2,1,0:T(8,128)S(1)}, f32[4,8,256]{2,1,0:T(8,128)S(1)}, u32[]{:S(2)}, u32[]{:S(2)}) collective-permute-start(f32[4,8,256]{2,1,0:T(8,128)S(1)} %get-tuple-element.49), channel_id=1, source_target_pairs={{1,0},{0,1},{17,16},{16,17},{3,2},{2,3},{19,18},{18,19},{5,4},{4,5... | collective-permute-start | bytes 98312 | tf_op jit(solution)/shard_map/ppermute | solution.py:568
  65.7 4.4 %collective-permute-done.12 = f32[4,8,256]{2,1,0:T(8,128)S(1)} collective-permute-done((f32[4,8,256]{2,1,0:T(8,128)S(1)}, f32[4,8,256]{2,1,0:T(8,128)S(1)}, u32[]{:S(2)}, u32[]{:S(2)}) %collective-permute-start.12) | collective-permute-done | bytes 32800 | tf_op jit(solution)/shard_map/ppermute | solution.py:568
  70.1 10.2 %all-to-all-done.3 = f32[32,4,8,128]{3,2,1,0:T(8,128)S(1)} async-done(((f32[32,4,8,128]{3,2,1,0:T(8,128)}), f32[32,4,8,128]{3,2,1,0:T(8,128)S(1)}, u32[]{:S(2)}, u32[]{:S(2)}) %all-to-all-start.3) | async-done | bytes 524320 | tf_op jit(solution)/shard_map/all_to_all | solution.py:695
  80.3 1.7 %shard_map.165 = (f32[32,16,128]{2,1,0:T(8,128)}, f32[8,16,256]{2,1,0:T(8,128)}) custom-call(f32[1024,128]{1,0:T(8,128)S(1)} %bitcast.25, f32[32,256]{1,0:T(8,128)S(1)} %bitcast.33, f32[32,256]{1,0:T(8,128)S(1)} %bitcast.30, f32[32,256]{1,0:T(8,128)S(1)} %bitcast.31, f32[32,256]{1,0:T(8,128)S(1)} %bitcast.32), custom_call_target="tpu_custom_call" | custom-call | flops 2200000000 | bytes 7200000 | tf_op jit(solution)/shard_map/pallas_call | solution.py:167
  82.1 2.6 %all-to-all-start.4 = ((f32[32,16,128]{2,1,0:T(8,128)}), f32[32,16,128]{2,1,0:T(8,128)S(1)}, u32[]{:S(2)}, u32[]{:S(2)}) async-start(f32[32,16,128]{2,1,0:T(8,128)} %get-tuple-element.53), calls=%async_computation.4 | async-start | bytes 524288 | tf_op jit(solution)/shard_map/all_to_all | solution.py:703
  84.7 1.7 %collective-permute-start.15 = (f32[128,128]{1,0:T(8,128)S(1)}, f32[128,128]{1,0:T(8,128)S(1)}, u32[]{:S(2)}, u32[]{:S(2)}) collective-permute-start(f32[128,128]{1,0:T(8,128)S(1)} %get-tuple-element.55), channel_id=1, source_target_pairs={{1,0},{0,1},{17,16},{16,17},{3,2},{2,3},{19,18},{18,19},{5,4},{4,5... | collective-permute-start | bytes 196616 | tf_op jit(solution)/shard_map/ppermute | solution.py:568
  86.9 4.2 %collective-permute-done.15.refs_3_ = f32[128,128]{1,0:T(8,128)S(1)} collective-permute-done((f32[128,128]{1,0:T(8,128)S(1)}, f32[128,128]{1,0:T(8,128)S(1)}, u32[]{:S(2)}, u32[]{:S(2)}) %collective-permute-start.15) | collective-permute-done | bytes 65568 | tf_op jit(solution)/shard_map/ppermute | solution.py:568
  92.1 3.7 %all-to-all-done.4 = f32[32,16,128]{2,1,0:T(8,128)S(1)} async-done(((f32[32,16,128]{2,1,0:T(8,128)}), f32[32,16,128]{2,1,0:T(8,128)S(1)}, u32[]{:S(2)}, u32[]{:S(2)}) %all-to-all-start.4) | async-done | bytes 262176 | tf_op jit(solution)/shard_map/all_to_all | solution.py:703
  (74 shorter events, 14.9 us)
Async XLA Ops:
  3.1 12.1 %collective-permute-start.2 = (f32[2,16,128]{2,1,0:T(8,128)}, f32[2,16,128]{2,1,0:T(8,128)S(1)}, u32[]{:S(2)}, u32[]{:S(2)}) collective-permute-start(f32[2,16,128]{2,1,0:T(8,128)} %get-tuple-element.32.refs_0_), channel_id=1, source_target_pairs={{6,0},{4,2},{2,4},{0,6},{14,8},{12,10},{10,12},{8,14},{7,1},{5,3},... | collective-permute-start | bytes 49160 | tf_op jit(solution)/shard_map/ppermute | solution.py:568
  7.1 8.0 %collective-permute-start.1 = (f32[2,16,128]{2,1,0:T(8,128)}, f32[2,16,128]{2,1,0:T(8,128)S(1)}, u32[]{:S(2)}, u32[]{:S(2)}) collective-permute-start(f32[2,16,128]{2,1,0:T(8,128)} %get-tuple-element.32.refs_0_), channel_id=1, source_target_pairs={{4,0},{6,2},{0,4},{2,6},{12,8},{14,10},{8,12},{10,14},{5,1},{7,3},... | collective-permute-start | bytes 49160 | tf_op jit(solution)/shard_map/ppermute | solution.py:568
  7.6 7.6 %collective-permute-start = (f32[2,16,128]{2,1,0:T(8,128)}, f32[2,16,128]{2,1,0:T(8,128)S(1)}, u32[]{:S(2)}, u32[]{:S(2)}) collective-permute-start(f32[2,16,128]{2,1,0:T(8,128)} %get-tuple-element.32.refs_0_), channel_id=1, source_target_pairs={{2,0},{0,2},{6,4},{4,6},{10,8},{8,10},{14,12},{12,14},{3,1},{1,3},... | collective-permute-start | bytes 49160 | tf_op jit(solution)/shard_map/ppermute | solution.py:568
  7.8 14.4 %all-to-all-start = ((f32[16,16,256]{2,1,0:T(8,128)}), f32[16,16,256]{2,1,0:T(8,128)S(1)}, u32[]{:S(2)}, u32[]{:S(2)}) async-start(f32[16,16,256]{2,1,0:T(8,128)} %get-tuple-element.31), calls=%async_computation | async-start | bytes 524288 | tf_op jit(solution)/shard_map/all_to_all | solution.py:602
  15.8 4.4 %collective-permute-start.5 = (f32[4,2,16,128]{3,2,1,0:T(8,128)S(1)}, f32[4,2,16,128]{3,2,1,0:T(8,128)S(1)}, u32[]{:S(2)}, u32[]{:S(2)}) collective-permute-start(f32[4,2,16,128]{3,2,1,0:T(8,128)S(1)} %shard_map.159.refs_1_), channel_id=1, source_target_pairs={{17,0},{16,1},{1,16},{0,17},{19,2},{18,3},{3,18},{2,19},{21,4},{20... | collective-permute-start | bytes 196616 | tf_op jit(solution)/shard_map/ppermute | solution.py:568
  15.9 4.3 %collective-permute-start.4 = (f32[4,2,16,128]{3,2,1,0:T(8,128)S(1)}, f32[4,2,16,128]{3,2,1,0:T(8,128)S(1)}, u32[]{:S(2)}, u32[]{:S(2)}) collective-permute-start(f32[4,2,16,128]{3,2,1,0:T(8,128)S(1)} %shard_map.159.refs_1_), channel_id=1, source_target_pairs={{16,0},{17,1},{0,16},{1,17},{18,2},{19,3},{2,18},{3,19},{20,4},{21... | collective-permute-start | bytes 196616 | tf_op jit(solution)/shard_map/ppermute | solution.py:568
  17.5 4.3 %collective-permute-start.3 = (f32[4,2,16,128]{3,2,1,0:T(8,128)S(1)}, f32[4,2,16,128]{3,2,1,0:T(8,128)S(1)}, u32[]{:S(2)}, u32[]{:S(2)}) collective-permute-start(f32[4,2,16,128]{3,2,1,0:T(8,128)S(1)} %shard_map.159.refs_1_), channel_id=1, source_target_pairs={{1,0},{0,1},{17,16},{16,17},{3,2},{2,3},{19,18},{18,19},{5,4},{4,5... | collective-permute-start | bytes 196616 | tf_op jit(solution)/shard_map/ppermute | solution.py:568
  22.1 13.5 %copy-start.3 = (f32[256,1024]{1,0:T(8,128)S(1)}, f32[256,1024]{1,0:T(8,128)}, u32[]{:S(2)}) copy-start(f32[256,1024]{1,0:T(8,128)} %refs_4_.2) | copy-start | bytes 3145732
  25.2 10.4 %all-to-all-start.1 = ((f32[16,8,256]{2,1,0:T(8,128)}), f32[16,8,256]{2,1,0:T(8,128)S(1)}, u32[]{:S(2)}, u32[]{:S(2)}) async-start(f32[16,8,256]{2,1,0:T(8,128)} %shard_map.160), calls=%async_computation.1 | async-start | bytes 262144 | tf_op jit(solution)/shard_map/all_to_all | solution.py:621
  41.5 11.3 %all-to-all-start.2 = ((f32[8,32,128]{2,1,0:T(8,128)}), f32[8,32,128]{2,1,0:T(8,128)S(1)}, u32[]{:S(2)}, u32[]{:S(2)}) async-start(f32[8,32,128]{2,1,0:T(8,128)} %get-tuple-element.40), calls=%async_computation.2 | async-start | bytes 262144 | tf_op jit(solution)/shard_map/all_to_all | solution.py:649
  45.7 4.9 %collective-permute-start.9 = (f32[128,128]{1,0:T(8,128)S(1)}, f32[128,128]{1,0:T(8,128)S(1)}, u32[]{:S(2)}, u32[]{:S(2)}) collective-permute-start(f32[128,128]{1,0:T(8,128)S(1)} %get-tuple-element.37), channel_id=1, source_target_pairs={{1,0},{0,1},{17,16},{16,17},{3,2},{2,3},{19,18},{18,19},{5,4},{4,5... | collective-permute-start | bytes 196616 | tf_op jit(solution)/shard_map/ppermute | solution.py:568
  46.4 6.4 %collective-permute-start.10 = (f32[128,128]{1,0:T(8,128)S(1)}, f32[128,128]{1,0:T(8,128)S(1)}, u32[]{:S(2)}, u32[]{:S(2)}) collective-permute-start(f32[128,128]{1,0:T(8,128)S(1)} %get-tuple-element.38), channel_id=1, source_target_pairs={{16,0},{17,1},{0,16},{1,17},{18,2},{19,3},{2,18},{3,19},{20,4},{21... | collective-permute-start | bytes 196616 | tf_op jit(solution)/shard_map/ppermute | solution.py:568
  46.4 6.4 %collective-permute-start.11 = (f32[128,128]{1,0:T(8,128)S(1)}, f32[128,128]{1,0:T(8,128)S(1)}, u32[]{:S(2)}, u32[]{:S(2)}) collective-permute-start(f32[128,128]{1,0:T(8,128)S(1)} %get-tuple-element.39), channel_id=1, source_target_pairs={{17,0},{16,1},{1,16},{0,17},{19,2},{18,3},{3,18},{2,19},{21,4},{20... | collective-permute-start | bytes 196616 | tf_op jit(solution)/shard_map/ppermute | solution.py:568
  48.6 4.3 %collective-permute-start.8 = (f32[32,128]{1,0:T(8,128)S(1)}, f32[32,128]{1,0:T(8,128)S(1)}, u32[]{:S(2)}, u32[]{:S(2)}) collective-permute-start(f32[32,128]{1,0:T(8,128)S(1)} %get-tuple-element.34.refs_0_), channel_id=1, source_target_pairs={{17,0},{16,1},{1,16},{0,17},{19,2},{18,3},{3,18},{2,19},{21,4},{20... | collective-permute-start | bytes 49160 | tf_op jit(solution)/shard_map/ppermute | solution.py:568
  48.9 3.9 %collective-permute-start.7 = (f32[32,128]{1,0:T(8,128)S(1)}, f32[32,128]{1,0:T(8,128)S(1)}, u32[]{:S(2)}, u32[]{:S(2)}) collective-permute-start(f32[32,128]{1,0:T(8,128)S(1)} %get-tuple-element.34.refs_0_), channel_id=1, source_target_pairs={{16,0},{17,1},{0,16},{1,17},{18,2},{19,3},{2,18},{3,19},{20,4},{21... | collective-permute-start | bytes 49160 | tf_op jit(solution)/shard_map/ppermute | solution.py:568
  50.6 3.7 %collective-permute-start.6 = (f32[32,128]{1,0:T(8,128)S(1)}, f32[32,128]{1,0:T(8,128)S(1)}, u32[]{:S(2)}, u32[]{:S(2)}) collective-permute-start(f32[32,128]{1,0:T(8,128)S(1)} %get-tuple-element.34.refs_0_), channel_id=1, source_target_pairs={{1,0},{0,1},{17,16},{16,17},{3,2},{2,3},{19,18},{18,19},{5,4},{4,5... | collective-permute-start | bytes 49160 | tf_op jit(solution)/shard_map/ppermute | solution.py:568
  58.4 21.9 %all-to-all-start.3 = ((f32[32,4,8,128]{3,2,1,0:T(8,128)}), f32[32,4,8,128]{3,2,1,0:T(8,128)S(1)}, u32[]{:S(2)}, u32[]{:S(2)}) async-start(f32[32,4,8,128]{3,2,1,0:T(8,128)} %get-tuple-element.47), calls=%async_computation.3 | async-start | bytes 1048576 | tf_op jit(solution)/shard_map/all_to_all | solution.py:695
  63.5 6.6 %collective-permute-start.12 = (f32[4,8,256]{2,1,0:T(8,128)S(1)}, f32[4,8,256]{2,1,0:T(8,128)S(1)}, u32[]{:S(2)}, u32[]{:S(2)}) collective-permute-start(f32[4,8,256]{2,1,0:T(8,128)S(1)} %get-tuple-element.49), channel_id=1, source_target_pairs={{1,0},{0,1},{17,16},{16,17},{3,2},{2,3},{19,18},{18,19},{5,4},{4,5... | collective-permute-start | bytes 98312 | tf_op jit(solution)/shard_map/ppermute | solution.py:568
  65.3 4.8 %collective-permute-start.13 = (f32[4,8,256]{2,1,0:T(8,128)S(1)}, f32[4,8,256]{2,1,0:T(8,128)S(1)}, u32[]{:S(2)}, u32[]{:S(2)}) collective-permute-start(f32[4,8,256]{2,1,0:T(8,128)S(1)} %get-tuple-element.50), channel_id=1, source_target_pairs={{16,0},{17,1},{0,16},{1,17},{18,2},{19,3},{2,18},{3,19},{20,4},{21... | collective-permute-start | bytes 98312 | tf_op jit(solution)/shard_map/ppermute | solution.py:568
  65.3 4.8 %collective-permute-start.14 = (f32[4,8,256]{2,1,0:T(8,128)S(1)}, f32[4,8,256]{2,1,0:T(8,128)S(1)}, u32[]{:S(2)}, u32[]{:S(2)}) collective-permute-start(f32[4,8,256]{2,1,0:T(8,128)S(1)} %get-tuple-element.51), channel_id=1, source_target_pairs={{17,0},{16,1},{1,16},{0,17},{19,2},{18,3},{3,18},{2,19},{21,4},{20... | collective-permute-start | bytes 98312 | tf_op jit(solution)/shard_map/ppermute | solution.py:568
  82.1 13.8 %all-to-all-start.4 = ((f32[32,16,128]{2,1,0:T(8,128)}), f32[32,16,128]{2,1,0:T(8,128)S(1)}, u32[]{:S(2)}, u32[]{:S(2)}) async-start(f32[32,16,128]{2,1,0:T(8,128)} %get-tuple-element.53), calls=%async_computation.4 | async-start | bytes 524288 | tf_op jit(solution)/shard_map/all_to_all | solution.py:703
  84.7 6.4 %collective-permute-start.15 = (f32[128,128]{1,0:T(8,128)S(1)}, f32[128,128]{1,0:T(8,128)S(1)}, u32[]{:S(2)}, u32[]{:S(2)}) collective-permute-start(f32[128,128]{1,0:T(8,128)S(1)} %get-tuple-element.55), channel_id=1, source_target_pairs={{1,0},{0,1},{17,16},{16,17},{3,2},{2,3},{19,18},{18,19},{5,4},{4,5... | collective-permute-start | bytes 196616 | tf_op jit(solution)/shard_map/ppermute | solution.py:568
  86.4 4.7 %collective-permute-start.16 = (f32[128,128]{1,0:T(8,128)S(1)}, f32[128,128]{1,0:T(8,128)S(1)}, u32[]{:S(2)}, u32[]{:S(2)}) collective-permute-start(f32[128,128]{1,0:T(8,128)S(1)} %get-tuple-element.56), channel_id=1, source_target_pairs={{16,0},{17,1},{0,16},{1,17},{18,2},{19,3},{2,18},{3,19},{20,4},{21... | collective-permute-start | bytes 196616 | tf_op jit(solution)/shard_map/ppermute | solution.py:568
  86.4 5.3 %collective-permute-start.17 = (f32[128,128]{1,0:T(8,128)S(1)}, f32[128,128]{1,0:T(8,128)S(1)}, u32[]{:S(2)}, u32[]{:S(2)}) collective-permute-start(f32[128,128]{1,0:T(8,128)S(1)} %get-tuple-element.57), channel_id=1, source_target_pairs={{17,0},{16,1},{1,16},{0,17},{19,2},{18,3},{3,18},{2,19},{21,4},{20... | collective-permute-start | bytes 196616 | tf_op jit(solution)/shard_map/ppermute | solution.py:568
  (14 other events, 56.3 us)

commit v13 on v11

--- a/solution.py
+++ b/solution.py
@@ -114,8 +114,8 @@
     work = {
         "bias_kernel": 2.0,
         "bias_part_kernel": 6.0,
-        "row_kernel": 4.5,
-        "pair_blocks_kernel": 8.0,
+        "row_kernel": 12.0,
+        "pair_blocks_kernel": 14.0,
         "column_kernel": 4.5,
         "msa_blocks_kernel": 0.5,
         "pair_kernel": 4.0,
@@ -648,6 +648,7 @@
     )
     pair = trade(pair, columns)
     right = lax.all_to_all(right, "gi", 0, 0, tiled=True)
+    right, *alignment = lax.optimization_barrier((right, *alignment))
     left = trade([left] * n_cols, columns)
     alignment = [block.reshape(-1, width) for block in trade(alignment, columns)]
     share = max(pair_width // n_all, 1)

time: 95 us -> 97.2 us (1.023)
  other arithmetic: 0.08 us -> 1.6 us
  waiting for transfers between devices: 35.2 us -> 36.2 us
    ppermute x18, starting transfers between devices: 16 us -> 14.3 us  [trade(): lax.ppermute(blocks[k], axes, [(t ^ k, t) for t in range(n) if t ^ k < n])]
    all_to_all x1, starting transfers between devices: 3.92 us -> 5.01 us  [per_device(): tri = lax.all_to_all(tri, everyone, 0, 0, tiled=True)]
    unnamed x41 -> x31, local copies, waits for them, and re-layouts: 2.12 us -> 2.1 us
  transfers between devices with their start and end apart: 23 -> 23, of which waited for: 13 -> 12; matrix products, arithmetic and copies ran while one was open for 2% -> 4% of each run, Pallas kernels for 6% -> 1%
where the time goes in v13:
time: 97.2 us; the launch traced here: 96.4 us
  waiting for transfers between devices  36.2 us (37%)
  starting transfers between devices  35.4 us (36%)
  Pallas kernels  17.9 us (18%)
  local copies, waits for them, and re-layouts  4.36 us (4%)
  other arithmetic  1.6 us (2%)
    pallas_call x9, Pallas kernels, call_near(): pl.pallas_call(lambda *refs: kernel(lambda: None, *refs), out_shape=[jax....  15.5 us
    ppermute x18, waiting for transfers between devices, trade(): lax.ppermute(blocks[k], axes, [(t ^ k, t) for t in range(n) if t ^ k < n])  15.4 us
    ppermute x18, starting transfers between devices, trade(): lax.ppermute(blocks[k], axes, [(t ^ k, t) for t in range(n) if t ^ k < n])  14.3 us
    all_to_all x1, waiting for transfers between devices, per_device(): tri = lax.all_to_all(tri, everyone, 0, 0, tiled=True)  10.2 us
    all_to_all x1, starting transfers between devices, per_device(): msa = lax.all_to_all(msa, 'gi', 0, 0, tiled=True)  6.15 us
    all_to_all x1, starting transfers between devices, per_device(): tri = lax.all_to_all(tri, everyone, 0, 0, tiled=True)  5.01 us
    all_to_all x1, starting transfers between devices, per_device(): lax.all_to_all(msa_first, everyone, 0, 0, tiled=True, axis_index_groups=h...  3.85 us
    all_to_all x1, waiting for transfers between devices, per_device(): product = lax.all_to_all(product, everyone, 0, 0, tiled=True)  3.73 us
  transfers between devices with their start and end apart: 23, of which 12 were waited for; matrix products, arithmetic and copies ran while one was open for 4% of the time, Pallas kernels for 1%

profile of v13, /device:TPU:0, one launch (start us, length us, event | category | flops | bytes accessed | tf_op | source)
XLA Modules:
  0.0 96.4 jit_solution(2278109360051674657)
XLA Ops:
  0.6 2.4 %shard_map.158 = (f32[16,16,256]{2,1,0:T(8,128)}, f32[2,16,128]{2,1,0:T(8,128)}) custom-call(f32[8,16,256]{2,1,0:T(8,128)} %refs_0_.2, f32[16,32,128]{2,1,0:T(8,128)} %refs_1_.3, f32[3,128]{1,0:T(4,128)} %refs_3_.3, f32[8,128]{1,0:T(8,128)} %bitcast.44), custom_call_target="tpu_custom_call" | custom-call | flops 2200000000 | bytes 7200000 | tf_op jit(solution)/shard_map/pallas_call | solution.py:154
  3.1 4.0 %collective-permute-start.2 = (f32[2,16,128]{2,1,0:T(8,128)}, f32[2,16,128]{2,1,0:T(8,128)S(1)}, u32[]{:S(2)}, u32[]{:S(2)}) collective-permute-start(f32[2,16,128]{2,1,0:T(8,128)} %get-tuple-element.32.refs_0_), channel_id=1, source_target_pairs={{6,0},{4,2},{2,4},{0,6},{14,8},{12,10},{10,12},{8,14},{7,1},{5,3},... | collective-permute-start | bytes 49160 | tf_op jit(solution)/shard_map/ppermute | solution.py:568
  7.8 6.1 %all-to-all-start = ((f32[16,16,256]{2,1,0:T(8,128)}), f32[16,16,256]{2,1,0:T(8,128)S(1)}, u32[]{:S(2)}, u32[]{:S(2)}) async-start(f32[16,16,256]{2,1,0:T(8,128)} %get-tuple-element.31), calls=%async_computation | async-start | bytes 524288 | tf_op jit(solution)/shard_map/all_to_all | solution.py:602
  14.9 1.6 %collective-permute-start.4 = (f32[4,2,16,128]{3,2,1,0:T(8,128)S(1)}, f32[4,2,16,128]{3,2,1,0:T(8,128)S(1)}, u32[]{:S(2)}, u32[]{:S(2)}) collective-permute-start(f32[4,2,16,128]{3,2,1,0:T(8,128)S(1)} %shard_map.159.refs_1_), channel_id=1, source_target_pairs={{16,0},{17,1},{0,16},{1,17},{18,2},{19,3},{2,18},{3,19},{20,4},{21... | collective-permute-start | bytes 196616 | tf_op jit(solution)/shard_map/ppermute | solution.py:568
  17.7 1.5 %collective-permute-done.5.refs_4_ = f32[4,2,16,128]{3,2,1,0:T(8,128)S(1)} collective-permute-done((f32[4,2,16,128]{3,2,1,0:T(8,128)S(1)}, f32[4,2,16,128]{3,2,1,0:T(8,128)S(1)}, u32[]{:S(2)}, u32[]{:S(2)}) %collective-permute-start.5) | collective-permute-done | bytes 65568 | tf_op jit(solution)/shard_map/ppermute | solution.py:568
  19.3 1.5 %collective-permute-done.3.refs_2_ = f32[4,2,16,128]{3,2,1,0:T(8,128)S(1)} collective-permute-done((f32[4,2,16,128]{3,2,1,0:T(8,128)S(1)}, f32[4,2,16,128]{3,2,1,0:T(8,128)S(1)}, u32[]{:S(2)}, u32[]{:S(2)}) %collective-permute-start.3) | collective-permute-done | bytes 65568 | tf_op jit(solution)/shard_map/ppermute | solution.py:568
  22.2 3.1 %shard_map.160 = f32[16,8,256]{2,1,0:T(8,128)} custom-call(f32[16,16,256]{2,1,0:T(8,128)S(1)} %all-to-all-done.refs_0_, f32[4,2,16,128]{3,2,1,0:T(8,128)S(1)} %shard_map.159.refs_1_, f32[4,2,16,128]{3,2,1,0:T(8,128)S(1)} %collective-permute-done.3.refs_2_, f32[4,2,16,128]{3,2,1,0:T(8,128)S(1)} %collective-permute-done.4.refs_3_, ...), custom_call_target="tpu_custom_call" | custom-call | flops 13200000000 | bytes 43200000 | tf_op jit(solution)/shard_map/pallas_call | solution.py:167
  25.3 3.9 %all-to-all-start.1 = ((f32[16,8,256]{2,1,0:T(8,128)}), f32[16,8,256]{2,1,0:T(8,128)S(1)}, u32[]{:S(2)}, u32[]{:S(2)}) async-start(f32[16,8,256]{2,1,0:T(8,128)} %shard_map.160), calls=%async_computation.1 | async-start | bytes 262144 | tf_op jit(solution)/shard_map/all_to_all | solution.py:621
  31.7 3.6 %all-to-all-done.1 = f32[16,8,256]{2,1,0:T(8,128)S(1)} async-done(((f32[16,8,256]{2,1,0:T(8,128)}), f32[16,8,256]{2,1,0:T(8,128)S(1)}, u32[]{:S(2)}, u32[]{:S(2)}) %all-to-all-start.1) | async-done | bytes 131104 | tf_op jit(solution)/shard_map/all_to_all | solution.py:621
  36.5 4.6 %shard_map.161 = (f32[32,128]{1,0:T(8,128)S(1)}, f32[8,32,128]{2,1,0:T(8,128)}, f32[128,256]{1,0:T(8,128)S(1)}) custom-call(f32[128,256]{1,0:T(8,128)S(1)} %bitcast.28, f32[4,256]{1,0:T(4,128)S(1)} %copy-done.11, f32[256,1024]{1,0:T(8,128)S(1)} %copy-done.2, f32[256,256]{1,0:T(8,128)S(1)} %copy-done.6, f32[256,1024]{1,0:T(8,128)S(1)} %copy-done.3, ...), custom_call_target="tpu_custom_call" | custom-call | flops 4950000128 | bytes 16200000 | tf_op jit(solution)/shard_map/pallas_call | solution.py:167
  41.2 3.5 %all-to-all-start.2 = ((f32[8,32,128]{2,1,0:T(8,128)}), f32[8,32,128]{2,1,0:T(8,128)S(1)}, u32[]{:S(2)}, u32[]{:S(2)}) async-start(f32[8,32,128]{2,1,0:T(8,128)} %get-tuple-element.40), calls=%async_computation.2 | async-start | bytes 262144 | tf_op jit(solution)/shard_map/all_to_all | solution.py:650
  45.6 1.6 %collective-permute-start.11 = (f32[128,128]{1,0:T(8,128)S(1)}, f32[128,128]{1,0:T(8,128)S(1)}, u32[]{:S(2)}, u32[]{:S(2)}) collective-permute-start(f32[128,128]{1,0:T(8,128)S(1)} %get-tuple-element.39), channel_id=1, source_target_pairs={{17,0},{16,1},{1,16},{0,17},{19,2},{18,3},{3,18},{2,19},{21,4},{20... | collective-permute-start | bytes 196616 | tf_op jit(solution)/shard_map/ppermute | solution.py:568
  50.0 1.9 %all-to-all-done.2 = f32[8,32,128]{2,1,0:T(8,128)S(1)} async-done(((f32[8,32,128]{2,1,0:T(8,128)}), f32[8,32,128]{2,1,0:T(8,128)S(1)}, u32[]{:S(2)}, u32[]{:S(2)}) %all-to-all-start.2) | async-done | bytes 131104 | tf_op jit(solution)/shard_map/all_to_all | solution.py:650
  52.0 1.7 %collective-permute-done.6.refs_1_ = f32[32,128]{1,0:T(8,128)S(1)} collective-permute-done((f32[32,128]{1,0:T(8,128)S(1)}, f32[32,128]{1,0:T(8,128)S(1)}, u32[]{:S(2)}, u32[]{:S(2)}) %collective-permute-start.6) | collective-permute-done | bytes 16416 | tf_op jit(solution)/shard_map/ppermute | solution.py:568
  53.7 4.0 %shard_map.164 = (f32[32,4,8,128]{3,2,1,0:T(8,128)}, f32[128,128]{1,0:T(8,128)S(1)}, f32[128,128]{1,0:T(8,128)S(1)}, f32[128,128]{1,0:T(8,128)S(1)}, f32[128,128]{1,0:T(8,128)S(1)}) custom-call(f32[32,128]{1,0:T(8,128)S(1)} %get-tuple-element.34.refs_0_, f32[32,128]{1,0:T(8,128)S(1)} %collective-permute-done.6.refs_1_, ...), custom_call_target="tpu_custom_call" | custom-call | flops 4400000000 | bytes 14400000 | tf_op jit(solution)/shard_map/pallas_call | solution.py:167
  57.7 5.0 %all-to-all-start.3 = ((f32[32,4,8,128]{3,2,1,0:T(8,128)}), f32[32,4,8,128]{3,2,1,0:T(8,128)S(1)}, u32[]{:S(2)}, u32[]{:S(2)}) async-start(f32[32,4,8,128]{3,2,1,0:T(8,128)} %get-tuple-element.47), calls=%async_computation.3 | async-start | bytes 1048576 | tf_op jit(solution)/shard_map/all_to_all | solution.py:696
  62.8 1.8 %collective-permute-start.12 = (f32[4,8,256]{2,1,0:T(8,128)S(1)}, f32[4,8,256]{2,1,0:T(8,128)S(1)}, u32[]{:S(2)}, u32[]{:S(2)}) collective-permute-start(f32[4,8,256]{2,1,0:T(8,128)S(1)} %get-tuple-element.49), channel_id=1, source_target_pairs={{1,0},{0,1},{17,16},{16,17},{3,2},{2,3},{19,18},{18,19},{5,4},{4,5... | collective-permute-start | bytes 98312 | tf_op jit(solution)/shard_map/ppermute | solution.py:568
  65.0 4.4 %collective-permute-done.12 = f32[4,8,256]{2,1,0:T(8,128)S(1)} collective-permute-done((f32[4,8,256]{2,1,0:T(8,128)S(1)}, f32[4,8,256]{2,1,0:T(8,128)S(1)}, u32[]{:S(2)}, u32[]{:S(2)}) %collective-permute-start.12) | collective-permute-done | bytes 32800 | tf_op jit(solution)/shard_map/ppermute | solution.py:568
  69.4 10.2 %all-to-all-done.3 = f32[32,4,8,128]{3,2,1,0:T(8,128)S(1)} async-done(((f32[32,4,8,128]{3,2,1,0:T(8,128)}), f32[32,4,8,128]{3,2,1,0:T(8,128)S(1)}, u32[]{:S(2)}, u32[]{:S(2)}) %all-to-all-start.3) | async-done | bytes 524320 | tf_op jit(solution)/shard_map/all_to_all | solution.py:696
  79.6 1.7 %shard_map.165 = (f32[32,16,128]{2,1,0:T(8,128)}, f32[8,16,256]{2,1,0:T(8,128)}) custom-call(f32[1024,128]{1,0:T(8,128)S(1)} %bitcast.25, f32[32,256]{1,0:T(8,128)S(1)} %bitcast.34, f32[32,256]{1,0:T(8,128)S(1)} %bitcast.31, f32[32,256]{1,0:T(8,128)S(1)} %bitcast.32, f32[32,256]{1,0:T(8,128)S(1)} %bitcast.33), custom_call_target="tpu_custom_call" | custom-call | flops 2200000000 | bytes 7200000 | tf_op jit(solution)/shard_map/pallas_call | solution.py:167
  81.3 2.6 %all-to-all-start.4 = ((f32[32,16,128]{2,1,0:T(8,128)}), f32[32,16,128]{2,1,0:T(8,128)S(1)}, u32[]{:S(2)}, u32[]{:S(2)}) async-start(f32[32,16,128]{2,1,0:T(8,128)} %get-tuple-element.53), calls=%async_computation.4 | async-start | bytes 524288 | tf_op jit(solution)/shard_map/all_to_all | solution.py:704
  83.9 1.7 %collective-permute-start.15 = (f32[128,128]{1,0:T(8,128)S(1)}, f32[128,128]{1,0:T(8,128)S(1)}, u32[]{:S(2)}, u32[]{:S(2)}) collective-permute-start(f32[128,128]{1,0:T(8,128)S(1)} %get-tuple-element.55), channel_id=1, source_target_pairs={{1,0},{0,1},{17,16},{16,17},{3,2},{2,3},{19,18},{18,19},{5,4},{4,5... | collective-permute-start | bytes 196616 | tf_op jit(solution)/shard_map/ppermute | solution.py:568
  86.1 4.2 %collective-permute-done.15.refs_3_ = f32[128,128]{1,0:T(8,128)S(1)} collective-permute-done((f32[128,128]{1,0:T(8,128)S(1)}, f32[128,128]{1,0:T(8,128)S(1)}, u32[]{:S(2)}, u32[]{:S(2)}) %collective-permute-start.15) | collective-permute-done | bytes 65568 | tf_op jit(solution)/shard_map/ppermute | solution.py:568
  91.4 3.7 %all-to-all-done.4 = f32[32,16,128]{2,1,0:T(8,128)S(1)} async-done(((f32[32,16,128]{2,1,0:T(8,128)}), f32[32,16,128]{2,1,0:T(8,128)S(1)}, u32[]{:S(2)}, u32[]{:S(2)}) %all-to-all-start.4) | async-done | bytes 262176 | tf_op jit(solution)/shard_map/all_to_all | solution.py:704
  (73 shorter events, 14.9 us)
Async XLA Ops:
  3.1 11.7 %collective-permute-start.2 = (f32[2,16,128]{2,1,0:T(8,128)}, f32[2,16,128]{2,1,0:T(8,128)S(1)}, u32[]{:S(2)}, u32[]{:S(2)}) collective-permute-start(f32[2,16,128]{2,1,0:T(8,128)} %get-tuple-element.32.refs_0_), channel_id=1, source_target_pairs={{6,0},{4,2},{2,4},{0,6},{14,8},{12,10},{10,12},{8,14},{7,1},{5,3},... | collective-permute-start | bytes 49160 | tf_op jit(solution)/shard_map/ppermute | solution.py:568
  7.1 7.7 %collective-permute-start.1 = (f32[2,16,128]{2,1,0:T(8,128)}, f32[2,16,128]{2,1,0:T(8,128)S(1)}, u32[]{:S(2)}, u32[]{:S(2)}) collective-permute-start(f32[2,16,128]{2,1,0:T(8,128)} %get-tuple-element.32.refs_0_), channel_id=1, source_target_pairs={{4,0},{6,2},{0,4},{2,6},{12,8},{14,10},{8,12},{10,14},{5,1},{7,3},... | collective-permute-start | bytes 49160 | tf_op jit(solution)/shard_map/ppermute | solution.py:568
  7.6 7.2 %collective-permute-start = (f32[2,16,128]{2,1,0:T(8,128)}, f32[2,16,128]{2,1,0:T(8,128)S(1)}, u32[]{:S(2)}, u32[]{:S(2)}) collective-permute-start(f32[2,16,128]{2,1,0:T(8,128)} %get-tuple-element.32.refs_0_), channel_id=1, source_target_pairs={{2,0},{0,2},{6,4},{4,6},{10,8},{8,10},{14,12},{12,14},{3,1},{1,3},... | collective-permute-start | bytes 49160 | tf_op jit(solution)/shard_map/ppermute | solution.py:568
  7.8 14.4 %all-to-all-start = ((f32[16,16,256]{2,1,0:T(8,128)}), f32[16,16,256]{2,1,0:T(8,128)S(1)}, u32[]{:S(2)}, u32[]{:S(2)}) async-start(f32[16,16,256]{2,1,0:T(8,128)} %get-tuple-element.31), calls=%async_computation | async-start | bytes 524288 | tf_op jit(solution)/shard_map/all_to_all | solution.py:602
  14.8 4.4 %collective-permute-start.5 = (f32[4,2,16,128]{3,2,1,0:T(8,128)S(1)}, f32[4,2,16,128]{3,2,1,0:T(8,128)S(1)}, u32[]{:S(2)}, u32[]{:S(2)}) collective-permute-start(f32[4,2,16,128]{3,2,1,0:T(8,128)S(1)} %shard_map.159.refs_1_), channel_id=1, source_target_pairs={{17,0},{16,1},{1,16},{0,17},{19,2},{18,3},{3,18},{2,19},{21,4},{20... | collective-permute-start | bytes 196616 | tf_op jit(solution)/shard_map/ppermute | solution.py:568
  14.9 4.3 %collective-permute-start.4 = (f32[4,2,16,128]{3,2,1,0:T(8,128)S(1)}, f32[4,2,16,128]{3,2,1,0:T(8,128)S(1)}, u32[]{:S(2)}, u32[]{:S(2)}) collective-permute-start(f32[4,2,16,128]{3,2,1,0:T(8,128)S(1)} %shard_map.159.refs_1_), channel_id=1, source_target_pairs={{16,0},{17,1},{0,16},{1,17},{18,2},{19,3},{2,18},{3,19},{20,4},{21... | collective-permute-start | bytes 196616 | tf_op jit(solution)/shard_map/ppermute | solution.py:568
  16.5 4.3 %collective-permute-start.3 = (f32[4,2,16,128]{3,2,1,0:T(8,128)S(1)}, f32[4,2,16,128]{3,2,1,0:T(8,128)S(1)}, u32[]{:S(2)}, u32[]{:S(2)}) collective-permute-start(f32[4,2,16,128]{3,2,1,0:T(8,128)S(1)} %shard_map.159.refs_1_), channel_id=1, source_target_pairs={{1,0},{0,1},{17,16},{16,17},{3,2},{2,3},{19,18},{18,19},{5,4},{4,5... | collective-permute-start | bytes 196616 | tf_op jit(solution)/shard_map/ppermute | solution.py:568
  22.1 13.2 %copy-start.3 = (f32[256,1024]{1,0:T(8,128)S(1)}, f32[256,1024]{1,0:T(8,128)}, u32[]{:S(2)}) copy-start(f32[256,1024]{1,0:T(8,128)} %refs_4_.2) | copy-start | bytes 3145732
  25.3 10.0 %all-to-all-start.1 = ((f32[16,8,256]{2,1,0:T(8,128)}), f32[16,8,256]{2,1,0:T(8,128)S(1)}, u32[]{:S(2)}, u32[]{:S(2)}) async-start(f32[16,8,256]{2,1,0:T(8,128)} %shard_map.160), calls=%async_computation.1 | async-start | bytes 262144 | tf_op jit(solution)/shard_map/all_to_all | solution.py:621
  41.2 10.8 %all-to-all-start.2 = ((f32[8,32,128]{2,1,0:T(8,128)}), f32[8,32,128]{2,1,0:T(8,128)S(1)}, u32[]{:S(2)}, u32[]{:S(2)}) async-start(f32[8,32,128]{2,1,0:T(8,128)} %get-tuple-element.40), calls=%async_computation.2 | async-start | bytes 262144 | tf_op jit(solution)/shard_map/all_to_all | solution.py:650
  44.9 5.0 %collective-permute-start.9 = (f32[128,128]{1,0:T(8,128)S(1)}, f32[128,128]{1,0:T(8,128)S(1)}, u32[]{:S(2)}, u32[]{:S(2)}) collective-permute-start(f32[128,128]{1,0:T(8,128)S(1)} %get-tuple-element.37), channel_id=1, source_target_pairs={{1,0},{0,1},{17,16},{16,17},{3,2},{2,3},{19,18},{18,19},{5,4},{4,5... | collective-permute-start | bytes 196616 | tf_op jit(solution)/shard_map/ppermute | solution.py:568
  45.6 6.4 %collective-permute-start.10 = (f32[128,128]{1,0:T(8,128)S(1)}, f32[128,128]{1,0:T(8,128)S(1)}, u32[]{:S(2)}, u32[]{:S(2)}) collective-permute-start(f32[128,128]{1,0:T(8,128)S(1)} %get-tuple-element.38), channel_id=1, source_target_pairs={{16,0},{17,1},{0,16},{1,17},{18,2},{19,3},{2,18},{3,19},{20,4},{21... | collective-permute-start | bytes 196616 | tf_op jit(solution)/shard_map/ppermute | solution.py:568
  45.6 6.4 %collective-permute-start.11 = (f32[128,128]{1,0:T(8,128)S(1)}, f32[128,128]{1,0:T(8,128)S(1)}, u32[]{:S(2)}, u32[]{:S(2)}) collective-permute-start(f32[128,128]{1,0:T(8,128)S(1)} %get-tuple-element.39), channel_id=1, source_target_pairs={{17,0},{16,1},{1,16},{0,17},{19,2},{18,3},{3,18},{2,19},{21,4},{20... | collective-permute-start | bytes 196616 | tf_op jit(solution)/shard_map/ppermute | solution.py:568
  47.8 4.2 %collective-permute-start.8 = (f32[32,128]{1,0:T(8,128)S(1)}, f32[32,128]{1,0:T(8,128)S(1)}, u32[]{:S(2)}, u32[]{:S(2)}) collective-permute-start(f32[32,128]{1,0:T(8,128)S(1)} %get-tuple-element.34.refs_0_), channel_id=1, source_target_pairs={{17,0},{16,1},{1,16},{0,17},{19,2},{18,3},{3,18},{2,19},{21,4},{20... | collective-permute-start | bytes 49160 | tf_op jit(solution)/shard_map/ppermute | solution.py:568
  48.0 3.9 %collective-permute-start.7 = (f32[32,128]{1,0:T(8,128)S(1)}, f32[32,128]{1,0:T(8,128)S(1)}, u32[]{:S(2)}, u32[]{:S(2)}) collective-permute-start(f32[32,128]{1,0:T(8,128)S(1)} %get-tuple-element.34.refs_0_), channel_id=1, source_target_pairs={{16,0},{17,1},{0,16},{1,17},{18,2},{19,3},{2,18},{3,19},{20,4},{21... | collective-permute-start | bytes 49160 | tf_op jit(solution)/shard_map/ppermute | solution.py:568
  50.0 3.7 %collective-permute-start.6 = (f32[32,128]{1,0:T(8,128)S(1)}, f32[32,128]{1,0:T(8,128)S(1)}, u32[]{:S(2)}, u32[]{:S(2)}) collective-permute-start(f32[32,128]{1,0:T(8,128)S(1)} %get-tuple-element.34.refs_0_), channel_id=1, source_target_pairs={{1,0},{0,1},{17,16},{16,17},{3,2},{2,3},{19,18},{18,19},{5,4},{4,5... | collective-permute-start | bytes 49160 | tf_op jit(solution)/shard_map/ppermute | solution.py:568
  57.7 21.8 %all-to-all-start.3 = ((f32[32,4,8,128]{3,2,1,0:T(8,128)}), f32[32,4,8,128]{3,2,1,0:T(8,128)S(1)}, u32[]{:S(2)}, u32[]{:S(2)}) async-start(f32[32,4,8,128]{3,2,1,0:T(8,128)} %get-tuple-element.47), calls=%async_computation.3 | async-start | bytes 1048576 | tf_op jit(solution)/shard_map/all_to_all | solution.py:696
  62.8 6.6 %collective-permute-start.12 = (f32[4,8,256]{2,1,0:T(8,128)S(1)}, f32[4,8,256]{2,1,0:T(8,128)S(1)}, u32[]{:S(2)}, u32[]{:S(2)}) collective-permute-start(f32[4,8,256]{2,1,0:T(8,128)S(1)} %get-tuple-element.49), channel_id=1, source_target_pairs={{1,0},{0,1},{17,16},{16,17},{3,2},{2,3},{19,18},{18,19},{5,4},{4,5... | collective-permute-start | bytes 98312 | tf_op jit(solution)/shard_map/ppermute | solution.py:568
  64.6 4.8 %collective-permute-start.13 = (f32[4,8,256]{2,1,0:T(8,128)S(1)}, f32[4,8,256]{2,1,0:T(8,128)S(1)}, u32[]{:S(2)}, u32[]{:S(2)}) collective-permute-start(f32[4,8,256]{2,1,0:T(8,128)S(1)} %get-tuple-element.50), channel_id=1, source_target_pairs={{16,0},{17,1},{0,16},{1,17},{18,2},{19,3},{2,18},{3,19},{20,4},{21... | collective-permute-start | bytes 98312 | tf_op jit(solution)/shard_map/ppermute | solution.py:568
  64.6 4.8 %collective-permute-start.14 = (f32[4,8,256]{2,1,0:T(8,128)S(1)}, f32[4,8,256]{2,1,0:T(8,128)S(1)}, u32[]{:S(2)}, u32[]{:S(2)}) collective-permute-start(f32[4,8,256]{2,1,0:T(8,128)S(1)} %get-tuple-element.51), channel_id=1, source_target_pairs={{17,0},{16,1},{1,16},{0,17},{19,2},{18,3},{3,18},{2,19},{21,4},{20... | collective-permute-start | bytes 98312 | tf_op jit(solution)/shard_map/ppermute | solution.py:568
  81.3 13.8 %all-to-all-start.4 = ((f32[32,16,128]{2,1,0:T(8,128)}), f32[32,16,128]{2,1,0:T(8,128)S(1)}, u32[]{:S(2)}, u32[]{:S(2)}) async-start(f32[32,16,128]{2,1,0:T(8,128)} %get-tuple-element.53), calls=%async_computation.4 | async-start | bytes 524288 | tf_op jit(solution)/shard_map/all_to_all | solution.py:704
  83.9 6.4 %collective-permute-start.15 = (f32[128,128]{1,0:T(8,128)S(1)}, f32[128,128]{1,0:T(8,128)S(1)}, u32[]{:S(2)}, u32[]{:S(2)}) collective-permute-start(f32[128,128]{1,0:T(8,128)S(1)} %get-tuple-element.55), channel_id=1, source_target_pairs={{1,0},{0,1},{17,16},{16,17},{3,2},{2,3},{19,18},{18,19},{5,4},{4,5... | collective-permute-start | bytes 196616 | tf_op jit(solution)/shard_map/ppermute | solution.py:568
  85.6 4.7 %collective-permute-start.16 = (f32[128,128]{1,0:T(8,128)S(1)}, f32[128,128]{1,0:T(8,128)S(1)}, u32[]{:S(2)}, u32[]{:S(2)}) collective-permute-start(f32[128,128]{1,0:T(8,128)S(1)} %get-tuple-element.56), channel_id=1, source_target_pairs={{16,0},{17,1},{0,16},{1,17},{18,2},{19,3},{2,18},{3,19},{20,4},{21... | collective-permute-start | bytes 196616 | tf_op jit(solution)/shard_map/ppermute | solution.py:568
  85.6 5.3 %collective-permute-start.17 = (f32[128,128]{1,0:T(8,128)S(1)}, f32[128,128]{1,0:T(8,128)S(1)}, u32[]{:S(2)}, u32[]{:S(2)}) collective-permute-start(f32[128,128]{1,0:T(8,128)S(1)} %get-tuple-element.57), channel_id=1, source_target_pairs={{17,0},{16,1},{1,16},{0,17},{19,2},{18,3},{3,18},{2,19},{21,4},{20... | collective-permute-start | bytes 196616 | tf_op jit(solution)/shard_map/ppermute | solution.py:568
  (14 other events, 82.1 us)

commit v14 on v11

--- a/solution.py
+++ b/solution.py
@@ -628,6 +628,14 @@
         feedforward_shrink_kernel,
         dyadic_sides_kernel.T,
     )
+    pair = call_near(
+        functools.partial(pair_blocks_kernel, few, residues),
+        [(positions // n_cols, pair_width)] * n_cols,
+        pair.reshape(positions, pair_width),
+        scratch=[(positions, pair_width)],
+    )
+    msa_first, _ = lax.optimization_barrier((msa_first, pair[0]))
+    pair = trade(pair, columns)
     left, right, alignment = call_near(
         functools.partial(column_kernel, few, heads),
         [(outer_width, count), (n_gi, outer_width, count), (count, width)],
@@ -640,14 +648,8 @@
         alignment,
         scratch=[(n_cols, per_part, each, width)],
     )
-    pair = call_near(
-        functools.partial(pair_blocks_kernel, few, residues),
-        [(positions // n_cols, pair_width)] * n_cols,
-        pair.reshape(positions, pair_width),
-        scratch=[(positions, pair_width)],
-    )
-    pair = trade(pair, columns)
     right = lax.all_to_all(right, "gi", 0, 0, tiled=True)
+    right, _ = lax.optimization_barrier((right, alignment[0]))
     left = trade([left] * n_cols, columns)
     alignment = [block.reshape(-1, width) for block in trade(alignment, columns)]
     share = max(pair_width // n_all, 1)

time: 95 us -> 98.7 us (1.039)
  waiting for transfers between devices: 35.2 us -> 36.8 us
  other arithmetic: 0.08 us -> 1.58 us
    all_to_all x1, waiting for transfers between devices: 3.94 us -> 5.9 us  [per_device(): lax.all_to_all(msa_first, everyone, 0, 0, tiled=True, axis_index_groups=h...]
    all_to_all x1, starting transfers between devices: 3.92 us -> 5.35 us  [per_device(): tri = lax.all_to_all(tri, everyone, 0, 0, tiled=True)]
    unnamed x41 -> x39, local copies, waits for them, and re-layouts: 2.12 us -> 2.98 us
  transfers between devices with their start and end apart: 23 -> 23, of which waited for: 13 -> 13; matrix products, arithmetic and copies ran while one was open for 2% -> 3% of each run, Pallas kernels for 6% -> 1%
where the time goes in v14:
time: 98.7 us; the launch traced here: 98 us
  waiting for transfers between devices  36.8 us (37%)
  starting transfers between devices  36.5 us (37%)
  Pallas kernels  17.9 us (18%)
  local copies, waits for them, and re-layouts  4.32 us (4%)
  other arithmetic  1.58 us (2%)
    pallas_call x9, Pallas kernels, call_near(): pl.pallas_call(lambda *refs: kernel(lambda: None, *refs), out_shape=[jax....  15.5 us
    ppermute x18, waiting for transfers between devices, trade(): lax.ppermute(blocks[k], axes, [(t ^ k, t) for t in range(n) if t ^ k < n])  15.3 us
    ppermute x18, starting transfers between devices, trade(): lax.ppermute(blocks[k], axes, [(t ^ k, t) for t in range(n) if t ^ k < n])  15.2 us
    all_to_all x1, waiting for transfers between devices, per_device(): tri = lax.all_to_all(tri, everyone, 0, 0, tiled=True)  10.2 us
    all_to_all x1, starting transfers between devices, per_device(): msa = lax.all_to_all(msa, 'gi', 0, 0, tiled=True)  6.15 us
    all_to_all x1, waiting for transfers between devices, per_device(): lax.all_to_all(msa_first, everyone, 0, 0, tiled=True, axis_index_groups=h...  5.9 us
    all_to_all x1, starting transfers between devices, per_device(): tri = lax.all_to_all(tri, everyone, 0, 0, tiled=True)  5.35 us
    all_to_all x1, starting transfers between devices, per_device(): lax.all_to_all(msa_first, everyone, 0, 0, tiled=True, axis_index_groups=h...  3.86 us
  transfers between devices with their start and end apart: 23, of which 13 were waited for; matrix products, arithmetic and copies ran while one was open for 3% of the time, Pallas kernels for 1%

profile of v14, /device:TPU:0, one launch (start us, length us, event | category | flops | bytes accessed | tf_op | source)
XLA Modules:
  0.0 98.0 jit_solution(7495849896630373454)
XLA Ops:
  0.6 2.4 %shard_map.158 = (f32[16,16,256]{2,1,0:T(8,128)}, f32[2,16,128]{2,1,0:T(8,128)}) custom-call(f32[8,16,256]{2,1,0:T(8,128)} %refs_0_.2, f32[16,32,128]{2,1,0:T(8,128)} %refs_1_.3, f32[3,128]{1,0:T(4,128)} %refs_3_.3, f32[8,128]{1,0:T(8,128)} %bitcast.44), custom_call_target="tpu_custom_call" | custom-call | flops 2200000000 | bytes 7200000 | tf_op jit(solution)/shard_map/pallas_call | solution.py:154
  3.1 4.0 %collective-permute-start.2 = (f32[2,16,128]{2,1,0:T(8,128)}, f32[2,16,128]{2,1,0:T(8,128)S(1)}, u32[]{:S(2)}, u32[]{:S(2)}) collective-permute-start(f32[2,16,128]{2,1,0:T(8,128)} %get-tuple-element.29.refs_0_), channel_id=1, source_target_pairs={{6,0},{4,2},{2,4},{0,6},{14,8},{12,10},{10,12},{8,14},{7,1},{5,3},... | collective-permute-start | bytes 49160 | tf_op jit(solution)/shard_map/ppermute | solution.py:568
  7.8 6.1 %all-to-all-start = ((f32[16,16,256]{2,1,0:T(8,128)}), f32[16,16,256]{2,1,0:T(8,128)S(1)}, u32[]{:S(2)}, u32[]{:S(2)}) async-start(f32[16,16,256]{2,1,0:T(8,128)} %get-tuple-element.28), calls=%async_computation | async-start | bytes 524288 | tf_op jit(solution)/shard_map/all_to_all | solution.py:602
  14.9 1.6 %collective-permute-start.4 = (f32[4,2,16,128]{3,2,1,0:T(8,128)S(1)}, f32[4,2,16,128]{3,2,1,0:T(8,128)S(1)}, u32[]{:S(2)}, u32[]{:S(2)}) collective-permute-start(f32[4,2,16,128]{3,2,1,0:T(8,128)S(1)} %shard_map.159.refs_1_), channel_id=1, source_target_pairs={{16,0},{17,1},{0,16},{1,17},{18,2},{19,3},{2,18},{3,19},{20,4},{21... | collective-permute-start | bytes 196616 | tf_op jit(solution)/shard_map/ppermute | solution.py:568
  17.8 1.5 %collective-permute-done.5.refs_4_ = f32[4,2,16,128]{3,2,1,0:T(8,128)S(1)} collective-permute-done((f32[4,2,16,128]{3,2,1,0:T(8,128)S(1)}, f32[4,2,16,128]{3,2,1,0:T(8,128)S(1)}, u32[]{:S(2)}, u32[]{:S(2)}) %collective-permute-start.5) | collective-permute-done | bytes 65568 | tf_op jit(solution)/shard_map/ppermute | solution.py:568
  19.3 1.5 %collective-permute-done.3.refs_2_ = f32[4,2,16,128]{3,2,1,0:T(8,128)S(1)} collective-permute-done((f32[4,2,16,128]{3,2,1,0:T(8,128)S(1)}, f32[4,2,16,128]{3,2,1,0:T(8,128)S(1)}, u32[]{:S(2)}, u32[]{:S(2)}) %collective-permute-start.3) | collective-permute-done | bytes 65568 | tf_op jit(solution)/shard_map/ppermute | solution.py:568
  20.8 1.3 %all-to-all-done.refs_0_ = f32[16,16,256]{2,1,0:T(8,128)S(1)} async-done(((f32[16,16,256]{2,1,0:T(8,128)}), f32[16,16,256]{2,1,0:T(8,128)S(1)}, u32[]{:S(2)}, u32[]{:S(2)}) %all-to-all-start) | async-done | bytes 262176 | tf_op jit(solution)/shard_map/all_to_all | solution.py:602
  22.1 3.1 %shard_map.160 = f32[16,8,256]{2,1,0:T(8,128)} custom-call(f32[16,16,256]{2,1,0:T(8,128)S(1)} %all-to-all-done.refs_0_, f32[4,2,16,128]{3,2,1,0:T(8,128)S(1)} %shard_map.159.refs_1_, f32[4,2,16,128]{3,2,1,0:T(8,128)S(1)} %collective-permute-done.3.refs_2_, f32[4,2,16,128]{3,2,1,0:T(8,128)S(1)} %collective-permute-done.4.refs_3_, ...), custom_call_target="tpu_custom_call" | custom-call | flops 4950000128 | bytes 16200000 | tf_op jit(solution)/shard_map/pallas_call | solution.py:167
  25.2 3.9 %all-to-all-start.1 = ((f32[16,8,256]{2,1,0:T(8,128)}), f32[16,8,256]{2,1,0:T(8,128)S(1)}, u32[]{:S(2)}, u32[]{:S(2)}) async-start(f32[16,8,256]{2,1,0:T(8,128)} %shard_map.160), calls=%async_computation.1 | async-start | bytes 262144 | tf_op jit(solution)/shard_map/all_to_all | solution.py:621
  29.4 5.9 %all-to-all-done.1 = f32[16,8,256]{2,1,0:T(8,128)S(1)} async-done(((f32[16,8,256]{2,1,0:T(8,128)}), f32[16,8,256]{2,1,0:T(8,128)S(1)}, u32[]{:S(2)}, u32[]{:S(2)}) %all-to-all-start.1) | async-done | bytes 131104 | tf_op jit(solution)/shard_map/all_to_all | solution.py:621
  36.5 4.6 %shard_map.162 = (f32[32,128]{1,0:T(8,128)S(1)}, f32[8,32,128]{2,1,0:T(8,128)}, f32[128,256]{1,0:T(8,128)S(1)}) custom-call(f32[128,256]{1,0:T(8,128)S(1)} %bitcast.28, f32[4,256]{1,0:T(4,128)S(1)} %copy-done.11, f32[256,1024]{1,0:T(8,128)S(1)} %copy-done.2, f32[256,256]{1,0:T(8,128)S(1)} %copy-done.7, f32[256,1024]{1,0:T(8,128)S(1)} %copy-done.3, ...), custom_call_target="tpu_custom_call" | custom-call | flops 4950000128 | bytes 16200000 | tf_op jit(solution)/shard_map/pallas_call | solution.py:167
  41.8 3.4 %all-to-all-start.2 = ((f32[8,32,128]{2,1,0:T(8,128)}), f32[8,32,128]{2,1,0:T(8,128)S(1)}, u32[]{:S(2)}, u32[]{:S(2)}) async-start(f32[8,32,128]{2,1,0:T(8,128)} %get-tuple-element.38), calls=%async_computation.2 | async-start | bytes 262144 | tf_op jit(solution)/shard_map/all_to_all | solution.py:651
  46.8 1.6 %collective-permute-start.11 = (f32[128,128]{1,0:T(8,128)S(1)}, f32[128,128]{1,0:T(8,128)S(1)}, u32[]{:S(2)}, u32[]{:S(2)}) collective-permute-start(f32[128,128]{1,0:T(8,128)S(1)} %get-tuple-element.37), channel_id=1, source_target_pairs={{17,0},{16,1},{1,16},{0,17},{19,2},{18,3},{3,18},{2,19},{21,4},{20... | collective-permute-start | bytes 196616 | tf_op jit(solution)/shard_map/ppermute | solution.py:568
  53.1 1.8 %collective-permute-done.6.refs_1_ = f32[32,128]{1,0:T(8,128)S(1)} collective-permute-done((f32[32,128]{1,0:T(8,128)S(1)}, f32[32,128]{1,0:T(8,128)S(1)}, u32[]{:S(2)}, u32[]{:S(2)}) %collective-permute-start.6) | collective-permute-done | bytes 16416 | tf_op jit(solution)/shard_map/ppermute | solution.py:568
  54.9 4.0 %shard_map.164 = (f32[32,4,8,128]{3,2,1,0:T(8,128)}, f32[128,128]{1,0:T(8,128)S(1)}, f32[128,128]{1,0:T(8,128)S(1)}, f32[128,128]{1,0:T(8,128)S(1)}, f32[128,128]{1,0:T(8,128)S(1)}) custom-call(f32[32,128]{1,0:T(8,128)S(1)} %get-tuple-element.34.refs_0_, f32[32,128]{1,0:T(8,128)S(1)} %collective-permute-done.6.refs_1_, ...), custom_call_target="tpu_custom_call" | custom-call | flops 4400000000 | bytes 14400000 | tf_op jit(solution)/shard_map/pallas_call | solution.py:167
  59.0 5.4 %all-to-all-start.3 = ((f32[32,4,8,128]{3,2,1,0:T(8,128)}), f32[32,4,8,128]{3,2,1,0:T(8,128)S(1)}, u32[]{:S(2)}, u32[]{:S(2)}) async-start(f32[32,4,8,128]{3,2,1,0:T(8,128)} %get-tuple-element.42), calls=%async_computation.3 | async-start | bytes 1048576 | tf_op jit(solution)/shard_map/all_to_all | solution.py:697
  64.3 1.8 %collective-permute-start.12 = (f32[4,8,256]{2,1,0:T(8,128)S(1)}, f32[4,8,256]{2,1,0:T(8,128)S(1)}, u32[]{:S(2)}, u32[]{:S(2)}) collective-permute-start(f32[4,8,256]{2,1,0:T(8,128)S(1)} %get-tuple-element.43), channel_id=1, source_target_pairs={{1,0},{0,1},{17,16},{16,17},{3,2},{2,3},{19,18},{18,19},{5,4},{4,5... | collective-permute-start | bytes 98312 | tf_op jit(solution)/shard_map/ppermute | solution.py:568
  66.5 4.4 %collective-permute-done.12 = f32[4,8,256]{2,1,0:T(8,128)S(1)} collective-permute-done((f32[4,8,256]{2,1,0:T(8,128)S(1)}, f32[4,8,256]{2,1,0:T(8,128)S(1)}, u32[]{:S(2)}, u32[]{:S(2)}) %collective-permute-start.12) | collective-permute-done | bytes 32800 | tf_op jit(solution)/shard_map/ppermute | solution.py:568
  70.9 10.2 %all-to-all-done.3 = f32[32,4,8,128]{3,2,1,0:T(8,128)S(1)} async-done(((f32[32,4,8,128]{3,2,1,0:T(8,128)}), f32[32,4,8,128]{3,2,1,0:T(8,128)S(1)}, u32[]{:S(2)}, u32[]{:S(2)}) %all-to-all-start.3) | async-done | bytes 524320 | tf_op jit(solution)/shard_map/all_to_all | solution.py:697
  81.2 1.7 %shard_map.165 = (f32[32,16,128]{2,1,0:T(8,128)}, f32[8,16,256]{2,1,0:T(8,128)}) custom-call(f32[1024,128]{1,0:T(8,128)S(1)} %bitcast.25, f32[32,256]{1,0:T(8,128)S(1)} %bitcast.34, f32[32,256]{1,0:T(8,128)S(1)} %bitcast.31, f32[32,256]{1,0:T(8,128)S(1)} %bitcast.32, f32[32,256]{1,0:T(8,128)S(1)} %bitcast.33), custom_call_target="tpu_custom_call" | custom-call | flops 2200000000 | bytes 7200000 | tf_op jit(solution)/shard_map/pallas_call | solution.py:167
  82.9 2.6 %all-to-all-start.4 = ((f32[32,16,128]{2,1,0:T(8,128)}), f32[32,16,128]{2,1,0:T(8,128)S(1)}, u32[]{:S(2)}, u32[]{:S(2)}) async-start(f32[32,16,128]{2,1,0:T(8,128)} %get-tuple-element.47), calls=%async_computation.4 | async-start | bytes 524288 | tf_op jit(solution)/shard_map/all_to_all | solution.py:705
  85.5 1.7 %collective-permute-start.15 = (f32[128,128]{1,0:T(8,128)S(1)}, f32[128,128]{1,0:T(8,128)S(1)}, u32[]{:S(2)}, u32[]{:S(2)}) collective-permute-start(f32[128,128]{1,0:T(8,128)S(1)} %get-tuple-element.49), channel_id=1, source_target_pairs={{1,0},{0,1},{17,16},{16,17},{3,2},{2,3},{19,18},{18,19},{5,4},{4,5... | collective-permute-start | bytes 196616 | tf_op jit(solution)/shard_map/ppermute | solution.py:568
  87.7 4.2 %collective-permute-done.15.refs_3_ = f32[128,128]{1,0:T(8,128)S(1)} collective-permute-done((f32[128,128]{1,0:T(8,128)S(1)}, f32[128,128]{1,0:T(8,128)S(1)}, u32[]{:S(2)}, u32[]{:S(2)}) %collective-permute-start.15) | collective-permute-done | bytes 65568 | tf_op jit(solution)/shard_map/ppermute | solution.py:568
  93.0 3.7 %all-to-all-done.4 = f32[32,16,128]{2,1,0:T(8,128)S(1)} async-done(((f32[32,16,128]{2,1,0:T(8,128)}), f32[32,16,128]{2,1,0:T(8,128)S(1)}, u32[]{:S(2)}, u32[]{:S(2)}) %all-to-all-start.4) | async-done | bytes 262176 | tf_op jit(solution)/shard_map/all_to_all | solution.py:705
  (81 shorter events, 14.4 us)
Async XLA Ops:
  3.1 10.9 %copy-start = (f32[128,640]{1,0:T(8,128)S(1)}, f32[128,640]{1,0:T(8,128)}, u32[]{:S(2)}) copy-start(f32[128,640]{1,0:T(8,128)} %refs_1_.5) | copy-start | bytes 983044
  3.1 11.7 %collective-permute-start.2 = (f32[2,16,128]{2,1,0:T(8,128)}, f32[2,16,128]{2,1,0:T(8,128)S(1)}, u32[]{:S(2)}, u32[]{:S(2)}) collective-permute-start(f32[2,16,128]{2,1,0:T(8,128)} %get-tuple-element.29.refs_0_), channel_id=1, source_target_pairs={{6,0},{4,2},{2,4},{0,6},{14,8},{12,10},{10,12},{8,14},{7,1},{5,3},... | collective-permute-start | bytes 49160 | tf_op jit(solution)/shard_map/ppermute | solution.py:568
  7.1 7.7 %collective-permute-start.1 = (f32[2,16,128]{2,1,0:T(8,128)}, f32[2,16,128]{2,1,0:T(8,128)S(1)}, u32[]{:S(2)}, u32[]{:S(2)}) collective-permute-start(f32[2,16,128]{2,1,0:T(8,128)} %get-tuple-element.29.refs_0_), channel_id=1, source_target_pairs={{4,0},{6,2},{0,4},{2,6},{12,8},{14,10},{8,12},{10,14},{5,1},{7,3},... | collective-permute-start | bytes 49160 | tf_op jit(solution)/shard_map/ppermute | solution.py:568
  7.6 7.2 %collective-permute-start = (f32[2,16,128]{2,1,0:T(8,128)}, f32[2,16,128]{2,1,0:T(8,128)S(1)}, u32[]{:S(2)}, u32[]{:S(2)}) collective-permute-start(f32[2,16,128]{2,1,0:T(8,128)} %get-tuple-element.29.refs_0_), channel_id=1, source_target_pairs={{2,0},{0,2},{6,4},{4,6},{10,8},{8,10},{14,12},{12,14},{3,1},{1,3},... | collective-permute-start | bytes 49160 | tf_op jit(solution)/shard_map/ppermute | solution.py:568
  7.8 14.4 %all-to-all-start = ((f32[16,16,256]{2,1,0:T(8,128)}), f32[16,16,256]{2,1,0:T(8,128)S(1)}, u32[]{:S(2)}, u32[]{:S(2)}) async-start(f32[16,16,256]{2,1,0:T(8,128)} %get-tuple-element.28), calls=%async_computation | async-start | bytes 524288 | tf_op jit(solution)/shard_map/all_to_all | solution.py:602
  14.9 4.4 %collective-permute-start.5 = (f32[4,2,16,128]{3,2,1,0:T(8,128)S(1)}, f32[4,2,16,128]{3,2,1,0:T(8,128)S(1)}, u32[]{:S(2)}, u32[]{:S(2)}) collective-permute-start(f32[4,2,16,128]{3,2,1,0:T(8,128)S(1)} %shard_map.159.refs_1_), channel_id=1, source_target_pairs={{17,0},{16,1},{1,16},{0,17},{19,2},{18,3},{3,18},{2,19},{21,4},{20... | collective-permute-start | bytes 196616 | tf_op jit(solution)/shard_map/ppermute | solution.py:568
  14.9 4.3 %collective-permute-start.4 = (f32[4,2,16,128]{3,2,1,0:T(8,128)S(1)}, f32[4,2,16,128]{3,2,1,0:T(8,128)S(1)}, u32[]{:S(2)}, u32[]{:S(2)}) collective-permute-start(f32[4,2,16,128]{3,2,1,0:T(8,128)S(1)} %shard_map.159.refs_1_), channel_id=1, source_target_pairs={{16,0},{17,1},{0,16},{1,17},{18,2},{19,3},{2,18},{3,19},{20,4},{21... | collective-permute-start | bytes 196616 | tf_op jit(solution)/shard_map/ppermute | solution.py:568
  16.5 4.3 %collective-permute-start.3 = (f32[4,2,16,128]{3,2,1,0:T(8,128)S(1)}, f32[4,2,16,128]{3,2,1,0:T(8,128)S(1)}, u32[]{:S(2)}, u32[]{:S(2)}) collective-permute-start(f32[4,2,16,128]{3,2,1,0:T(8,128)S(1)} %shard_map.159.refs_1_), channel_id=1, source_target_pairs={{1,0},{0,1},{17,16},{16,17},{3,2},{2,3},{19,18},{18,19},{5,4},{4,5... | collective-permute-start | bytes 196616 | tf_op jit(solution)/shard_map/ppermute | solution.py:568
  25.2 10.0 %all-to-all-start.1 = ((f32[16,8,256]{2,1,0:T(8,128)}), f32[16,8,256]{2,1,0:T(8,128)S(1)}, u32[]{:S(2)}, u32[]{:S(2)}) async-start(f32[16,8,256]{2,1,0:T(8,128)} %shard_map.160), calls=%async_computation.1 | async-start | bytes 262144 | tf_op jit(solution)/shard_map/all_to_all | solution.py:621
  41.8 10.7 %all-to-all-start.2 = ((f32[8,32,128]{2,1,0:T(8,128)}), f32[8,32,128]{2,1,0:T(8,128)S(1)}, u32[]{:S(2)}, u32[]{:S(2)}) async-start(f32[8,32,128]{2,1,0:T(8,128)} %get-tuple-element.38), calls=%async_computation.2 | async-start | bytes 262144 | tf_op jit(solution)/shard_map/all_to_all | solution.py:651
  46.2 5.0 %collective-permute-start.9 = (f32[128,128]{1,0:T(8,128)S(1)}, f32[128,128]{1,0:T(8,128)S(1)}, u32[]{:S(2)}, u32[]{:S(2)}) collective-permute-start(f32[128,128]{1,0:T(8,128)S(1)} %get-tuple-element.35), channel_id=1, source_target_pairs={{1,0},{0,1},{17,16},{16,17},{3,2},{2,3},{19,18},{18,19},{5,4},{4,5... | collective-permute-start | bytes 196616 | tf_op jit(solution)/shard_map/ppermute | solution.py:568
  46.8 5.7 %collective-permute-start.10 = (f32[128,128]{1,0:T(8,128)S(1)}, f32[128,128]{1,0:T(8,128)S(1)}, u32[]{:S(2)}, u32[]{:S(2)}) collective-permute-start(f32[128,128]{1,0:T(8,128)S(1)} %get-tuple-element.36), channel_id=1, source_target_pairs={{16,0},{17,1},{0,16},{1,17},{18,2},{19,3},{2,18},{3,19},{20,4},{21... | collective-permute-start | bytes 196616 | tf_op jit(solution)/shard_map/ppermute | solution.py:568
  46.8 5.7 %collective-permute-start.11 = (f32[128,128]{1,0:T(8,128)S(1)}, f32[128,128]{1,0:T(8,128)S(1)}, u32[]{:S(2)}, u32[]{:S(2)}) collective-permute-start(f32[128,128]{1,0:T(8,128)S(1)} %get-tuple-element.37), channel_id=1, source_target_pairs={{17,0},{16,1},{1,16},{0,17},{19,2},{18,3},{3,18},{2,19},{21,4},{20... | collective-permute-start | bytes 196616 | tf_op jit(solution)/shard_map/ppermute | solution.py:568
  49.9 3.2 %collective-permute-start.8 = (f32[32,128]{1,0:T(8,128)S(1)}, f32[32,128]{1,0:T(8,128)S(1)}, u32[]{:S(2)}, u32[]{:S(2)}) collective-permute-start(f32[32,128]{1,0:T(8,128)S(1)} %get-tuple-element.34.refs_0_), channel_id=1, source_target_pairs={{17,0},{16,1},{1,16},{0,17},{19,2},{18,3},{3,18},{2,19},{21,4},{20... | collective-permute-start | bytes 49160 | tf_op jit(solution)/shard_map/ppermute | solution.py:568
  50.1 3.0 %collective-permute-start.7 = (f32[32,128]{1,0:T(8,128)S(1)}, f32[32,128]{1,0:T(8,128)S(1)}, u32[]{:S(2)}, u32[]{:S(2)}) collective-permute-start(f32[32,128]{1,0:T(8,128)S(1)} %get-tuple-element.34.refs_0_), channel_id=1, source_target_pairs={{16,0},{17,1},{0,16},{1,17},{18,2},{19,3},{2,18},{3,19},{20,4},{21... | collective-permute-start | bytes 49160 | tf_op jit(solution)/shard_map/ppermute | solution.py:568
  51.2 3.7 %collective-permute-start.6 = (f32[32,128]{1,0:T(8,128)S(1)}, f32[32,128]{1,0:T(8,128)S(1)}, u32[]{:S(2)}, u32[]{:S(2)}) collective-permute-start(f32[32,128]{1,0:T(8,128)S(1)} %get-tuple-element.34.refs_0_), channel_id=1, source_target_pairs={{1,0},{0,1},{17,16},{16,17},{3,2},{2,3},{19,18},{18,19},{5,4},{4,5... | collective-permute-start | bytes 49160 | tf_op jit(solution)/shard_map/ppermute | solution.py:568
  59.0 22.2 %all-to-all-start.3 = ((f32[32,4,8,128]{3,2,1,0:T(8,128)}), f32[32,4,8,128]{3,2,1,0:T(8,128)S(1)}, u32[]{:S(2)}, u32[]{:S(2)}) async-start(f32[32,4,8,128]{3,2,1,0:T(8,128)} %get-tuple-element.42), calls=%async_computation.3 | async-start | bytes 1048576 | tf_op jit(solution)/shard_map/all_to_all | solution.py:697
  64.3 6.6 %collective-permute-start.12 = (f32[4,8,256]{2,1,0:T(8,128)S(1)}, f32[4,8,256]{2,1,0:T(8,128)S(1)}, u32[]{:S(2)}, u32[]{:S(2)}) collective-permute-start(f32[4,8,256]{2,1,0:T(8,128)S(1)} %get-tuple-element.43), channel_id=1, source_target_pairs={{1,0},{0,1},{17,16},{16,17},{3,2},{2,3},{19,18},{18,19},{5,4},{4,5... | collective-permute-start | bytes 98312 | tf_op jit(solution)/shard_map/ppermute | solution.py:568
  66.2 4.8 %collective-permute-start.13 = (f32[4,8,256]{2,1,0:T(8,128)S(1)}, f32[4,8,256]{2,1,0:T(8,128)S(1)}, u32[]{:S(2)}, u32[]{:S(2)}) collective-permute-start(f32[4,8,256]{2,1,0:T(8,128)S(1)} %get-tuple-element.44), channel_id=1, source_target_pairs={{16,0},{17,1},{0,16},{1,17},{18,2},{19,3},{2,18},{3,19},{20,4},{21... | collective-permute-start | bytes 98312 | tf_op jit(solution)/shard_map/ppermute | solution.py:568
  66.2 4.8 %collective-permute-start.14 = (f32[4,8,256]{2,1,0:T(8,128)S(1)}, f32[4,8,256]{2,1,0:T(8,128)S(1)}, u32[]{:S(2)}, u32[]{:S(2)}) collective-permute-start(f32[4,8,256]{2,1,0:T(8,128)S(1)} %get-tuple-element.45), channel_id=1, source_target_pairs={{17,0},{16,1},{1,16},{0,17},{19,2},{18,3},{3,18},{2,19},{21,4},{20... | collective-permute-start | bytes 98312 | tf_op jit(solution)/shard_map/ppermute | solution.py:568
  82.9 13.8 %all-to-all-start.4 = ((f32[32,16,128]{2,1,0:T(8,128)}), f32[32,16,128]{2,1,0:T(8,128)S(1)}, u32[]{:S(2)}, u32[]{:S(2)}) async-start(f32[32,16,128]{2,1,0:T(8,128)} %get-tuple-element.47), calls=%async_computation.4 | async-start | bytes 524288 | tf_op jit(solution)/shard_map/all_to_all | solution.py:705
  85.5 6.4 %collective-permute-start.15 = (f32[128,128]{1,0:T(8,128)S(1)}, f32[128,128]{1,0:T(8,128)S(1)}, u32[]{:S(2)}, u32[]{:S(2)}) collective-permute-start(f32[128,128]{1,0:T(8,128)S(1)} %get-tuple-element.49), channel_id=1, source_target_pairs={{1,0},{0,1},{17,16},{16,17},{3,2},{2,3},{19,18},{18,19},{5,4},{4,5... | collective-permute-start | bytes 196616 | tf_op jit(solution)/shard_map/ppermute | solution.py:568
  87.2 4.7 %collective-permute-start.16 = (f32[128,128]{1,0:T(8,128)S(1)}, f32[128,128]{1,0:T(8,128)S(1)}, u32[]{:S(2)}, u32[]{:S(2)}) collective-permute-start(f32[128,128]{1,0:T(8,128)S(1)} %get-tuple-element.50), channel_id=1, source_target_pairs={{16,0},{17,1},{0,16},{1,17},{18,2},{19,3},{2,18},{3,19},{20,4},{21... | collective-permute-start | bytes 196616 | tf_op jit(solution)/shard_map/ppermute | solution.py:568
  87.2 5.3 %collective-permute-start.17 = (f32[128,128]{1,0:T(8,128)S(1)}, f32[128,128]{1,0:T(8,128)S(1)}, u32[]{:S(2)}, u32[]{:S(2)}) collective-permute-start(f32[128,128]{1,0:T(8,128)S(1)} %get-tuple-element.51), channel_id=1, source_target_pairs={{17,0},{16,1},{1,16},{0,17},{19,2},{18,3},{3,18},{2,19},{21,4},{20... | collective-permute-start | bytes 196616 | tf_op jit(solution)/shard_map/ppermute | solution.py:568
  (18 other events, 70.3 us)

commit v15 on v11

--- a/solution.py
+++ b/solution.py
@@ -116,7 +116,8 @@
         "bias_part_kernel": 6.0,
         "row_kernel": 4.5,
         "pair_blocks_kernel": 8.0,
-        "column_kernel": 4.5,
+        "column_kernel": 6.0,
+        "transition_kernel": 3.0,
         "msa_blocks_kernel": 0.5,
         "pair_kernel": 4.0,
         "triangle_kernel": 2.0,
@@ -163,13 +164,17 @@
     )(*[bare(operand) for operand in operands])
 
 
-def call_near(kernel, outs, *operands, scratch=()):
+def call_near(kernel, outs, *operands, scratch=(), sems=()):
     return pl.pallas_call(
         lambda *refs: kernel(lambda: None, *refs),
-        out_shape=[jax.ShapeDtypeStruct(out, jnp.float32) for out in outs],
+        out_shape=[
+            jax.ShapeDtypeStruct(out[0] if isinstance(out, list) else out, jnp.float32)
+            for out in outs
+        ],
         in_specs=[vmem] * len(operands),
-        out_specs=[vmem] * len(outs),
-        scratch_shapes=[pltpu.VMEM(shape, jnp.float32) for shape in scratch],
+        out_specs=[far if isinstance(out, list) else vmem for out in outs],
+        scratch_shapes=[pltpu.VMEM(shape, jnp.float32) for shape in scratch]
+        + [pltpu.SemaphoreType.DMA((n,)) for n in sems],
         compiler_params=params,
         cost_estimate=cost(kernel),
     )(*operands)
@@ -296,14 +301,10 @@
                 )
 
 
-def column_kernel(
-    few, heads, ready, msa_ref, gains_ref, qkvg_ref, final_ref, expand_ref, shrink_ref, sides_ref,
-    left_ref, right_ref, out_ref
-):
+def column_kernel(few, heads, ready, msa_ref, gains_ref, qkvg_ref, final_ref, out_ref):
     ready()
     count, width = msa_ref.shape
     inner = final_ref.shape[0]
-    half = sides_ref.shape[0] // 2
     first = msa_ref[...]
     projected = multiply(layer_normalise(first, gains_ref[1:2, :]), qkvg_ref[...])
     query, key, value, gate = (projected[:, k * inner : (k + 1) * inner] for k in range(4))
@@ -314,7 +315,15 @@
         holds = lax.broadcasted_iota(jnp.int32, shape, 1)
         allowed = lax.rem(asks, few) == lax.rem(holds, few)
     attended = attend(query, key, value, None, heads, allowed)
-    second = first + multiply(sigmoid(gate) * attended, final_ref[...])
+    out_ref[...] = first + multiply(sigmoid(gate) * attended, final_ref[...])
+
+
+def transition_kernel(
+    ready, msa_ref, gains_ref, expand_ref, shrink_ref, sides_ref, left_ref, right_ref, out_ref
+):
+    ready()
+    half = sides_ref.shape[0] // 2
+    second = msa_ref[...]
     expanded = multiply(layer_normalise(second, gains_ref[2:3, :]), expand_ref[...])
     third = second + multiply(jnp.maximum(expanded, 0.0), shrink_ref[...])
     out_ref[...] = third
@@ -434,10 +443,10 @@
     few, n_gi, n_cols, ready, *rest
 ):
     left_refs, pair_refs = rest[:n_cols], rest[n_cols : 2 * n_cols]
-    right_ref, gain_ref, matrix_ref, triangle_ref, tri_ref = rest[2 * n_cols : 2 * n_cols + 5]
+    right_ref, gain_ref, matrix_ref, triangle_ref, tri_far = rest[2 * n_cols : 2 * n_cols + 5]
     chunks = rest[2 * n_cols + 5 : 3 * n_cols + 5]
     rest = rest[3 * n_cols + 5 :]
-    left_ref, slots, pair_ref, first_ref = rest
+    left_ref, slots, pair_ref, first_ref, tri_ref, sems = rest
     me = column_index()
     groups_j = n_gi // n_cols
     block = pair_refs[0].shape[0]
@@ -489,15 +498,20 @@
     projected = multiply(
         triangle_ref[pl.ds(0, 4 * width), :], layer_normalise(first, gain_ref[...], axis=0)
     )
-    tri = sigmoid(projected[2 * width : 4 * width]) * projected[: 2 * width]
-    slot_count, _, each, _ = tri_ref.shape
+    slot_count, _, each, _ = tri_far.shape
+    copies = []
     for g in range(groups):
-        tri_ref[:, g] = tri[:, g * lanes : (g + 1) * lanes].reshape(slot_count, each, lanes)
+        here = slice(g * lanes, (g + 1) * lanes)
+        tri = sigmoid(projected[2 * width : 4 * width, here]) * projected[: 2 * width, here]
+        tri_ref[g] = tri.reshape(slot_count, each, lanes)
+        copies.append(pltpu.make_async_copy(tri_ref.at[g], tri_far.at[:, g], sems.at[g]))
+        copies[-1].start()
     first_ref[...] = first.T
     for k in range(n_cols):
         for o in range(groups_j):
             rows = pl.ds((me ^ k) * groups_j + o, half, stride=n_gi)
             chunks[k][pl.ds(o * half, half), :] = first_ref[rows, :]
+    wait_all(copies)
 
 
 def final_kernel(
@@ -620,19 +634,22 @@
 
     msa_first = lax.all_to_all(msa_first, everyone, 0, 0, tiled=True, axis_index_groups=halves)
     count = n_half * each
-    weights = (
+    (msa_second,) = call_near(
+        functools.partial(column_kernel, few, heads),
+        [(count, width)],
+        msa_first.reshape(count, width),
         layernorm_scales,
         vertical_qkvg_kernel,
         vertical_final_kernel,
+    )
+    left, right, alignment = call_near(
+        transition_kernel,
+        [(outer_width, count), (n_gi, outer_width, count), (count, width)],
+        msa_second,
+        layernorm_scales,
         feedforward_expand_kernel,
         feedforward_shrink_kernel,
         dyadic_sides_kernel.T,
-    )
-    left, right, alignment = call_near(
-        functools.partial(column_kernel, few, heads),
-        [(outer_width, count), (n_gi, outer_width, count), (count, width)],
-        msa_first.reshape(count, width),
-        *weights,
     )
     alignment = call_near(
         functools.partial(msa_blocks_kernel, n_branch, n_gj),
@@ -664,7 +681,7 @@
     matrix = jnp.transpose(matrix, (3, 2, 1, 0)).reshape(pair_width, -1)
     tri, *first = call_near(
         functools.partial(pair_kernel, few, n_gi, n_cols),
-        [(slots, positions // lanes, 2 * share, lanes)]
+        [[(slots, positions // lanes, 2 * share, lanes)]]
         + [(positions // n_cols, pair_width)] * n_cols,
         *left,
         *pair,
@@ -677,7 +694,9 @@
             (positions, pair_width),
             (positions, pair_width),
             (positions, pair_width),
+            (positions // lanes, slots, 2 * share, lanes),
         ],
+        sems=[positions // lanes],
     )
 
     first, gate = call_near(

time: 95 us -> 93.4 us (0.983)
  local copies, waits for them, and re-layouts: 4.14 us -> 1.58 us
    unnamed x41 -> x29, local copies, waits for them, and re-layouts: 2.12 us -> 0.88 us
    pallas_call x9 -> x10, Pallas kernels: 15.5 us -> 15.8 us  [call_near(): pl.pallas_call(lambda *refs: kernel(lambda: None, *refs), out_shape=[jax....]
  transfers between devices with their start and end apart: 23 -> 23, of which waited for: 13 -> 13; matrix products, arithmetic and copies ran while one was open for 2% -> 1% of each run, Pallas kernels for 6% -> 6%
where the time goes in v15:
time: 93.4 us; the launch traced here: 92.7 us
  starting transfers between devices  36.1 us (39%)
  waiting for transfers between devices  35.9 us (38%)
  Pallas kernels  18.2 us (19%)
  local copies, waits for them, and re-layouts  1.58 us (2%)
    ppermute x18, starting transfers between devices, trade(): lax.ppermute(blocks[k], axes, [(t ^ k, t) for t in range(n) if t ^ k < n])  16 us
    pallas_call x10, Pallas kernels, call_near(): pl.pallas_call(lambda *refs: kernel(lambda: None, *refs), out_shape=[jax....  15.8 us
    ppermute x18, waiting for transfers between devices, trade(): lax.ppermute(blocks[k], axes, [(t ^ k, t) for t in range(n) if t ^ k < n])  15.5 us
    all_to_all x1, waiting for transfers between devices, per_device(): tri = lax.all_to_all(tri, everyone, 0, 0, tiled=True)  10.2 us
    all_to_all x1, starting transfers between devices, per_device(): msa = lax.all_to_all(msa, 'gi', 0, 0, tiled=True)  6.15 us
    all_to_all x1, waiting for transfers between devices, per_device(): lax.all_to_all(msa_first, everyone, 0, 0, tiled=True, axis_index_groups=h...  3.96 us
    all_to_all x1, starting transfers between devices, per_device(): tri = lax.all_to_all(tri, everyone, 0, 0, tiled=True)  3.91 us
    all_to_all x1, starting transfers between devices, per_device(): lax.all_to_all(msa_first, everyone, 0, 0, tiled=True, axis_index_groups=h...  3.85 us
  transfers between devices with their start and end apart: 23, of which 13 were waited for; matrix products, arithmetic and copies ran while one was open for 1% of the time, Pallas kernels for 6%

profile of v15, /device:TPU:0, one launch (start us, length us, event | category | flops | bytes accessed | tf_op | source)
XLA Modules:
  0.0 92.7 jit_solution(14919914319160880305)
XLA Ops:
  0.6 2.4 %shard_map.158 = (f32[16,16,256]{2,1,0:T(8,128)}, f32[2,16,128]{2,1,0:T(8,128)}) custom-call(f32[8,16,256]{2,1,0:T(8,128)} %refs_0_.2, f32[16,32,128]{2,1,0:T(8,128)} %refs_1_.4, f32[3,128]{1,0:T(4,128)} %refs_3_.5, f32[8,128]{1,0:T(8,128)} %bitcast.44), custom_call_target="tpu_custom_call" | custom-call | flops 2200000000 | bytes 7200000 | tf_op jit(solution)/shard_map/pallas_call | solution.py:155
  3.1 4.0 %collective-permute-start.2 = (f32[2,16,128]{2,1,0:T(8,128)}, f32[2,16,128]{2,1,0:T(8,128)S(1)}, u32[]{:S(2)}, u32[]{:S(2)}) collective-permute-start(f32[2,16,128]{2,1,0:T(8,128)} %get-tuple-element.27.refs_0_), channel_id=1, source_target_pairs={{6,0},{4,2},{2,4},{0,6},{14,8},{12,10},{10,12},{8,14},{7,1},{5,3},... | collective-permute-start | bytes 49160 | tf_op jit(solution)/shard_map/ppermute | solution.py:582
  7.8 6.1 %all-to-all-start = ((f32[16,16,256]{2,1,0:T(8,128)}), f32[16,16,256]{2,1,0:T(8,128)S(1)}, u32[]{:S(2)}, u32[]{:S(2)}) async-start(f32[16,16,256]{2,1,0:T(8,128)} %get-tuple-element.26), calls=%async_computation | async-start | bytes 524288 | tf_op jit(solution)/shard_map/all_to_all | solution.py:616
  14.9 1.6 %collective-permute-start.4 = (f32[4,2,16,128]{3,2,1,0:T(8,128)S(1)}, f32[4,2,16,128]{3,2,1,0:T(8,128)S(1)}, u32[]{:S(2)}, u32[]{:S(2)}) collective-permute-start(f32[4,2,16,128]{3,2,1,0:T(8,128)S(1)} %shard_map.159.refs_1_), channel_id=1, source_target_pairs={{16,0},{17,1},{0,16},{1,17},{18,2},{19,3},{2,18},{3,19},{20,4},{21... | collective-permute-start | bytes 196616 | tf_op jit(solution)/shard_map/ppermute | solution.py:582
  17.1 2.1 %collective-permute-done.5.refs_4_ = f32[4,2,16,128]{3,2,1,0:T(8,128)S(1)} collective-permute-done((f32[4,2,16,128]{3,2,1,0:T(8,128)S(1)}, f32[4,2,16,128]{3,2,1,0:T(8,128)S(1)}, u32[]{:S(2)}, u32[]{:S(2)}) %collective-permute-start.5) | collective-permute-done | bytes 65568 | tf_op jit(solution)/shard_map/ppermute | solution.py:582
  19.2 1.5 %collective-permute-done.3.refs_2_ = f32[4,2,16,128]{3,2,1,0:T(8,128)S(1)} collective-permute-done((f32[4,2,16,128]{3,2,1,0:T(8,128)S(1)}, f32[4,2,16,128]{3,2,1,0:T(8,128)S(1)}, u32[]{:S(2)}, u32[]{:S(2)}) %collective-permute-start.3) | collective-permute-done | bytes 65568 | tf_op jit(solution)/shard_map/ppermute | solution.py:582
  22.1 3.1 %shard_map.160 = f32[16,8,256]{2,1,0:T(8,128)} custom-call(f32[16,16,256]{2,1,0:T(8,128)S(1)} %all-to-all-done.refs_0_, f32[4,2,16,128]{3,2,1,0:T(8,128)S(1)} %shard_map.159.refs_1_, f32[4,2,16,128]{3,2,1,0:T(8,128)S(1)} %collective-permute-done.3.refs_2_, f32[4,2,16,128]{3,2,1,0:T(8,128)S(1)} %collective-permute-done.4.refs_3_, ...), custom_call_target="tpu_custom_call" | custom-call | flops 4950000128 | bytes 16200000 | tf_op jit(solution)/shard_map/pallas_call | solution.py:168
  25.3 3.9 %all-to-all-start.1 = ((f32[16,8,256]{2,1,0:T(8,128)}), f32[16,8,256]{2,1,0:T(8,128)S(1)}, u32[]{:S(2)}, u32[]{:S(2)}) async-start(f32[16,8,256]{2,1,0:T(8,128)} %shard_map.160), calls=%async_computation.1 | async-start | bytes 262144 | tf_op jit(solution)/shard_map/all_to_all | solution.py:635
  29.4 2.0 %collective-permute-start.9 = (f32[128,128]{1,0:T(8,128)S(1)}, f32[128,128]{1,0:T(8,128)S(1)}, u32[]{:S(2)}, u32[]{:S(2)}) collective-permute-start(f32[128,128]{1,0:T(8,128)S(1)} %get-tuple-element.32), channel_id=1, source_target_pairs={{1,0},{0,1},{17,16},{16,17},{3,2},{2,3},{19,18},{18,19},{5,4},{4,5... | collective-permute-start | bytes 196616 | tf_op jit(solution)/shard_map/ppermute | solution.py:582
  31.4 4.0 %all-to-all-done.1 = f32[16,8,256]{2,1,0:T(8,128)S(1)} async-done(((f32[16,8,256]{2,1,0:T(8,128)}), f32[16,8,256]{2,1,0:T(8,128)S(1)}, u32[]{:S(2)}, u32[]{:S(2)}) %all-to-all-start.1) | async-done | bytes 131104 | tf_op jit(solution)/shard_map/all_to_all | solution.py:635
  35.3 2.7 %shard_map.161.refs_0_ = f32[128,256]{1,0:T(8,128)S(1)} custom-call(f32[128,256]{1,0:T(8,128)S(1)} %bitcast.28, f32[4,256]{1,0:T(4,128)S(1)} %copy-done.11, f32[256,1024]{1,0:T(8,128)S(1)} %copy-done.2, f32[256,256]{1,0:T(8,128)S(1)} %copy-done.7), custom_call_target="tpu_custom_call" | custom-call | flops 6600000000 | bytes 21600000 | tf_op jit(solution)/shard_map/pallas_call | solution.py:168
  38.0 2.2 %shard_map.162 = (f32[32,128]{1,0:T(8,128)S(1)}, f32[8,32,128]{2,1,0:T(8,128)}, f32[128,256]{1,0:T(8,128)S(1)}) custom-call(f32[128,256]{1,0:T(8,128)S(1)} %shard_map.161.refs_0_, f32[4,256]{1,0:T(4,128)S(1)} %copy-done.11, f32[256,1024]{1,0:T(8,128)S(1)} %copy-done.3, f32[1024,256]{1,0:T(8,128)S(1)} %copy-done.4, f32[64,256]{1,0:T(8,128)S(1)} %bitcast.30), custom_call_target="tpu_custom_call" | custom-call | flops 3300000000 | bytes 10800000 | tf_op jit(solution)/shard_map/pallas_call | solution.py:168
  40.2 3.5 %all-to-all-start.2 = ((f32[8,32,128]{2,1,0:T(8,128)}), f32[8,32,128]{2,1,0:T(8,128)S(1)}, u32[]{:S(2)}, u32[]{:S(2)}) async-start(f32[8,32,128]{2,1,0:T(8,128)} %get-tuple-element.35), calls=%async_computation.2 | async-start | bytes 262144 | tf_op jit(solution)/shard_map/all_to_all | solution.py:667
  48.1 1.8 %collective-permute-done.6.refs_1_ = f32[32,128]{1,0:T(8,128)S(1)} collective-permute-done((f32[32,128]{1,0:T(8,128)S(1)}, f32[32,128]{1,0:T(8,128)S(1)}, u32[]{:S(2)}, u32[]{:S(2)}) %collective-permute-start.6) | collective-permute-done | bytes 16416 | tf_op jit(solution)/shard_map/ppermute | solution.py:582
  51.1 4.1 %shard_map.164 = (f32[32,4,8,128]{3,2,1,0:T(8,128)}, f32[128,128]{1,0:T(8,128)S(1)}, f32[128,128]{1,0:T(8,128)S(1)}, f32[128,128]{1,0:T(8,128)S(1)}, f32[128,128]{1,0:T(8,128)S(1)}) custom-call(f32[32,128]{1,0:T(8,128)S(1)} %get-tuple-element.29.refs_0_, f32[32,128]{1,0:T(8,128)S(1)} %collective-permute-done.6.refs_1_, ...), custom_call_target="tpu_custom_call" | custom-call | flops 4400000000 | bytes 14400000 | tf_op jit(solution)/shard_map/pallas_call | solution.py:168
  55.1 3.9 %all-to-all-start.3 = ((f32[32,4,8,128]{3,2,1,0:T(8,128)}), f32[32,4,8,128]{3,2,1,0:T(8,128)S(1)}, u32[]{:S(2)}, u32[]{:S(2)}) async-start(f32[32,4,8,128]{3,2,1,0:T(8,128)} %get-tuple-element.36), calls=%async_computation.3 | async-start | bytes 1048576 | tf_op jit(solution)/shard_map/all_to_all | solution.py:714
  59.1 1.8 %collective-permute-start.12 = (f32[4,8,256]{2,1,0:T(8,128)S(1)}, f32[4,8,256]{2,1,0:T(8,128)S(1)}, u32[]{:S(2)}, u32[]{:S(2)}) collective-permute-start(f32[4,8,256]{2,1,0:T(8,128)S(1)} %get-tuple-element.39), channel_id=1, source_target_pairs={{1,0},{0,1},{17,16},{16,17},{3,2},{2,3},{19,18},{18,19},{5,4},{4,5... | collective-permute-start | bytes 98312 | tf_op jit(solution)/shard_map/ppermute | solution.py:582
  61.3 4.4 %collective-permute-done.12 = f32[4,8,256]{2,1,0:T(8,128)S(1)} collective-permute-done((f32[4,8,256]{2,1,0:T(8,128)S(1)}, f32[4,8,256]{2,1,0:T(8,128)S(1)}, u32[]{:S(2)}, u32[]{:S(2)}) %collective-permute-start.12) | collective-permute-done | bytes 32800 | tf_op jit(solution)/shard_map/ppermute | solution.py:582
  65.7 10.2 %all-to-all-done.3 = f32[32,4,8,128]{3,2,1,0:T(8,128)S(1)} async-done(((f32[32,4,8,128]{3,2,1,0:T(8,128)}), f32[32,4,8,128]{3,2,1,0:T(8,128)S(1)}, u32[]{:S(2)}, u32[]{:S(2)}) %all-to-all-start.3) | async-done | bytes 524320 | tf_op jit(solution)/shard_map/all_to_all | solution.py:714
  75.9 1.7 %shard_map.166 = (f32[32,16,128]{2,1,0:T(8,128)}, f32[8,16,256]{2,1,0:T(8,128)}) custom-call(f32[1024,128]{1,0:T(8,128)S(1)} %bitcast.25, f32[32,256]{1,0:T(8,128)S(1)} %bitcast.34, f32[32,256]{1,0:T(8,128)S(1)} %bitcast.31, f32[32,256]{1,0:T(8,128)S(1)} %bitcast.32, f32[32,256]{1,0:T(8,128)S(1)} %bitcast.33), custom_call_target="tpu_custom_call" | custom-call | flops 2200000000 | bytes 7200000 | tf_op jit(solution)/shard_map/pallas_call | solution.py:168
  77.6 2.6 %all-to-all-start.4 = ((f32[32,16,128]{2,1,0:T(8,128)}), f32[32,16,128]{2,1,0:T(8,128)S(1)}, u32[]{:S(2)}, u32[]{:S(2)}) async-start(f32[32,16,128]{2,1,0:T(8,128)} %get-tuple-element.43), calls=%async_computation.4 | async-start | bytes 524288 | tf_op jit(solution)/shard_map/all_to_all | solution.py:722
  80.2 1.7 %collective-permute-start.15 = (f32[128,128]{1,0:T(8,128)S(1)}, f32[128,128]{1,0:T(8,128)S(1)}, u32[]{:S(2)}, u32[]{:S(2)}) collective-permute-start(f32[128,128]{1,0:T(8,128)S(1)} %get-tuple-element.45), channel_id=1, source_target_pairs={{1,0},{0,1},{17,16},{16,17},{3,2},{2,3},{19,18},{18,19},{5,4},{4,5... | collective-permute-start | bytes 196616 | tf_op jit(solution)/shard_map/ppermute | solution.py:582
  82.4 4.2 %collective-permute-done.15.refs_3_ = f32[128,128]{1,0:T(8,128)S(1)} collective-permute-done((f32[128,128]{1,0:T(8,128)S(1)}, f32[128,128]{1,0:T(8,128)S(1)}, u32[]{:S(2)}, u32[]{:S(2)}) %collective-permute-start.15) | collective-permute-done | bytes 65568 | tf_op jit(solution)/shard_map/ppermute | solution.py:582
  87.7 3.7 %all-to-all-done.4 = f32[32,16,128]{2,1,0:T(8,128)S(1)} async-done(((f32[32,16,128]{2,1,0:T(8,128)}), f32[32,16,128]{2,1,0:T(8,128)S(1)}, u32[]{:S(2)}, u32[]{:S(2)}) %all-to-all-start.4) | async-done | bytes 262176 | tf_op jit(solution)/shard_map/all_to_all | solution.py:722
  (72 shorter events, 12.6 us)
Async XLA Ops:
  3.1 10.9 %copy-start = (f32[128,640]{1,0:T(8,128)S(1)}, f32[128,640]{1,0:T(8,128)}, u32[]{:S(2)}) copy-start(f32[128,640]{1,0:T(8,128)} %refs_1_.7) | copy-start | bytes 983044
  3.1 11.7 %collective-permute-start.2 = (f32[2,16,128]{2,1,0:T(8,128)}, f32[2,16,128]{2,1,0:T(8,128)S(1)}, u32[]{:S(2)}, u32[]{:S(2)}) collective-permute-start(f32[2,16,128]{2,1,0:T(8,128)} %get-tuple-element.27.refs_0_), channel_id=1, source_target_pairs={{6,0},{4,2},{2,4},{0,6},{14,8},{12,10},{10,12},{8,14},{7,1},{5,3},... | collective-permute-start | bytes 49160 | tf_op jit(solution)/shard_map/ppermute | solution.py:582
  7.1 7.7 %collective-permute-start.1 = (f32[2,16,128]{2,1,0:T(8,128)}, f32[2,16,128]{2,1,0:T(8,128)S(1)}, u32[]{:S(2)}, u32[]{:S(2)}) collective-permute-start(f32[2,16,128]{2,1,0:T(8,128)} %get-tuple-element.27.refs_0_), channel_id=1, source_target_pairs={{4,0},{6,2},{0,4},{2,6},{12,8},{14,10},{8,12},{10,14},{5,1},{7,3},... | collective-permute-start | bytes 49160 | tf_op jit(solution)/shard_map/ppermute | solution.py:582
  7.6 7.2 %collective-permute-start = (f32[2,16,128]{2,1,0:T(8,128)}, f32[2,16,128]{2,1,0:T(8,128)S(1)}, u32[]{:S(2)}, u32[]{:S(2)}) collective-permute-start(f32[2,16,128]{2,1,0:T(8,128)} %get-tuple-element.27.refs_0_), channel_id=1, source_target_pairs={{2,0},{0,2},{6,4},{4,6},{10,8},{8,10},{14,12},{12,14},{3,1},{1,3},... | collective-permute-start | bytes 49160 | tf_op jit(solution)/shard_map/ppermute | solution.py:582
  7.8 14.4 %all-to-all-start = ((f32[16,16,256]{2,1,0:T(8,128)}), f32[16,16,256]{2,1,0:T(8,128)S(1)}, u32[]{:S(2)}, u32[]{:S(2)}) async-start(f32[16,16,256]{2,1,0:T(8,128)} %get-tuple-element.26), calls=%async_computation | async-start | bytes 524288 | tf_op jit(solution)/shard_map/all_to_all | solution.py:616
  14.8 4.4 %collective-permute-start.5 = (f32[4,2,16,128]{3,2,1,0:T(8,128)S(1)}, f32[4,2,16,128]{3,2,1,0:T(8,128)S(1)}, u32[]{:S(2)}, u32[]{:S(2)}) collective-permute-start(f32[4,2,16,128]{3,2,1,0:T(8,128)S(1)} %shard_map.159.refs_1_), channel_id=1, source_target_pairs={{17,0},{16,1},{1,16},{0,17},{19,2},{18,3},{3,18},{2,19},{21,4},{20... | collective-permute-start | bytes 196616 | tf_op jit(solution)/shard_map/ppermute | solution.py:582
  14.9 4.3 %collective-permute-start.4 = (f32[4,2,16,128]{3,2,1,0:T(8,128)S(1)}, f32[4,2,16,128]{3,2,1,0:T(8,128)S(1)}, u32[]{:S(2)}, u32[]{:S(2)}) collective-permute-start(f32[4,2,16,128]{3,2,1,0:T(8,128)S(1)} %shard_map.159.refs_1_), channel_id=1, source_target_pairs={{16,0},{17,1},{0,16},{1,17},{18,2},{19,3},{2,18},{3,19},{20,4},{21... | collective-permute-start | bytes 196616 | tf_op jit(solution)/shard_map/ppermute | solution.py:582
  16.5 4.3 %collective-permute-start.3 = (f32[4,2,16,128]{3,2,1,0:T(8,128)S(1)}, f32[4,2,16,128]{3,2,1,0:T(8,128)S(1)}, u32[]{:S(2)}, u32[]{:S(2)}) collective-permute-start(f32[4,2,16,128]{3,2,1,0:T(8,128)S(1)} %shard_map.159.refs_1_), channel_id=1, source_target_pairs={{1,0},{0,1},{17,16},{16,17},{3,2},{2,3},{19,18},{18,19},{5,4},{4,5... | collective-permute-start | bytes 196616 | tf_op jit(solution)/shard_map/ppermute | solution.py:582
  25.3 10.0 %all-to-all-start.1 = ((f32[16,8,256]{2,1,0:T(8,128)}), f32[16,8,256]{2,1,0:T(8,128)S(1)}, u32[]{:S(2)}, u32[]{:S(2)}) async-start(f32[16,8,256]{2,1,0:T(8,128)} %shard_map.160), calls=%async_computation.1 | async-start | bytes 262144 | tf_op jit(solution)/shard_map/all_to_all | solution.py:635
  29.4 16.8 %collective-permute-start.9 = (f32[128,128]{1,0:T(8,128)S(1)}, f32[128,128]{1,0:T(8,128)S(1)}, u32[]{:S(2)}, u32[]{:S(2)}) collective-permute-start(f32[128,128]{1,0:T(8,128)S(1)} %get-tuple-element.32), channel_id=1, source_target_pairs={{1,0},{0,1},{17,16},{16,17},{3,2},{2,3},{19,18},{18,19},{5,4},{4,5... | collective-permute-start | bytes 196616 | tf_op jit(solution)/shard_map/ppermute | solution.py:582
  40.2 10.9 %all-to-all-start.2 = ((f32[8,32,128]{2,1,0:T(8,128)}), f32[8,32,128]{2,1,0:T(8,128)S(1)}, u32[]{:S(2)}, u32[]{:S(2)}) async-start(f32[8,32,128]{2,1,0:T(8,128)} %get-tuple-element.35), calls=%async_computation.2 | async-start | bytes 262144 | tf_op jit(solution)/shard_map/all_to_all | solution.py:667
  43.8 3.4 %collective-permute-start.10 = (f32[128,128]{1,0:T(8,128)S(1)}, f32[128,128]{1,0:T(8,128)S(1)}, u32[]{:S(2)}, u32[]{:S(2)}) collective-permute-start(f32[128,128]{1,0:T(8,128)S(1)} %get-tuple-element.33), channel_id=1, source_target_pairs={{16,0},{17,1},{0,16},{1,17},{18,2},{19,3},{2,18},{3,19},{20,4},{21... | collective-permute-start | bytes 196616 | tf_op jit(solution)/shard_map/ppermute | solution.py:582
  43.9 3.9 %collective-permute-start.11 = (f32[128,128]{1,0:T(8,128)S(1)}, f32[128,128]{1,0:T(8,128)S(1)}, u32[]{:S(2)}, u32[]{:S(2)}) collective-permute-start(f32[128,128]{1,0:T(8,128)S(1)} %get-tuple-element.34), channel_id=1, source_target_pairs={{17,0},{16,1},{1,16},{0,17},{19,2},{18,3},{3,18},{2,19},{21,4},{20... | collective-permute-start | bytes 196616 | tf_op jit(solution)/shard_map/ppermute | solution.py:582
  44.4 3.7 %collective-permute-start.8 = (f32[32,128]{1,0:T(8,128)S(1)}, f32[32,128]{1,0:T(8,128)S(1)}, u32[]{:S(2)}, u32[]{:S(2)}) collective-permute-start(f32[32,128]{1,0:T(8,128)S(1)} %get-tuple-element.29.refs_0_), channel_id=1, source_target_pairs={{17,0},{16,1},{1,16},{0,17},{19,2},{18,3},{3,18},{2,19},{21,4},{20... | collective-permute-start | bytes 49160 | tf_op jit(solution)/shard_map/ppermute | solution.py:582
  45.7 2.4 %collective-permute-start.7 = (f32[32,128]{1,0:T(8,128)S(1)}, f32[32,128]{1,0:T(8,128)S(1)}, u32[]{:S(2)}, u32[]{:S(2)}) collective-permute-start(f32[32,128]{1,0:T(8,128)S(1)} %get-tuple-element.29.refs_0_), channel_id=1, source_target_pairs={{16,0},{17,1},{0,16},{1,17},{18,2},{19,3},{2,18},{3,19},{20,4},{21... | collective-permute-start | bytes 49160 | tf_op jit(solution)/shard_map/ppermute | solution.py:582
  46.2 3.7 %collective-permute-start.6 = (f32[32,128]{1,0:T(8,128)S(1)}, f32[32,128]{1,0:T(8,128)S(1)}, u32[]{:S(2)}, u32[]{:S(2)}) collective-permute-start(f32[32,128]{1,0:T(8,128)S(1)} %get-tuple-element.29.refs_0_), channel_id=1, source_target_pairs={{1,0},{0,1},{17,16},{16,17},{3,2},{2,3},{19,18},{18,19},{5,4},{4,5... | collective-permute-start | bytes 49160 | tf_op jit(solution)/shard_map/ppermute | solution.py:582
  55.1 20.7 %all-to-all-start.3 = ((f32[32,4,8,128]{3,2,1,0:T(8,128)}), f32[32,4,8,128]{3,2,1,0:T(8,128)S(1)}, u32[]{:S(2)}, u32[]{:S(2)}) async-start(f32[32,4,8,128]{3,2,1,0:T(8,128)} %get-tuple-element.36), calls=%async_computation.3 | async-start | bytes 1048576 | tf_op jit(solution)/shard_map/all_to_all | solution.py:714
  59.1 6.6 %collective-permute-start.12 = (f32[4,8,256]{2,1,0:T(8,128)S(1)}, f32[4,8,256]{2,1,0:T(8,128)S(1)}, u32[]{:S(2)}, u32[]{:S(2)}) collective-permute-start(f32[4,8,256]{2,1,0:T(8,128)S(1)} %get-tuple-element.39), channel_id=1, source_target_pairs={{1,0},{0,1},{17,16},{16,17},{3,2},{2,3},{19,18},{18,19},{5,4},{4,5... | collective-permute-start | bytes 98312 | tf_op jit(solution)/shard_map/ppermute | solution.py:582
  60.9 4.7 %collective-permute-start.13 = (f32[4,8,256]{2,1,0:T(8,128)S(1)}, f32[4,8,256]{2,1,0:T(8,128)S(1)}, u32[]{:S(2)}, u32[]{:S(2)}) collective-permute-start(f32[4,8,256]{2,1,0:T(8,128)S(1)} %get-tuple-element.40), channel_id=1, source_target_pairs={{16,0},{17,1},{0,16},{1,17},{18,2},{19,3},{2,18},{3,19},{20,4},{21... | collective-permute-start | bytes 98312 | tf_op jit(solution)/shard_map/ppermute | solution.py:582
  60.9 4.7 %collective-permute-start.14 = (f32[4,8,256]{2,1,0:T(8,128)S(1)}, f32[4,8,256]{2,1,0:T(8,128)S(1)}, u32[]{:S(2)}, u32[]{:S(2)}) collective-permute-start(f32[4,8,256]{2,1,0:T(8,128)S(1)} %get-tuple-element.41), channel_id=1, source_target_pairs={{17,0},{16,1},{1,16},{0,17},{19,2},{18,3},{3,18},{2,19},{21,4},{20... | collective-permute-start | bytes 98312 | tf_op jit(solution)/shard_map/ppermute | solution.py:582
  77.6 13.8 %all-to-all-start.4 = ((f32[32,16,128]{2,1,0:T(8,128)}), f32[32,16,128]{2,1,0:T(8,128)S(1)}, u32[]{:S(2)}, u32[]{:S(2)}) async-start(f32[32,16,128]{2,1,0:T(8,128)} %get-tuple-element.43), calls=%async_computation.4 | async-start | bytes 524288 | tf_op jit(solution)/shard_map/all_to_all | solution.py:722
  80.2 6.4 %collective-permute-start.15 = (f32[128,128]{1,0:T(8,128)S(1)}, f32[128,128]{1,0:T(8,128)S(1)}, u32[]{:S(2)}, u32[]{:S(2)}) collective-permute-start(f32[128,128]{1,0:T(8,128)S(1)} %get-tuple-element.45), channel_id=1, source_target_pairs={{1,0},{0,1},{17,16},{16,17},{3,2},{2,3},{19,18},{18,19},{5,4},{4,5... | collective-permute-start | bytes 196616 | tf_op jit(solution)/shard_map/ppermute | solution.py:582
  81.9 4.7 %collective-permute-start.16 = (f32[128,128]{1,0:T(8,128)S(1)}, f32[128,128]{1,0:T(8,128)S(1)}, u32[]{:S(2)}, u32[]{:S(2)}) collective-permute-start(f32[128,128]{1,0:T(8,128)S(1)} %get-tuple-element.46), channel_id=1, source_target_pairs={{16,0},{17,1},{0,16},{1,17},{18,2},{19,3},{2,18},{3,19},{20,4},{21... | collective-permute-start | bytes 196616 | tf_op jit(solution)/shard_map/ppermute | solution.py:582
  81.9 5.3 %collective-permute-start.17 = (f32[128,128]{1,0:T(8,128)S(1)}, f32[128,128]{1,0:T(8,128)S(1)}, u32[]{:S(2)}, u32[]{:S(2)}) collective-permute-start(f32[128,128]{1,0:T(8,128)S(1)} %get-tuple-element.47), channel_id=1, source_target_pairs={{17,0},{16,1},{1,16},{0,17},{19,2},{18,3},{3,18},{2,19},{21,4},{20... | collective-permute-start | bytes 196616 | tf_op jit(solution)/shard_map/ppermute | solution.py:582
  (13 other events, 50.4 us)

commit v16 on v15

--- a/solution.py
+++ b/solution.py
@@ -45,6 +45,15 @@
         return lax.dot_general(a, b, numbers, preferred_element_type=jnp.float32)
 
     (lh, ll), (rh, rl) = split(left), split(right)
+    depth_axis = 1 if across else 0
+    if left.shape[1] == lanes:
+        both = one(
+            jnp.concatenate([lh, ll], axis=1), jnp.concatenate([rh, rh], axis=depth_axis)
+        )
+        return both + one(lh, rl)
+    if right.shape[1 - depth_axis] == lanes:
+        both = one(lh, jnp.concatenate([rh, rl], axis=1 - depth_axis))
+        return both[:, :lanes] + (both[:, lanes:] + one(ll, rh))
     return one(lh, rh) + (one(lh, rl) + one(ll, rh))
 
 

time: 93.4 us -> 92 us (0.985)
  Pallas kernels: 18.2 us -> 16.9 us
    pallas_call x10, Pallas kernels: 15.8 us -> 14.5 us  [call_near(): pl.pallas_call(lambda *refs: kernel(lambda: None, *refs), out_shape=[jax....]
where the time goes in v16:
time: 92 us; the launch traced here: 91.4 us
  starting transfers between devices  36.1 us (39%)
  waiting for transfers between devices  35.9 us (39%)
  Pallas kernels  16.9 us (18%)
  local copies, waits for them, and re-layouts  1.58 us (2%)
  between operations  0.93 us (1%)
    ppermute x18, starting transfers between devices, trade(): lax.ppermute(blocks[k], axes, [(t ^ k, t) for t in range(n) if t ^ k < n])  16 us
    ppermute x18, waiting for transfers between devices, trade(): lax.ppermute(blocks[k], axes, [(t ^ k, t) for t in range(n) if t ^ k < n])  15.4 us
    pallas_call x10, Pallas kernels, call_near(): pl.pallas_call(lambda *refs: kernel(lambda: None, *refs), out_shape=[jax....  14.5 us
    all_to_all x1, waiting for transfers between devices, per_device(): tri = lax.all_to_all(tri, everyone, 0, 0, tiled=True)  10.2 us
    all_to_all x1, starting transfers between devices, per_device(): msa = lax.all_to_all(msa, 'gi', 0, 0, tiled=True)  6.15 us
    all_to_all x1, waiting for transfers between devices, per_device(): lax.all_to_all(msa_first, everyone, 0, 0, tiled=True, axis_index_groups=h...  3.96 us
    all_to_all x1, starting transfers between devices, per_device(): tri = lax.all_to_all(tri, everyone, 0, 0, tiled=True)  3.91 us
    all_to_all x1, starting transfers between devices, per_device(): lax.all_to_all(msa_first, everyone, 0, 0, tiled=True, axis_index_groups=h...  3.85 us
  transfers between devices with their start and end apart: 23, of which 13 were waited for; matrix products, arithmetic and copies ran while one was open for 1% of the time, Pallas kernels for 6%

profile of v16, /device:TPU:0, one launch (start us, length us, event | category | flops | bytes accessed | tf_op | source)
XLA Modules:
  0.0 91.4 jit_solution(16771221568839201826)
XLA Ops:
  0.6 2.4 %shard_map.158 = (f32[16,16,256]{2,1,0:T(8,128)}, f32[2,16,128]{2,1,0:T(8,128)}) custom-call(f32[8,16,256]{2,1,0:T(8,128)} %refs_0_.2, f32[16,32,128]{2,1,0:T(8,128)} %refs_1_.4, f32[3,128]{1,0:T(4,128)} %refs_3_.5, f32[8,128]{1,0:T(8,128)} %bitcast.44), custom_call_target="tpu_custom_call" | custom-call | flops 2200000000 | bytes 7200000 | tf_op jit(solution)/shard_map/pallas_call | solution.py:164
  3.1 4.0 %collective-permute-start.2 = (f32[2,16,128]{2,1,0:T(8,128)}, f32[2,16,128]{2,1,0:T(8,128)S(1)}, u32[]{:S(2)}, u32[]{:S(2)}) collective-permute-start(f32[2,16,128]{2,1,0:T(8,128)} %get-tuple-element.27.refs_0_), channel_id=1, source_target_pairs={{6,0},{4,2},{2,4},{0,6},{14,8},{12,10},{10,12},{8,14},{7,1},{5,3},... | collective-permute-start | bytes 49160 | tf_op jit(solution)/shard_map/ppermute | solution.py:591
  7.8 6.1 %all-to-all-start = ((f32[16,16,256]{2,1,0:T(8,128)}), f32[16,16,256]{2,1,0:T(8,128)S(1)}, u32[]{:S(2)}, u32[]{:S(2)}) async-start(f32[16,16,256]{2,1,0:T(8,128)} %get-tuple-element.26), calls=%async_computation | async-start | bytes 524288 | tf_op jit(solution)/shard_map/all_to_all | solution.py:625
  14.9 1.6 %collective-permute-start.4 = (f32[4,2,16,128]{3,2,1,0:T(8,128)S(1)}, f32[4,2,16,128]{3,2,1,0:T(8,128)S(1)}, u32[]{:S(2)}, u32[]{:S(2)}) collective-permute-start(f32[4,2,16,128]{3,2,1,0:T(8,128)S(1)} %shard_map.159.refs_1_), channel_id=1, source_target_pairs={{16,0},{17,1},{0,16},{1,17},{18,2},{19,3},{2,18},{3,19},{20,4},{21... | collective-permute-start | bytes 196616 | tf_op jit(solution)/shard_map/ppermute | solution.py:591
  17.1 2.1 %collective-permute-done.5.refs_4_ = f32[4,2,16,128]{3,2,1,0:T(8,128)S(1)} collective-permute-done((f32[4,2,16,128]{3,2,1,0:T(8,128)S(1)}, f32[4,2,16,128]{3,2,1,0:T(8,128)S(1)}, u32[]{:S(2)}, u32[]{:S(2)}) %collective-permute-start.5) | collective-permute-done | bytes 65568 | tf_op jit(solution)/shard_map/ppermute | solution.py:591
  19.2 1.5 %collective-permute-done.3.refs_2_ = f32[4,2,16,128]{3,2,1,0:T(8,128)S(1)} collective-permute-done((f32[4,2,16,128]{3,2,1,0:T(8,128)S(1)}, f32[4,2,16,128]{3,2,1,0:T(8,128)S(1)}, u32[]{:S(2)}, u32[]{:S(2)}) %collective-permute-start.3) | collective-permute-done | bytes 65568 | tf_op jit(solution)/shard_map/ppermute | solution.py:591
  22.1 2.7 %shard_map.160 = f32[16,8,256]{2,1,0:T(8,128)} custom-call(f32[16,16,256]{2,1,0:T(8,128)S(1)} %all-to-all-done.refs_0_, f32[4,2,16,128]{3,2,1,0:T(8,128)S(1)} %shard_map.159.refs_1_, f32[4,2,16,128]{3,2,1,0:T(8,128)S(1)} %collective-permute-done.3.refs_2_, f32[4,2,16,128]{3,2,1,0:T(8,128)S(1)} %collective-permute-done.4.refs_3_, ...), custom_call_target="tpu_custom_call" | custom-call | flops 4950000128 | bytes 16200000 | tf_op jit(solution)/shard_map/pallas_call | solution.py:177
  24.8 3.8 %all-to-all-start.1 = ((f32[16,8,256]{2,1,0:T(8,128)}), f32[16,8,256]{2,1,0:T(8,128)S(1)}, u32[]{:S(2)}, u32[]{:S(2)}) async-start(f32[16,8,256]{2,1,0:T(8,128)} %shard_map.160), calls=%async_computation.1 | async-start | bytes 262144 | tf_op jit(solution)/shard_map/all_to_all | solution.py:644
  28.9 2.0 %collective-permute-start.9 = (f32[128,128]{1,0:T(8,128)S(1)}, f32[128,128]{1,0:T(8,128)S(1)}, u32[]{:S(2)}, u32[]{:S(2)}) collective-permute-start(f32[128,128]{1,0:T(8,128)S(1)} %get-tuple-element.32), channel_id=1, source_target_pairs={{1,0},{0,1},{17,16},{16,17},{3,2},{2,3},{19,18},{18,19},{5,4},{4,5... | collective-permute-start | bytes 196616 | tf_op jit(solution)/shard_map/ppermute | solution.py:591
  30.9 4.0 %all-to-all-done.1 = f32[16,8,256]{2,1,0:T(8,128)S(1)} async-done(((f32[16,8,256]{2,1,0:T(8,128)}), f32[16,8,256]{2,1,0:T(8,128)S(1)}, u32[]{:S(2)}, u32[]{:S(2)}) %all-to-all-start.1) | async-done | bytes 131104 | tf_op jit(solution)/shard_map/all_to_all | solution.py:644
  34.9 2.2 %shard_map.161.refs_0_ = f32[128,256]{1,0:T(8,128)S(1)} custom-call(f32[128,256]{1,0:T(8,128)S(1)} %bitcast.28, f32[4,256]{1,0:T(4,128)S(1)} %copy-done.11, f32[256,1024]{1,0:T(8,128)S(1)} %copy-done.2, f32[256,256]{1,0:T(8,128)S(1)} %copy-done.7), custom_call_target="tpu_custom_call" | custom-call | flops 6600000000 | bytes 21600000 | tf_op jit(solution)/shard_map/pallas_call | solution.py:177
  37.1 2.2 %shard_map.162 = (f32[32,128]{1,0:T(8,128)S(1)}, f32[8,32,128]{2,1,0:T(8,128)}, f32[128,256]{1,0:T(8,128)S(1)}) custom-call(f32[128,256]{1,0:T(8,128)S(1)} %shard_map.161.refs_0_, f32[4,256]{1,0:T(4,128)S(1)} %copy-done.11, f32[256,1024]{1,0:T(8,128)S(1)} %copy-done.3, f32[1024,256]{1,0:T(8,128)S(1)} %copy-done.4, f32[64,256]{1,0:T(8,128)S(1)} %bitcast.30), custom_call_target="tpu_custom_call" | custom-call | flops 3300000000 | bytes 10800000 | tf_op jit(solution)/shard_map/pallas_call | solution.py:177
  39.3 3.5 %all-to-all-start.2 = ((f32[8,32,128]{2,1,0:T(8,128)}), f32[8,32,128]{2,1,0:T(8,128)S(1)}, u32[]{:S(2)}, u32[]{:S(2)}) async-start(f32[8,32,128]{2,1,0:T(8,128)} %get-tuple-element.35), calls=%async_computation.2 | async-start | bytes 262144 | tf_op jit(solution)/shard_map/all_to_all | solution.py:676
  47.2 1.8 %collective-permute-done.6.refs_1_ = f32[32,128]{1,0:T(8,128)S(1)} collective-permute-done((f32[32,128]{1,0:T(8,128)S(1)}, f32[32,128]{1,0:T(8,128)S(1)}, u32[]{:S(2)}, u32[]{:S(2)}) %collective-permute-start.6) | collective-permute-done | bytes 16416 | tf_op jit(solution)/shard_map/ppermute | solution.py:591
  50.2 3.7 %shard_map.164 = (f32[32,4,8,128]{3,2,1,0:T(8,128)}, f32[128,128]{1,0:T(8,128)S(1)}, f32[128,128]{1,0:T(8,128)S(1)}, f32[128,128]{1,0:T(8,128)S(1)}, f32[128,128]{1,0:T(8,128)S(1)}) custom-call(f32[32,128]{1,0:T(8,128)S(1)} %get-tuple-element.29.refs_0_, f32[32,128]{1,0:T(8,128)S(1)} %collective-permute-done.6.refs_1_, ...), custom_call_target="tpu_custom_call" | custom-call | flops 4400000000 | bytes 14400000 | tf_op jit(solution)/shard_map/pallas_call | solution.py:177
  53.9 3.9 %all-to-all-start.3 = ((f32[32,4,8,128]{3,2,1,0:T(8,128)}), f32[32,4,8,128]{3,2,1,0:T(8,128)S(1)}, u32[]{:S(2)}, u32[]{:S(2)}) async-start(f32[32,4,8,128]{3,2,1,0:T(8,128)} %get-tuple-element.36), calls=%async_computation.3 | async-start | bytes 1048576 | tf_op jit(solution)/shard_map/all_to_all | solution.py:723
  57.8 1.8 %collective-permute-start.12 = (f32[4,8,256]{2,1,0:T(8,128)S(1)}, f32[4,8,256]{2,1,0:T(8,128)S(1)}, u32[]{:S(2)}, u32[]{:S(2)}) collective-permute-start(f32[4,8,256]{2,1,0:T(8,128)S(1)} %get-tuple-element.39), channel_id=1, source_target_pairs={{1,0},{0,1},{17,16},{16,17},{3,2},{2,3},{19,18},{18,19},{5,4},{4,5... | collective-permute-start | bytes 98312 | tf_op jit(solution)/shard_map/ppermute | solution.py:591
  60.0 4.4 %collective-permute-done.12 = f32[4,8,256]{2,1,0:T(8,128)S(1)} collective-permute-done((f32[4,8,256]{2,1,0:T(8,128)S(1)}, f32[4,8,256]{2,1,0:T(8,128)S(1)}, u32[]{:S(2)}, u32[]{:S(2)}) %collective-permute-start.12) | collective-permute-done | bytes 32800 | tf_op jit(solution)/shard_map/ppermute | solution.py:591
  64.4 10.2 %all-to-all-done.3 = f32[32,4,8,128]{3,2,1,0:T(8,128)S(1)} async-done(((f32[32,4,8,128]{3,2,1,0:T(8,128)}), f32[32,4,8,128]{3,2,1,0:T(8,128)S(1)}, u32[]{:S(2)}, u32[]{:S(2)}) %all-to-all-start.3) | async-done | bytes 524320 | tf_op jit(solution)/shard_map/all_to_all | solution.py:723
  74.6 1.7 %shard_map.166 = (f32[32,16,128]{2,1,0:T(8,128)}, f32[8,16,256]{2,1,0:T(8,128)}) custom-call(f32[1024,128]{1,0:T(8,128)S(1)} %bitcast.25, f32[32,256]{1,0:T(8,128)S(1)} %bitcast.34, f32[32,256]{1,0:T(8,128)S(1)} %bitcast.31, f32[32,256]{1,0:T(8,128)S(1)} %bitcast.32, f32[32,256]{1,0:T(8,128)S(1)} %bitcast.33), custom_call_target="tpu_custom_call" | custom-call | flops 2200000000 | bytes 7200000 | tf_op jit(solution)/shard_map/pallas_call | solution.py:177
  76.3 2.6 %all-to-all-start.4 = ((f32[32,16,128]{2,1,0:T(8,128)}), f32[32,16,128]{2,1,0:T(8,128)S(1)}, u32[]{:S(2)}, u32[]{:S(2)}) async-start(f32[32,16,128]{2,1,0:T(8,128)} %get-tuple-element.43), calls=%async_computation.4 | async-start | bytes 524288 | tf_op jit(solution)/shard_map/all_to_all | solution.py:731
  78.9 1.7 %collective-permute-start.15 = (f32[128,128]{1,0:T(8,128)S(1)}, f32[128,128]{1,0:T(8,128)S(1)}, u32[]{:S(2)}, u32[]{:S(2)}) collective-permute-start(f32[128,128]{1,0:T(8,128)S(1)} %get-tuple-element.45), channel_id=1, source_target_pairs={{1,0},{0,1},{17,16},{16,17},{3,2},{2,3},{19,18},{18,19},{5,4},{4,5... | collective-permute-start | bytes 196616 | tf_op jit(solution)/shard_map/ppermute | solution.py:591
  81.1 4.2 %collective-permute-done.15.refs_3_ = f32[128,128]{1,0:T(8,128)S(1)} collective-permute-done((f32[128,128]{1,0:T(8,128)S(1)}, f32[128,128]{1,0:T(8,128)S(1)}, u32[]{:S(2)}, u32[]{:S(2)}) %collective-permute-start.15) | collective-permute-done | bytes 65568 | tf_op jit(solution)/shard_map/ppermute | solution.py:591
  86.4 3.7 %all-to-all-done.4 = f32[32,16,128]{2,1,0:T(8,128)S(1)} async-done(((f32[32,16,128]{2,1,0:T(8,128)}), f32[32,16,128]{2,1,0:T(8,128)S(1)}, u32[]{:S(2)}, u32[]{:S(2)}) %all-to-all-start.4) | async-done | bytes 262176 | tf_op jit(solution)/shard_map/all_to_all | solution.py:731
  (72 shorter events, 12.6 us)
Async XLA Ops:
  3.1 10.9 %copy-start = (f32[128,640]{1,0:T(8,128)S(1)}, f32[128,640]{1,0:T(8,128)}, u32[]{:S(2)}) copy-start(f32[128,640]{1,0:T(8,128)} %refs_1_.7) | copy-start | bytes 983044
  3.1 11.7 %collective-permute-start.2 = (f32[2,16,128]{2,1,0:T(8,128)}, f32[2,16,128]{2,1,0:T(8,128)S(1)}, u32[]{:S(2)}, u32[]{:S(2)}) collective-permute-start(f32[2,16,128]{2,1,0:T(8,128)} %get-tuple-element.27.refs_0_), channel_id=1, source_target_pairs={{6,0},{4,2},{2,4},{0,6},{14,8},{12,10},{10,12},{8,14},{7,1},{5,3},... | collective-permute-start | bytes 49160 | tf_op jit(solution)/shard_map/ppermute | solution.py:591
  7.1 7.7 %collective-permute-start.1 = (f32[2,16,128]{2,1,0:T(8,128)}, f32[2,16,128]{2,1,0:T(8,128)S(1)}, u32[]{:S(2)}, u32[]{:S(2)}) collective-permute-start(f32[2,16,128]{2,1,0:T(8,128)} %get-tuple-element.27.refs_0_), channel_id=1, source_target_pairs={{4,0},{6,2},{0,4},{2,6},{12,8},{14,10},{8,12},{10,14},{5,1},{7,3},... | collective-permute-start | bytes 49160 | tf_op jit(solution)/shard_map/ppermute | solution.py:591
  7.6 7.2 %collective-permute-start = (f32[2,16,128]{2,1,0:T(8,128)}, f32[2,16,128]{2,1,0:T(8,128)S(1)}, u32[]{:S(2)}, u32[]{:S(2)}) collective-permute-start(f32[2,16,128]{2,1,0:T(8,128)} %get-tuple-element.27.refs_0_), channel_id=1, source_target_pairs={{2,0},{0,2},{6,4},{4,6},{10,8},{8,10},{14,12},{12,14},{3,1},{1,3},... | collective-permute-start | bytes 49160 | tf_op jit(solution)/shard_map/ppermute | solution.py:591
  7.8 14.4 %all-to-all-start = ((f32[16,16,256]{2,1,0:T(8,128)}), f32[16,16,256]{2,1,0:T(8,128)S(1)}, u32[]{:S(2)}, u32[]{:S(2)}) async-start(f32[16,16,256]{2,1,0:T(8,128)} %get-tuple-element.26), calls=%async_computation | async-start | bytes 524288 | tf_op jit(solution)/shard_map/all_to_all | solution.py:625
  14.8 4.4 %collective-permute-start.5 = (f32[4,2,16,128]{3,2,1,0:T(8,128)S(1)}, f32[4,2,16,128]{3,2,1,0:T(8,128)S(1)}, u32[]{:S(2)}, u32[]{:S(2)}) collective-permute-start(f32[4,2,16,128]{3,2,1,0:T(8,128)S(1)} %shard_map.159.refs_1_), channel_id=1, source_target_pairs={{17,0},{16,1},{1,16},{0,17},{19,2},{18,3},{3,18},{2,19},{21,4},{20... | collective-permute-start | bytes 196616 | tf_op jit(solution)/shard_map/ppermute | solution.py:591
  14.9 4.3 %collective-permute-start.4 = (f32[4,2,16,128]{3,2,1,0:T(8,128)S(1)}, f32[4,2,16,128]{3,2,1,0:T(8,128)S(1)}, u32[]{:S(2)}, u32[]{:S(2)}) collective-permute-start(f32[4,2,16,128]{3,2,1,0:T(8,128)S(1)} %shard_map.159.refs_1_), channel_id=1, source_target_pairs={{16,0},{17,1},{0,16},{1,17},{18,2},{19,3},{2,18},{3,19},{20,4},{21... | collective-permute-start | bytes 196616 | tf_op jit(solution)/shard_map/ppermute | solution.py:591
  16.5 4.3 %collective-permute-start.3 = (f32[4,2,16,128]{3,2,1,0:T(8,128)S(1)}, f32[4,2,16,128]{3,2,1,0:T(8,128)S(1)}, u32[]{:S(2)}, u32[]{:S(2)}) collective-permute-start(f32[4,2,16,128]{3,2,1,0:T(8,128)S(1)} %shard_map.159.refs_1_), channel_id=1, source_target_pairs={{1,0},{0,1},{17,16},{16,17},{3,2},{2,3},{19,18},{18,19},{5,4},{4,5... | collective-permute-start | bytes 196616 | tf_op jit(solution)/shard_map/ppermute | solution.py:591
  24.8 10.0 %all-to-all-start.1 = ((f32[16,8,256]{2,1,0:T(8,128)}), f32[16,8,256]{2,1,0:T(8,128)S(1)}, u32[]{:S(2)}, u32[]{:S(2)}) async-start(f32[16,8,256]{2,1,0:T(8,128)} %shard_map.160), calls=%async_computation.1 | async-start | bytes 262144 | tf_op jit(solution)/shard_map/all_to_all | solution.py:644
  28.9 16.3 %collective-permute-start.9 = (f32[128,128]{1,0:T(8,128)S(1)}, f32[128,128]{1,0:T(8,128)S(1)}, u32[]{:S(2)}, u32[]{:S(2)}) collective-permute-start(f32[128,128]{1,0:T(8,128)S(1)} %get-tuple-element.32), channel_id=1, source_target_pairs={{1,0},{0,1},{17,16},{16,17},{3,2},{2,3},{19,18},{18,19},{5,4},{4,5... | collective-permute-start | bytes 196616 | tf_op jit(solution)/shard_map/ppermute | solution.py:591
  39.3 10.9 %all-to-all-start.2 = ((f32[8,32,128]{2,1,0:T(8,128)}), f32[8,32,128]{2,1,0:T(8,128)S(1)}, u32[]{:S(2)}, u32[]{:S(2)}) async-start(f32[8,32,128]{2,1,0:T(8,128)} %get-tuple-element.35), calls=%async_computation.2 | async-start | bytes 262144 | tf_op jit(solution)/shard_map/all_to_all | solution.py:676
  42.9 3.4 %collective-permute-start.10 = (f32[128,128]{1,0:T(8,128)S(1)}, f32[128,128]{1,0:T(8,128)S(1)}, u32[]{:S(2)}, u32[]{:S(2)}) collective-permute-start(f32[128,128]{1,0:T(8,128)S(1)} %get-tuple-element.33), channel_id=1, source_target_pairs={{16,0},{17,1},{0,16},{1,17},{18,2},{19,3},{2,18},{3,19},{20,4},{21... | collective-permute-start | bytes 196616 | tf_op jit(solution)/shard_map/ppermute | solution.py:591
  43.0 3.9 %collective-permute-start.11 = (f32[128,128]{1,0:T(8,128)S(1)}, f32[128,128]{1,0:T(8,128)S(1)}, u32[]{:S(2)}, u32[]{:S(2)}) collective-permute-start(f32[128,128]{1,0:T(8,128)S(1)} %get-tuple-element.34), channel_id=1, source_target_pairs={{17,0},{16,1},{1,16},{0,17},{19,2},{18,3},{3,18},{2,19},{21,4},{20... | collective-permute-start | bytes 196616 | tf_op jit(solution)/shard_map/ppermute | solution.py:591
  43.5 3.7 %collective-permute-start.8 = (f32[32,128]{1,0:T(8,128)S(1)}, f32[32,128]{1,0:T(8,128)S(1)}, u32[]{:S(2)}, u32[]{:S(2)}) collective-permute-start(f32[32,128]{1,0:T(8,128)S(1)} %get-tuple-element.29.refs_0_), channel_id=1, source_target_pairs={{17,0},{16,1},{1,16},{0,17},{19,2},{18,3},{3,18},{2,19},{21,4},{20... | collective-permute-start | bytes 49160 | tf_op jit(solution)/shard_map/ppermute | solution.py:591
  44.8 2.4 %collective-permute-start.7 = (f32[32,128]{1,0:T(8,128)S(1)}, f32[32,128]{1,0:T(8,128)S(1)}, u32[]{:S(2)}, u32[]{:S(2)}) collective-permute-start(f32[32,128]{1,0:T(8,128)S(1)} %get-tuple-element.29.refs_0_), channel_id=1, source_target_pairs={{16,0},{17,1},{0,16},{1,17},{18,2},{19,3},{2,18},{3,19},{20,4},{21... | collective-permute-start | bytes 49160 | tf_op jit(solution)/shard_map/ppermute | solution.py:591
  45.2 3.7 %collective-permute-start.6 = (f32[32,128]{1,0:T(8,128)S(1)}, f32[32,128]{1,0:T(8,128)S(1)}, u32[]{:S(2)}, u32[]{:S(2)}) collective-permute-start(f32[32,128]{1,0:T(8,128)S(1)} %get-tuple-element.29.refs_0_), channel_id=1, source_target_pairs={{1,0},{0,1},{17,16},{16,17},{3,2},{2,3},{19,18},{18,19},{5,4},{4,5... | collective-permute-start | bytes 49160 | tf_op jit(solution)/shard_map/ppermute | solution.py:591
  53.9 20.7 %all-to-all-start.3 = ((f32[32,4,8,128]{3,2,1,0:T(8,128)}), f32[32,4,8,128]{3,2,1,0:T(8,128)S(1)}, u32[]{:S(2)}, u32[]{:S(2)}) async-start(f32[32,4,8,128]{3,2,1,0:T(8,128)} %get-tuple-element.36), calls=%async_computation.3 | async-start | bytes 1048576 | tf_op jit(solution)/shard_map/all_to_all | solution.py:723
  57.8 6.6 %collective-permute-start.12 = (f32[4,8,256]{2,1,0:T(8,128)S(1)}, f32[4,8,256]{2,1,0:T(8,128)S(1)}, u32[]{:S(2)}, u32[]{:S(2)}) collective-permute-start(f32[4,8,256]{2,1,0:T(8,128)S(1)} %get-tuple-element.39), channel_id=1, source_target_pairs={{1,0},{0,1},{17,16},{16,17},{3,2},{2,3},{19,18},{18,19},{5,4},{4,5... | collective-permute-start | bytes 98312 | tf_op jit(solution)/shard_map/ppermute | solution.py:591
  59.6 4.7 %collective-permute-start.13 = (f32[4,8,256]{2,1,0:T(8,128)S(1)}, f32[4,8,256]{2,1,0:T(8,128)S(1)}, u32[]{:S(2)}, u32[]{:S(2)}) collective-permute-start(f32[4,8,256]{2,1,0:T(8,128)S(1)} %get-tuple-element.40), channel_id=1, source_target_pairs={{16,0},{17,1},{0,16},{1,17},{18,2},{19,3},{2,18},{3,19},{20,4},{21... | collective-permute-start | bytes 98312 | tf_op jit(solution)/shard_map/ppermute | solution.py:591
  59.7 4.7 %collective-permute-start.14 = (f32[4,8,256]{2,1,0:T(8,128)S(1)}, f32[4,8,256]{2,1,0:T(8,128)S(1)}, u32[]{:S(2)}, u32[]{:S(2)}) collective-permute-start(f32[4,8,256]{2,1,0:T(8,128)S(1)} %get-tuple-element.41), channel_id=1, source_target_pairs={{17,0},{16,1},{1,16},{0,17},{19,2},{18,3},{3,18},{2,19},{21,4},{20... | collective-permute-start | bytes 98312 | tf_op jit(solution)/shard_map/ppermute | solution.py:591
  76.3 13.8 %all-to-all-start.4 = ((f32[32,16,128]{2,1,0:T(8,128)}), f32[32,16,128]{2,1,0:T(8,128)S(1)}, u32[]{:S(2)}, u32[]{:S(2)}) async-start(f32[32,16,128]{2,1,0:T(8,128)} %get-tuple-element.43), calls=%async_computation.4 | async-start | bytes 524288 | tf_op jit(solution)/shard_map/all_to_all | solution.py:731
  78.9 6.4 %collective-permute-start.15 = (f32[128,128]{1,0:T(8,128)S(1)}, f32[128,128]{1,0:T(8,128)S(1)}, u32[]{:S(2)}, u32[]{:S(2)}) collective-permute-start(f32[128,128]{1,0:T(8,128)S(1)} %get-tuple-element.45), channel_id=1, source_target_pairs={{1,0},{0,1},{17,16},{16,17},{3,2},{2,3},{19,18},{18,19},{5,4},{4,5... | collective-permute-start | bytes 196616 | tf_op jit(solution)/shard_map/ppermute | solution.py:591
  80.6 4.7 %collective-permute-start.16 = (f32[128,128]{1,0:T(8,128)S(1)}, f32[128,128]{1,0:T(8,128)S(1)}, u32[]{:S(2)}, u32[]{:S(2)}) collective-permute-start(f32[128,128]{1,0:T(8,128)S(1)} %get-tuple-element.46), channel_id=1, source_target_pairs={{16,0},{17,1},{0,16},{1,17},{18,2},{19,3},{2,18},{3,19},{20,4},{21... | collective-permute-start | bytes 196616 | tf_op jit(solution)/shard_map/ppermute | solution.py:591
  80.6 5.3 %collective-permute-start.17 = (f32[128,128]{1,0:T(8,128)S(1)}, f32[128,128]{1,0:T(8,128)S(1)}, u32[]{:S(2)}, u32[]{:S(2)}) collective-permute-start(f32[128,128]{1,0:T(8,128)S(1)} %get-tuple-element.47), channel_id=1, source_target_pairs={{17,0},{16,1},{1,16},{0,17},{19,2},{18,3},{3,18},{2,19},{21,4},{20... | collective-permute-start | bytes 196616 | tf_op jit(solution)/shard_map/ppermute | solution.py:591
  (13 other events, 49.0 us)

commit v17 on v16

--- a/solution.py
+++ b/solution.py
@@ -44,9 +44,10 @@
     def one(a, b):
         return lax.dot_general(a, b, numbers, preferred_element_type=jnp.float32)
 
-    (lh, ll), (rh, rl) = split(left), split(right)
+    lh, ll = left if isinstance(left, tuple) else split(left)
+    rh, rl = split(right)
     depth_axis = 1 if across else 0
-    if left.shape[1] == lanes:
+    if lh.shape[1] == lanes:
         both = one(
             jnp.concatenate([lh, ll], axis=1), jnp.concatenate([rh, rh], axis=depth_axis)
         )
@@ -87,8 +88,10 @@
 def attend(query, key, value, bias, heads, allowed=None):
     count, inner = query.shape
     masks = head_masks((count, inner), heads)
-    spread = jnp.concatenate([jnp.where(m, query, 0.0) for m in masks], axis=0)
-    scores = multiply(spread, key, across=True) * (1.0 / math.sqrt(inner // heads))
+    ones = [jnp.where(m, 1.0, 0.0).astype(jnp.bfloat16) for m in masks]
+    pair = split(query * (1.0 / math.sqrt(inner // heads)))
+    spread = tuple(jnp.concatenate([half * one for one in ones], axis=0) for half in pair)
+    scores = multiply(spread, key, across=True)
     if bias is not None:
         scores = scores + bias
     if allowed is not None:
@@ -206,24 +209,30 @@
 ):
     rows = msa_far.shape[0]
     repeats = copies_far.shape[0] // rows
+    step = max(pair_far.shape[0] // 4, 1)
+    starts = range(0, pair_far.shape[0], step)
     copies = start_copies(
-        [(msa_far, msa_ref), (gains_far, gains_ref), (matrix_far, matrix_ref), (pair_far, pair_ref)],
+        [(msa_far, msa_ref), (gains_far, gains_ref), (matrix_far, matrix_ref)]
+        + [(pair_far.at[pl.ds(n, step)], pair_ref.at[pl.ds(n, step)]) for n in starts],
         sems,
     )
     residues, pair_cols, _ = pair_ref.shape
     heads = matrix_ref.shape[0]
     per = lanes // pair_cols
     ready()
-    wait_all(copies)
-    copies = start_copies(
+    wait_all(copies[:1])
+    back = start_copies(
         [(msa_ref, copies_far.at[pl.ds(n * rows, rows)]) for n in range(repeats)], out_sems
     )
-    normal = layer_normalise(pair_ref[...], gains_ref[0:1, :][None])
+    wait_all(copies[1:3])
     for i in range(residues):
-        here = multiply(matrix_ref[...], normal[i], across=True)
+        if i % step == 0:
+            wait_all([copies[3 + i // step]])
+            normal = layer_normalise(pair_ref[pl.ds(i, step)], gains_ref[0:1, :][None])
+        here = multiply(matrix_ref[...], normal[i % step], across=True)
         for h in range(heads):
             out_ref[h // per, i : i + 1, pl.ds(h % per * pair_cols, pair_cols)] = here[h : h + 1]
-    wait_all(copies)
+    wait_all(back)
 
 
 def pair_blocks_kernel(few, residues, ready, pair_ref, *rest):
@@ -620,7 +629,7 @@
             pair_norm_gains.shape,
             (heads, pair_width),
         ],
-        sems=[4, parts],
+        sems=[3 + len(range(0, residues, max(residues // 4, 1))), parts],
     )
     msa = lax.all_to_all(msa, "gi", 0, 0, tiled=True)
     (bias,) = call_near(

time: 92 us -> 92.8 us (level)
  no operation moved by 1% of the time
where the time goes in v17:
time: 92.8 us; the launch traced here: 92.2 us
  starting transfers between devices  36 us (39%)
  waiting for transfers between devices  35.9 us (39%)
  Pallas kernels  17.6 us (19%)
  local copies, waits for them, and re-layouts  1.58 us (2%)
  between operations  0.93 us (1%)
    ppermute x18, starting transfers between devices, trade(): lax.ppermute(blocks[k], axes, [(t ^ k, t) for t in range(n) if t ^ k < n])  16 us
    ppermute x18, waiting for transfers between devices, trade(): lax.ppermute(blocks[k], axes, [(t ^ k, t) for t in range(n) if t ^ k < n])  15.4 us
    pallas_call x10, Pallas kernels, call_near(): pl.pallas_call(lambda *refs: kernel(lambda: None, *refs), out_shape=[jax....  14.4 us
    all_to_all x1, waiting for transfers between devices, per_device(): tri = lax.all_to_all(tri, everyone, 0, 0, tiled=True)  10.2 us
    all_to_all x1, starting transfers between devices, per_device(): msa = lax.all_to_all(msa, 'gi', 0, 0, tiled=True)  6.15 us
    all_to_all x1, waiting for transfers between devices, per_device(): lax.all_to_all(msa_first, everyone, 0, 0, tiled=True, axis_index_groups=h...  3.96 us
    all_to_all x1, starting transfers between devices, per_device(): tri = lax.all_to_all(tri, everyone, 0, 0, tiled=True)  3.91 us
    all_to_all x1, starting transfers between devices, per_device(): lax.all_to_all(msa_first, everyone, 0, 0, tiled=True, axis_index_groups=h...  3.85 us
  transfers between devices with their start and end apart: 23, of which 13 were waited for; matrix products, arithmetic and copies ran while one was open for 1% of the time, Pallas kernels for 6%

profile of v17, /device:TPU:0, one launch (start us, length us, event | category | flops | bytes accessed | tf_op | source)
XLA Modules:
  0.0 92.2 jit_solution(2034978743230209961)
XLA Ops:
  0.6 3.2 %shard_map.158 = (f32[16,16,256]{2,1,0:T(8,128)}, f32[2,16,128]{2,1,0:T(8,128)}) custom-call(f32[8,16,256]{2,1,0:T(8,128)} %refs_0_.2, f32[16,32,128]{2,1,0:T(8,128)} %refs_1_.4, f32[3,128]{1,0:T(4,128)} %refs_3_.5, f32[8,128]{1,0:T(8,128)} %bitcast.44), custom_call_target="tpu_custom_call" | custom-call | flops 2200000000 | bytes 7200000 | tf_op jit(solution)/shard_map/pallas_call | solution.py:167
  3.9 4.0 %collective-permute-start.2 = (f32[2,16,128]{2,1,0:T(8,128)}, f32[2,16,128]{2,1,0:T(8,128)S(1)}, u32[]{:S(2)}, u32[]{:S(2)}) collective-permute-start(f32[2,16,128]{2,1,0:T(8,128)} %get-tuple-element.27.refs_0_), channel_id=1, source_target_pairs={{6,0},{4,2},{2,4},{0,6},{14,8},{12,10},{10,12},{8,14},{7,1},{5,3},... | collective-permute-start | bytes 49160 | tf_op jit(solution)/shard_map/ppermute | solution.py:600
  8.6 6.1 %all-to-all-start = ((f32[16,16,256]{2,1,0:T(8,128)}), f32[16,16,256]{2,1,0:T(8,128)S(1)}, u32[]{:S(2)}, u32[]{:S(2)}) async-start(f32[16,16,256]{2,1,0:T(8,128)} %get-tuple-element.26), calls=%async_computation | async-start | bytes 524288 | tf_op jit(solution)/shard_map/all_to_all | solution.py:634
  15.7 1.6 %collective-permute-start.4 = (f32[4,2,16,128]{3,2,1,0:T(8,128)S(1)}, f32[4,2,16,128]{3,2,1,0:T(8,128)S(1)}, u32[]{:S(2)}, u32[]{:S(2)}) collective-permute-start(f32[4,2,16,128]{3,2,1,0:T(8,128)S(1)} %shard_map.159.refs_1_), channel_id=1, source_target_pairs={{16,0},{17,1},{0,16},{1,17},{18,2},{19,3},{2,18},{3,19},{20,4},{21... | collective-permute-start | bytes 196616 | tf_op jit(solution)/shard_map/ppermute | solution.py:600
  17.9 2.1 %collective-permute-done.5.refs_4_ = f32[4,2,16,128]{3,2,1,0:T(8,128)S(1)} collective-permute-done((f32[4,2,16,128]{3,2,1,0:T(8,128)S(1)}, f32[4,2,16,128]{3,2,1,0:T(8,128)S(1)}, u32[]{:S(2)}, u32[]{:S(2)}) %collective-permute-start.5) | collective-permute-done | bytes 65568 | tf_op jit(solution)/shard_map/ppermute | solution.py:600
  20.0 1.5 %collective-permute-done.3.refs_2_ = f32[4,2,16,128]{3,2,1,0:T(8,128)S(1)} collective-permute-done((f32[4,2,16,128]{3,2,1,0:T(8,128)S(1)}, f32[4,2,16,128]{3,2,1,0:T(8,128)S(1)}, u32[]{:S(2)}, u32[]{:S(2)}) %collective-permute-start.3) | collective-permute-done | bytes 65568 | tf_op jit(solution)/shard_map/ppermute | solution.py:600
  22.9 2.7 %shard_map.160 = f32[16,8,256]{2,1,0:T(8,128)} custom-call(f32[16,16,256]{2,1,0:T(8,128)S(1)} %all-to-all-done.refs_0_, f32[4,2,16,128]{3,2,1,0:T(8,128)S(1)} %shard_map.159.refs_1_, f32[4,2,16,128]{3,2,1,0:T(8,128)S(1)} %collective-permute-done.3.refs_2_, f32[4,2,16,128]{3,2,1,0:T(8,128)S(1)} %collective-permute-done.4.refs_3_, ...), custom_call_target="tpu_custom_call" | custom-call | flops 4950000128 | bytes 16200000 | tf_op jit(solution)/shard_map/pallas_call | solution.py:180
  25.6 3.9 %all-to-all-start.1 = ((f32[16,8,256]{2,1,0:T(8,128)}), f32[16,8,256]{2,1,0:T(8,128)S(1)}, u32[]{:S(2)}, u32[]{:S(2)}) async-start(f32[16,8,256]{2,1,0:T(8,128)} %shard_map.160), calls=%async_computation.1 | async-start | bytes 262144 | tf_op jit(solution)/shard_map/all_to_all | solution.py:653
  29.7 2.0 %collective-permute-start.9 = (f32[128,128]{1,0:T(8,128)S(1)}, f32[128,128]{1,0:T(8,128)S(1)}, u32[]{:S(2)}, u32[]{:S(2)}) collective-permute-start(f32[128,128]{1,0:T(8,128)S(1)} %get-tuple-element.32), channel_id=1, source_target_pairs={{1,0},{0,1},{17,16},{16,17},{3,2},{2,3},{19,18},{18,19},{5,4},{4,5... | collective-permute-start | bytes 196616 | tf_op jit(solution)/shard_map/ppermute | solution.py:600
  31.7 4.0 %all-to-all-done.1 = f32[16,8,256]{2,1,0:T(8,128)S(1)} async-done(((f32[16,8,256]{2,1,0:T(8,128)}), f32[16,8,256]{2,1,0:T(8,128)S(1)}, u32[]{:S(2)}, u32[]{:S(2)}) %all-to-all-start.1) | async-done | bytes 131104 | tf_op jit(solution)/shard_map/all_to_all | solution.py:653
  35.7 2.2 %shard_map.161.refs_0_ = f32[128,256]{1,0:T(8,128)S(1)} custom-call(f32[128,256]{1,0:T(8,128)S(1)} %bitcast.28, f32[4,256]{1,0:T(4,128)S(1)} %copy-done.11, f32[256,1024]{1,0:T(8,128)S(1)} %copy-done.2, f32[256,256]{1,0:T(8,128)S(1)} %copy-done.7), custom_call_target="tpu_custom_call" | custom-call | flops 6600000000 | bytes 21600000 | tf_op jit(solution)/shard_map/pallas_call | solution.py:180
  37.9 2.2 %shard_map.162 = (f32[32,128]{1,0:T(8,128)S(1)}, f32[8,32,128]{2,1,0:T(8,128)}, f32[128,256]{1,0:T(8,128)S(1)}) custom-call(f32[128,256]{1,0:T(8,128)S(1)} %shard_map.161.refs_0_, f32[4,256]{1,0:T(4,128)S(1)} %copy-done.11, f32[256,1024]{1,0:T(8,128)S(1)} %copy-done.3, f32[1024,256]{1,0:T(8,128)S(1)} %copy-done.4, f32[64,256]{1,0:T(8,128)S(1)} %bitcast.30), custom_call_target="tpu_custom_call" | custom-call | flops 3300000000 | bytes 10800000 | tf_op jit(solution)/shard_map/pallas_call | solution.py:180
  40.1 3.5 %all-to-all-start.2 = ((f32[8,32,128]{2,1,0:T(8,128)}), f32[8,32,128]{2,1,0:T(8,128)S(1)}, u32[]{:S(2)}, u32[]{:S(2)}) async-start(f32[8,32,128]{2,1,0:T(8,128)} %get-tuple-element.35), calls=%async_computation.2 | async-start | bytes 262144 | tf_op jit(solution)/shard_map/all_to_all | solution.py:685
  48.0 1.8 %collective-permute-done.6.refs_1_ = f32[32,128]{1,0:T(8,128)S(1)} collective-permute-done((f32[32,128]{1,0:T(8,128)S(1)}, f32[32,128]{1,0:T(8,128)S(1)}, u32[]{:S(2)}, u32[]{:S(2)}) %collective-permute-start.6) | collective-permute-done | bytes 16416 | tf_op jit(solution)/shard_map/ppermute | solution.py:600
  50.9 3.7 %shard_map.164 = (f32[32,4,8,128]{3,2,1,0:T(8,128)}, f32[128,128]{1,0:T(8,128)S(1)}, f32[128,128]{1,0:T(8,128)S(1)}, f32[128,128]{1,0:T(8,128)S(1)}, f32[128,128]{1,0:T(8,128)S(1)}) custom-call(f32[32,128]{1,0:T(8,128)S(1)} %get-tuple-element.29.refs_0_, f32[32,128]{1,0:T(8,128)S(1)} %collective-permute-done.6.refs_1_, ...), custom_call_target="tpu_custom_call" | custom-call | flops 4400000000 | bytes 14400000 | tf_op jit(solution)/shard_map/pallas_call | solution.py:180
  54.6 3.9 %all-to-all-start.3 = ((f32[32,4,8,128]{3,2,1,0:T(8,128)}), f32[32,4,8,128]{3,2,1,0:T(8,128)S(1)}, u32[]{:S(2)}, u32[]{:S(2)}) async-start(f32[32,4,8,128]{3,2,1,0:T(8,128)} %get-tuple-element.36), calls=%async_computation.3 | async-start | bytes 1048576 | tf_op jit(solution)/shard_map/all_to_all | solution.py:732
  58.6 1.8 %collective-permute-start.12 = (f32[4,8,256]{2,1,0:T(8,128)S(1)}, f32[4,8,256]{2,1,0:T(8,128)S(1)}, u32[]{:S(2)}, u32[]{:S(2)}) collective-permute-start(f32[4,8,256]{2,1,0:T(8,128)S(1)} %get-tuple-element.39), channel_id=1, source_target_pairs={{1,0},{0,1},{17,16},{16,17},{3,2},{2,3},{19,18},{18,19},{5,4},{4,5... | collective-permute-start | bytes 98312 | tf_op jit(solution)/shard_map/ppermute | solution.py:600
  60.8 4.4 %collective-permute-done.12 = f32[4,8,256]{2,1,0:T(8,128)S(1)} collective-permute-done((f32[4,8,256]{2,1,0:T(8,128)S(1)}, f32[4,8,256]{2,1,0:T(8,128)S(1)}, u32[]{:S(2)}, u32[]{:S(2)}) %collective-permute-start.12) | collective-permute-done | bytes 32800 | tf_op jit(solution)/shard_map/ppermute | solution.py:600
  65.2 10.2 %all-to-all-done.3 = f32[32,4,8,128]{3,2,1,0:T(8,128)S(1)} async-done(((f32[32,4,8,128]{3,2,1,0:T(8,128)}), f32[32,4,8,128]{3,2,1,0:T(8,128)S(1)}, u32[]{:S(2)}, u32[]{:S(2)}) %all-to-all-start.3) | async-done | bytes 524320 | tf_op jit(solution)/shard_map/all_to_all | solution.py:732
  75.4 1.7 %shard_map.166 = (f32[32,16,128]{2,1,0:T(8,128)}, f32[8,16,256]{2,1,0:T(8,128)}) custom-call(f32[1024,128]{1,0:T(8,128)S(1)} %bitcast.25, f32[32,256]{1,0:T(8,128)S(1)} %bitcast.34, f32[32,256]{1,0:T(8,128)S(1)} %bitcast.31, f32[32,256]{1,0:T(8,128)S(1)} %bitcast.32, f32[32,256]{1,0:T(8,128)S(1)} %bitcast.33), custom_call_target="tpu_custom_call" | custom-call | flops 2200000000 | bytes 7200000 | tf_op jit(solution)/shard_map/pallas_call | solution.py:180
  77.1 2.6 %all-to-all-start.4 = ((f32[32,16,128]{2,1,0:T(8,128)}), f32[32,16,128]{2,1,0:T(8,128)S(1)}, u32[]{:S(2)}, u32[]{:S(2)}) async-start(f32[32,16,128]{2,1,0:T(8,128)} %get-tuple-element.43), calls=%async_computation.4 | async-start | bytes 524288 | tf_op jit(solution)/shard_map/all_to_all | solution.py:740
  79.6 1.7 %collective-permute-start.15 = (f32[128,128]{1,0:T(8,128)S(1)}, f32[128,128]{1,0:T(8,128)S(1)}, u32[]{:S(2)}, u32[]{:S(2)}) collective-permute-start(f32[128,128]{1,0:T(8,128)S(1)} %get-tuple-element.45), channel_id=1, source_target_pairs={{1,0},{0,1},{17,16},{16,17},{3,2},{2,3},{19,18},{18,19},{5,4},{4,5... | collective-permute-start | bytes 196616 | tf_op jit(solution)/shard_map/ppermute | solution.py:600
  81.9 4.2 %collective-permute-done.15.refs_3_ = f32[128,128]{1,0:T(8,128)S(1)} collective-permute-done((f32[128,128]{1,0:T(8,128)S(1)}, f32[128,128]{1,0:T(8,128)S(1)}, u32[]{:S(2)}, u32[]{:S(2)}) %collective-permute-start.15) | collective-permute-done | bytes 65568 | tf_op jit(solution)/shard_map/ppermute | solution.py:600
  87.2 3.7 %all-to-all-done.4 = f32[32,16,128]{2,1,0:T(8,128)S(1)} async-done(((f32[32,16,128]{2,1,0:T(8,128)}), f32[32,16,128]{2,1,0:T(8,128)S(1)}, u32[]{:S(2)}, u32[]{:S(2)}) %all-to-all-start.4) | async-done | bytes 262176 | tf_op jit(solution)/shard_map/all_to_all | solution.py:740
  (72 shorter events, 12.6 us)
Async XLA Ops:
  3.9 10.9 %copy-start = (f32[128,640]{1,0:T(8,128)S(1)}, f32[128,640]{1,0:T(8,128)}, u32[]{:S(2)}) copy-start(f32[128,640]{1,0:T(8,128)} %refs_1_.7) | copy-start | bytes 983044
  3.9 11.7 %collective-permute-start.2 = (f32[2,16,128]{2,1,0:T(8,128)}, f32[2,16,128]{2,1,0:T(8,128)S(1)}, u32[]{:S(2)}, u32[]{:S(2)}) collective-permute-start(f32[2,16,128]{2,1,0:T(8,128)} %get-tuple-element.27.refs_0_), channel_id=1, source_target_pairs={{6,0},{4,2},{2,4},{0,6},{14,8},{12,10},{10,12},{8,14},{7,1},{5,3},... | collective-permute-start | bytes 49160 | tf_op jit(solution)/shard_map/ppermute | solution.py:600
  7.9 7.7 %collective-permute-start.1 = (f32[2,16,128]{2,1,0:T(8,128)}, f32[2,16,128]{2,1,0:T(8,128)S(1)}, u32[]{:S(2)}, u32[]{:S(2)}) collective-permute-start(f32[2,16,128]{2,1,0:T(8,128)} %get-tuple-element.27.refs_0_), channel_id=1, source_target_pairs={{4,0},{6,2},{0,4},{2,6},{12,8},{14,10},{8,12},{10,14},{5,1},{7,3},... | collective-permute-start | bytes 49160 | tf_op jit(solution)/shard_map/ppermute | solution.py:600
  8.4 7.2 %collective-permute-start = (f32[2,16,128]{2,1,0:T(8,128)}, f32[2,16,128]{2,1,0:T(8,128)S(1)}, u32[]{:S(2)}, u32[]{:S(2)}) collective-permute-start(f32[2,16,128]{2,1,0:T(8,128)} %get-tuple-element.27.refs_0_), channel_id=1, source_target_pairs={{2,0},{0,2},{6,4},{4,6},{10,8},{8,10},{14,12},{12,14},{3,1},{1,3},... | collective-permute-start | bytes 49160 | tf_op jit(solution)/shard_map/ppermute | solution.py:600
  8.6 14.4 %all-to-all-start = ((f32[16,16,256]{2,1,0:T(8,128)}), f32[16,16,256]{2,1,0:T(8,128)S(1)}, u32[]{:S(2)}, u32[]{:S(2)}) async-start(f32[16,16,256]{2,1,0:T(8,128)} %get-tuple-element.26), calls=%async_computation | async-start | bytes 524288 | tf_op jit(solution)/shard_map/all_to_all | solution.py:634
  15.6 4.4 %collective-permute-start.5 = (f32[4,2,16,128]{3,2,1,0:T(8,128)S(1)}, f32[4,2,16,128]{3,2,1,0:T(8,128)S(1)}, u32[]{:S(2)}, u32[]{:S(2)}) collective-permute-start(f32[4,2,16,128]{3,2,1,0:T(8,128)S(1)} %shard_map.159.refs_1_), channel_id=1, source_target_pairs={{17,0},{16,1},{1,16},{0,17},{19,2},{18,3},{3,18},{2,19},{21,4},{20... | collective-permute-start | bytes 196616 | tf_op jit(solution)/shard_map/ppermute | solution.py:600
  15.7 4.3 %collective-permute-start.4 = (f32[4,2,16,128]{3,2,1,0:T(8,128)S(1)}, f32[4,2,16,128]{3,2,1,0:T(8,128)S(1)}, u32[]{:S(2)}, u32[]{:S(2)}) collective-permute-start(f32[4,2,16,128]{3,2,1,0:T(8,128)S(1)} %shard_map.159.refs_1_), channel_id=1, source_target_pairs={{16,0},{17,1},{0,16},{1,17},{18,2},{19,3},{2,18},{3,19},{20,4},{21... | collective-permute-start | bytes 196616 | tf_op jit(solution)/shard_map/ppermute | solution.py:600
  17.3 4.3 %collective-permute-start.3 = (f32[4,2,16,128]{3,2,1,0:T(8,128)S(1)}, f32[4,2,16,128]{3,2,1,0:T(8,128)S(1)}, u32[]{:S(2)}, u32[]{:S(2)}) collective-permute-start(f32[4,2,16,128]{3,2,1,0:T(8,128)S(1)} %shard_map.159.refs_1_), channel_id=1, source_target_pairs={{1,0},{0,1},{17,16},{16,17},{3,2},{2,3},{19,18},{18,19},{5,4},{4,5... | collective-permute-start | bytes 196616 | tf_op jit(solution)/shard_map/ppermute | solution.py:600
  25.6 10.0 %all-to-all-start.1 = ((f32[16,8,256]{2,1,0:T(8,128)}), f32[16,8,256]{2,1,0:T(8,128)S(1)}, u32[]{:S(2)}, u32[]{:S(2)}) async-start(f32[16,8,256]{2,1,0:T(8,128)} %shard_map.160), calls=%async_computation.1 | async-start | bytes 262144 | tf_op jit(solution)/shard_map/all_to_all | solution.py:653
  29.7 16.3 %collective-permute-start.9 = (f32[128,128]{1,0:T(8,128)S(1)}, f32[128,128]{1,0:T(8,128)S(1)}, u32[]{:S(2)}, u32[]{:S(2)}) collective-permute-start(f32[128,128]{1,0:T(8,128)S(1)} %get-tuple-element.32), channel_id=1, source_target_pairs={{1,0},{0,1},{17,16},{16,17},{3,2},{2,3},{19,18},{18,19},{5,4},{4,5... | collective-permute-start | bytes 196616 | tf_op jit(solution)/shard_map/ppermute | solution.py:600
  40.1 10.9 %all-to-all-start.2 = ((f32[8,32,128]{2,1,0:T(8,128)}), f32[8,32,128]{2,1,0:T(8,128)S(1)}, u32[]{:S(2)}, u32[]{:S(2)}) async-start(f32[8,32,128]{2,1,0:T(8,128)} %get-tuple-element.35), calls=%async_computation.2 | async-start | bytes 262144 | tf_op jit(solution)/shard_map/all_to_all | solution.py:685
  43.7 3.4 %collective-permute-start.10 = (f32[128,128]{1,0:T(8,128)S(1)}, f32[128,128]{1,0:T(8,128)S(1)}, u32[]{:S(2)}, u32[]{:S(2)}) collective-permute-start(f32[128,128]{1,0:T(8,128)S(1)} %get-tuple-element.33), channel_id=1, source_target_pairs={{16,0},{17,1},{0,16},{1,17},{18,2},{19,3},{2,18},{3,19},{20,4},{21... | collective-permute-start | bytes 196616 | tf_op jit(solution)/shard_map/ppermute | solution.py:600
  43.7 3.9 %collective-permute-start.11 = (f32[128,128]{1,0:T(8,128)S(1)}, f32[128,128]{1,0:T(8,128)S(1)}, u32[]{:S(2)}, u32[]{:S(2)}) collective-permute-start(f32[128,128]{1,0:T(8,128)S(1)} %get-tuple-element.34), channel_id=1, source_target_pairs={{17,0},{16,1},{1,16},{0,17},{19,2},{18,3},{3,18},{2,19},{21,4},{20... | collective-permute-start | bytes 196616 | tf_op jit(solution)/shard_map/ppermute | solution.py:600
  44.3 3.7 %collective-permute-start.8 = (f32[32,128]{1,0:T(8,128)S(1)}, f32[32,128]{1,0:T(8,128)S(1)}, u32[]{:S(2)}, u32[]{:S(2)}) collective-permute-start(f32[32,128]{1,0:T(8,128)S(1)} %get-tuple-element.29.refs_0_), channel_id=1, source_target_pairs={{17,0},{16,1},{1,16},{0,17},{19,2},{18,3},{3,18},{2,19},{21,4},{20... | collective-permute-start | bytes 49160 | tf_op jit(solution)/shard_map/ppermute | solution.py:600
  45.6 2.4 %collective-permute-start.7 = (f32[32,128]{1,0:T(8,128)S(1)}, f32[32,128]{1,0:T(8,128)S(1)}, u32[]{:S(2)}, u32[]{:S(2)}) collective-permute-start(f32[32,128]{1,0:T(8,128)S(1)} %get-tuple-element.29.refs_0_), channel_id=1, source_target_pairs={{16,0},{17,1},{0,16},{1,17},{18,2},{19,3},{2,18},{3,19},{20,4},{21... | collective-permute-start | bytes 49160 | tf_op jit(solution)/shard_map/ppermute | solution.py:600
  46.0 3.7 %collective-permute-start.6 = (f32[32,128]{1,0:T(8,128)S(1)}, f32[32,128]{1,0:T(8,128)S(1)}, u32[]{:S(2)}, u32[]{:S(2)}) collective-permute-start(f32[32,128]{1,0:T(8,128)S(1)} %get-tuple-element.29.refs_0_), channel_id=1, source_target_pairs={{1,0},{0,1},{17,16},{16,17},{3,2},{2,3},{19,18},{18,19},{5,4},{4,5... | collective-permute-start | bytes 49160 | tf_op jit(solution)/shard_map/ppermute | solution.py:600
  54.6 20.7 %all-to-all-start.3 = ((f32[32,4,8,128]{3,2,1,0:T(8,128)}), f32[32,4,8,128]{3,2,1,0:T(8,128)S(1)}, u32[]{:S(2)}, u32[]{:S(2)}) async-start(f32[32,4,8,128]{3,2,1,0:T(8,128)} %get-tuple-element.36), calls=%async_computation.3 | async-start | bytes 1048576 | tf_op jit(solution)/shard_map/all_to_all | solution.py:732
  58.6 6.6 %collective-permute-start.12 = (f32[4,8,256]{2,1,0:T(8,128)S(1)}, f32[4,8,256]{2,1,0:T(8,128)S(1)}, u32[]{:S(2)}, u32[]{:S(2)}) collective-permute-start(f32[4,8,256]{2,1,0:T(8,128)S(1)} %get-tuple-element.39), channel_id=1, source_target_pairs={{1,0},{0,1},{17,16},{16,17},{3,2},{2,3},{19,18},{18,19},{5,4},{4,5... | collective-permute-start | bytes 98312 | tf_op jit(solution)/shard_map/ppermute | solution.py:600
  60.4 4.7 %collective-permute-start.13 = (f32[4,8,256]{2,1,0:T(8,128)S(1)}, f32[4,8,256]{2,1,0:T(8,128)S(1)}, u32[]{:S(2)}, u32[]{:S(2)}) collective-permute-start(f32[4,8,256]{2,1,0:T(8,128)S(1)} %get-tuple-element.40), channel_id=1, source_target_pairs={{16,0},{17,1},{0,16},{1,17},{18,2},{19,3},{2,18},{3,19},{20,4},{21... | collective-permute-start | bytes 98312 | tf_op jit(solution)/shard_map/ppermute | solution.py:600
  60.4 4.7 %collective-permute-start.14 = (f32[4,8,256]{2,1,0:T(8,128)S(1)}, f32[4,8,256]{2,1,0:T(8,128)S(1)}, u32[]{:S(2)}, u32[]{:S(2)}) collective-permute-start(f32[4,8,256]{2,1,0:T(8,128)S(1)} %get-tuple-element.41), channel_id=1, source_target_pairs={{17,0},{16,1},{1,16},{0,17},{19,2},{18,3},{3,18},{2,19},{21,4},{20... | collective-permute-start | bytes 98312 | tf_op jit(solution)/shard_map/ppermute | solution.py:600
  77.1 13.8 %all-to-all-start.4 = ((f32[32,16,128]{2,1,0:T(8,128)}), f32[32,16,128]{2,1,0:T(8,128)S(1)}, u32[]{:S(2)}, u32[]{:S(2)}) async-start(f32[32,16,128]{2,1,0:T(8,128)} %get-tuple-element.43), calls=%async_computation.4 | async-start | bytes 524288 | tf_op jit(solution)/shard_map/all_to_all | solution.py:740
  79.6 6.4 %collective-permute-start.15 = (f32[128,128]{1,0:T(8,128)S(1)}, f32[128,128]{1,0:T(8,128)S(1)}, u32[]{:S(2)}, u32[]{:S(2)}) collective-permute-start(f32[128,128]{1,0:T(8,128)S(1)} %get-tuple-element.45), channel_id=1, source_target_pairs={{1,0},{0,1},{17,16},{16,17},{3,2},{2,3},{19,18},{18,19},{5,4},{4,5... | collective-permute-start | bytes 196616 | tf_op jit(solution)/shard_map/ppermute | solution.py:600
  81.3 4.7 %collective-permute-start.16 = (f32[128,128]{1,0:T(8,128)S(1)}, f32[128,128]{1,0:T(8,128)S(1)}, u32[]{:S(2)}, u32[]{:S(2)}) collective-permute-start(f32[128,128]{1,0:T(8,128)S(1)} %get-tuple-element.46), channel_id=1, source_target_pairs={{16,0},{17,1},{0,16},{1,17},{18,2},{19,3},{2,18},{3,19},{20,4},{21... | collective-permute-start | bytes 196616 | tf_op jit(solution)/shard_map/ppermute | solution.py:600
  81.4 5.3 %collective-permute-start.17 = (f32[128,128]{1,0:T(8,128)S(1)}, f32[128,128]{1,0:T(8,128)S(1)}, u32[]{:S(2)}, u32[]{:S(2)}) collective-permute-start(f32[128,128]{1,0:T(8,128)S(1)} %get-tuple-element.47), channel_id=1, source_target_pairs={{17,0},{16,1},{1,16},{0,17},{19,2},{18,3},{3,18},{2,19},{21,4},{20... | collective-permute-start | bytes 196616 | tf_op jit(solution)/shard_map/ppermute | solution.py:600
  (13 other events, 49.0 us)
